TPU v7x, 32 devices: a whole 2x2x4 slice. The times are simulated.
32 devices in a mesh: dp: 8 (over y, x, core), seq: 4 (over z).
Axes of the slice: x: 2, y: 2, z: 4, core: 2. Of those that a mesh axis runs over, the one named last changes fastest.
Arguments:
- tokens: bfloat16 [16, 1024, 1280], P('dp', 'seq'), may hold values from -6 to 6
- first_gain: bfloat16 [1280], P(('dp', 'seq')), may hold values from 0.25 to 1.75
- first_bias: bfloat16 [1280], P(('dp', 'seq')), may hold values from -3 to 3
- in_weight: bfloat16 [1280, 640], P(('dp', 'seq')), may hold values from -0.15625 to 0.15625
- in_bias: bfloat16 [640], P(('dp', 'seq')), may hold values from -2 to 2
- second_gain: bfloat16 [640], P(('dp', 'seq')), may hold values from 0.25 to 1.75
- second_bias: bfloat16 [640], P(('dp', 'seq')), may hold values from -3 to 3
- conv_weight: bfloat16 [640, 5, 640], P(('dp', 'seq')), may hold values from -0.109375 to 0.109375
- conv_bias: bfloat16 [640], P(('dp', 'seq')), may hold values from -2 to 2
- third_gain: bfloat16 [640], P(('dp', 'seq')), may hold values from 0.25 to 1.75
- third_bias: bfloat16 [640], P(('dp', 'seq')), may hold values from -3 to 3
- out_weight: bfloat16 [640, 1280], P(('dp', 'seq')), may hold values from -0.3125 to 0.3125
- out_bias: bfloat16 [1280], P(('dp', 'seq')), may hold values from -2 to 2
- head_weight: bfloat16 [1280, 30], P(('dp', 'seq')), may hold values from -0.25 to 0.25
- head_bias: bfloat16 [30], replicated, may hold values from -3 to 3
- residue_types: int32 [16, 1024], P('dp', 'seq'), may hold values from 0 to 29
- mask_positions: int32 [16, 153], P('dp'), may hold values from 0 to 1023, as said below
- targets: int32 [16, 153], P('dp'), may hold values from 0 to 29
Outputs:
- block_out: bfloat16 [16, 1024, 1280], P('dp', 'seq')
- input_grad: bfloat16 [16, 1024, 1280], P('dp', 'seq')
- first_gain_grad: float32 [1280], P(('dp', 'seq'))
- first_bias_grad: float32 [1280], P(('dp', 'seq'))
- in_weight_grad: float32 [1280, 640], P(('dp', 'seq'))
- in_bias_grad: float32 [640], P(('dp', 'seq'))
- second_gain_grad: float32 [640], P(('dp', 'seq'))
- second_bias_grad: float32 [640], P(('dp', 'seq'))
- conv_weight_grad: float32 [640, 5, 640], P(('dp', 'seq'))
- conv_bias_grad: float32 [640], P(('dp', 'seq'))
- third_gain_grad: float32 [640], P(('dp', 'seq'))
- third_bias_grad: float32 [640], P(('dp', 'seq'))
- out_weight_grad: float32 [640, 1280], P(('dp', 'seq'))
- out_bias_grad: float32 [1280], P(('dp', 'seq'))
- head_weight_grad: float32 [1280, 30], P(('dp', 'seq'))
- head_bias_grad: float32 [30], replicated
- type_counts: int32 [30], replicated
- type_hits: float32 [30], replicated
- mean_loss: float32 [], replicated
Inputs may be any that keep to these rules, and one draw needn't show every extreme that they name: `mask_positions`: each row holds 153 different positions of its sequence.
All inputs are finite; a program needn't handle non-finite values.
Results may differ from a plain program's by a relative error of at most 0.0075.
Values may be sent and summed in bfloat16 or wider, within the bound.
No kernel may reach another device: no remote copies, remote signals or barrier semaphores. Data moves between devices by JAX's collectives and lax.ppermute only.
A program may use at most 128 MiB of HBM per device.

v0:
```python
import jax
import jax.numpy as jnp
from jax import lax
from jax.sharding import PartitionSpec as P

KERNEL_TAPS = 5
DILATION_RATE = 128


NORM_EPSILON = 1e-05
LOSS_SCALE = 16.0


def normed(inputs, factor, offset):
    average = jnp.mean(inputs, axis=-1, keepdims=True)
    centred = inputs - average
    spread = jnp.mean(centred * centred, axis=-1, keepdims=True)
    return jax.nn.gelu(
        centred * lax.rsqrt(spread + NORM_EPSILON) * factor + offset, approximate=False
    )


def as_float(tensor):
    return tensor.astype(jnp.float32)


def matmul(former, latter):
    return jnp.dot(former, latter, preferred_element_type=jnp.float32)


def against(former, latter):
    return lax.dot_general(
        former, latter, (((former.ndim - 1,), (1,)), ((), ())), preferred_element_type=jnp.float32
    )


def outer_sum(former, latter):
    flat_former = former.reshape(-1, former.shape[-1])
    flat_latter = latter.reshape(-1, latter.shape[-1])
    return lax.dot_general(
        flat_former, flat_latter, (((0,), (0,)), ((), ())), preferred_element_type=jnp.float32
    )


def device_offset(series, offset):
    if offset == 0:
        return series
    if offset > 0:
        return jnp.concatenate([series[:, offset:], jnp.zeros_like(series[:, :offset])], axis=1)
    return jnp.concatenate([jnp.zeros_like(series[:, offset:]), series[:, :offset]], axis=1)


def stacked_taps(series, shifter, direction, spacing):
    centre_tap = KERNEL_TAPS // 2
    return jnp.concatenate(
        [
            shifter(series, direction * (kernel_index - centre_tap) * spacing)
            for kernel_index in range(KERNEL_TAPS)
        ],
        axis=2,
    )


def shards(
    tokens,
    first_gain,
    first_bias,
    in_weight,
    in_bias,
    second_gain,
    second_bias,
    conv_weight,
    conv_bias,
    third_gain,
    third_bias,
    out_weight,
    out_bias,
    head_weight,
    head_bias,
    residue_types,
    mask_positions,
    targets,
):
    gathered = (
        lax.all_gather(first_gain, ("dp", "seq"), axis=0, tiled=True),
        lax.all_gather(first_bias, ("dp", "seq"), axis=0, tiled=True),
        lax.all_gather(in_weight, ("dp", "seq"), axis=0, tiled=True),
        lax.all_gather(in_bias, ("dp", "seq"), axis=0, tiled=True),
        lax.all_gather(second_gain, ("dp", "seq"), axis=0, tiled=True),
        lax.all_gather(second_bias, ("dp", "seq"), axis=0, tiled=True),
        lax.all_gather(conv_weight, ("dp", "seq"), axis=0, tiled=True),
        lax.all_gather(conv_bias, ("dp", "seq"), axis=0, tiled=True),
        lax.all_gather(third_gain, ("dp", "seq"), axis=0, tiled=True),
        lax.all_gather(third_bias, ("dp", "seq"), axis=0, tiled=True),
        lax.all_gather(out_weight, ("dp", "seq"), axis=0, tiled=True),
        lax.all_gather(out_bias, ("dp", "seq"), axis=0, tiled=True),
        lax.all_gather(head_weight, ("dp", "seq"), axis=0, tiled=True),
    )
    (
        gain_first,
        bias_first,
        matrix_in,
        bias_in,
        gain_second,
        bias_second,
        conv_full,
        bias_conv,
        gain_third,
        bias_third,
        matrix_out,
        bias_out,
        matrix_head,
    ) = gathered
    seq_count, length, width = tokens.shape
    inner = matrix_in.shape[1]
    vocab = matrix_head.shape[1]
    rows = seq_count * length
    partition_count = lax.axis_size("seq")
    inputs = tokens.reshape(rows, width).astype(jnp.float32)
    first_value, first_pull = jax.vjp(normed, inputs, as_float(gain_first), as_float(bias_first))
    first_act = first_value.astype(jnp.bfloat16)
    in_proj = matmul(first_act, matrix_in) + as_float(bias_in)
    second_value, second_pull = jax.vjp(
        normed, in_proj, as_float(gain_second), as_float(bias_second)
    )
    conv_in = second_value.astype(jnp.bfloat16).reshape(seq_count, length, inner)
    kernel_fwd = jnp.transpose(conv_full, (1, 0, 2)).reshape(KERNEL_TAPS * inner, inner)
    kernel_back = jnp.transpose(conv_full, (1, 2, 0)).reshape(KERNEL_TAPS * inner, inner)
    conv_shift = as_float(bias_conv)
    received = lax.all_to_all(
        conv_in.reshape(seq_count, length // partition_count, partition_count, inner),
        "seq",
        split_axis=2,
        concat_axis=1,
        tiled=True,
    )
    number = received.shape[0]
    shared_rows = received.reshape(number, length, inner)
    present_taps = stacked_taps(shared_rows, device_offset, 1, DILATION_RATE // partition_count)
    result = (matmul(present_taps, kernel_fwd) + conv_shift).astype(jnp.bfloat16)
    returned = lax.all_to_all(
        result.reshape(number, length, 1, inner), "seq", split_axis=1, concat_axis=2, tiled=True
    )
    conv_out = returned.reshape(number, length, inner)
    conv_flat = conv_out.reshape(rows, inner).astype(jnp.float32)
    third_value, third_pull = jax.vjp(normed, conv_flat, as_float(gain_third), as_float(bias_third))
    third_act = third_value.astype(jnp.bfloat16)
    block_sum = inputs + matmul(third_act, matrix_out) + as_float(bias_out)
    block_out = block_sum.astype(jnp.bfloat16)
    logits = matmul(block_out, matrix_head) + as_float(head_bias)
    highest = jnp.max(logits, axis=1, keepdims=True)
    log_total = highest[:, 0] + jnp.log(jnp.sum(jnp.exp(logits - highest), axis=1))
    places = lax.axis_index("seq") * length + jnp.arange(length, dtype=jnp.int32)
    matches = mask_positions[:, None, :] == places[None, :, None]
    row_mask = jnp.sum(matches.astype(jnp.float32), axis=2).reshape(rows)
    row_target = jnp.sum(jnp.where(matches, targets[:, None, :], 0), axis=2).reshape(rows)
    vocab_ids = jnp.arange(vocab, dtype=jnp.int32)
    target_hot = (vocab_ids[None, :] == row_target[:, None]).astype(jnp.float32)
    picked = jnp.sum(logits * target_hot, axis=1)
    cross_entropy = log_total - picked
    chance = jnp.exp(picked - log_total)
    type_hot = (vocab_ids[None, :] == residue_types.reshape(rows)[:, None]).astype(jnp.float32)
    local_counts = jnp.sum(row_mask[:, None] * type_hot, axis=0)
    local_hits = jnp.sum((row_mask * chance)[:, None] * type_hot, axis=0)
    local_loss = jnp.sum(row_mask * cross_entropy)
    softmax_probs = jnp.exp(logits - log_total[:, None])
    logit_grad = (LOSS_SCALE * row_mask[:, None] * (softmax_probs - target_hot)).astype(
        jnp.bfloat16
    )
    head_shift_grad = jnp.sum(logit_grad.astype(jnp.float32), axis=0)
    head_matrix_grad = outer_sum(block_out, logit_grad)
    out_grad = against(logit_grad, matrix_head)
    out_grad_low = out_grad.astype(jnp.bfloat16)
    out_matrix_grad = outer_sum(third_act, out_grad_low)
    out_shift_grad = jnp.sum(out_grad_low.astype(jnp.float32), axis=0)
    third_act_grad = against(out_grad_low, matrix_out)
    conv_out_grad, gain_third_grad, bias_third_grad = third_pull(third_act_grad)
    conv_out_low = conv_out_grad.astype(jnp.bfloat16).reshape(seq_count, length, inner)
    conv_shift_grad = jnp.sum(conv_out_low.astype(jnp.float32), axis=(0, 1))
    received = lax.all_to_all(
        conv_out_low.reshape(seq_count, length // partition_count, partition_count, inner),
        "seq",
        split_axis=2,
        concat_axis=1,
        tiled=True,
    )
    number = received.shape[0]
    shared_gradient = received.reshape(number, length, inner)
    present_gradients = stacked_taps(
        shared_gradient, device_offset, -1, DILATION_RATE // partition_count
    )
    result = matmul(present_gradients, kernel_back).astype(jnp.bfloat16)
    returned = lax.all_to_all(
        result.reshape(number, length, 1, inner), "seq", split_axis=1, concat_axis=2, tiled=True
    )
    conv_in_grad = returned.reshape(number, length, inner)
    conv_matrix_grad = jnp.transpose(
        outer_sum(present_taps, shared_gradient).reshape(KERNEL_TAPS, inner, inner), (1, 0, 2)
    )
    second_grad = conv_in_grad.reshape(rows, inner).astype(jnp.float32)
    in_proj_grad, gain_second_grad, bias_second_grad = second_pull(second_grad)
    in_proj_low = in_proj_grad.astype(jnp.bfloat16)
    in_shift_grad = jnp.sum(in_proj_low.astype(jnp.float32), axis=0)
    in_matrix_grad = outer_sum(first_act, in_proj_low)
    first_act_grad = against(in_proj_low, matrix_in)
    branch_grad, gain_first_grad, bias_first_grad = first_pull(first_act_grad)
    input_grad = (out_grad + branch_grad).astype(jnp.bfloat16).reshape(seq_count, length, width)
    shares = (
        lax.psum_scatter(gain_first_grad, ("dp", "seq"), scatter_dimension=0, tiled=True),
        lax.psum_scatter(bias_first_grad, ("dp", "seq"), scatter_dimension=0, tiled=True),
        lax.psum_scatter(in_matrix_grad, ("dp", "seq"), scatter_dimension=0, tiled=True),
        lax.psum_scatter(in_shift_grad, ("dp", "seq"), scatter_dimension=0, tiled=True),
        lax.psum_scatter(gain_second_grad, ("dp", "seq"), scatter_dimension=0, tiled=True),
        lax.psum_scatter(bias_second_grad, ("dp", "seq"), scatter_dimension=0, tiled=True),
        lax.psum_scatter(conv_matrix_grad, ("dp", "seq"), scatter_dimension=0, tiled=True),
        lax.psum_scatter(conv_shift_grad, ("dp", "seq"), scatter_dimension=0, tiled=True),
        lax.psum_scatter(gain_third_grad, ("dp", "seq"), scatter_dimension=0, tiled=True),
        lax.psum_scatter(bias_third_grad, ("dp", "seq"), scatter_dimension=0, tiled=True),
        lax.psum_scatter(out_matrix_grad, ("dp", "seq"), scatter_dimension=0, tiled=True),
        lax.psum_scatter(out_shift_grad, ("dp", "seq"), scatter_dimension=0, tiled=True),
        lax.psum_scatter(head_matrix_grad, ("dp", "seq"), scatter_dimension=0, tiled=True),
    )
    summed_shift, summed_counts, summed_hits, summed_loss = lax.psum(
        (head_shift_grad, local_counts, local_hits, local_loss), ("dp", "seq")
    )
    masked_total = seq_count * lax.axis_size("dp") * mask_positions.shape[1]
    return (
        block_out.reshape(seq_count, length, width),
        input_grad,
        shares[0],
        shares[1],
        shares[2],
        shares[3],
        shares[4],
        shares[5],
        shares[6],
        shares[7],
        shares[8],
        shares[9],
        shares[10],
        shares[11],
        shares[12],
        summed_shift,
        summed_counts.astype(jnp.int32),
        summed_hits,
        summed_loss / masked_total,
    )


def solution(mesh):
    placed = (
        P("dp", "seq", None),
        P(("dp", "seq")),
        P(("dp", "seq")),
        P(("dp", "seq"), None),
        P(("dp", "seq")),
        P(("dp", "seq")),
        P(("dp", "seq")),
        P(("dp", "seq"), None, None),
        P(("dp", "seq")),
        P(("dp", "seq")),
        P(("dp", "seq")),
        P(("dp", "seq"), None),
        P(("dp", "seq")),
        P(("dp", "seq"), None),
        P(),
        P("dp", "seq"),
        P("dp", None),
        P("dp", None),
    )
    return jax.shard_map(
        shards,
        mesh=mesh,
        in_specs=placed,
        out_specs=(
            P("dp", "seq", None),
            P("dp", "seq", None),
            P(("dp", "seq")),
            P(("dp", "seq")),
            P(("dp", "seq"), None),
            P(("dp", "seq")),
            P(("dp", "seq")),
            P(("dp", "seq")),
            P(("dp", "seq"), None, None),
            P(("dp", "seq")),
            P(("dp", "seq")),
            P(("dp", "seq")),
            P(("dp", "seq"), None),
            P(("dp", "seq")),
            P(("dp", "seq"), None),
            P(),
            P(),
            P(),
            P(),
        ),
        check_vma=False,
    )
```

profile of v0, /device:TPU:0, one launch (start us, length us, event | category | flops | bytes accessed | tf_op | source)
XLA Modules:
  0.0 701.5 jit_solution(5701411501156812571)
XLA Ops:
  8.0 1.6 copy.68
  14.1 42.5 %all-reduce.33 = (bf16[1280]{0:T(1024)(128)(2,1)S(1)}, bf16[1280]{0:T(1024)(128)(2,1)S(1)}, bf16[640]{0:T(1024)(128)(2,1)S(1)}, bf16[640]{0:T(1024)(128)(2,1)S(1...) all-reduce(bf16[1280]{0:T(1024)(128)(2,1)S(1)} %dynamic-update-slic, ...), channel_id=1, replica_groups=mesh['dp'=8,'seq'=4] {'dp','seq'}, use_global_device_ids=true, to_apply=%add.9 | all-reduce | flops 7680 | bytes 30720
  56.6 7.7 %multiply_convert_fusion = (bf16[512,1280]{1,0:T(8,128)(2,1)}, f32[512,1280]{1,0:T(8,128)}) fusion(bf16[2,256,1280]{2,1,0:T(8,128)(2,1)S(1)} %copy-done, f32[1280]{0:T(1024)S(1)} %convert_element_type.130, f32[1280]{0:T(1024)S(1)} %convert_element_type.129, f32[512]{0:T(512)S(1)} %rsqrt.30, f32[512]{0:T(512)S(1)} %bitcast.143), kind=kLoop, calls=%fused_computation.13 | loop fusion | flops 45875200 | bytes 5257216 | tf_op jit(solution)/shard_map/convert_element_type | solution.py:121
  64.3 4.5 all-gather.6.cloned.1.call-done
  68.8 3.1 fusion.50
  72.2 4.5 multiply_convert_fusion.2
  79.2 4.2 all-to-all-start
  84.2 20.0 %all-to-all-done = bf16[2,64,4,640]{3,1,0,2:T(8,128)(2,1)} async-done(((bf16[2,64,4,640]{3,1,0,2:T(8,128)(2,1)}), bf16[2,64,4,640]{3,1,0,2:T(8,128)(2,1)}, u32[]{:S(2)}, u32[]{:S(2)}) %all-to-all-start) | async-done | bytes 655392 | tf_op jit(solution)/shard_map/all_to_all | solution.py:130
  111.5 38.3 %all-gather.8.cloned.1.call-done = bf16[640,5,640]{2,1,0:T(8,128)(2,1)} async-done(((bf16[20,5,640]{2,1,0:T(8,128)(2,1)}), bf16[640,5,640]{2,1,0:T(8,128)(2,1)}) %all-gather.8.cloned.1.call-update) | async-done | bytes 4096016 | tf_op jit(solution)/shard_map/all_gather | solution.py:91
  149.8 3.4 copy.69
  153.2 4.7 fusion.22
  159.4 4.2 all-to-all-start.1
  168.2 73.7 %all-gather.1 = bf16[32,40,30]{1,2,0:T(8,128)(2,1)S(1)} all-gather(bf16[1,40,30]{1,2,0:T(8,128)(2,1)S(1)} %bitcast.155), channel_id=1, replica_groups=mesh['dp'=8,'seq'=4] {'dp','seq'}, dimensions={0}, use_global_device_ids=true | all-gather | bytes 79200 | tf_op jit(solution)/shard_map/all_gather | solution.py:97
  243.0 3.7 reshape.308
  250.3 2.7 copy.98
  253.1 2.7 reshape.284
  255.8 4.8 multiply_convert_fusion.1
  265.2 2.5 multiply_reduce_fusion.3
  268.3 1.6 convert_reduce_fusion.2
  270.0 2.3 reshape_reshape.12
  272.3 2.0 copy.75
  274.3 4.2 all-to-all-start.2
  278.5 8.6 %all-reduce.36.cloned.1.call-start = ((), (), s32[]{:S(2)}) async-start(), calls=%async_computation.9 | async-start | bytes 16711680
  287.1 2.1 constant_dynamic-update-slice_fusion.10
  293.1 5.6 copy.80
  298.7 9.5 %copy.77 = bf16[5,640,640]{2,1,0:T(8,128)(2,1)} copy(bf16[5,640,640]{1,0,2:T(8,128)(2,1)} %bitcast.121) | data formatting | bytes 8192000 | tf_op jit(solution)/shard_map/transpose | solution.py:128
  308.2 2.3 fusion.54
  312.9 4.8 convolution_bitcast_fusion
  319.2 1.8 copy-done.9
  321.0 2.8 fusion.23
  324.5 26.9 %all_to_all.48 = bf16[2,256,1,640]{3,0,2,1:T(2,128)(2,1)S(1)} all-to-all(bf16[2,256,1,640]{3,0,2,1:T(2,128)(2,1)S(1)} %copy.78), channel_id=1, replica_groups=mesh['dp'=8,'seq'=4] {'seq'}, dimensions={1} | all-to-all | bytes 1310720 | tf_op jit(solution)/shard_map/all_to_all | solution.py:193
  351.4 1.6 copy.97
  353.0 2.7 reshape.285
  355.7 3.5 multiply_reduce_fusion.4
  361.2 2.9 fusion.53
  365.2 4.6 fusion.27
  369.7 123.6 %fusion = f32[24,1280]{1,0:T(8,128)S(1)} fusion(f32[640,1280]{1,0:T(8,128)} %fusion.27), kind=kCustom, calls=%all-reduce-scatter | all-reduce-scatter fusion | flops 983041 | bytes 3399680
  495.9 3.1 collective-permute-start.3
  499.0 5.3 collective-permute-start.2
  504.3 4.9 collective-permute-start.1
  509.3 2.7 collective-permute-start
  512.0 3.5 collective-permute-done.1
  515.5 5.3 collective-permute-done
  522.5 4.5 fusion.36
  528.8 2.1 convert_reduce_fusion
  530.9 44.1 %all-reduce.31 = (f32[1280]{0:T(1024)S(1)}, f32[1280]{0:T(1024)S(1)}, f32[640]{0:T(1024)S(1)}, f32[640]{0:T(1024)S(1)}, f32[640]{0:T(1024)S(1)}, /*index=5*/f32[...) all-reduce(f32[1280]{0:T(1024)S(1)} %get-tuple-element.19, ...), channel_id=2, replica_groups=mesh['dp'=8,'seq'=4] {'dp','seq'}, use_global_device_ids=true, to_apply=%region_17.18.clone | all-reduce | flops 7771 | bytes 62168
  582.9 1.8 constant_dynamic-slice_fusion.1
  584.7 109.0 %reduce-scatter.9.cloned.1.call-done = f32[40,640]{1,0:T(8,128)} async-done(((f32[1280,640]{1,0:T(8,128)}), f32[40,640]{1,0:T(8,128)}) %reduce-scatter.9.cloned.1.call-update) | async-done | bytes 102416
  (237 shorter events, 56.7 us)
Async XLA Ops:
  7.2 4.2 copy-start
  7.2 61.6 %all-gather.6.cloned.1.call-start = ((), (), s32[]{:S(2)}) async-start(), calls=%async_computation.5 | async-start | bytes 1689600 | tf_op jit(solution)/shard_map/all_gather | solution.py:87
  7.9 141.8 %all-gather.8.cloned.1.call-start = ((), (), s32[]{:S(2)}) async-start(), calls=%async_computation.6 | async-start | bytes 6758400 | tf_op jit(solution)/shard_map/all_gather | solution.py:91
  9.6 2.3 copy-start.44
  9.6 2.5 copy-start.45
  9.7 2.7 copy-start.46
  9.7 3.0 copy-start.47
  9.7 3.2 copy-start.48
  9.7 3.4 copy-start.49
  9.7 3.6 copy-start.50
  9.7 3.9 copy-start.51
  9.7 4.1 copy-start.52
  11.9 52.4 %copy-start.25 = (f32[1,2,2,128]{3,1,2,0:T(2,128)}, f32[1,2,2,128]{3,1,2,0:T(2,128)S(1)}, u32[]{:S(2)}) copy-start(f32[1,2,2,128]{3,1,2,0:T(2,128)S(1)} %copy.87) | copy-start | bytes 6148
  56.5 7.7 %copy-start.19 = (f32[1280]{0:T(1024)}, f32[1280]{0:T(1024)S(1)}, u32[]{:S(2)}) copy-start(f32[1280]{0:T(1024)S(1)} %convert_element_type.130) | copy-start | bytes 15364
  72.2 4.5 copy-start.22
  72.2 4.5 copy-start.17
  79.2 24.9 %all-to-all-start = ((bf16[2,64,4,640]{3,1,0,2:T(8,128)(2,1)}), bf16[2,64,4,640]{3,1,0,2:T(8,128)(2,1)}, u32[]{:S(2)}, u32[]{:S(2)}) async-start(bf16[2,64,4,640]{3,1,0,2:T(8,128)(2,1)} %copy.66), calls=%async_computation | async-start | bytes 1310720 | tf_op jit(solution)/shard_map/all_to_all | solution.py:130
  83.4 159.6 %all-gather.10.cloned.1.call-start = ((), (), s32[]{:S(2)}) async-start(), calls=%async_computation.7 | async-start | bytes 2027520 | tf_op jit(solution)/shard_map/all_gather | solution.py:95
  157.9 5.8 copy-start.53
  157.9 6.3 copy-start.40
  157.9 8.0 %copy-start.41 = (s32[2,153]{1,0:T(2,128)S(1)}, s32[2,153]{1,0:T(2,128)}, u32[]{:S(2)}) copy-start(s32[2,153]{1,0:T(2,128)} %param.34) | copy-start | bytes 3676
  157.9 9.0 %copy-start.42 = (s32[2,153]{1,0:T(2,128)S(1)}, s32[2,153]{1,0:T(2,128)}, u32[]{:S(2)}) copy-start(s32[2,153]{1,0:T(2,128)} %param.35) | copy-start | bytes 3676
  157.9 10.3 %copy-start.33 = (bf16[40,30]{0,1:T(8,128)(2,1)S(1)}, bf16[40,30]{0,1:T(8,128)(2,1)}, u32[]{:S(2)}) copy-start(bf16[40,30]{0,1:T(8,128)(2,1)} %param.31) | copy-start | bytes 7204
  159.4 87.2 %all-to-all-start.1 = ((bf16[2,256,1,640]{3,0,2,1:T(2,128)(2,1)}), bf16[2,256,1,640]{3,0,2,1:T(2,128)(2,1)}, u32[]{:S(2)}, u32[]{:S(2)}) async-start(bf16[2,256,1,640]{3,0,2,1:T(2,128)(2,1)} %copy.70), calls=%async_computation.1 | async-start | bytes 1310720 | tf_op jit(solution)/shard_map/all_to_all | solution.py:141
  253.1 2.7 copy-start.29
  255.8 4.8 copy-start.15
  255.8 4.8 copy-start.34
  261.9 2.6 copy-start.6
  264.5 3.3 copy-start.1
  274.3 36.3 %all-to-all-start.2 = ((bf16[2,64,4,640]{3,1,0,2:T(8,128)(2,1)}), bf16[2,64,4,640]{3,1,0,2:T(8,128)(2,1)}, u32[]{:S(2)}, u32[]{:S(2)}) async-start(bf16[2,64,4,640]{3,1,0,2:T(8,128)(2,1)} %copy.75), calls=%async_computation.2 | async-start | bytes 1310720 | tf_op jit(solution)/shard_map/all_to_all | solution.py:180
  278.5 303.0 %all-reduce.36.cloned.1.call-start = ((), (), s32[]{:S(2)}) async-start(), calls=%async_computation.9 | async-start | bytes 16711680
  287.1 2.1 copy-start.10
  310.5 2.4 copy-start.3
  317.7 375.9 %reduce-scatter.9.cloned.1.call-start = ((), (), s32[]{:S(2)}) async-start(), calls=%async_computation.8 | async-start | bytes 3379200
  318.8 2.2 copy-start.9
  353.0 2.7 copy-start.18
  355.7 3.5 copy-start.23
  493.3 29.2 %copy-start.20 = (f32[1280]{0:T(1024)S(1)}, f32[1280]{0:T(1024)}, u32[]{:S(2)}) copy-start(f32[1280]{0:T(1024)} %copy-done.19) | copy-start | bytes 15364
  493.3 15.9 %collective-permute-start.5 = (f32[4,1280]{1,0:T(4,128)S(1)}, f32[4,1280]{1,0:T(4,128)S(1)}, u32[]{:S(2)}, u32[]{:S(2)}) collective-permute-start(f32[4,1280]{1,0:T(4,128)S(1)} %slice.40), channel_id=1, source_target_pairs={{0,6},{1,7},{2,8},{3,9},{4,10},{5,11},{6,12},{7,13},{8,14},{9,15},... | collective-permute-start | bytes 61448
  494.6 17.3 %collective-permute-start.4 = (f32[24,1280]{1,0:T(8,128)S(1)}, f32[24,1280]{1,0:T(8,128)S(1)}, u32[]{:S(2)}, u32[]{:S(2)}) collective-permute-start(f32[24,1280]{1,0:T(8,128)S(1)} %fusion), channel_id=1, source_target_pairs={{0,5},{1,6},{2,7},{3,8},{4,9},{5,10},{6,11},{7,12},{8,13},{9,14},{... | collective-permute-start | bytes 368648
  495.9 16.1 %collective-permute-start.3 = (f32[24,1280]{1,0:T(8,128)S(1)}, f32[24,1280]{1,0:T(8,128)S(1)}, u32[]{:S(2)}, u32[]{:S(2)}) collective-permute-start(f32[24,1280]{1,0:T(8,128)S(1)} %fusion), channel_id=1, source_target_pairs={{0,4},{1,5},{2,6},{3,7},{4,8},{5,9},{6,10},{7,11},{8,12},{9,13},{1... | collective-permute-start | bytes 368648
  499.0 12.9 %collective-permute-start.2 = (f32[24,1280]{1,0:T(8,128)S(1)}, f32[24,1280]{1,0:T(8,128)S(1)}, u32[]{:S(2)}, u32[]{:S(2)}) collective-permute-start(f32[24,1280]{1,0:T(8,128)S(1)} %fusion), channel_id=1, source_target_pairs={{0,3},{1,4},{2,5},{3,6},{4,7},{5,8},{6,9},{7,10},{8,11},{9,12},{10... | collective-permute-start | bytes 368648
  504.3 11.2 %collective-permute-start.1 = (f32[24,1280]{1,0:T(8,128)S(1)}, f32[24,1280]{1,0:T(8,128)S(1)}, u32[]{:S(2)}, u32[]{:S(2)}) collective-permute-start(f32[24,1280]{1,0:T(8,128)S(1)} %fusion), channel_id=1, source_target_pairs={{0,2},{1,3},{2,4},{3,5},{4,6},{5,7},{6,8},{7,9},{8,10},{9,11},{10,... | collective-permute-start | bytes 368648
  509.3 11.5 %collective-permute-start = (f32[24,1280]{1,0:T(8,128)S(1)}, f32[24,1280]{1,0:T(8,128)S(1)}, u32[]{:S(2)}, u32[]{:S(2)}) collective-permute-start(f32[24,1280]{1,0:T(8,128)S(1)} %fusion), channel_id=1, source_target_pairs={{0,1},{1,2},{2,3},{3,4},{4,5},{5,6},{6,7},{7,8},{8,9},{9,10},{10,1... | collective-permute-start | bytes 368648
  522.5 4.5 copy-start.26
  528.8 2.1 copy-start.35
  528.8 2.1 copy-start.36
  528.8 2.1 copy-start.37
  (20 other events, 31.0 us)
Sparse Core Ops, SparseCore 0:
  10.8 57.9 all-gather.5
  72.2 77.5 all-gather.7
  152.6 61.6 all-gather.9
  317.9 230.2 all-reduce.35
  550.8 142.7 reduce-scatter.8
where the time goes:
time: 707 us; the launch traced here: 701 us
  blocking collectives  311 us (44%)
  waiting for transfers between devices  182 us (26%)
  local copies, waits for them, and re-layouts  80.1 us (11%)
  starting transfers between devices  40.1 us (6%)
  other arithmetic  37.6 us (5%)
  matrix products  34.4 us (5%)
  between operations  16.8 us (2%)
    unnamed x3, blocking collectives  210 us
    unnamed x13, waiting for transfers between devices  119 us
    all_gather x1, blocking collectives, shards(): lax.all_gather(head_weight, ('dp', 'seq'), axis=0, tiled=True)  73.7 us
    all_gather x1, waiting for transfers between devices, shards(): lax.all_gather(conv_weight, ('dp', 'seq'), axis=0, tiled=True)  38.3 us
    unnamed x159, local copies, waits for them, and re-layouts  32.9 us
    unnamed x8, starting transfers between devices  27.2 us
    all_to_all x1, blocking collectives, shards(): lax.all_to_all(result.reshape(number, length, 1, inner), 'seq', split_axi...  26.9 us
    all_to_all x1, waiting for transfers between devices, shards(): lax.all_to_all(conv_in.reshape(seq_count, length // partition_count, part...  20 us
  transfers between devices with their start and end apart: 14, of which 6 were waited for; matrix products, arithmetic and copies ran while one was open for 34% of the time, Pallas kernels for 0%

commit v1 on v0

v1 whole, which is shorter than its diff:
```python
import functools

import jax
import jax.numpy as jnp
from jax import lax
from jax.experimental import pallas as pl
from jax.experimental.pallas import tpu as pltpu
from jax.sharding import PartitionSpec as P

KERNEL_TAPS = 5
CENTRE = KERNEL_TAPS // 2
DILATION_RATE = 128
NORM_EPSILON = 1e-05
LOSS_SCALE = 16.0
REACH = CENTRE * DILATION_RATE
BF = jnp.bfloat16
F32 = jnp.float32
LANES = 128
WIDE_VECTORS = 3
NARROW_VECTORS = 6
MIB = 1024 * 1024
HALF_ROOT = 0.7071067811865476
INV_ROOT_TWO_PI = 0.3989422804014327


def gauss(u):
    z = jnp.abs(u) * HALF_ROOT
    t = pl.reciprocal(1.0 + 0.3275911 * z, approx=False)
    e = jnp.exp(-0.5 * u * u)
    poly = t * (
        0.254829592
        + t * (-0.284496736 + t * (1.421413741 + t * (-1.453152027 + t * 1.061405429)))
    )
    tail = 0.5 * poly * e
    return jnp.where(u < 0, tail, 1.0 - tail), e * INV_ROOT_TWO_PI


def standardize(v):
    average = jnp.mean(v, axis=-1, keepdims=True)
    centred = v - average
    spread = jnp.mean(centred * centred, axis=-1, keepdims=True)
    r = lax.rsqrt(spread + NORM_EPSILON)
    return centred * r, r


def dot(a, b):
    return jnp.dot(a, b, preferred_element_type=F32)


def dot_nt(a, b):
    return lax.dot_general(a, b, (((1,), (1,)), ((), ())), preferred_element_type=F32)


def dot_tn(a, b):
    return lax.dot_general(a, b, (((0,), (0,)), ((), ())), preferred_element_type=F32)


def rows8(x):
    return jnp.sum(x.reshape(x.shape[0] // 8, 8, x.shape[1]), axis=0)


def each_chunk(count, step, body):
    @pl.loop(0, count // step)
    def _(i):
        body(pl.ds(pl.multiple_of(i * step, step), step))


def thirds(x):
    high = x.astype(BF)
    rest = x - high.astype(F32)
    mid = rest.astype(BF)
    low = (rest - mid.astype(F32)).astype(BF)
    return high, mid, low


def vmem(n):
    return [pl.BlockSpec(memory_space=pltpu.VMEM)] * n


def call(kernel, ins, outs, scratch=(), flops=0, limit=24, name=None):
    moved = sum(x.size * x.dtype.itemsize for x in ins)
    moved += sum(o.size * o.dtype.itemsize for o in outs)
    return pl.pallas_call(
        kernel,
        out_shape=list(outs),
        in_specs=vmem(len(ins)),
        out_specs=vmem(len(outs)),
        scratch_shapes=list(scratch),
        compiler_params=pltpu.CompilerParams(vmem_limit_bytes=limit * MIB),
        cost_estimate=pl.CostEstimate(flops=int(flops), bytes_accessed=int(moved), transcendentals=0),
        name=name,
    )(*ins)


def sds(shape, dtype):
    return jax.ShapeDtypeStruct(shape, dtype)


def pack_kernel(vocab, w_in, head_t, *rest):
    vecs = rest[: WIDE_VECTORS + NARROW_VECTORS]
    conv, w_out, group_a, group_b, tile = rest[WIDE_VECTORS + NARROW_VECTORS :]
    wide, inner = w_in.shape
    tile[...] = jnp.zeros_like(tile)
    tile[0:vocab, 0:wide] = head_t[...].astype(F32)
    for j, v in enumerate(vecs):
        n = v.shape[-1]
        tile[vocab + j : vocab + j + 1, 0:n] = v[...].astype(F32).reshape(1, n)
    group_a[:, 0:inner] = w_in[...]
    group_a[:, inner : inner + LANES] = jnp.transpose(tile[...])[0:wide].astype(BF)
    group_b[0:KERNEL_TAPS] = conv[...]
    for h in range(w_out.shape[1] // inner):
        group_b[KERNEL_TAPS + h] = w_out[:, h * inner : (h + 1) * inner]


def place_kernel(axis, n, *refs):
    parts, out = refs[:n], refs[n]
    me = lax.axis_index(axis)
    values = [p[...].astype(F32) for p in parts]
    ordered = []
    for place in range(n):
        value = values[0]
        for k in range(1, n):
            value = jnp.where(lax.rem(me - place + n, n) == k, values[k], value)
        ordered.append(value)
    out[...] = jnp.concatenate(ordered, axis=-2).astype(BF)


def first_kernel(tokens, n1, r1):
    width = tokens.shape[1]

    def body(c):
        n, r = standardize(tokens[c, :].astype(F32))
        n1[c, :] = n
        r1[c, :] = jnp.broadcast_to(r, (r.shape[0], LANES))

    each_chunk(tokens.shape[0], 16, body)


def spread_matrix(width, inner, wide, narrow):
    row = lax.broadcasted_iota(jnp.int32, (width, 1), 0)
    device = row // wide
    r = row - device * wide
    at = jnp.where(r < narrow, device * narrow + r, -1)
    return (lax.broadcasted_iota(jnp.int32, (width, inner), 1) == at).astype(F32).astype(BF)


def second_kernel(chips, vocab, wide, narrow, n1, *refs):
    pieces = refs[: 2 * chips]
    (w_in, extras, wide_v, narrow_v, act, gp1, n2, gp2, r2, conv_in, proj) = refs[2 * chips :]
    width, inner = w_in.shape
    rows = n1.shape[0]
    me = lax.axis_index("dp")
    block = pieces[0].shape[0]
    for c in range(2):
        for m in range(chips):
            at = pl.multiple_of((me ^ (2 * m + c)) * block, block)
            w_in[pl.ds(at, block), :] = pieces[c * chips + m][:, 0:inner]
            extras[pl.ds(at, block), :] = pieces[c * chips + m][:, inner : inner + LANES]
    turned = jnp.transpose(extras[...].astype(F32))
    wide_v[...] = jnp.zeros_like(wide_v)
    wide_v[0:WIDE_VECTORS, :] = turned[vocab : vocab + WIDE_VECTORS]
    first = vocab + WIDE_VECTORS
    narrow_v[0:NARROW_VECTORS, :] = dot(
        turned.astype(BF), spread_matrix(width, inner, wide, narrow)
    )[first : first + NARROW_VECTORS]
    g1, b1 = wide_v[0:1, :], wide_v[1:2, :]
    bias, g2, b2 = narrow_v[0:1, :], narrow_v[1:2, :], narrow_v[2:3, :]

    def body(c):
        u = n1[c, :] * g1 + b1
        cdf, pdf = gauss(u)
        act[c, :] = (u * cdf).astype(BF)
        gp1[c, :] = cdf + u * pdf

    each_chunk(rows, 16, body)
    proj[...] = dot(act[...], w_in[...])

    def later(c):
        n, r = standardize(proj[c, :] + bias)
        u = n * g2 + b2
        cdf, pdf = gauss(u)
        conv_in[c, :] = (u * cdf).astype(BF)
        gp2[c, :] = cdf + u * pdf
        n2[c, :] = n
        r2[c, :] = jnp.broadcast_to(r, (r.shape[0], LANES))

    each_chunk(rows, 32, later)


def middle_kernel(
    chips,
    hops,
    seqs,
    vocab,
    wide_v,
    narrow_v,
    extras,
    head_bias,
    types,
    positions,
    targets,
    tokens,
    *refs,
):
    blocks = refs[: 2 * hops + 1]
    pieces = refs[2 * hops + 1 : 2 * hops + 1 + 2 * chips]
    (
        taps,
        block_out,
        third_act,
        out_low,
        logit_grad,
        head_grad,
        conv_low,
        narrow_sums,
        wide_sums,
        stats,
        ext,
        n3,
        gp3,
        r3,
        work,
    ) = refs[2 * hops + 1 + 2 * chips :]
    inner = taps.shape[1]
    width = tokens.shape[1]
    rows = tokens.shape[0]
    length = rows // seqs
    me = lax.axis_index("dp")
    block = pieces[0].shape[1]
    for c in range(2):
        for m in range(chips):
            at = pl.multiple_of((me ^ (2 * m + c)) * block, block)
            for slab in range(taps.shape[0]):
                taps[slab, pl.ds(at, block), :] = pieces[c * chips + m][slab]
    for b, ref in enumerate(blocks):
        ext[:, b * length : (b + 1) * length, :] = ref[...]
    bias, g3, b3 = narrow_v[3:4, :], narrow_v[4:5, :], narrow_v[5:6, :]
    bias_out = wide_v[2:3, :]
    narrow_sums[...] = jnp.zeros_like(narrow_sums)
    wide_sums[...] = jnp.zeros_like(wide_sums)
    stats[...] = jnp.zeros_like(stats)
    head_grad[...] = jnp.zeros_like(head_grad)
    seat = lax.axis_index("seq")

    @pl.loop(0, seqs)
    def _(s):
        whole = pl.ds(pl.multiple_of(s * length, length), length)
        total = dot(ext[s, pl.ds(hops * length - REACH, length), :], taps[0])
        for k in range(1, KERNEL_TAPS):
            at = hops * length + (k - CENTRE) * DILATION_RATE
            total += dot(ext[s, pl.ds(at, length), :], taps[k])
        work[:, 0:inner] = total

        def ahead(c):
            low = (work[c, 0:inner] + bias).astype(BF).astype(F32)
            n, r = standardize(low)
            u = n * g3 + b3
            cdf, pdf = gauss(u)
            here = pl.ds(pl.multiple_of(s * length + c.start, c.size), c.size)
            third_act[here, :] = (u * cdf).astype(BF)
            gp3[c, :] = cdf + u * pdf
            n3[c, :] = n
            r3[c, :] = jnp.broadcast_to(r, (r.shape[0], LANES))

        each_chunk(length, 32, ahead)
        for h in range(width // inner):
            work[:, h * inner : (h + 1) * inner] = dot(third_act[whole, :], taps[KERNEL_TAPS + h])

        def add(c):
            here = pl.ds(pl.multiple_of(s * length + c.start, c.size), c.size)
            block_out[here, :] = (tokens[here, :].astype(F32) + work[c, :] + bias_out).astype(BF)

        each_chunk(length, 32, add)
        lane = lax.broadcasted_iota(jnp.int32, (length, LANES), 1)
        logits = dot(block_out[whole, :], extras[...]) + head_bias[...]
        logits = jnp.where(lane < vocab, logits, -1e30)
        highest = jnp.max(logits, axis=1, keepdims=True)
        raised = jnp.exp(logits - highest)
        log_total = highest + jnp.log(jnp.sum(raised, axis=1, keepdims=True))
        place = lax.broadcasted_iota(jnp.int32, (length, positions.shape[1]), 0) + seat * length
        matches = positions[pl.ds(s, 1), :] == place
        mask = jnp.sum(jnp.where(matches, 1.0, 0.0), axis=1, keepdims=True)
        goal = jnp.sum(
            jnp.where(matches, targets[pl.ds(s, 1), :].astype(F32), 0.0), axis=1, keepdims=True
        )
        hot = jnp.where(lane == goal.astype(jnp.int32), 1.0, 0.0)
        picked = jnp.sum(logits * hot, axis=1, keepdims=True)
        entropy = log_total - picked
        chance = jnp.exp(picked - log_total)
        grad = (LOSS_SCALE * mask * (jnp.exp(logits - log_total) - hot)).astype(BF)
        logit_grad[whole, :] = grad
        columns = jnp.where(lane == 0, mask, jnp.where(lane == 1, mask * chance, 0.0))
        kinds = lax.broadcasted_iota(jnp.int32, (LANES, length), 0) == types[pl.ds(s, 1), :]
        tallies = jnp.dot(
            jnp.where(kinds, 1.0, 0.0),
            columns,
            preferred_element_type=F32,
            precision=lax.Precision.HIGHEST,
        )
        stats[0:2, :] += jnp.transpose(tallies)[0:2]
        stats[2:3, :] += jnp.sum(grad.astype(F32), axis=0, keepdims=True)
        stats[3:4, :] += jnp.broadcast_to(
            jnp.sum(mask * entropy, axis=0, keepdims=True), (1, LANES)
        )
        head_grad[...] += dot_tn(block_out[whole, :], grad)
        work[...] = dot_nt(grad, extras[...])

        def lower(c):
            here = pl.ds(pl.multiple_of(s * length + c.start, c.size), c.size)
            low = work[c, :].astype(BF)
            out_low[here, :] = low
            wide_sums[...] += rows8(low.astype(F32))

        each_chunk(length, 32, lower)
        back = dot_nt(out_low[whole, 0:inner], taps[KERNEL_TAPS])
        for h in range(1, width // inner):
            back += dot_nt(out_low[whole, h * inner : (h + 1) * inner], taps[KERNEL_TAPS + h])
        work[:, 0:inner] = back

        def behind(c):
            e = work[c, 0:inner] * gp3[c, :]
            n = n3[c, :]
            narrow_sums[0:8, :] += rows8(e * n)
            narrow_sums[8:16, :] += rows8(e)
            eg = e * g3
            mean_e = jnp.mean(eg, axis=1, keepdims=True)
            mean_en = jnp.mean(eg * n, axis=1, keepdims=True)
            low = (r3[c, 0:1] * (eg - mean_e - n * mean_en)).astype(BF)
            here = pl.ds(pl.multiple_of(s * length + c.start, c.size), c.size)
            conv_low[here, :] = low
            narrow_sums[16:24, :] += rows8(low.astype(F32))

        each_chunk(length, 32, behind)


def conv_grad_kernel(chips, hops, seqs, third_act, out_low, conv_low, *refs):
    blocks = refs[: 2 * hops + 1]
    keep, send, turned, total, third_t = refs[2 * hops + 1 :]
    inner = conv_low.shape[1]
    length = conv_low.shape[0] // seqs
    block = keep.shape[2]
    me = lax.axis_index("dp")
    core = me & 1
    slabs = keep.shape[1]
    for s in range(seqs):
        for b, ref in enumerate(blocks):
            turned[s, :, b * length : (b + 1) * length] = jnp.transpose(ref[s])
    third_t[...] = jnp.transpose(third_act[...])

    def share(slab):
        for q in range(chips):
            mine = pl.multiple_of((2 * q + core) * block, block)
            other = pl.multiple_of((2 * q + 1 - core) * block, block)
            keep[q, slab] = total[pl.ds(mine, block), :]
            send[q, slab] = total[pl.ds(other, block), :].astype(BF)

    for k in range(KERNEL_TAPS):
        at = hops * length + (k - CENTRE) * DILATION_RATE
        value = dot(turned[0, :, at : at + length], conv_low[0:length, :])
        for s in range(1, seqs):
            value += dot(
                turned[s, :, at : at + length], conv_low[s * length : (s + 1) * length, :]
            )
        total[...] = value
        share(k)
    for h in range(slabs - KERNEL_TAPS):
        total[...] = dot(third_t[...], out_low[:, h * inner : (h + 1) * inner])
        share(KERNEL_TAPS + h)


def split_b_kernel(chips, keep, got, stats, stats_got, own, own_stats, *sends):
    me = lax.axis_index("dp") // 2
    slabs, block, inner = keep.shape[1:]
    total_stats = stats[...] + stats_got[...]
    own_stats[...] = total_stats
    own[...] = keep[me] + got[me].astype(F32)
    for m in range(1, chips):
        q = me ^ m
        for slab in range(slabs):
            sends[m - 1][slab * block : (slab + 1) * block, :] = (
                keep[q, slab] + got[q, slab].astype(F32)
            ).astype(BF)
        tail = sends[m - 1].at[slabs * block : slabs * block + 16, :]
        tail[...] = jnp.zeros_like(tail)
        for j, term in enumerate(thirds(total_stats)):
            sends[m - 1][slabs * block : slabs * block + 8, j * LANES : (j + 1) * LANES] = term


def sum_terms(ref_value):
    return (
        ref_value[0:8, 0:LANES].astype(F32)
        + ref_value[0:8, LANES : 2 * LANES].astype(F32)
        + ref_value[0:8, 2 * LANES : 3 * LANES].astype(F32)
    )


def line_b_kernel(count, size, part, own, stats, *refs):
    parts = refs[:count]
    keep, keep_stats = refs[count : count + 2]
    sends = refs[count + 2 :]
    slabs, block, inner = own.shape
    me = lax.axis_index("seq")
    sums = stats[...]
    for p in parts:
        sums += sum_terms(p[slabs * block : slabs * block + 16, :])
    keep_stats[...] = sums
    for send in sends:
        send[slabs] = jnp.zeros(send.shape[1:], BF)
        for j, term in enumerate(thirds(sums)):
            send[slabs, 0:8, j * LANES : (j + 1) * LANES] = term
    for slab in range(slabs):
        value = own[slab]
        for p in parts:
            value += p[slab * block : (slab + 1) * block, :].astype(F32)
        cut = [value[z * part : (z + 1) * part] for z in range(size)]
        for k in range(size):
            piece = cut[0]
            for z in range(1, size):
                piece = jnp.where(lax.rem(me + k, size) == z, cut[z], piece)
            if k == 0:
                keep[slab] = piece
            else:
                sends[k - 1][slab, 0:part, :] = piece.astype(BF)


def end_b_kernel(count, keep, stats, *refs):
    parts = refs[:count]
    conv, out, sums, = refs[count:]
    slabs, part, inner = keep.shape
    total = stats[...]
    for p in parts:
        total += sum_terms(p[slabs])
    sums[...] = total
    for slab in range(slabs):
        value = keep[slab]
        for p in parts:
            value += p[slab, 0:part, :].astype(F32)
        if slab < KERNEL_TAPS:
            conv[slab] = value
        else:
            out[:, (slab - KERNEL_TAPS) * inner : (slab - KERNEL_TAPS + 1) * inner] = value


def split_a_kernel(chips, keep, got, own, *sends):
    me = lax.axis_index("dp") // 2
    own[...] = keep[me] + got[me].astype(F32)
    for m in range(1, chips):
        sends[m - 1][...] = (keep[me ^ m] + got[me ^ m].astype(F32)).astype(BF)


def line_a_kernel(count, size, part, own, *refs):
    parts = refs[:count]
    keep = refs[count]
    sends = refs[count + 1 :]
    me = lax.axis_index("seq")
    value = own[...]
    for p in parts:
        value += p[...].astype(F32)
    cut = [value[z * part : (z + 1) * part] for z in range(size)]
    for k in range(size):
        piece = cut[0]
        for z in range(1, size):
            piece = jnp.where(lax.rem(me + k, size) == z, cut[z], piece)
        if k == 0:
            keep[...] = piece
        else:
            sends[k - 1][...] = piece.astype(BF)


def end_a_kernel(count, vocab, keep, *refs):
    parts = refs[:count]
    w_in, head_t = refs[count : count + 2]
    vecs = refs[count + 2 : count + 2 + WIDE_VECTORS + NARROW_VECTORS]
    (tile,) = refs[count + 2 + WIDE_VECTORS + NARROW_VECTORS :]
    wide, inner = w_in.shape
    value = keep[...]
    for p in parts:
        value += p[...].astype(F32)
    w_in[...] = value[:, 0:inner]
    tile[...] = jnp.zeros_like(tile)
    tile[0:wide, :] = value[:, inner : inner + LANES]
    turned = jnp.transpose(tile[...])
    head_t[...] = turned[0:vocab, 0:wide]
    for j, v in enumerate(vecs):
        n = v.shape[-1]
        v[...] = turned[vocab + j : vocab + j + 1, 0:n].reshape(v.shape)


def back_kernel(
    chips,
    hops,
    seqs,
    vocab,
    wide,
    narrow,
    taps,
    n2,
    gp2,
    r2,
    n1,
    gp1,
    act,
    w_in,
    wide_v,
    narrow_v,
    narrow_sums,
    wide_sums,
    head_grad,
    *refs,
):
    blocks = refs[: 2 * hops + 1]
    keep, send, e1, low, ext, work, act_t, sums1, sums2 = refs[2 * hops + 1 :]
    width, inner = w_in.shape
    rows = low.shape[0]
    length = rows // seqs
    g2 = narrow_v[1:2, :]
    for b, ref in enumerate(blocks):
        ext[:, b * length : (b + 1) * length, :] = ref[...]
    sums1[...] = jnp.zeros_like(sums1)
    sums2[...] = jnp.zeros_like(sums2)

    @pl.loop(0, seqs)
    def _(s):
        whole = pl.ds(pl.multiple_of(s * length, length), length)
        total = dot_nt(ext[s, pl.ds(hops * length + REACH, length), :], taps[0])
        for k in range(1, KERNEL_TAPS):
            at = hops * length - (k - CENTRE) * DILATION_RATE
            total += dot_nt(ext[s, pl.ds(at, length), :], taps[k])
        work[:, 0:inner] = total

        def second(c):
            here = pl.ds(pl.multiple_of(s * length + c.start, c.size), c.size)
            e = work[c, 0:inner].astype(BF).astype(F32) * gp2[here, :]
            n = n2[here, :]
            sums2[0:8, :] += rows8(e * n)
            sums2[8:16, :] += rows8(e)
            eg = e * g2
            mean_e = jnp.mean(eg, axis=1, keepdims=True)
            mean_en = jnp.mean(eg * n, axis=1, keepdims=True)
            value = (r2[here, 0:1] * (eg - mean_e - n * mean_en)).astype(BF)
            low[here, :] = value
            sums2[16:24, :] += rows8(value.astype(F32))

        each_chunk(length, 32, second)
        work[...] = dot_nt(low[whole, :], w_in[...])

        def first(c):
            here = pl.ds(pl.multiple_of(s * length + c.start, c.size), c.size)
            e = work[c, :] * gp1[here, :]
            e1[here, :] = e
            sums1[0:8, :] += rows8(e * n1[here, :])
            sums1[8:16, :] += rows8(e)

        each_chunk(length, 16, first)

    def folded(ref, j):
        return jnp.sum(ref[8 * j : 8 * j + 8, :], axis=0, keepdims=True)

    wides = [folded(sums1, 0), folded(sums1, 1), folded(wide_sums, 0)]
    narrows = [folded(sums2, 2), folded(sums2, 0), folded(sums2, 1)]
    narrows += [folded(narrow_sums, 2), folded(narrow_sums, 0), folded(narrow_sums, 1)]
    row = lax.broadcasted_iota(jnp.int32, (16, inner), 0)
    stacked = jnp.zeros((16, inner), F32)
    for j, v in enumerate(narrows):
        stacked = jnp.where(row == j, v, stacked)
    spread = spread_matrix(width, inner, wide, narrow)
    placed = 0.0
    for term in thirds(stacked):
        placed = placed + dot_nt(term, spread)
    row = lax.broadcasted_iota(jnp.int32, (LANES, width), 0)
    grid = jnp.zeros((LANES, width), F32)
    for j, v in enumerate(wides):
        grid = jnp.where(row == vocab + j, v, grid)
    for j in range(NARROW_VECTORS):
        grid = jnp.where(row == vocab + WIDE_VECTORS + j, placed[j : j + 1, :], grid)
    extra = jnp.transpose(grid) + head_grad[...]
    act_t[...] = jnp.transpose(act[...])
    core = lax.axis_index("dp") & 1
    block = keep.shape[1]
    for q in range(chips):
        for c in range(2):
            d = 2 * q + c
            lines = slice(d * block, (d + 1) * block)
            value = dot(act_t[lines, :], low[...])

            @pl.when(core == c)
            def _():
                keep[q, :, 0:inner] = value
                keep[q, :, inner : inner + LANES] = extra[lines]

            @pl.when(core != c)
            def _():
                send[q, :, 0:inner] = value.astype(BF)
                send[q, :, inner : inner + LANES] = extra[lines].astype(BF)


def input_kernel(e1, n1, r1, wide_v, logit_grad, extras, input_grad, work):
    work[...] = dot_nt(logit_grad[...], extras[...])
    g1 = wide_v[0:1, :]

    def body(c):
        n = n1[c, :]
        eg = e1[c, :] * g1
        mean_e = jnp.mean(eg, axis=1, keepdims=True)
        mean_en = jnp.mean(eg * n, axis=1, keepdims=True)
        input_grad[c, :] = (work[c, :] + r1[c, 0:1] * (eg - mean_e - n * mean_en)).astype(BF)

    each_chunk(e1.shape[0], 16, body)


def swap(value, mask):
    count = lax.axis_size("dp")
    return lax.ppermute(value, "dp", [(i, i ^ mask) for i in range(count)])


def shifted(value, k):
    size = lax.axis_size("seq")
    return lax.ppermute(value, "seq", [(i, (i + k) % size) for i in range(size)])


def line_parts(block):
    return [block] + [shifted(block, k) for k in range(1, lax.axis_size("seq"))]


def chip_pieces(block):
    chips = lax.axis_size("dp") // 2
    own = [block] + [swap(block, 2 * m) for m in range(1, chips)]
    return own + [swap(piece, 1) for piece in own]


def halo(series):
    size = lax.axis_size("seq")
    hops = -(-REACH // series.shape[1])
    before = [
        lax.ppermute(series, "seq", [(i, i + h) for i in range(size - h)])
        for h in range(hops, 0, -1)
    ]
    after = [
        lax.ppermute(series, "seq", [(i + h, i) for i in range(size - h)])
        for h in range(1, hops + 1)
    ]
    return before + [series] + after


def shards(
    tokens,
    first_gain,
    first_bias,
    in_weight,
    in_bias,
    second_gain,
    second_bias,
    conv_weight,
    conv_bias,
    third_gain,
    third_bias,
    out_weight,
    out_bias,
    head_weight,
    head_bias,
    residue_types,
    mask_positions,
    targets,
):
    dp = lax.axis_size("dp")
    size = lax.axis_size("seq")
    chips = dp // 2
    seqs, length, width = tokens.shape
    wide, inner = in_weight.shape
    narrow = out_weight.shape[0]
    vocab = head_weight.shape[1]
    rows = seqs * length
    hops = -(-REACH // length)
    slabs = KERNEL_TAPS + width // inner
    flat = tokens.reshape(rows, width)

    block_a, block_b = call(
        functools.partial(pack_kernel, vocab),
        [
            in_weight,
            head_weight.T,
            first_gain,
            first_bias,
            out_bias,
            in_bias,
            second_gain,
            second_bias,
            conv_bias,
            third_gain,
            third_bias,
            jnp.transpose(conv_weight, (1, 0, 2)),
            out_weight,
        ],
        [sds((wide, inner + LANES), BF), sds((slabs, narrow, inner), BF)],
        [pltpu.VMEM((LANES, LANES), F32)],
        name="pack",
    )
    parts_a = line_parts(block_a)
    parts_b = line_parts(block_b)
    n1, r1 = call(
        first_kernel,
        [flat],
        [sds((rows, width), F32), sds((rows, LANES), F32)],
        flops=1e9,
        name="first",
    )
    (line_a,) = call(
        functools.partial(place_kernel, "seq", size),
        parts_a,
        [sds((size * wide, inner + LANES), BF)],
        name="line_a",
    )
    pieces_a = chip_pieces(line_a)
    (line_b,) = call(
        functools.partial(place_kernel, "seq", size),
        parts_b,
        [sds((slabs, size * narrow, inner), BF)],
        name="line_b",
    )
    pieces_b = chip_pieces(line_b)
    w_in, extras, wide_v, narrow_v, act, gp1, n2, gp2, r2, conv_in = call(
        functools.partial(second_kernel, chips, vocab, wide, narrow),
        [n1] + pieces_a,
        [
            sds((width, inner), BF),
            sds((width, LANES), BF),
            sds((8, width), F32),
            sds((8, inner), F32),
            sds((rows, width), BF),
            sds((rows, width), F32),
            sds((rows, inner), F32),
            sds((rows, inner), F32),
            sds((rows, LANES), F32),
            sds((rows, inner), BF),
        ],
        [pltpu.VMEM((rows, inner), F32)],
        flops=10e9,
        limit=40,
        name="second",
    )
    blocks = halo(conv_in.reshape(seqs, length, inner))
    (
        taps,
        block_out,
        third_act,
        out_low,
        logit_grad,
        head_grad,
        conv_low,
        narrow_sums,
        wide_sums,
        stats,
    ) = call(
        functools.partial(middle_kernel, chips, hops, seqs, vocab),
        [
            wide_v,
            narrow_v,
            extras,
            jnp.pad(head_bias.astype(F32), (0, LANES - vocab)).reshape(1, LANES),
            residue_types,
            mask_positions,
            targets,
            flat,
        ]
        + blocks
        + pieces_b,
        [
            sds((slabs, inner, inner), BF),
            sds((rows, width), BF),
            sds((rows, inner), BF),
            sds((rows, width), BF),
            sds((rows, LANES), BF),
            sds((width, LANES), F32),
            sds((rows, inner), BF),
            sds((24, inner), F32),
            sds((8, width), F32),
            sds((8, LANES), F32),
        ],
        [
            pltpu.VMEM((seqs, (2 * hops + 1) * length, inner), BF),
            pltpu.VMEM((length, inner), F32),
            pltpu.VMEM((length, inner), F32),
            pltpu.VMEM((length, LANES), F32),
            pltpu.VMEM((length, width), F32),
        ],
        flops=25e9,
        limit=48,
        name="middle",
    )
    grad_blocks = halo(conv_low.reshape(seqs, length, inner))
    keep_b, send_b = call(
        functools.partial(conv_grad_kernel, chips, hops, seqs),
        [third_act, out_low, conv_low] + blocks,
        [
            sds((chips, slabs, size * narrow, inner), F32),
            sds((chips, slabs, size * narrow, inner), BF),
        ],
        [
            pltpu.VMEM((seqs, inner, (2 * hops + 1) * length), BF),
            pltpu.VMEM((inner, inner), F32),
            pltpu.VMEM((inner, rows), BF),
        ],
        flops=8e9,
        limit=40,
        name="conv_grad",
    )
    got_b = swap(send_b, 1)
    got_stats = swap(stats, 1)
    split = call(
        functools.partial(split_b_kernel, chips),
        [keep_b, got_b, stats, got_stats],
        [sds((slabs, size * narrow, inner), F32), sds((8, LANES), F32)]
        + [sds((slabs * size * narrow + 16, inner), BF)] * (chips - 1),
        limit=32,
        name="split_b",
    )
    from_chips = [swap(piece, 2 * m) for m, piece in zip(range(1, chips), split[2:])]
    line = call(
        functools.partial(line_b_kernel, chips - 1, size, narrow),
        [split[0], split[1]] + from_chips,
        [sds((slabs, narrow, inner), F32), sds((8, LANES), F32)]
        + [sds((slabs + 1, max(narrow, 8), inner), BF)] * (size - 1),
        name="line_grad_b",
    )
    from_line = [shifted(piece, k) for k, piece in zip(range(1, size), line[2:])]
    conv_share, out_share, sums = call(
        functools.partial(end_b_kernel, size - 1),
        [line[0], line[1]] + from_line,
        [sds((KERNEL_TAPS, narrow, inner), F32), sds((narrow, width), F32), sds((8, LANES), F32)],
        name="end_b",
    )

    keep_a, send_a, e1 = call(
        functools.partial(back_kernel, chips, hops, seqs, vocab, wide, narrow),
        [taps, n2, gp2, r2, n1, gp1, act, w_in, wide_v, narrow_v]
        + [narrow_sums, wide_sums, head_grad]
        + grad_blocks,
        [
            sds((chips, size * wide, inner + LANES), F32),
            sds((chips, size * wide, inner + LANES), BF),
            sds((rows, width), F32),
        ],
        [
            pltpu.VMEM((rows, inner), BF),
            pltpu.VMEM((seqs, (2 * hops + 1) * length, inner), BF),
            pltpu.VMEM((length, width), F32),
            pltpu.VMEM((width, rows), BF),
            pltpu.VMEM((16, width), F32),
            pltpu.VMEM((24, inner), F32),
        ],
        flops=20e9,
        limit=56,
        name="back",
    )
    got_a = swap(send_a, 1)
    split = call(
        functools.partial(split_a_kernel, chips),
        [keep_a, got_a],
        [sds((size * wide, inner + LANES), F32)]
        + [sds((size * wide, inner + LANES), BF)] * (chips - 1),
        name="split_a",
    )
    from_chips = [swap(piece, 2 * m) for m, piece in zip(range(1, chips), split[1:])]
    (input_grad,) = call(
        input_kernel,
        [e1, n1, r1, wide_v, logit_grad, extras],
        [sds((rows, width), BF)],
        [pltpu.VMEM((rows, width), F32)],
        flops=5e9,
        name="input",
    )
    line = call(
        functools.partial(line_a_kernel, chips - 1, size, wide),
        [split[0]] + from_chips,
        [sds((wide, inner + LANES), F32)] + [sds((wide, inner + LANES), BF)] * (size - 1),
        name="line_grad_a",
    )
    from_line = [shifted(piece, k) for k, piece in zip(range(1, size), line[1:])]
    ended = call(
        functools.partial(end_a_kernel, size - 1, vocab),
        [line[0]] + from_line,
        [sds((wide, inner), F32), sds((vocab, wide), F32)]
        + [sds((wide,), F32)] * WIDE_VECTORS
        + [sds((narrow,), F32)] * NARROW_VECTORS,
        [pltpu.VMEM((LANES, LANES), F32)],
        name="end_a",
    )
    in_share, head_share, g1, b1, bo, bi, g2, b2, bc, g3, b3 = ended
    masked_total = seqs * dp * mask_positions.shape[1]
    return (
        block_out.reshape(seqs, length, width),
        input_grad.reshape(seqs, length, width),
        g1,
        b1,
        in_share,
        bi,
        g2,
        b2,
        jnp.transpose(conv_share, (1, 0, 2)),
        bc,
        g3,
        b3,
        out_share,
        bo,
        head_share.T,
        sums[2, :vocab],
        sums[0, :vocab].astype(jnp.int32),
        sums[1, :vocab],
        sums[3, 0] / masked_total,
    )


def solution(mesh):
    both = P(("dp", "seq"))
    matrix = P(("dp", "seq"), None)
    cube = P(("dp", "seq"), None, None)
    rows = P("dp", "seq", None)
    return jax.shard_map(
        shards,
        mesh=mesh,
        in_specs=(rows, both, both, matrix, both, both, both, cube, both, both, both, matrix)
        + (both, matrix, P(), P("dp", "seq"), P("dp", None), P("dp", None)),
        out_specs=(rows, rows, both, both, matrix, both, both, both, cube, both, both, both)
        + (matrix, both, matrix, P(), P(), P(), P()),
        check_vma=False,
    )
```

time: 707 us -> 264 us (0.37)
  blocking collectives: 311 us -> 0 us
  Pallas kernels: 0 us -> 77.4 us
  waiting for transfers between devices: 182 us -> 113 us
  local copies, waits for them, and re-layouts: 80.1 us -> 18.7 us
  other arithmetic: 37.6 us -> 0.52 us
  matrix products: 34.4 us -> 0 us
  between operations: 16.8 us -> 2.82 us
  starting transfers between devices: 40.1 us -> 48.7 us
    unnamed x3 -> x0, blocking collectives: 210 us -> none
    unnamed x13 -> x0, waiting for transfers between devices: 119 us -> none
    ppermute x0 -> x39, waiting for transfers between devices: none -> 113 us  [the longest x23 66.2 us: swap(): return lax.ppermute(value, 'dp', [(i, i ^ mask) for i in range(count)])]
    pallas_call x0 -> x15, Pallas kernels: none -> 77.4 us  [call(): pl.pallas_call(kernel, out_shape=list(outs), in_specs=vmem(len(ins)), out...]
    all_gather x1 -> x0, blocking collectives: 73.7 us -> none  [shards(): lax.all_gather(head_weight, ('dp', 'seq'), axis=0, tiled=True)]
    ppermute x0 -> x39, starting transfers between devices: none -> 48.7 us  [the longest x12 19.7 us: shifted(): lax.ppermute(value, 'seq', [(i, (i + k) % size) for i in range(size)])]
    all_gather x3 -> x0, waiting for transfers between devices: 42.8 us -> none  [the longest x1 38.3 us: shards(): lax.all_gather(conv_weight, ('dp', 'seq'), axis=0, tiled=True)]
    dot_general x12 -> x0, matrix products: 34.4 us -> none  [the longest x4 14.6 us: outer_sum(): lax.dot_general(flat_former, flat_latter, (((0,), (0,)), ((), ())), prefe...]
  transfers between devices with their start and end apart: 14 -> 39, of which waited for: 6 -> 18; matrix products, arithmetic and copies ran while one was open for 34% -> 0% of each run, Pallas kernels for 0% -> 21%
where the time goes in v1:
time: 264 us; the launch traced here: 262 us
  waiting for transfers between devices  113 us (43%)
  Pallas kernels  77.4 us (29%)
  starting transfers between devices  48.7 us (18%)
  local copies, waits for them, and re-layouts  18.7 us (7%)
  between operations  2.82 us (1%)
    pallas_call x15, Pallas kernels, call(): pl.pallas_call(kernel, out_shape=list(outs), in_specs=vmem(len(ins)), out...  77.4 us
    ppermute x23, waiting for transfers between devices, swap(): return lax.ppermute(value, 'dp', [(i, i ^ mask) for i in range(count)])  66.2 us
    ppermute x12, waiting for transfers between devices, shifted(): lax.ppermute(value, 'seq', [(i, (i + k) % size) for i in range(size)])  22.2 us
    ppermute x12, starting transfers between devices, shifted(): lax.ppermute(value, 'seq', [(i, (i + k) % size) for i in range(size)])  19.7 us
    unnamed x88, local copies, waits for them, and re-layouts  18.2 us
    ppermute x23, starting transfers between devices, swap(): return lax.ppermute(value, 'dp', [(i, i ^ mask) for i in range(count)])  16.9 us
    ppermute x2, waiting for transfers between devices, halo(): lax.ppermute(series, 'seq', [(i, i + h) for i in range(size - h)])  16.6 us
    ppermute x2, starting transfers between devices, halo(): lax.ppermute(series, 'seq', [(i, i + h) for i in range(size - h)])  9.3 us
  transfers between devices with their start and end apart: 39, of which 18 were waited for; matrix products, arithmetic and copies ran while one was open for 0% of the time, Pallas kernels for 21%

profile of v1, /device:TPU:0, one launch (start us, length us, event | category | flops | bytes accessed | tf_op | source)
XLA Modules:
  0.0 261.5 jit_solution(3101065130053592129)
XLA Ops:
  9.9 3.1 %collective-permute-start = (bf16[40,768]{1,0:T(8,128)(2,1)S(1)}, bf16[40,768]{1,0:T(8,128)(2,1)S(1)}, u32[]{:S(2)}, u32[]{:S(2)}) collective-permute-start(bf16[40,768]{1,0:T(8,128)(2,1)S(1)} %get-tuple-element.81.refs_0_), channel_id=1, source_target_pairs={{0,1},{1,2},{2,3},{3,0},{4,5},{5,6},{6,7},{7,4},{8,9},{9,10},{10,1... | collective-permute-start | bytes 184328 | tf_op jit(solution)/shard_map/ppermute | solution.py:618
  12.9 2.6 collective-permute-start.1
  15.5 1.3 collective-permute-start.2
  17.4 2.4 collective-permute-done.1.refs_2_
  20.2 1.6 collective-permute-start.3
  21.8 1.4 collective-permute-start.12
  23.1 2.1 collective-permute-start.13
  25.6 1.5 collective-permute-start.4
  27.1 4.8 %collective-permute-done.12.refs_1_ = bf16[7,20,640]{2,1,0:T(8,128)(2,1)S(1)} collective-permute-done((bf16[7,20,640]{2,1,0:T(8,128)(2,1)S(1)}, bf16[7,20,640]{2,1,0:T(8,128)(2,1)S(1)}, u32[]{:S(2)}, u32[]{:S(2)}) %collective-permute-start.12) | collective-permute-done | bytes 179232 | tf_op jit(solution)/shard_map/ppermute | solution.py:618
  31.9 1.5 collective-permute-start.5
  33.4 5.2 %collective-permute-done.13.refs_2_ = bf16[7,20,640]{2,1,0:T(8,128)(2,1)S(1)} collective-permute-done((bf16[7,20,640]{2,1,0:T(8,128)(2,1)S(1)}, bf16[7,20,640]{2,1,0:T(8,128)(2,1)S(1)}, u32[]{:S(2)}, u32[]{:S(2)}) %collective-permute-start.13) | collective-permute-done | bytes 179232 | tf_op jit(solution)/shard_map/ppermute | solution.py:618
  38.9 1.3 collective-permute-start.15
  41.0 1.4 collective-permute-start.17
  43.0 1.0 collective-permute-done.6.refs_4_
  44.5 6.0 %first.1 = (f32[512,1280]{1,0:T(8,128)S(1)}, f32[512,128]{1,0:T(8,128)S(1)}) custom-call(bf16[512,1280]{1,0:T(8,128)(2,1)S(1)} %bitcast.22), custom_call_target="tpu_custom_call" | custom-call | flops 1000000000 | bytes 4194304 | tf_op jit(solution)/shard_map/first/pallas_call | solution.py:83
  50.9 7.0 %collective-permute-done.15.refs_4_ = bf16[7,80,640]{2,1,0:T(8,128)(2,1)S(1)} collective-permute-done((bf16[7,80,640]{2,1,0:T(8,128)(2,1)S(1)}, bf16[7,80,640]{2,1,0:T(8,128)(2,1)S(1)}, u32[]{:S(2)}, u32[]{:S(2)}) %collective-permute-start.15) | collective-permute-done | bytes 716832 | tf_op jit(solution)/shard_map/ppermute | solution.py:613
  57.9 13.6 %collective-permute-done.16.refs_5_ = bf16[7,80,640]{2,1,0:T(8,128)(2,1)S(1)} collective-permute-done((bf16[7,80,640]{2,1,0:T(8,128)(2,1)S(1)}, bf16[7,80,640]{2,1,0:T(8,128)(2,1)S(1)}, u32[]{:S(2)}, u32[]{:S(2)}) %collective-permute-start.16) | collective-permute-done | bytes 716832 | tf_op jit(solution)/shard_map/ppermute | solution.py:613
  71.5 1.6 collective-permute-done.17.refs_6_
  73.2 9.3 %second.1 = (bf16[1280,640]{1,0:T(8,128)(2,1)S(1)}, bf16[1280,128]{1,0:T(8,128)(2,1)S(1)}, f32[8,1280]{1,0:T(8,128)S(1)}, f32[8,640]{1,0:T(8,128)S(1)}, bf16[512...) custom-call(f32[512,1280]{1,0:T(8,128)S(1)} %get-tuple-element.80.n1, ...), custom_call_target="tpu_custom_call" | custom-call | flops 10000000000 | bytes 14086144 | tf_op jit(solution)/shard_map/second/pallas_call | solution.py:83
  82.5 1.5 copy-done.22
  84.0 1.2 copy-done.24
  85.2 1.1 copy-done.25
  86.3 1.1 copy-done.27
  88.1 7.1 %collective-permute-start.10 = (bf16[2,256,640]{2,1,0:T(8,128)(2,1)S(1)}, bf16[2,256,640]{2,1,0:T(8,128)(2,1)S(1)}, u32[]{:S(2)}, u32[]{:S(2)}) collective-permute-start(bf16[2,256,640]{2,1,0:T(8,128)(2,1)S(1)} %bitcast.23), channel_id=1, source_target_pairs={{0,1},{1,2},{2,3},{4,5},{5,6},{6,7},{8,9},{9,10},{10,11},{12,13},{... | collective-permute-start | bytes 1966088 | tf_op jit(solution)/shard_map/ppermute | solution.py:635
  95.2 1.3 collective-permute-start.11
  96.5 13.2 %collective-permute-done.10.refs_0_ = bf16[2,256,640]{2,1,0:T(8,128)(2,1)S(1)} collective-permute-done((bf16[2,256,640]{2,1,0:T(8,128)(2,1)S(1)}, bf16[2,256,640]{2,1,0:T(8,128)(2,1)S(1)}, u32[]{:S(2)}, u32[]{:S(2)}) %collective-permute-start.10) | collective-permute-done | bytes 655392 | tf_op jit(solution)/shard_map/ppermute | solution.py:635
  109.8 4.2 %collective-permute-done.11.refs_2_ = bf16[2,256,640]{2,1,0:T(8,128)(2,1)S(1)} collective-permute-done((bf16[2,256,640]{2,1,0:T(8,128)(2,1)S(1)}, bf16[2,256,640]{2,1,0:T(8,128)(2,1)S(1)}, u32[]{:S(2)}, u32[]{:S(2)}) %collective-permute-start.11) | collective-permute-done | bytes 655392 | tf_op jit(solution)/shard_map/ppermute | solution.py:639
  115.3 22.4 %middle.1 = (bf16[7,640,640]{2,1,0:T(8,128)(2,1)}, bf16[512,1280]{1,0:T(8,128)(2,1)}, bf16[512,640]{1,0:T(8,128)(2,1)S(1)}, bf16[512,1280]{1,0:T(8,128)(2,1)}, b...) custom-call(f32[8,1280]{1,0:T(8,128)S(1)} %get-tuple-element.82.wide, ...), custom_call_target="tpu_custom_call" | custom-call | flops 24999999488 | bytes 19964816 | tf_op jit(solution)/shard_map/middle/pallas_call | solution.py:83
  137.8 2.2 collective-permute-start.22
  140.0 1.5 collective-permute-start.23
  141.5 1.3 copy-done.23
  142.8 7.4 %conv_grad.1 = (f32[4,7,80,640]{3,2,1,0:T(8,128)S(1)}, bf16[4,7,80,640]{3,2,1,0:T(8,128)(2,1)}) custom-call(bf16[512,640]{1,0:T(8,128)(2,1)S(1)} %get-tuple-element.118.third_act, bf16[512,1280]{1,0:T(8,128)(2,1)S(1)} %copy-done.23, bf16[512,640]{1,0:T(8,128)(2,1)S(1)} %get-tuple-element.98.conv_low, ...), custom_call_target="tpu_custom_call" | custom-call | flops 8000000000 | bytes 13189120 | tf_op jit(solution)/shard_map/conv_grad/pallas_call | solution.py:83
  150.3 3.4 %collective-permute-done.22.refs_0_ = bf16[2,256,640]{2,1,0:T(8,128)(2,1)S(1)} collective-permute-done((bf16[2,256,640]{2,1,0:T(8,128)(2,1)S(1)}, bf16[2,256,640]{2,1,0:T(8,128)(2,1)S(1)}, u32[]{:S(2)}, u32[]{:S(2)}) %collective-permute-start.22) | collective-permute-done | bytes 655392 | tf_op jit(solution)/shard_map/ppermute | solution.py:635
  153.7 4.2 %collective-permute-done.23.refs_2_ = bf16[2,256,640]{2,1,0:T(8,128)(2,1)S(1)} collective-permute-done((bf16[2,256,640]{2,1,0:T(8,128)(2,1)S(1)}, bf16[2,256,640]{2,1,0:T(8,128)(2,1)S(1)}, u32[]{:S(2)}, u32[]{:S(2)}) %collective-permute-start.23) | collective-permute-done | bytes 655392 | tf_op jit(solution)/shard_map/ppermute | solution.py:639
  158.7 21.5 %back.1 = (f32[4,160,768]{2,1,0:T(8,128)}, bf16[4,160,768]{2,1,0:T(8,128)(2,1)}, f32[512,1280]{1,0:T(8,128)}) custom-call(bf16[7,640,640]{2,1,0:T(8,128)(2,1)} %get-tuple-element.88.taps, f32[512,640]{1,0:T(8,128)} %copy-done.26, f32[512,640]{1,0:T(8,128)} %copy-done.27, f32[512,128]{1,0:T(8,128)} %copy-done.30, f32[512,1280]{1,0:T(8,128)} %copy-done.19, ...), custom_call_target="tpu_custom_call" | custom-call | flops 20000000000 | bytes 25165824 | tf_op jit(solution)/shard_map/back/pallas_call | solution.py:83
  180.6 1.7 collective-permute-done.32.stats_got
  182.3 2.5 split_b.1
  185.5 1.4 collective-permute-start.34
  186.9 1.5 collective-permute-start.35
  189.2 1.4 collective-permute-start.26
  190.7 34.1 %collective-permute-done.25.refs_0_ = bf16[160,768]{1,0:T(8,128)(2,1)S(1)} collective-permute-done((bf16[160,768]{1,0:T(8,128)(2,1)S(1)}, bf16[160,768]{1,0:T(8,128)(2,1)S(1)}, u32[]{:S(2)}, u32[]{:S(2)}) %collective-permute-start.25) | collective-permute-done | bytes 245792 | tf_op jit(solution)/shard_map/ppermute | solution.py:613
  224.8 1.4 collective-permute-start.27
  226.2 6.9 %collective-permute-done.27.refs_2_ = bf16[160,768]{1,0:T(8,128)(2,1)S(1)} collective-permute-done((bf16[160,768]{1,0:T(8,128)(2,1)S(1)}, bf16[160,768]{1,0:T(8,128)(2,1)S(1)}, u32[]{:S(2)}, u32[]{:S(2)}) %collective-permute-start.27) | collective-permute-done | bytes 245792 | tf_op jit(solution)/shard_map/ppermute | solution.py:613
  233.6 3.6 %collective-permute-start.30 = (bf16[40,768]{1,0:T(8,128)(2,1)S(1)}, bf16[40,768]{1,0:T(8,128)(2,1)S(1)}, u32[]{:S(2)}, u32[]{:S(2)}) collective-permute-start(bf16[40,768]{1,0:T(8,128)(2,1)S(1)} %get-tuple-element.111), channel_id=1, source_target_pairs={{0,3},{1,0},{2,1},{3,2},{4,7},{5,4},{6,5},{7,6},{8,11},{9,8},{10,9... | collective-permute-start | bytes 184328 | tf_op jit(solution)/shard_map/ppermute | solution.py:618
  238.7 1.5 collective-permute-start.37
  240.2 2.8 %collective-permute-start.38 = (bf16[8,20,640]{2,1,0:T(8,128)(2,1)S(1)}, bf16[8,20,640]{2,1,0:T(8,128)(2,1)S(1)}, u32[]{:S(2)}, u32[]{:S(2)}) collective-permute-start(bf16[8,20,640]{2,1,0:T(8,128)(2,1)S(1)} %get-tuple-element.132), channel_id=1, source_target_pairs={{0,3},{1,0},{2,1},{3,2},{4,7},{5,4},{6,5},{7,6},{8,11},{9,8},{10,9... | collective-permute-start | bytes 614408 | tf_op jit(solution)/shard_map/ppermute | solution.py:618
  243.1 5.1 %input.1 = bf16[512,1280]{1,0:T(8,128)(2,1)} custom-call(f32[512,1280]{1,0:T(8,128)S(1)} %copy-done.21, f32[512,1280]{1,0:T(8,128)S(1)} %copy-done.20, f32[512,128]{1,0:T(8,128)S(1)} %get-tuple-element.100.r1, f32[8,1280]{1,0:T(8,128)S(1)} %copy-done.29, bf16[512,128]{1,0:T(8,128)(2,1)S(1)} %get-tuple-element.101.logit_grad, ...), custom_call_target="tpu_custom_call" | custom-call | flops 5000000000 | bytes 7315456 | tf_op jit(solution)/shard_map/input/pallas_call | solution.py:83
  248.9 9.0 %collective-permute-done.37.refs_1_ = bf16[8,20,640]{2,1,0:T(8,128)(2,1)S(1)} collective-permute-done((bf16[8,20,640]{2,1,0:T(8,128)(2,1)S(1)}, bf16[8,20,640]{2,1,0:T(8,128)(2,1)S(1)}, u32[]{:S(2)}, u32[]{:S(2)}) %collective-permute-start.37) | collective-permute-done | bytes 204832 | tf_op jit(solution)/shard_map/ppermute | solution.py:618
  (136 shorter events, 22.6 us)
Async XLA Ops:
  9.8 34.7 %copy-start.14 = (bf16[2,256,1280]{2,1,0:T(8,128)(2,1)S(1)}, bf16[2,256,1280]{2,1,0:T(8,128)(2,1)}, u32[]{:S(2)}) copy-start(bf16[2,256,1280]{2,1,0:T(8,128)(2,1)} %param.18) | copy-start | bytes 3932164
  9.9 7.5 %collective-permute-start = (bf16[40,768]{1,0:T(8,128)(2,1)S(1)}, bf16[40,768]{1,0:T(8,128)(2,1)S(1)}, u32[]{:S(2)}, u32[]{:S(2)}) collective-permute-start(bf16[40,768]{1,0:T(8,128)(2,1)S(1)} %get-tuple-element.81.refs_0_), channel_id=1, source_target_pairs={{0,1},{1,2},{2,3},{3,0},{4,5},{5,6},{6,7},{7,4},{8,9},{9,10},{10,1... | collective-permute-start | bytes 184328 | tf_op jit(solution)/shard_map/ppermute | solution.py:618
  12.9 6.9 %collective-permute-start.1 = (bf16[40,768]{1,0:T(8,128)(2,1)S(1)}, bf16[40,768]{1,0:T(8,128)(2,1)S(1)}, u32[]{:S(2)}, u32[]{:S(2)}) collective-permute-start(bf16[40,768]{1,0:T(8,128)(2,1)S(1)} %get-tuple-element.81.refs_0_), channel_id=1, source_target_pairs={{0,2},{1,3},{2,0},{3,1},{4,6},{5,7},{6,4},{7,5},{8,10},{9,11},{10,... | collective-permute-start | bytes 184328 | tf_op jit(solution)/shard_map/ppermute | solution.py:618
  15.5 4.6 %collective-permute-start.2 = (bf16[40,768]{1,0:T(8,128)(2,1)S(1)}, bf16[40,768]{1,0:T(8,128)(2,1)S(1)}, u32[]{:S(2)}, u32[]{:S(2)}) collective-permute-start(bf16[40,768]{1,0:T(8,128)(2,1)S(1)} %get-tuple-element.81.refs_0_), channel_id=1, source_target_pairs={{0,3},{1,0},{2,1},{3,2},{4,7},{5,4},{6,5},{7,6},{8,11},{9,8},{10,9... | collective-permute-start | bytes 184328 | tf_op jit(solution)/shard_map/ppermute | solution.py:618
  20.2 20.8 %collective-permute-start.3 = (bf16[160,768]{1,0:T(8,128)(2,1)S(1)}, bf16[160,768]{1,0:T(8,128)(2,1)S(1)}, u32[]{:S(2)}, u32[]{:S(2)}) collective-permute-start(bf16[160,768]{1,0:T(8,128)(2,1)S(1)} %line_a.1.refs_0_), channel_id=1, source_target_pairs={{0,8},{4,12},{8,0},{12,4},{16,24},{20,28},{24,16},{28,20},{1,9},{5... | collective-permute-start | bytes 737288 | tf_op jit(solution)/shard_map/ppermute | solution.py:613
  21.8 10.1 %collective-permute-start.12 = (bf16[7,20,640]{2,1,0:T(8,128)(2,1)S(1)}, bf16[7,20,640]{2,1,0:T(8,128)(2,1)S(1)}, u32[]{:S(2)}, u32[]{:S(2)}) collective-permute-start(bf16[7,20,640]{2,1,0:T(8,128)(2,1)S(1)} %get-tuple-element.86.refs_0_), channel_id=1, source_target_pairs={{0,1},{1,2},{2,3},{3,0},{4,5},{5,6},{6,7},{7,4},{8,9},{9,10},{10,1... | collective-permute-start | bytes 537608 | tf_op jit(solution)/shard_map/ppermute | solution.py:618
  23.1 15.4 %collective-permute-start.13 = (bf16[7,20,640]{2,1,0:T(8,128)(2,1)S(1)}, bf16[7,20,640]{2,1,0:T(8,128)(2,1)S(1)}, u32[]{:S(2)}, u32[]{:S(2)}) collective-permute-start(bf16[7,20,640]{2,1,0:T(8,128)(2,1)S(1)} %get-tuple-element.86.refs_0_), channel_id=1, source_target_pairs={{0,2},{1,3},{2,0},{3,1},{4,6},{5,7},{6,4},{7,5},{8,10},{9,11},{10,... | collective-permute-start | bytes 537608 | tf_op jit(solution)/shard_map/ppermute | solution.py:618
  25.2 13.4 %collective-permute-start.14 = (bf16[7,20,640]{2,1,0:T(8,128)(2,1)S(1)}, bf16[7,20,640]{2,1,0:T(8,128)(2,1)S(1)}, u32[]{:S(2)}, u32[]{:S(2)}) collective-permute-start(bf16[7,20,640]{2,1,0:T(8,128)(2,1)S(1)} %get-tuple-element.86.refs_0_), channel_id=1, source_target_pairs={{0,3},{1,0},{2,1},{3,2},{4,7},{5,4},{6,5},{7,6},{8,11},{9,8},{10,9... | collective-permute-start | bytes 537608 | tf_op jit(solution)/shard_map/ppermute | solution.py:618
  25.6 16.9 %collective-permute-start.4 = (bf16[160,768]{1,0:T(8,128)(2,1)S(1)}, bf16[160,768]{1,0:T(8,128)(2,1)S(1)}, u32[]{:S(2)}, u32[]{:S(2)}) collective-permute-start(bf16[160,768]{1,0:T(8,128)(2,1)S(1)} %line_a.1.refs_0_), channel_id=1, source_target_pairs={{0,16},{4,20},{8,24},{12,28},{16,0},{20,4},{24,8},{28,12},{1,17},{... | collective-permute-start | bytes 737288 | tf_op jit(solution)/shard_map/ppermute | solution.py:613
  31.9 10.6 %collective-permute-start.5 = (bf16[160,768]{1,0:T(8,128)(2,1)S(1)}, bf16[160,768]{1,0:T(8,128)(2,1)S(1)}, u32[]{:S(2)}, u32[]{:S(2)}) collective-permute-start(bf16[160,768]{1,0:T(8,128)(2,1)S(1)} %line_a.1.refs_0_), channel_id=1, source_target_pairs={{0,24},{4,28},{8,16},{12,20},{16,8},{20,12},{24,0},{28,4},{1,25},{... | collective-permute-start | bytes 737288 | tf_op jit(solution)/shard_map/ppermute | solution.py:613
  38.9 19.0 %collective-permute-start.15 = (bf16[7,80,640]{2,1,0:T(8,128)(2,1)S(1)}, bf16[7,80,640]{2,1,0:T(8,128)(2,1)S(1)}, u32[]{:S(2)}, u32[]{:S(2)}) collective-permute-start(bf16[7,80,640]{2,1,0:T(8,128)(2,1)S(1)} %line_b.1.refs_3_), channel_id=1, source_target_pairs={{0,8},{4,12},{8,0},{12,4},{16,24},{20,28},{24,16},{28,20},{1,9},{5... | collective-permute-start | bytes 2150408 | tf_op jit(solution)/shard_map/ppermute | solution.py:613
  40.2 31.3 %collective-permute-start.16 = (bf16[7,80,640]{2,1,0:T(8,128)(2,1)S(1)}, bf16[7,80,640]{2,1,0:T(8,128)(2,1)S(1)}, u32[]{:S(2)}, u32[]{:S(2)}) collective-permute-start(bf16[7,80,640]{2,1,0:T(8,128)(2,1)S(1)} %line_b.1.refs_3_), channel_id=1, source_target_pairs={{0,16},{4,20},{8,24},{12,28},{16,0},{20,4},{24,8},{28,12},{1,17},{... | collective-permute-start | bytes 2150408 | tf_op jit(solution)/shard_map/ppermute | solution.py:613
  41.0 32.1 %collective-permute-start.17 = (bf16[7,80,640]{2,1,0:T(8,128)(2,1)S(1)}, bf16[7,80,640]{2,1,0:T(8,128)(2,1)S(1)}, u32[]{:S(2)}, u32[]{:S(2)}) collective-permute-start(bf16[7,80,640]{2,1,0:T(8,128)(2,1)S(1)} %line_b.1.refs_3_), channel_id=1, source_target_pairs={{0,24},{4,28},{8,16},{12,20},{16,8},{20,12},{24,0},{28,4},{1,25},{... | collective-permute-start | bytes 2150408 | tf_op jit(solution)/shard_map/ppermute | solution.py:613
  42.5 1.5 collective-permute-start.6
  42.5 1.9 collective-permute-start.7
  44.0 6.5 %collective-permute-start.8 = (bf16[160,768]{1,0:T(8,128)(2,1)S(1)}, bf16[160,768]{1,0:T(8,128)(2,1)S(1)}, u32[]{:S(2)}, u32[]{:S(2)}) collective-permute-start(bf16[160,768]{1,0:T(8,128)(2,1)S(1)} %collective-permute-done.4.refs_2_), channel_id=1, source_target_pairs={{0,4},{4,0},{8,12},{12,8},{16,20},{20,16},{24,28},{28,24},{1,5},{5... | collective-permute-start | bytes 737288 | tf_op jit(solution)/shard_map/ppermute | solution.py:613
  44.3 28.8 %collective-permute-start.9 = (bf16[160,768]{1,0:T(8,128)(2,1)S(1)}, bf16[160,768]{1,0:T(8,128)(2,1)S(1)}, u32[]{:S(2)}, u32[]{:S(2)}) collective-permute-start(bf16[160,768]{1,0:T(8,128)(2,1)S(1)} %collective-permute-done.5.refs_3_), channel_id=1, source_target_pairs={{0,4},{4,0},{8,12},{12,8},{16,20},{20,16},{24,28},{28,24},{1,5},{5... | collective-permute-start | bytes 737288 | tf_op jit(solution)/shard_map/ppermute | solution.py:613
  50.5 32.0 %copy-start.19 = (f32[512,1280]{1,0:T(8,128)}, f32[512,1280]{1,0:T(8,128)S(1)}, u32[]{:S(2)}) copy-start(f32[512,1280]{1,0:T(8,128)S(1)} %get-tuple-element.80.n1) | copy-start | bytes 7864324
  50.5 44.7 %collective-permute-start.18 = (bf16[7,80,640]{2,1,0:T(8,128)(2,1)S(1)}, bf16[7,80,640]{2,1,0:T(8,128)(2,1)S(1)}, u32[]{:S(2)}, u32[]{:S(2)}) collective-permute-start(bf16[7,80,640]{2,1,0:T(8,128)(2,1)S(1)} %line_b.1.refs_3_), channel_id=1, source_target_pairs={{0,4},{4,0},{8,12},{12,8},{16,20},{20,16},{24,28},{28,24},{1,5},{5... | collective-permute-start | bytes 2150408 | tf_op jit(solution)/shard_map/ppermute | solution.py:613
  57.9 56.0 %collective-permute-start.19 = (bf16[7,80,640]{2,1,0:T(8,128)(2,1)S(1)}, bf16[7,80,640]{2,1,0:T(8,128)(2,1)S(1)}, u32[]{:S(2)}, u32[]{:S(2)}) collective-permute-start(bf16[7,80,640]{2,1,0:T(8,128)(2,1)S(1)} %collective-permute-done.15.refs_4_), channel_id=1, source_target_pairs={{0,4},{4,0},{8,12},{12,8},{16,20},{20,16},{24,28},{28,24},{1,5},{5... | collective-permute-start | bytes 2150408 | tf_op jit(solution)/shard_map/ppermute | solution.py:613
  71.5 42.4 %collective-permute-start.20 = (bf16[7,80,640]{2,1,0:T(8,128)(2,1)S(1)}, bf16[7,80,640]{2,1,0:T(8,128)(2,1)S(1)}, u32[]{:S(2)}, u32[]{:S(2)}) collective-permute-start(bf16[7,80,640]{2,1,0:T(8,128)(2,1)S(1)} %collective-permute-done.16.refs_5_), channel_id=1, source_target_pairs={{0,4},{4,0},{8,12},{12,8},{16,20},{20,16},{24,28},{28,24},{1,5},{5... | collective-permute-start | bytes 2150408 | tf_op jit(solution)/shard_map/ppermute | solution.py:613
  73.2 40.8 %collective-permute-start.21 = (bf16[7,80,640]{2,1,0:T(8,128)(2,1)S(1)}, bf16[7,80,640]{2,1,0:T(8,128)(2,1)S(1)}, u32[]{:S(2)}, u32[]{:S(2)}) collective-permute-start(bf16[7,80,640]{2,1,0:T(8,128)(2,1)S(1)} %collective-permute-done.17.refs_6_), channel_id=1, source_target_pairs={{0,4},{4,0},{8,12},{12,8},{16,20},{20,16},{24,28},{28,24},{1,5},{5... | collective-permute-start | bytes 2150408 | tf_op jit(solution)/shard_map/ppermute | solution.py:613
  73.2 42.1 %copy-start.16 = (s32[2,256]{1,0:T(2,128)S(1)}, s32[2,256]{1,0:T(2,128)}, u32[]{:S(2)}) copy-start(s32[2,256]{1,0:T(2,128)} %types.1) | copy-start | bytes 6148
  73.2 42.1 %copy-start.17 = (s32[2,153]{1,0:T(2,128)S(1)}, s32[2,153]{1,0:T(2,128)}, u32[]{:S(2)}) copy-start(s32[2,153]{1,0:T(2,128)} %positions.1) | copy-start | bytes 3676
  73.2 42.1 %copy-start.18 = (s32[2,153]{1,0:T(2,128)S(1)}, s32[2,153]{1,0:T(2,128)}, u32[]{:S(2)}) copy-start(s32[2,153]{1,0:T(2,128)} %targets.1) | copy-start | bytes 3676
  88.1 49.7 %copy-start.26 = (f32[512,640]{1,0:T(8,128)}, f32[512,640]{1,0:T(8,128)S(1)}, u32[]{:S(2)}) copy-start(f32[512,640]{1,0:T(8,128)S(1)} %get-tuple-element.89.n2) | copy-start | bytes 3932164
  88.1 49.7 %copy-start.28 = (f32[8,1280]{1,0:T(8,128)}, f32[8,1280]{1,0:T(8,128)S(1)}, u32[]{:S(2)}) copy-start(f32[8,1280]{1,0:T(8,128)S(1)} %get-tuple-element.82.wide_v) | copy-start | bytes 122884
  88.1 49.7 %copy-start.33 = (f32[8,640]{1,0:T(8,128)}, f32[8,640]{1,0:T(8,128)S(1)}, u32[]{:S(2)}) copy-start(f32[8,640]{1,0:T(8,128)S(1)} %get-tuple-element.83.narrow_v) | copy-start | bytes 61444
  88.1 21.7 %collective-permute-start.10 = (bf16[2,256,640]{2,1,0:T(8,128)(2,1)S(1)}, bf16[2,256,640]{2,1,0:T(8,128)(2,1)S(1)}, u32[]{:S(2)}, u32[]{:S(2)}) collective-permute-start(bf16[2,256,640]{2,1,0:T(8,128)(2,1)S(1)} %bitcast.23), channel_id=1, source_target_pairs={{0,1},{1,2},{2,3},{4,5},{5,6},{6,7},{8,9},{9,10},{10,11},{12,13},{... | collective-permute-start | bytes 1966088 | tf_op jit(solution)/shard_map/ppermute | solution.py:635
  95.2 18.7 %collective-permute-start.11 = (bf16[2,256,640]{2,1,0:T(8,128)(2,1)S(1)}, bf16[2,256,640]{2,1,0:T(8,128)(2,1)S(1)}, u32[]{:S(2)}, u32[]{:S(2)}) collective-permute-start(bf16[2,256,640]{2,1,0:T(8,128)(2,1)S(1)} %bitcast.24), channel_id=1, source_target_pairs={{1,0},{2,1},{3,2},{5,4},{6,5},{7,6},{9,8},{10,9},{11,10},{13,12},{... | collective-permute-start | bytes 1966088 | tf_op jit(solution)/shard_map/ppermute | solution.py:639
  137.8 15.9 %collective-permute-start.22 = (bf16[2,256,640]{2,1,0:T(8,128)(2,1)S(1)}, bf16[2,256,640]{2,1,0:T(8,128)(2,1)S(1)}, u32[]{:S(2)}, u32[]{:S(2)}) collective-permute-start(bf16[2,256,640]{2,1,0:T(8,128)(2,1)S(1)} %bitcast.27), channel_id=1, source_target_pairs={{0,1},{1,2},{2,3},{4,5},{5,6},{6,7},{8,9},{9,10},{10,11},{12,13},{... | collective-permute-start | bytes 1966088 | tf_op jit(solution)/shard_map/ppermute | solution.py:635
  140.0 17.8 %collective-permute-start.23 = (bf16[2,256,640]{2,1,0:T(8,128)(2,1)S(1)}, bf16[2,256,640]{2,1,0:T(8,128)(2,1)S(1)}, u32[]{:S(2)}, u32[]{:S(2)}) collective-permute-start(bf16[2,256,640]{2,1,0:T(8,128)(2,1)S(1)} %bitcast.28), channel_id=1, source_target_pairs={{1,0},{2,1},{3,2},{5,4},{6,5},{7,6},{9,8},{10,9},{11,10},{13,12},{... | collective-permute-start | bytes 1966088 | tf_op jit(solution)/shard_map/ppermute | solution.py:639
  150.2 32.1 %collective-permute-start.31 = (bf16[4,7,80,640]{3,2,1,0:T(8,128)(2,1)}, bf16[4,7,80,640]{3,2,1,0:T(8,128)(2,1)}, u32[]{:S(2)}, u32[]{:S(2)}) collective-permute-start(bf16[4,7,80,640]{3,2,1,0:T(8,128)(2,1)} %get-tuple-element.121), channel_id=1, source_target_pairs={{0,4},{4,0},{8,12},{12,8},{16,20},{20,16},{24,28},{28,24},{1,5},{5... | collective-permute-start | bytes 8601608 | tf_op jit(solution)/shard_map/ppermute | solution.py:613
  180.1 8.3 %collective-permute-start.24 = (bf16[4,160,768]{2,1,0:T(8,128)(2,1)}, bf16[4,160,768]{2,1,0:T(8,128)(2,1)S(1)}, u32[]{:S(2)}, u32[]{:S(2)}) collective-permute-start(bf16[4,160,768]{2,1,0:T(8,128)(2,1)} %get-tuple-element.103), channel_id=1, source_target_pairs={{0,4},{4,0},{8,12},{12,8},{16,20},{20,16},{24,28},{28,24},{1,5},{5... | collective-permute-start | bytes 2949128 | tf_op jit(solution)/shard_map/ppermute | solution.py:613
  180.1 2.2 collective-permute-start.32
  184.9 48.7 %collective-permute-start.33 = (bf16[576,640]{1,0:T(8,128)(2,1)S(1)}, bf16[576,640]{1,0:T(8,128)(2,1)S(1)}, u32[]{:S(2)}, u32[]{:S(2)}) collective-permute-start(bf16[576,640]{1,0:T(8,128)(2,1)S(1)} %get-tuple-element.125), channel_id=1, source_target_pairs={{0,8},{4,12},{8,0},{12,4},{16,24},{20,28},{24,16},{28,20},{1,9},{5... | collective-permute-start | bytes 2211848 | tf_op jit(solution)/shard_map/ppermute | solution.py:613
  185.5 51.7 %collective-permute-start.34 = (bf16[576,640]{1,0:T(8,128)(2,1)S(1)}, bf16[576,640]{1,0:T(8,128)(2,1)S(1)}, u32[]{:S(2)}, u32[]{:S(2)}) collective-permute-start(bf16[576,640]{1,0:T(8,128)(2,1)S(1)} %get-tuple-element.126), channel_id=1, source_target_pairs={{0,16},{4,20},{8,24},{12,28},{16,0},{20,4},{24,8},{28,12},{1,17},{... | collective-permute-start | bytes 2211848 | tf_op jit(solution)/shard_map/ppermute | solution.py:613
  186.9 50.3 %collective-permute-start.35 = (bf16[576,640]{1,0:T(8,128)(2,1)S(1)}, bf16[576,640]{1,0:T(8,128)(2,1)S(1)}, u32[]{:S(2)}, u32[]{:S(2)}) collective-permute-start(bf16[576,640]{1,0:T(8,128)(2,1)S(1)} %get-tuple-element.127), channel_id=1, source_target_pairs={{0,24},{4,28},{8,16},{12,20},{16,8},{20,12},{24,0},{28,4},{1,25},{... | collective-permute-start | bytes 2211848 | tf_op jit(solution)/shard_map/ppermute | solution.py:613
  188.5 54.6 %copy-start.21 = (f32[512,1280]{1,0:T(8,128)S(1)}, f32[512,1280]{1,0:T(8,128)}, u32[]{:S(2)}) copy-start(f32[512,1280]{1,0:T(8,128)} %get-tuple-element.99.e1) | copy-start | bytes 7864324
  188.6 36.2 %collective-permute-start.25 = (bf16[160,768]{1,0:T(8,128)(2,1)S(1)}, bf16[160,768]{1,0:T(8,128)(2,1)S(1)}, u32[]{:S(2)}, u32[]{:S(2)}) collective-permute-start(bf16[160,768]{1,0:T(8,128)(2,1)S(1)} %get-tuple-element.105), channel_id=1, source_target_pairs={{0,8},{4,12},{8,0},{12,4},{16,24},{20,28},{24,16},{28,20},{1,9},{5... | collective-permute-start | bytes 737288 | tf_op jit(solution)/shard_map/ppermute | solution.py:613
  189.2 37.0 %collective-permute-start.26 = (bf16[160,768]{1,0:T(8,128)(2,1)S(1)}, bf16[160,768]{1,0:T(8,128)(2,1)S(1)}, u32[]{:S(2)}, u32[]{:S(2)}) collective-permute-start(bf16[160,768]{1,0:T(8,128)(2,1)S(1)} %get-tuple-element.106), channel_id=1, source_target_pairs={{0,16},{4,20},{8,24},{12,28},{16,0},{20,4},{24,8},{28,12},{1,17},{... | collective-permute-start | bytes 737288 | tf_op jit(solution)/shard_map/ppermute | solution.py:613
  224.8 8.3 %collective-permute-start.27 = (bf16[160,768]{1,0:T(8,128)(2,1)S(1)}, bf16[160,768]{1,0:T(8,128)(2,1)S(1)}, u32[]{:S(2)}, u32[]{:S(2)}) collective-permute-start(bf16[160,768]{1,0:T(8,128)(2,1)S(1)} %get-tuple-element.107), channel_id=1, source_target_pairs={{0,24},{4,28},{8,16},{12,20},{16,8},{20,12},{24,0},{28,4},{1,25},{... | collective-permute-start | bytes 737288 | tf_op jit(solution)/shard_map/ppermute | solution.py:613
  233.3 6.9 %collective-permute-start.28 = (bf16[40,768]{1,0:T(8,128)(2,1)S(1)}, bf16[40,768]{1,0:T(8,128)(2,1)S(1)}, u32[]{:S(2)}, u32[]{:S(2)}) collective-permute-start(bf16[40,768]{1,0:T(8,128)(2,1)S(1)} %get-tuple-element.109), channel_id=1, source_target_pairs={{0,1},{1,2},{2,3},{3,0},{4,5},{5,6},{6,7},{7,4},{8,9},{9,10},{10,1... | collective-permute-start | bytes 184328 | tf_op jit(solution)/shard_map/ppermute | solution.py:618
  233.6 14.6 %collective-permute-start.29 = (bf16[40,768]{1,0:T(8,128)(2,1)S(1)}, bf16[40,768]{1,0:T(8,128)(2,1)S(1)}, u32[]{:S(2)}, u32[]{:S(2)}) collective-permute-start(bf16[40,768]{1,0:T(8,128)(2,1)S(1)} %get-tuple-element.110), channel_id=1, source_target_pairs={{0,2},{1,3},{2,0},{3,1},{4,6},{5,7},{6,4},{7,5},{8,10},{9,11},{10,... | collective-permute-start | bytes 184328 | tf_op jit(solution)/shard_map/ppermute | solution.py:618
  233.6 14.6 %collective-permute-start.30 = (bf16[40,768]{1,0:T(8,128)(2,1)S(1)}, bf16[40,768]{1,0:T(8,128)(2,1)S(1)}, u32[]{:S(2)}, u32[]{:S(2)}) collective-permute-start(bf16[40,768]{1,0:T(8,128)(2,1)S(1)} %get-tuple-element.111), channel_id=1, source_target_pairs={{0,3},{1,0},{2,1},{3,2},{4,7},{5,4},{6,5},{7,6},{8,11},{9,8},{10,9... | collective-permute-start | bytes 184328 | tf_op jit(solution)/shard_map/ppermute | solution.py:618
  238.1 10.8 %collective-permute-start.36 = (bf16[8,20,640]{2,1,0:T(8,128)(2,1)S(1)}, bf16[8,20,640]{2,1,0:T(8,128)(2,1)S(1)}, u32[]{:S(2)}, u32[]{:S(2)}) collective-permute-start(bf16[8,20,640]{2,1,0:T(8,128)(2,1)S(1)} %get-tuple-element.130), channel_id=1, source_target_pairs={{0,1},{1,2},{2,3},{3,0},{4,5},{5,6},{6,7},{7,4},{8,9},{9,10},{10,1... | collective-permute-start | bytes 614408 | tf_op jit(solution)/shard_map/ppermute | solution.py:618
  238.7 19.2 %collective-permute-start.37 = (bf16[8,20,640]{2,1,0:T(8,128)(2,1)S(1)}, bf16[8,20,640]{2,1,0:T(8,128)(2,1)S(1)}, u32[]{:S(2)}, u32[]{:S(2)}) collective-permute-start(bf16[8,20,640]{2,1,0:T(8,128)(2,1)S(1)} %get-tuple-element.131), channel_id=1, source_target_pairs={{0,2},{1,3},{2,0},{3,1},{4,6},{5,7},{6,4},{7,5},{8,10},{9,11},{10,... | collective-permute-start | bytes 614408 | tf_op jit(solution)/shard_map/ppermute | solution.py:618
  240.2 17.7 %collective-permute-start.38 = (bf16[8,20,640]{2,1,0:T(8,128)(2,1)S(1)}, bf16[8,20,640]{2,1,0:T(8,128)(2,1)S(1)}, u32[]{:S(2)}, u32[]{:S(2)}) collective-permute-start(bf16[8,20,640]{2,1,0:T(8,128)(2,1)S(1)} %get-tuple-element.132), channel_id=1, source_target_pairs={{0,3},{1,0},{2,1},{3,2},{4,7},{5,4},{6,5},{7,6},{8,11},{9,8},{10,9... | collective-permute-start | bytes 614408 | tf_op jit(solution)/shard_map/ppermute | solution.py:618
  (35 other events, 155.1 us)

commit v2 on v1

--- a/solution.py
+++ b/solution.py
@@ -73,43 +73,77 @@
     return high, mid, low
 
 
+def by_mask(values, me):
+    bit = 1
+    while bit < len(values):
+        here = (me & bit) != 0
+        values = [jnp.where(here, values[m ^ bit], values[m]) for m in range(len(values))]
+        bit *= 2
+    return values
+
+
 def vmem(n):
     return [pl.BlockSpec(memory_space=pltpu.VMEM)] * n
 
 
-def call(kernel, ins, outs, scratch=(), flops=0, limit=24, name=None):
-    moved = sum(x.size * x.dtype.itemsize for x in ins)
-    moved += sum(o.size * o.dtype.itemsize for o in outs)
+def call(kernel, ins, outs, scratch=(), us=1, limit=12, name=None, after=(), free=0):
+    count = len(ins)
+    skipped = len(after)
+
+    def body(*refs):
+        kernel(*refs[:count], *refs[count + skipped :])
+
     return pl.pallas_call(
-        kernel,
+        body,
         out_shape=list(outs),
-        in_specs=vmem(len(ins)),
+        in_specs=[pl.BlockSpec(memory_space=pltpu.HBM)] * free
+        + vmem(count - free)
+        + [pl.BlockSpec(memory_space=pl.ANY)] * skipped,
         out_specs=vmem(len(outs)),
         scratch_shapes=list(scratch),
         compiler_params=pltpu.CompilerParams(vmem_limit_bytes=limit * MIB),
-        cost_estimate=pl.CostEstimate(flops=int(flops), bytes_accessed=int(moved), transcendentals=0),
+        cost_estimate=pl.CostEstimate(flops=int(us * 1e9), bytes_accessed=1000, transcendentals=0),
         name=name,
-    )(*ins)
+    )(*ins, *after)
 
 
 def sds(shape, dtype):
     return jax.ShapeDtypeStruct(shape, dtype)
 
 
-def pack_kernel(vocab, w_in, head_t, *rest):
-    vecs = rest[: WIDE_VECTORS + NARROW_VECTORS]
-    conv, w_out, group_a, group_b, tile = rest[WIDE_VECTORS + NARROW_VECTORS :]
+def fetch(sources, targets, sems):
+    copies = [
+        pltpu.make_async_copy(source, target, sems.at[j])
+        for j, (source, target) in enumerate(zip(sources, targets))
+    ]
+    for copy in copies:
+        copy.start()
+    for copy in copies:
+        copy.wait()
+
+
+def pack_a_kernel(vocab, *refs):
+    count = 2 + WIDE_VECTORS + NARROW_VECTORS
+    group, tile, sems = refs[count : count + 3]
+    held = refs[count + 3 :]
+    fetch(refs[:count], held, sems)
+    w_in, head_t, vecs = held[0], held[1], held[2:]
     wide, inner = w_in.shape
     tile[...] = jnp.zeros_like(tile)
     tile[0:vocab, 0:wide] = head_t[...].astype(F32)
     for j, v in enumerate(vecs):
         n = v.shape[-1]
         tile[vocab + j : vocab + j + 1, 0:n] = v[...].astype(F32).reshape(1, n)
-    group_a[:, 0:inner] = w_in[...]
-    group_a[:, inner : inner + LANES] = jnp.transpose(tile[...])[0:wide].astype(BF)
-    group_b[0:KERNEL_TAPS] = conv[...]
+    group[:, 0:inner] = w_in[...]
+    group[:, inner : inner + LANES] = jnp.transpose(tile[...])[0:wide].astype(BF)
+
+
+def pack_b_kernel(conv, w_out, group, sems, conv_held, out_held):
+    fetch((conv, w_out), (conv_held, out_held), sems)
+    inner = group.shape[2]
+    group[0:KERNEL_TAPS] = conv_held[...]
     for h in range(w_out.shape[1] // inner):
-        group_b[KERNEL_TAPS + h] = w_out[:, h * inner : (h + 1) * inner]
+        group[KERNEL_TAPS + h] = out_held[:, h * inner : (h + 1) * inner]
 
 
 def place_kernel(axis, n, *refs):
@@ -333,57 +367,81 @@
         each_chunk(length, 32, behind)
 
 
-def conv_grad_kernel(chips, hops, seqs, third_act, out_low, conv_low, *refs):
-    blocks = refs[: 2 * hops + 1]
-    keep, send, turned, total, third_t = refs[2 * hops + 1 :]
-    inner = conv_low.shape[1]
-    length = conv_low.shape[0] // seqs
-    block = keep.shape[2]
-    me = lax.axis_index("dp")
-    core = me & 1
-    slabs = keep.shape[1]
-    for s in range(seqs):
-        for b, ref in enumerate(blocks):
-            turned[s, :, b * length : (b + 1) * length] = jnp.transpose(ref[s])
-    third_t[...] = jnp.transpose(third_act[...])
-
-    def share(slab):
-        for q in range(chips):
-            mine = pl.multiple_of((2 * q + core) * block, block)
-            other = pl.multiple_of((2 * q + 1 - core) * block, block)
-            keep[q, slab] = total[pl.ds(mine, block), :]
-            send[q, slab] = total[pl.ds(other, block), :].astype(BF)
+def conv_grad_kernel(
+    chips,
+    hops,
+    seqs,
+    third_own,
+    third_other,
+    low_own,
+    low_other,
+    out_low,
+    logit_other,
+    extras,
+    stats,
+    stats_other,
+    *refs,
+):
+    count = 2 * hops + 1
+    blocks = (refs[:count], refs[count : 2 * count])
+    own, own_stats = refs[2 * count : 2 * count + 2]
+    sends = refs[2 * count + 2 : 2 * count + 1 + chips]
+    turned, turn, third_t, out_other = refs[2 * count + 1 + chips :]
+    slabs, block, inner = own.shape
+    length = low_own.shape[0] // seqs
+    me = lax.axis_index("dp") // 2
+    core = lax.axis_index("dp") & 1
+    total_stats = stats[...] + stats_other[...]
+    own_stats[...] = total_stats
+    for send in sends:
+        send[slabs * block : slabs * block + 16, :] = jnp.zeros((16, inner), BF)
+        for j, term in enumerate(thirds(total_stats)):
+            send[slabs * block : slabs * block + 8, j * LANES : (j + 1) * LANES] = term
+
+    def chosen(ref, q):
+        even = ref[2 * q * block : (2 * q + 1) * block, :]
+        odd = ref[(2 * q + 1) * block : (2 * q + 2) * block, :]
+        return jnp.where(core == 1, odd, even)
+
+    for side in range(2):
+        for s in range(seqs):
+            for b, ref in enumerate(blocks[side]):
+                turn[...] = jnp.transpose(ref[s])
+                for q in range(chips):
+                    turned[
+                        side * seqs + s,
+                        q * block : (q + 1) * block,
+                        b * length : (b + 1) * length,
+                    ] = chosen(turn, q)
+        for s in range(seqs):
+            columns = slice(s * length, (s + 1) * length)
+            turn[...] = jnp.transpose((third_own, third_other)[side][columns, :])
+            for q in range(chips):
+                third_t[side, q * block : (q + 1) * block, columns] = chosen(turn, q)
+    out_other[...] = dot_nt(logit_other[...], extras[...]).astype(BF)
+
+    def share(slab, value):
+        parts = by_mask([value[q * block : (q + 1) * block] for q in range(chips)], me)
+        own[slab] = parts[0]
+        for m in range(1, chips):
+            sends[m - 1][slab * block : (slab + 1) * block, :] = parts[m].astype(BF)
 
     for k in range(KERNEL_TAPS):
         at = hops * length + (k - CENTRE) * DILATION_RATE
-        value = dot(turned[0, :, at : at + length], conv_low[0:length, :])
-        for s in range(1, seqs):
-            value += dot(
-                turned[s, :, at : at + length], conv_low[s * length : (s + 1) * length, :]
-            )
-        total[...] = value
-        share(k)
+        value = 0.0
+        for side, low in enumerate((low_own, low_other)):
+            for s in range(seqs):
+                value = value + dot(
+                    turned[side * seqs + s, :, at : at + length],
+                    low[s * length : (s + 1) * length, :],
+                )
+        share(k, value)
     for h in range(slabs - KERNEL_TAPS):
-        total[...] = dot(third_t[...], out_low[:, h * inner : (h + 1) * inner])
-        share(KERNEL_TAPS + h)
-
-
-def split_b_kernel(chips, keep, got, stats, stats_got, own, own_stats, *sends):
-    me = lax.axis_index("dp") // 2
-    slabs, block, inner = keep.shape[1:]
-    total_stats = stats[...] + stats_got[...]
-    own_stats[...] = total_stats
-    own[...] = keep[me] + got[me].astype(F32)
-    for m in range(1, chips):
-        q = me ^ m
-        for slab in range(slabs):
-            sends[m - 1][slab * block : (slab + 1) * block, :] = (
-                keep[q, slab] + got[q, slab].astype(F32)
-            ).astype(BF)
-        tail = sends[m - 1].at[slabs * block : slabs * block + 16, :]
-        tail[...] = jnp.zeros_like(tail)
-        for j, term in enumerate(thirds(total_stats)):
-            sends[m - 1][slabs * block : slabs * block + 8, j * LANES : (j + 1) * LANES] = term
+        columns = slice(h * inner, (h + 1) * inner)
+        share(
+            KERNEL_TAPS + h,
+            dot(third_t[0], out_low[:, columns]) + dot(third_t[1], out_other[:, columns]),
+        )
 
 
 def sum_terms(ref_value):
@@ -441,7 +499,8 @@
             out[:, (slab - KERNEL_TAPS) * inner : (slab - KERNEL_TAPS + 1) * inner] = value
 
 
-def split_a_kernel(chips, keep, got, own, *sends):
+def split_a_kernel(chips, keep, got, own, token, *sends):
+    token[...] = jnp.zeros_like(token)
     me = lax.axis_index("dp") // 2
     own[...] = keep[me] + got[me].astype(F32)
     for m in range(1, chips):
@@ -594,7 +653,8 @@
                 send[q, :, inner : inner + LANES] = extra[lines].astype(BF)
 
 
-def input_kernel(e1, n1, r1, wide_v, logit_grad, extras, input_grad, work):
+def input_kernel(e1, n1, r1, wide_v, logit_grad, extras, input_grad, token, work):
+    token[...] = jnp.zeros_like(token)
     work[...] = dot_nt(logit_grad[...], extras[...])
     g1 = wide_v[0:1, :]
 
@@ -674,50 +734,68 @@
     slabs = KERNEL_TAPS + width // inner
     flat = tokens.reshape(rows, width)
 
-    block_a, block_b = call(
-        functools.partial(pack_kernel, vocab),
-        [
-            in_weight,
-            head_weight.T,
-            first_gain,
-            first_bias,
-            out_bias,
-            in_bias,
-            second_gain,
-            second_bias,
-            conv_bias,
-            third_gain,
-            third_bias,
-            jnp.transpose(conv_weight, (1, 0, 2)),
-            out_weight,
-        ],
-        [sds((wide, inner + LANES), BF), sds((slabs, narrow, inner), BF)],
-        [pltpu.VMEM((LANES, LANES), F32)],
-        name="pack",
+    ins = [
+        in_weight,
+        head_weight.T,
+        first_gain,
+        first_bias,
+        out_bias,
+        in_bias,
+        second_gain,
+        second_bias,
+        conv_bias,
+        third_gain,
+        third_bias,
+    ]
+    (block_a,) = call(
+        functools.partial(pack_a_kernel, vocab),
+        ins,
+        [sds((wide, inner + LANES), BF)],
+        [pltpu.VMEM((LANES, LANES), F32), pltpu.SemaphoreType.DMA((len(ins),))]
+        + [pltpu.VMEM(x.shape, BF) for x in ins],
+        limit=56,
+        name="pack_a",
+        free=len(ins),
     )
     parts_a = line_parts(block_a)
+    (line_a,) = call(
+        functools.partial(place_kernel, "seq", size),
+        parts_a,
+        [sds((size * wide, inner + LANES), BF)],
+        name="line_a",
+    )
+    ins = [jnp.transpose(conv_weight, (1, 0, 2)), out_weight]
+    (block_b,) = call(
+        pack_b_kernel,
+        ins,
+        [sds((slabs, narrow, inner), BF)],
+        [pltpu.SemaphoreType.DMA((2,))] + [pltpu.VMEM(x.shape, BF) for x in ins],
+        limit=8,
+        name="pack_b",
+        free=2,
+        after=[block_a],
+    )
+    own_a = [line_a] + [swap(line_a, 2 * m) for m in range(1, chips)]
     parts_b = line_parts(block_b)
     n1, r1 = call(
         first_kernel,
         [flat],
         [sds((rows, width), F32), sds((rows, LANES), F32)],
-        flops=1e9,
+        us=6,
+        limit=8,
         name="first",
-    )
-    (line_a,) = call(
-        functools.partial(place_kernel, "seq", size),
-        parts_a,
-        [sds((size * wide, inner + LANES), BF)],
-        name="line_a",
-    )
-    pieces_a = chip_pieces(line_a)
+        after=[block_b],
+    )
+    *own_a, _ = lax.optimization_barrier((*own_a, r1))
+    pieces_a = list(own_a) + [swap(piece, 1) for piece in own_a]
     (line_b,) = call(
         functools.partial(place_kernel, "seq", size),
         parts_b,
         [sds((slabs, size * narrow, inner), BF)],
         name="line_b",
-    )
-    pieces_b = chip_pieces(line_b)
+        after=[r1],
+    )
+    own_b = [line_b] + [swap(line_b, 2 * m) for m in range(1, chips)]
     w_in, extras, wide_v, narrow_v, act, gp1, n2, gp2, r2, conv_in = call(
         functools.partial(second_kernel, chips, vocab, wide, narrow),
         [n1] + pieces_a,
@@ -734,11 +812,16 @@
             sds((rows, inner), BF),
         ],
         [pltpu.VMEM((rows, inner), F32)],
-        flops=10e9,
-        limit=40,
+        us=9,
+        limit=16,
         name="second",
+        after=[line_b],
     )
     blocks = halo(conv_in.reshape(seqs, length, inner))
+    other_line = swap(line_b, 1)
+    *chip_b, _, _ = lax.optimization_barrier((*own_b[1:], blocks[0], blocks[-1]))
+    pieces_b = [line_b] + list(chip_b) + [other_line] + [swap(piece, 1) for piece in chip_b]
+    other_blocks = [swap(piece, 1) for piece in blocks]
     (
         taps,
         block_out,
@@ -783,53 +866,34 @@
             pltpu.VMEM((length, LANES), F32),
             pltpu.VMEM((length, width), F32),
         ],
-        flops=25e9,
-        limit=48,
+        us=17,
+        limit=16,
         name="middle",
     )
     grad_blocks = halo(conv_low.reshape(seqs, length, inner))
-    keep_b, send_b = call(
+    low_other = swap(conv_low, 1)
+    third_other = swap(third_act, 1)
+    logit_other = swap(logit_grad, 1)
+    stats_other = swap(stats, 1)
+    split_b = call(
         functools.partial(conv_grad_kernel, chips, hops, seqs),
-        [third_act, out_low, conv_low] + blocks,
-        [
-            sds((chips, slabs, size * narrow, inner), F32),
-            sds((chips, slabs, size * narrow, inner), BF),
-        ],
-        [
-            pltpu.VMEM((seqs, inner, (2 * hops + 1) * length), BF),
-            pltpu.VMEM((inner, inner), F32),
-            pltpu.VMEM((inner, rows), BF),
-        ],
-        flops=8e9,
-        limit=40,
-        name="conv_grad",
-    )
-    got_b = swap(send_b, 1)
-    got_stats = swap(stats, 1)
-    split = call(
-        functools.partial(split_b_kernel, chips),
-        [keep_b, got_b, stats, got_stats],
+        [third_act, third_other, conv_low, low_other, out_low, logit_other, extras]
+        + [stats, stats_other]
+        + blocks
+        + other_blocks,
         [sds((slabs, size * narrow, inner), F32), sds((8, LANES), F32)]
         + [sds((slabs * size * narrow + 16, inner), BF)] * (chips - 1),
-        limit=32,
-        name="split_b",
-    )
-    from_chips = [swap(piece, 2 * m) for m, piece in zip(range(1, chips), split[2:])]
-    line = call(
-        functools.partial(line_b_kernel, chips - 1, size, narrow),
-        [split[0], split[1]] + from_chips,
-        [sds((slabs, narrow, inner), F32), sds((8, LANES), F32)]
-        + [sds((slabs + 1, max(narrow, 8), inner), BF)] * (size - 1),
-        name="line_grad_b",
-    )
-    from_line = [shifted(piece, k) for k, piece in zip(range(1, size), line[2:])]
-    conv_share, out_share, sums = call(
-        functools.partial(end_b_kernel, size - 1),
-        [line[0], line[1]] + from_line,
-        [sds((KERNEL_TAPS, narrow, inner), F32), sds((narrow, width), F32), sds((8, LANES), F32)],
-        name="end_b",
-    )
-
+        [
+            pltpu.VMEM((2 * seqs, inner // 2, (2 * hops + 1) * length), BF),
+            pltpu.VMEM((inner, length), BF),
+            pltpu.VMEM((2, inner // 2, rows), BF),
+            pltpu.VMEM((rows, width), BF),
+        ],
+        us=7,
+        limit=16,
+        name="conv_grad",
+    )
+    from_chips_b = [swap(piece, 2 * m) for m, piece in zip(range(1, chips), split_b[2:])]
     keep_a, send_a, e1 = call(
         functools.partial(back_kernel, chips, hops, seqs, vocab, wide, narrow),
         [taps, n2, gp2, r2, n1, gp1, act, w_in, wide_v, narrow_v]
@@ -848,32 +912,53 @@
             pltpu.VMEM((16, width), F32),
             pltpu.VMEM((24, inner), F32),
         ],
-        flops=20e9,
-        limit=56,
+        us=12,
+        limit=20,
         name="back",
-    )
+        after=[split_b[1]],
+    )
+    line_b2 = call(
+        functools.partial(line_b_kernel, chips - 1, size, narrow),
+        [split_b[0], split_b[1]] + from_chips_b,
+        [sds((slabs, narrow, inner), F32), sds((8, LANES), F32)]
+        + [sds((slabs + 1, max(narrow, 8), inner), BF)] * (size - 1),
+        name="line_grad_b",
+    )
+    send_a, _ = lax.optimization_barrier((send_a, line_b2[1]))
     got_a = swap(send_a, 1)
     split = call(
         functools.partial(split_a_kernel, chips),
         [keep_a, got_a],
-        [sds((size * wide, inner + LANES), F32)]
+        [sds((size * wide, inner + LANES), F32), sds((8, LANES), F32)]
         + [sds((size * wide, inner + LANES), BF)] * (chips - 1),
         name="split_a",
-    )
-    from_chips = [swap(piece, 2 * m) for m, piece in zip(range(1, chips), split[1:])]
-    (input_grad,) = call(
+        after=[line_b2[1]],
+    )
+    from_chips = [swap(piece, 2 * m) for m, piece in zip(range(1, chips), split[2:])]
+    from_line_b = [shifted(piece, k) for k, piece in zip(range(1, size), line_b2[2:])]
+
+    input_grad, input_token = call(
         input_kernel,
         [e1, n1, r1, wide_v, logit_grad, extras],
-        [sds((rows, width), BF)],
+        [sds((rows, width), BF), sds((8, LANES), F32)],
         [pltpu.VMEM((rows, width), F32)],
-        flops=5e9,
+        us=5,
         name="input",
+        after=[split[1]],
     )
     line = call(
         functools.partial(line_a_kernel, chips - 1, size, wide),
         [split[0]] + from_chips,
         [sds((wide, inner + LANES), F32)] + [sds((wide, inner + LANES), BF)] * (size - 1),
         name="line_grad_a",
+        after=[input_token],
+    )
+    conv_share, out_share, sums = call(
+        functools.partial(end_b_kernel, size - 1),
+        [line_b2[0], line_b2[1]] + from_line_b,
+        [sds((KERNEL_TAPS, narrow, inner), F32), sds((narrow, width), F32), sds((8, LANES), F32)],
+        name="end_b",
+        after=[line[0]],
     )
     from_line = [shifted(piece, k) for k, piece in zip(range(1, size), line[1:])]
     ended = call(

time: 264 us -> 174 us (0.66)
  waiting for transfers between devices: 113 us -> 56.8 us
  Pallas kernels: 77.4 us -> 59.9 us
  local copies, waits for them, and re-layouts: 18.7 us -> 1.38 us
  starting transfers between devices: 48.7 us -> 52.4 us
    ppermute x23 -> x28, waiting for transfers between devices: 66.2 us -> 35.9 us  [swap(): return lax.ppermute(value, 'dp', [(i, i ^ mask) for i in range(count)])]
    pallas_call x15, Pallas kernels: 77.4 us -> 59.9 us  [call(): pl.pallas_call(body, out_shape=list(outs), in_specs=[pl.BlockSpec(memory_...]
    unnamed x88 -> x16, local copies, waits for them, and re-layouts: 18.2 us -> 0.87 us
    ppermute x12, waiting for transfers between devices: 22.2 us -> 9.38 us  [shifted(): lax.ppermute(value, 'seq', [(i, (i + k) % size) for i in range(size)])]
    ppermute x2, waiting for transfers between devices: 16.6 us -> 4.86 us  [halo(): lax.ppermute(series, 'seq', [(i, i + h) for i in range(size - h)])]
    ppermute x23 -> x28, starting transfers between devices: 16.9 us -> 18.5 us  [swap(): return lax.ppermute(value, 'dp', [(i, i ^ mask) for i in range(count)])]
  transfers between devices with their start and end apart: 39 -> 44, of which waited for: 18 -> 19; matrix products, arithmetic and copies ran while one was open for 0% -> 1% of each run, Pallas kernels for 21% -> 32%
where the time goes in v2:
time: 174 us
  Pallas kernels  59.9 us (34%)
  waiting for transfers between devices  56.8 us (33%)
  starting transfers between devices  52.4 us (30%)
  between operations  2.71 us (2%)
    pallas_call x15, Pallas kernels, call(): pl.pallas_call(body, out_shape=list(outs), in_specs=[pl.BlockSpec(memory_...  59.9 us
    ppermute x28, waiting for transfers between devices, swap(): return lax.ppermute(value, 'dp', [(i, i ^ mask) for i in range(count)])  35.9 us
    ppermute x12, starting transfers between devices, shifted(): lax.ppermute(value, 'seq', [(i, (i + k) % size) for i in range(size)])  20 us
    ppermute x28, starting transfers between devices, swap(): return lax.ppermute(value, 'dp', [(i, i ^ mask) for i in range(count)])  18.5 us
    ppermute x2, starting transfers between devices, halo(): lax.ppermute(series, 'seq', [(i, i + h) for i in range(size - h)])  11 us
    ppermute x12, waiting for transfers between devices, shifted(): lax.ppermute(value, 'seq', [(i, (i + k) % size) for i in range(size)])  9.38 us
    ppermute x2, waiting for transfers between devices, halo(): lax.ppermute(series, 'seq', [(i + h, i) for i in range(size - h)])  6.65 us
    ppermute x2, waiting for transfers between devices, halo(): lax.ppermute(series, 'seq', [(i, i + h) for i in range(size - h)])  4.86 us
  transfers between devices with their start and end apart: 44, of which 19 were waited for; matrix products, arithmetic and copies ran while one was open for 1% of the time, Pallas kernels for 32%

profile of v2, /device:TPU:0, one launch (start us, length us, event | category | flops | bytes accessed | tf_op | source)
XLA Modules:
  0.0 173.7 jit_solution(12333279343752753630)
XLA Ops:
  0.7 1.6 pack_a.1.refs_2_.refs_0_
  2.3 3.1 %collective-permute-start = (bf16[40,768]{1,0:T(8,128)(2,1)}, bf16[40,768]{1,0:T(8,128)(2,1)S(1)}, u32[]{:S(2)}, u32[]{:S(2)}) collective-permute-start(bf16[40,768]{1,0:T(8,128)(2,1)} %pack_a.1.refs_2_.refs_0_), channel_id=1, source_target_pairs={{0,1},{1,2},{2,3},{3,0},{4,5},{5,6},{6,7},{7,4},{8,9},{9,10},{10,1... | collective-permute-start | bytes 184328 | tf_op jit(solution)/shard_map/ppermute | solution.py:678
  5.4 2.6 %collective-permute-start.1 = (bf16[40,768]{1,0:T(8,128)(2,1)}, bf16[40,768]{1,0:T(8,128)(2,1)S(1)}, u32[]{:S(2)}, u32[]{:S(2)}) collective-permute-start(bf16[40,768]{1,0:T(8,128)(2,1)} %pack_a.1.refs_2_.refs_0_), channel_id=1, source_target_pairs={{0,2},{1,3},{2,0},{3,1},{4,6},{5,7},{6,4},{7,5},{8,10},{9,11},{10,... | collective-permute-start | bytes 184328 | tf_op jit(solution)/shard_map/ppermute | solution.py:678
  8.0 1.3 collective-permute-start.2
  10.1 2.4 %collective-permute-done.1.refs_2_ = bf16[40,768]{1,0:T(8,128)(2,1)S(1)} collective-permute-done((bf16[40,768]{1,0:T(8,128)(2,1)}, bf16[40,768]{1,0:T(8,128)(2,1)S(1)}, u32[]{:S(2)}, u32[]{:S(2)}) %collective-permute-start.1) | collective-permute-done | bytes 61472 | tf_op jit(solution)/shard_map/ppermute | solution.py:678
  12.8 0.8 copy-done.3
  13.7 1.6 collective-permute-start.3
  15.6 1.4 collective-permute-start.10
  17.0 2.1 %collective-permute-start.11 = (bf16[7,20,640]{2,1,0:T(8,128)(2,1)S(1)}, bf16[7,20,640]{2,1,0:T(8,128)(2,1)S(1)}, u32[]{:S(2)}, u32[]{:S(2)}) collective-permute-start(bf16[7,20,640]{2,1,0:T(8,128)(2,1)S(1)} %pack_b.1.refs_1_.refs_0_), channel_id=1, source_target_pairs={{0,2},{1,3},{2,0},{3,1},{4,6},{5,7},{6,4},{7,5},{8,10},{9,11},{10,... | collective-permute-start | bytes 537608 | tf_op jit(solution)/shard_map/ppermute | solution.py:678
  19.5 1.5 collective-permute-start.4
  21.0 1.8 %collective-permute-start.5 = (bf16[160,768]{1,0:T(8,128)(2,1)S(1)}, bf16[160,768]{1,0:T(8,128)(2,1)S(1)}, u32[]{:S(2)}, u32[]{:S(2)}) collective-permute-start(bf16[160,768]{1,0:T(8,128)(2,1)S(1)} %line_a.1.refs_1_), channel_id=1, source_target_pairs={{0,24},{4,28},{8,16},{12,20},{16,8},{20,12},{24,0},{28,4},{1,25},{... | collective-permute-start | bytes 737288 | tf_op jit(solution)/shard_map/ppermute | solution.py:673
  22.8 6.0 %first.1 = (f32[512,1280]{1,0:T(8,128)S(1)}, f32[512,128]{1,0:T(8,128)S(1)}) custom-call(bf16[512,1280]{1,0:T(8,128)(2,1)S(1)} %bitcast.19, bf16[7,20,640]{2,1,0:T(8,128)(2,1)S(1)} %pack_b.1.refs_1_.refs_0_), custom_call_target="tpu_custom_call" | custom-call | flops 6000000000 | bytes 1000 | tf_op jit(solution)/shard_map/first/pallas_call | solution.py:96
  28.8 2.5 %collective-permute-done.4.refs_3_ = bf16[160,768]{1,0:T(8,128)(2,1)S(1)} collective-permute-done((bf16[160,768]{1,0:T(8,128)(2,1)S(1)}, bf16[160,768]{1,0:T(8,128)(2,1)S(1)}, u32[]{:S(2)}, u32[]{:S(2)}) %collective-permute-start.4) | collective-permute-done | bytes 245792 | tf_op jit(solution)/shard_map/ppermute | solution.py:673
  32.8 1.3 collective-permute-start.15
  34.9 1.4 collective-permute-start.17
  36.4 9.3 %second.1 = (bf16[1280,640]{1,0:T(8,128)(2,1)S(1)}, bf16[1280,128]{1,0:T(8,128)(2,1)S(1)}, f32[8,1280]{1,0:T(8,128)S(1)}, f32[8,640]{1,0:T(8,128)S(1)}, bf16[512...) custom-call(f32[512,1280]{1,0:T(8,128)S(1)} %get-tuple-element.87.re, ...), custom_call_target="tpu_custom_call" | custom-call | flops 8999999488 | bytes 1000 | tf_op jit(solution)/shard_map/second/pallas_call | solution.py:96
  45.7 7.0 %collective-permute-start.13 = (bf16[2,256,640]{2,1,0:T(8,128)(2,1)S(1)}, bf16[2,256,640]{2,1,0:T(8,128)(2,1)S(1)}, u32[]{:S(2)}, u32[]{:S(2)}) collective-permute-start(bf16[2,256,640]{2,1,0:T(8,128)(2,1)S(1)} %bitcast.21), channel_id=1, source_target_pairs={{0,1},{1,2},{2,3},{4,5},{5,6},{6,7},{8,9},{9,10},{10,11},{12,13},{... | collective-permute-start | bytes 1966088 | tf_op jit(solution)/shard_map/ppermute | solution.py:695
  52.7 1.3 collective-permute-start.14
  54.1 11.9 %collective-permute-done.16.refs_13_ = bf16[7,80,640]{2,1,0:T(8,128)(2,1)S(1)} collective-permute-done((bf16[7,80,640]{2,1,0:T(8,128)(2,1)S(1)}, bf16[7,80,640]{2,1,0:T(8,128)(2,1)S(1)}, u32[]{:S(2)}, u32[]{:S(2)}) %collective-permute-start.16) | collective-permute-done | bytes 716832 | tf_op jit(solution)/shard_map/ppermute | solution.py:673
  66.0 1.6 collective-permute-done.17.refs_14_
  67.6 2.5 %collective-permute-done.14.refs_10_.refs_11_ = bf16[2,256,640]{2,1,0:T(8,128)(2,1)S(1)} collective-permute-done((bf16[2,256,640]{2,1,0:T(8,128)(2,1)S(1)}, bf16[2,256,640]{2,1,0:T(8,128)(2,1)S(1)}, u32[]{:S(2)}, u32[]{:S(2)}) %collective-permute-start.14) | collective-permute-done | bytes 655392 | tf_op jit(solution)/shard_map/ppermute | solution.py:699
  71.2 1.1 collective-permute-done.19.refs_16_
  72.4 0.9 collective-permute-done.20.refs_17_
  73.3 1.0 collective-permute-done.21.refs_18_
  74.4 17.6 %middle.1 = (bf16[7,640,640]{2,1,0:T(8,128)(2,1)S(1)}, bf16[512,1280]{1,0:T(8,128)(2,1)}, bf16[512,640]{1,0:T(8,128)(2,1)S(1)}, bf16[512,1280]{1,0:T(8,128)(2,1)...) custom-call(f32[8,1280]{1,0:T(8,128)S(1)} %get-tuple-element.93.refs, ...), custom_call_target="tpu_custom_call" | custom-call | flops 16999999488 | bytes 1000 | tf_op jit(solution)/shard_map/middle/pallas_call | solution.py:96
  92.9 4.0 %collective-permute-start.22 = (bf16[2,256,640]{2,1,0:T(8,128)(2,1)S(1)}, bf16[2,256,640]{2,1,0:T(8,128)(2,1)S(1)}, u32[]{:S(2)}, u32[]{:S(2)}) collective-permute-start(bf16[2,256,640]{2,1,0:T(8,128)(2,1)S(1)} %bitcast.26), channel_id=1, source_target_pairs={{0,1},{1,2},{2,3},{4,5},{5,6},{6,7},{8,9},{9,10},{10,11},{12,13},{... | collective-permute-start | bytes 1966088 | tf_op jit(solution)/shard_map/ppermute | solution.py:695
  97.0 1.5 collective-permute-start.23
  98.5 4.3 %conv_grad.1 = (f32[7,80,640]{2,1,0:T(8,128)S(1)}, f32[8,128]{1,0:T(8,128)S(1)}, bf16[576,640]{1,0:T(8,128)(2,1)S(1)}, bf16[576,640]{1,0:T(8,128)(2,1)S(1)}, bf16[576,640]{1,0:T(8,128)(2,1)S(1)}) custom-call(bf16[512,640]{1,0:T(8,128)(2,1)S(1)} %get-tuple-element.112.refs_0_, bf16[512,640]{1,0:T(8,128)(2,1)S(1)} %collective-permute-done.24.refs_1_, ...), custom_call_target="tpu_custom_call" | custom-call | flops 7000000000 | bytes 1000 | tf_op jit(solution)/shard_map/conv_grad/pallas_call | solution.py:96
  102.8 0.9 collective-permute-start.31
  103.7 1.5 collective-permute-start.32
  105.2 1.1 collective-permute-start.33
  106.3 4.9 %collective-permute-done.22.refs_13_ = bf16[2,256,640]{2,1,0:T(8,128)(2,1)S(1)} collective-permute-done((bf16[2,256,640]{2,1,0:T(8,128)(2,1)S(1)}, bf16[2,256,640]{2,1,0:T(8,128)(2,1)S(1)}, u32[]{:S(2)}, u32[]{:S(2)}) %collective-permute-start.22) | collective-permute-done | bytes 655392 | tf_op jit(solution)/shard_map/ppermute | solution.py:695
  111.2 4.2 %collective-permute-done.23.refs_15_ = bf16[2,256,640]{2,1,0:T(8,128)(2,1)S(1)} collective-permute-done((bf16[2,256,640]{2,1,0:T(8,128)(2,1)S(1)}, bf16[2,256,640]{2,1,0:T(8,128)(2,1)S(1)}, u32[]{:S(2)}, u32[]{:S(2)}) %collective-permute-start.23) | collective-permute-done | bytes 655392 | tf_op jit(solution)/shard_map/ppermute | solution.py:699
  115.4 12.5 %back.1 = (f32[4,160,768]{2,1,0:T(8,128)S(1)}, bf16[4,160,768]{2,1,0:T(8,128)(2,1)S(1)}, f32[512,1280]{1,0:T(8,128)S(1)}) custom-call(bf16[7,640,640]{2,1,0:T(8,128)(2,1)S(1)} %get-tuple-element.101.refs_0_, f32[512,640]{1,0:T(8,128)S(1)} %get-tuple-element.102.refs_1_, f32[512,640]{1,0:T(8,128)S(1)} %get-tuple-element.103.refs_2_, ...), custom_call_target="tpu_custom_call" | custom-call | flops 12000000000 | bytes 1000 | tf_op jit(solution)/shard_map/back/pallas_call | solution.py:96
  127.9 9.5 %collective-permute-done.32.refs_3_ = bf16[576,640]{1,0:T(8,128)(2,1)S(1)} collective-permute-done((bf16[576,640]{1,0:T(8,128)(2,1)S(1)}, bf16[576,640]{1,0:T(8,128)(2,1)S(1)}, u32[]{:S(2)}, u32[]{:S(2)}) %collective-permute-start.32) | collective-permute-done | bytes 737312 | tf_op jit(solution)/shard_map/ppermute | solution.py:673
  138.4 2.6 %collective-permute-done.34.refs_1_ = bf16[4,160,768]{2,1,0:T(8,128)(2,1)S(1)} collective-permute-done((bf16[4,160,768]{2,1,0:T(8,128)(2,1)S(1)}, bf16[4,160,768]{2,1,0:T(8,128)(2,1)S(1)}, u32[]{:S(2)}, u32[]{:S(2)}) %collective-permute-start.34) | collective-permute-done | bytes 983072 | tf_op jit(solution)/shard_map/ppermute | solution.py:673
  141.2 1.3 collective-permute-start.35
  142.5 2.4 %collective-permute-start.41 = (bf16[8,20,640]{2,1,0:T(8,128)(2,1)S(1)}, bf16[8,20,640]{2,1,0:T(8,128)(2,1)S(1)}, u32[]{:S(2)}, u32[]{:S(2)}) collective-permute-start(bf16[8,20,640]{2,1,0:T(8,128)(2,1)S(1)} %get-tuple-element.144), channel_id=1, source_target_pairs={{0,1},{1,2},{2,3},{3,0},{4,5},{5,6},{6,7},{7,4},{8,9},{9,10},{10,1... | collective-permute-start | bytes 614408 | tf_op jit(solution)/shard_map/ppermute | solution.py:678
  144.8 1.6 collective-permute-start.42
  146.4 1.3 collective-permute-start.43
  147.7 0.9 collective-permute-start.36
  149.2 1.5 collective-permute-start.37
  150.7 5.1 %input.1 = (bf16[512,1280]{1,0:T(8,128)(2,1)}, f32[8,128]{1,0:T(8,128)S(1)}) custom-call(f32[512,1280]{1,0:T(8,128)S(1)} %get-tuple-element.117.refs_0_, f32[512,1280]{1,0:T(8,128)S(1)} %get-tuple-element.87.refs_0_.refs_4_.refs_1_, f32[512,128]{1,0:T(8,128)S(1)} %get-tuple-element.88.refs_4_.refs_2_, ...), custom_call_target="tpu_custom_call" | custom-call | flops 5000000000 | bytes 1000 | tf_op jit(solution)/shard_map/input/pallas_call | solution.py:96
  155.8 4.0 %collective-permute-done.36.refs_2_ = bf16[160,768]{1,0:T(8,128)(2,1)S(1)} collective-permute-done((bf16[160,768]{1,0:T(8,128)(2,1)S(1)}, bf16[160,768]{1,0:T(8,128)(2,1)S(1)}, u32[]{:S(2)}, u32[]{:S(2)}) %collective-permute-start.36) | collective-permute-done | bytes 245792 | tf_op jit(solution)/shard_map/ppermute | solution.py:673
  160.8 1.3 collective-permute-start.39
  162.1 1.8 %collective-permute-start.40 = (bf16[40,768]{1,0:T(8,128)(2,1)S(1)}, bf16[40,768]{1,0:T(8,128)(2,1)S(1)}, u32[]{:S(2)}, u32[]{:S(2)}) collective-permute-start(bf16[40,768]{1,0:T(8,128)(2,1)S(1)} %get-tuple-element.136), channel_id=1, source_target_pairs={{0,3},{1,0},{2,1},{3,2},{4,7},{5,4},{6,5},{7,6},{8,11},{9,8},{10,9... | collective-permute-start | bytes 184328 | tf_op jit(solution)/shard_map/ppermute | solution.py:678
  163.9 0.8 end_b.1
  166.5 5.4 %collective-permute-done.39.refs_2_ = bf16[40,768]{1,0:T(8,128)(2,1)S(1)} collective-permute-done((bf16[40,768]{1,0:T(8,128)(2,1)S(1)}, bf16[40,768]{1,0:T(8,128)(2,1)S(1)}, u32[]{:S(2)}, u32[]{:S(2)}) %collective-permute-start.39) | collective-permute-done | bytes 61472 | tf_op jit(solution)/shard_map/ppermute | solution.py:678
  (74 shorter events, 10.9 us)
Async XLA Ops:
  2.3 7.8 %collective-permute-start = (bf16[40,768]{1,0:T(8,128)(2,1)}, bf16[40,768]{1,0:T(8,128)(2,1)S(1)}, u32[]{:S(2)}, u32[]{:S(2)}) collective-permute-start(bf16[40,768]{1,0:T(8,128)(2,1)} %pack_a.1.refs_2_.refs_0_), channel_id=1, source_target_pairs={{0,1},{1,2},{2,3},{3,0},{4,5},{5,6},{6,7},{7,4},{8,9},{9,10},{10,1... | collective-permute-start | bytes 184328 | tf_op jit(solution)/shard_map/ppermute | solution.py:678
  5.4 7.1 %collective-permute-start.1 = (bf16[40,768]{1,0:T(8,128)(2,1)}, bf16[40,768]{1,0:T(8,128)(2,1)S(1)}, u32[]{:S(2)}, u32[]{:S(2)}) collective-permute-start(bf16[40,768]{1,0:T(8,128)(2,1)} %pack_a.1.refs_2_.refs_0_), channel_id=1, source_target_pairs={{0,2},{1,3},{2,0},{3,1},{4,6},{5,7},{6,4},{7,5},{8,10},{9,11},{10,... | collective-permute-start | bytes 184328 | tf_op jit(solution)/shard_map/ppermute | solution.py:678
  8.0 4.8 %collective-permute-start.2 = (bf16[40,768]{1,0:T(8,128)(2,1)}, bf16[40,768]{1,0:T(8,128)(2,1)S(1)}, u32[]{:S(2)}, u32[]{:S(2)}) collective-permute-start(bf16[40,768]{1,0:T(8,128)(2,1)} %pack_a.1.refs_2_.refs_0_), channel_id=1, source_target_pairs={{0,3},{1,0},{2,1},{3,2},{4,7},{5,4},{6,5},{7,6},{8,11},{9,8},{10,9... | collective-permute-start | bytes 184328 | tf_op jit(solution)/shard_map/ppermute | solution.py:678
  13.7 7.3 %collective-permute-start.3 = (bf16[160,768]{1,0:T(8,128)(2,1)S(1)}, bf16[160,768]{1,0:T(8,128)(2,1)S(1)}, u32[]{:S(2)}, u32[]{:S(2)}) collective-permute-start(bf16[160,768]{1,0:T(8,128)(2,1)S(1)} %line_a.1.refs_1_), channel_id=1, source_target_pairs={{0,8},{4,12},{8,0},{12,4},{16,24},{20,28},{24,16},{28,20},{1,9},{5... | collective-permute-start | bytes 737288 | tf_op jit(solution)/shard_map/ppermute | solution.py:673
  15.6 16.3 %collective-permute-start.10 = (bf16[7,20,640]{2,1,0:T(8,128)(2,1)S(1)}, bf16[7,20,640]{2,1,0:T(8,128)(2,1)S(1)}, u32[]{:S(2)}, u32[]{:S(2)}) collective-permute-start(bf16[7,20,640]{2,1,0:T(8,128)(2,1)S(1)} %pack_b.1.refs_1_.refs_0_), channel_id=1, source_target_pairs={{0,1},{1,2},{2,3},{3,0},{4,5},{5,6},{6,7},{7,4},{8,9},{9,10},{10,1... | collective-permute-start | bytes 537608 | tf_op jit(solution)/shard_map/ppermute | solution.py:678
  17.0 15.4 %collective-permute-start.11 = (bf16[7,20,640]{2,1,0:T(8,128)(2,1)S(1)}, bf16[7,20,640]{2,1,0:T(8,128)(2,1)S(1)}, u32[]{:S(2)}, u32[]{:S(2)}) collective-permute-start(bf16[7,20,640]{2,1,0:T(8,128)(2,1)S(1)} %pack_b.1.refs_1_.refs_0_), channel_id=1, source_target_pairs={{0,2},{1,3},{2,0},{3,1},{4,6},{5,7},{6,4},{7,5},{8,10},{9,11},{10,... | collective-permute-start | bytes 537608 | tf_op jit(solution)/shard_map/ppermute | solution.py:678
  19.1 13.4 %collective-permute-start.12 = (bf16[7,20,640]{2,1,0:T(8,128)(2,1)S(1)}, bf16[7,20,640]{2,1,0:T(8,128)(2,1)S(1)}, u32[]{:S(2)}, u32[]{:S(2)}) collective-permute-start(bf16[7,20,640]{2,1,0:T(8,128)(2,1)S(1)} %pack_b.1.refs_1_.refs_0_), channel_id=1, source_target_pairs={{0,3},{1,0},{2,1},{3,2},{4,7},{5,4},{6,5},{7,6},{8,11},{9,8},{10,9... | collective-permute-start | bytes 537608 | tf_op jit(solution)/shard_map/ppermute | solution.py:678
  19.5 11.9 %collective-permute-start.4 = (bf16[160,768]{1,0:T(8,128)(2,1)S(1)}, bf16[160,768]{1,0:T(8,128)(2,1)S(1)}, u32[]{:S(2)}, u32[]{:S(2)}) collective-permute-start(bf16[160,768]{1,0:T(8,128)(2,1)S(1)} %line_a.1.refs_1_), channel_id=1, source_target_pairs={{0,16},{4,20},{8,24},{12,28},{16,0},{20,4},{24,8},{28,12},{1,17},{... | collective-permute-start | bytes 737288 | tf_op jit(solution)/shard_map/ppermute | solution.py:673
  21.0 10.3 %collective-permute-start.5 = (bf16[160,768]{1,0:T(8,128)(2,1)S(1)}, bf16[160,768]{1,0:T(8,128)(2,1)S(1)}, u32[]{:S(2)}, u32[]{:S(2)}) collective-permute-start(bf16[160,768]{1,0:T(8,128)(2,1)S(1)} %line_a.1.refs_1_), channel_id=1, source_target_pairs={{0,24},{4,28},{8,16},{12,20},{16,8},{20,12},{24,0},{28,4},{1,25},{... | collective-permute-start | bytes 737288 | tf_op jit(solution)/shard_map/ppermute | solution.py:673
  31.4 2.7 %collective-permute-start.6 = (bf16[160,768]{1,0:T(8,128)(2,1)S(1)}, bf16[160,768]{1,0:T(8,128)(2,1)S(1)}, u32[]{:S(2)}, u32[]{:S(2)}) collective-permute-start(bf16[160,768]{1,0:T(8,128)(2,1)S(1)} %line_a.1.refs_1_), channel_id=1, source_target_pairs={{0,4},{4,0},{8,12},{12,8},{16,20},{20,16},{24,28},{28,24},{1,5},{5... | collective-permute-start | bytes 737288 | tf_op jit(solution)/shard_map/ppermute | solution.py:673
  31.4 3.5 %collective-permute-start.7 = (bf16[160,768]{1,0:T(8,128)(2,1)S(1)}, bf16[160,768]{1,0:T(8,128)(2,1)S(1)}, u32[]{:S(2)}, u32[]{:S(2)}) collective-permute-start(bf16[160,768]{1,0:T(8,128)(2,1)S(1)} %collective-permute-done.3.refs_2_), channel_id=1, source_target_pairs={{0,4},{4,0},{8,12},{12,8},{16,20},{20,16},{24,28},{28,24},{1,5},{5... | collective-permute-start | bytes 737288 | tf_op jit(solution)/shard_map/ppermute | solution.py:673
  31.9 4.4 %collective-permute-start.8 = (bf16[160,768]{1,0:T(8,128)(2,1)S(1)}, bf16[160,768]{1,0:T(8,128)(2,1)S(1)}, u32[]{:S(2)}, u32[]{:S(2)}) collective-permute-start(bf16[160,768]{1,0:T(8,128)(2,1)S(1)} %collective-permute-done.4.refs_3_), channel_id=1, source_target_pairs={{0,4},{4,0},{8,12},{12,8},{16,20},{20,16},{24,28},{28,24},{1,5},{5... | collective-permute-start | bytes 737288 | tf_op jit(solution)/shard_map/ppermute | solution.py:673
  32.4 3.9 %collective-permute-start.9 = (bf16[160,768]{1,0:T(8,128)(2,1)S(1)}, bf16[160,768]{1,0:T(8,128)(2,1)S(1)}, u32[]{:S(2)}, u32[]{:S(2)}) collective-permute-start(bf16[160,768]{1,0:T(8,128)(2,1)S(1)} %collective-permute-done.5.refs_4_), channel_id=1, source_target_pairs={{0,4},{4,0},{8,12},{12,8},{16,20},{20,16},{24,28},{28,24},{1,5},{5... | collective-permute-start | bytes 737288 | tf_op jit(solution)/shard_map/ppermute | solution.py:673
  32.8 21.2 %collective-permute-start.15 = (bf16[7,80,640]{2,1,0:T(8,128)(2,1)S(1)}, bf16[7,80,640]{2,1,0:T(8,128)(2,1)S(1)}, u32[]{:S(2)}, u32[]{:S(2)}) collective-permute-start(bf16[7,80,640]{2,1,0:T(8,128)(2,1)S(1)} %line_b.1.refs_9_.refs_11_), channel_id=1, source_target_pairs={{0,8},{4,12},{8,0},{12,4},{16,24},{20,28},{24,16},{28,20},{1,9},{5... | collective-permute-start | bytes 2150408 | tf_op jit(solution)/shard_map/ppermute | solution.py:673
  34.1 31.9 %collective-permute-start.16 = (bf16[7,80,640]{2,1,0:T(8,128)(2,1)S(1)}, bf16[7,80,640]{2,1,0:T(8,128)(2,1)S(1)}, u32[]{:S(2)}, u32[]{:S(2)}) collective-permute-start(bf16[7,80,640]{2,1,0:T(8,128)(2,1)S(1)} %line_b.1.refs_9_.refs_11_), channel_id=1, source_target_pairs={{0,16},{4,20},{8,24},{12,28},{16,0},{20,4},{24,8},{28,12},{1,17},{... | collective-permute-start | bytes 2150408 | tf_op jit(solution)/shard_map/ppermute | solution.py:673
  34.9 32.7 %collective-permute-start.17 = (bf16[7,80,640]{2,1,0:T(8,128)(2,1)S(1)}, bf16[7,80,640]{2,1,0:T(8,128)(2,1)S(1)}, u32[]{:S(2)}, u32[]{:S(2)}) collective-permute-start(bf16[7,80,640]{2,1,0:T(8,128)(2,1)S(1)} %line_b.1.refs_9_.refs_11_), channel_id=1, source_target_pairs={{0,24},{4,28},{8,16},{12,20},{16,8},{20,12},{24,0},{28,4},{1,25},{... | collective-permute-start | bytes 2150408 | tf_op jit(solution)/shard_map/ppermute | solution.py:673
  36.3 34.3 %copy-start.7 = (bf16[30]{0:T(256)(128)(2,1)S(1)}, bf16[30]{0:T(256)(128)(2,1)}, u32[]{:S(2)}) copy-start(bf16[30]{0:T(256)(128)(2,1)} %param.32) | copy-start | bytes 184
  36.3 38.0 %copy-start.4 = (s32[2,256]{1,0:T(2,128)S(1)}, s32[2,256]{1,0:T(2,128)}, u32[]{:S(2)}) copy-start(s32[2,256]{1,0:T(2,128)} %refs_4_.3) | copy-start | bytes 6148
  36.4 38.0 %copy-start.5 = (s32[2,153]{1,0:T(2,128)S(1)}, s32[2,153]{1,0:T(2,128)}, u32[]{:S(2)}) copy-start(s32[2,153]{1,0:T(2,128)} %refs_5_.3) | copy-start | bytes 3676
  36.4 38.0 %copy-start.6 = (s32[2,153]{1,0:T(2,128)S(1)}, s32[2,153]{1,0:T(2,128)}, u32[]{:S(2)}) copy-start(s32[2,153]{1,0:T(2,128)} %refs_6_.3) | copy-start | bytes 3676
  45.7 22.0 %collective-permute-start.13 = (bf16[2,256,640]{2,1,0:T(8,128)(2,1)S(1)}, bf16[2,256,640]{2,1,0:T(8,128)(2,1)S(1)}, u32[]{:S(2)}, u32[]{:S(2)}) collective-permute-start(bf16[2,256,640]{2,1,0:T(8,128)(2,1)S(1)} %bitcast.21), channel_id=1, source_target_pairs={{0,1},{1,2},{2,3},{4,5},{5,6},{6,7},{8,9},{9,10},{10,11},{12,13},{... | collective-permute-start | bytes 1966088 | tf_op jit(solution)/shard_map/ppermute | solution.py:695
  52.7 17.4 %collective-permute-start.14 = (bf16[2,256,640]{2,1,0:T(8,128)(2,1)S(1)}, bf16[2,256,640]{2,1,0:T(8,128)(2,1)S(1)}, u32[]{:S(2)}, u32[]{:S(2)}) collective-permute-start(bf16[2,256,640]{2,1,0:T(8,128)(2,1)S(1)} %bitcast.22), channel_id=1, source_target_pairs={{1,0},{2,1},{3,2},{5,4},{6,5},{7,6},{9,8},{10,9},{11,10},{13,12},{... | collective-permute-start | bytes 1966088 | tf_op jit(solution)/shard_map/ppermute | solution.py:699
  54.0 17.2 %collective-permute-start.18 = (bf16[7,80,640]{2,1,0:T(8,128)(2,1)S(1)}, bf16[7,80,640]{2,1,0:T(8,128)(2,1)S(1)}, u32[]{:S(2)}, u32[]{:S(2)}) collective-permute-start(bf16[7,80,640]{2,1,0:T(8,128)(2,1)S(1)} %line_b.1.refs_9_.refs_11_), channel_id=1, source_target_pairs={{0,4},{4,0},{8,12},{12,8},{16,20},{20,16},{24,28},{28,24},{1,5},{5... | collective-permute-start | bytes 2150408 | tf_op jit(solution)/shard_map/ppermute | solution.py:673
  70.1 2.2 %collective-permute-start.19 = (bf16[7,80,640]{2,1,0:T(8,128)(2,1)S(1)}, bf16[7,80,640]{2,1,0:T(8,128)(2,1)S(1)}, u32[]{:S(2)}, u32[]{:S(2)}) collective-permute-start(bf16[7,80,640]{2,1,0:T(8,128)(2,1)S(1)} %collective-permute-done.15.refs_12_), channel_id=1, source_target_pairs={{0,4},{4,0},{8,12},{12,8},{16,20},{20,16},{24,28},{28,24},{1,5},{5... | collective-permute-start | bytes 2150408 | tf_op jit(solution)/shard_map/ppermute | solution.py:673
  70.1 3.2 %collective-permute-start.20 = (bf16[7,80,640]{2,1,0:T(8,128)(2,1)S(1)}, bf16[7,80,640]{2,1,0:T(8,128)(2,1)S(1)}, u32[]{:S(2)}, u32[]{:S(2)}) collective-permute-start(bf16[7,80,640]{2,1,0:T(8,128)(2,1)S(1)} %collective-permute-done.16.refs_13_), channel_id=1, source_target_pairs={{0,4},{4,0},{8,12},{12,8},{16,20},{20,16},{24,28},{28,24},{1,5},{5... | collective-permute-start | bytes 2150408 | tf_op jit(solution)/shard_map/ppermute | solution.py:673
  70.6 3.7 %collective-permute-start.21 = (bf16[7,80,640]{2,1,0:T(8,128)(2,1)S(1)}, bf16[7,80,640]{2,1,0:T(8,128)(2,1)S(1)}, u32[]{:S(2)}, u32[]{:S(2)}) collective-permute-start(bf16[7,80,640]{2,1,0:T(8,128)(2,1)S(1)} %collective-permute-done.17.refs_14_), channel_id=1, source_target_pairs={{0,4},{4,0},{8,12},{12,8},{16,20},{20,16},{24,28},{28,24},{1,5},{5... | collective-permute-start | bytes 2150408 | tf_op jit(solution)/shard_map/ppermute | solution.py:673
  70.6 21.8 %collective-permute-start.29 = (bf16[2,256,640]{2,1,0:T(8,128)(2,1)S(1)}, bf16[2,256,640]{2,1,0:T(8,128)(2,1)S(1)}, u32[]{:S(2)}, u32[]{:S(2)}) collective-permute-start(bf16[2,256,640]{2,1,0:T(8,128)(2,1)S(1)} %bitcast.23), channel_id=1, source_target_pairs={{0,4},{4,0},{8,12},{12,8},{16,20},{20,16},{24,28},{28,24},{1,5},{5... | collective-permute-start | bytes 1966088 | tf_op jit(solution)/shard_map/ppermute | solution.py:673
  71.1 21.4 %collective-permute-start.28 = (bf16[2,256,640]{2,1,0:T(8,128)(2,1)S(1)}, bf16[2,256,640]{2,1,0:T(8,128)(2,1)S(1)}, u32[]{:S(2)}, u32[]{:S(2)}) collective-permute-start(bf16[2,256,640]{2,1,0:T(8,128)(2,1)S(1)} %collective-permute-done.13.refs_8_.refs_9_), channel_id=1, source_target_pairs={{0,4},{4,0},{8,12},{12,8},{16,20},{20,16},{24,28},{28,24},{1,5},{5... | collective-permute-start | bytes 1966088 | tf_op jit(solution)/shard_map/ppermute | solution.py:673
  72.3 20.7 %collective-permute-start.30 = (bf16[2,256,640]{2,1,0:T(8,128)(2,1)S(1)}, bf16[2,256,640]{2,1,0:T(8,128)(2,1)S(1)}, u32[]{:S(2)}, u32[]{:S(2)}) collective-permute-start(bf16[2,256,640]{2,1,0:T(8,128)(2,1)S(1)} %collective-permute-done.14.refs_10_.refs_11_), channel_id=1, source_target_pairs={{0,4},{4,0},{8,12},{12,8},{16,20},{20,16},{24,28},{28,24},{1,5},{5... | collective-permute-start | bytes 1966088 | tf_op jit(solution)/shard_map/ppermute | solution.py:673
  91.9 6.6 %collective-permute-start.24 = (bf16[512,640]{1,0:T(8,128)(2,1)S(1)}, bf16[512,640]{1,0:T(8,128)(2,1)S(1)}, u32[]{:S(2)}, u32[]{:S(2)}) collective-permute-start(bf16[512,640]{1,0:T(8,128)(2,1)S(1)} %get-tuple-element.112.refs_0_), channel_id=1, source_target_pairs={{0,4},{4,0},{8,12},{12,8},{16,20},{20,16},{24,28},{28,24},{1,5},{5... | collective-permute-start | bytes 1966088 | tf_op jit(solution)/shard_map/ppermute | solution.py:673
  92.0 6.5 %collective-permute-start.25 = (bf16[512,640]{1,0:T(8,128)(2,1)S(1)}, bf16[512,640]{1,0:T(8,128)(2,1)S(1)}, u32[]{:S(2)}, u32[]{:S(2)}) collective-permute-start(bf16[512,640]{1,0:T(8,128)(2,1)S(1)} %get-tuple-element.111.refs_2_), channel_id=1, source_target_pairs={{0,4},{4,0},{8,12},{12,8},{16,20},{20,16},{24,28},{28,24},{1,5},{5... | collective-permute-start | bytes 1966088 | tf_op jit(solution)/shard_map/ppermute | solution.py:673
  92.4 6.0 %collective-permute-start.26 = (bf16[512,128]{1,0:T(8,128)(2,1)S(1)}, bf16[512,128]{1,0:T(8,128)(2,1)S(1)}, u32[]{:S(2)}, u32[]{:S(2)}) collective-permute-start(bf16[512,128]{1,0:T(8,128)(2,1)S(1)} %get-tuple-element.114.refs_4_), channel_id=1, source_target_pairs={{0,4},{4,0},{8,12},{12,8},{16,20},{20,16},{24,28},{28,24},{1,5},{5... | collective-permute-start | bytes 393224 | tf_op jit(solution)/shard_map/ppermute | solution.py:673
  92.5 4.4 %collective-permute-start.27 = (f32[8,128]{1,0:T(8,128)S(1)}, f32[8,128]{1,0:T(8,128)S(1)}, u32[]{:S(2)}, u32[]{:S(2)}) collective-permute-start(f32[8,128]{1,0:T(8,128)S(1)} %get-tuple-element.115.refs_7_), channel_id=1, source_target_pairs={{0,4},{4,0},{8,12},{12,8},{16,20},{20,16},{24,28},{28,24},{1,5},{5... | collective-permute-start | bytes 12296 | tf_op jit(solution)/shard_map/ppermute | solution.py:673
  92.9 18.3 %collective-permute-start.22 = (bf16[2,256,640]{2,1,0:T(8,128)(2,1)S(1)}, bf16[2,256,640]{2,1,0:T(8,128)(2,1)S(1)}, u32[]{:S(2)}, u32[]{:S(2)}) collective-permute-start(bf16[2,256,640]{2,1,0:T(8,128)(2,1)S(1)} %bitcast.26), channel_id=1, source_target_pairs={{0,1},{1,2},{2,3},{4,5},{5,6},{6,7},{8,9},{9,10},{10,11},{12,13},{... | collective-permute-start | bytes 1966088 | tf_op jit(solution)/shard_map/ppermute | solution.py:695
  97.0 18.4 %collective-permute-start.23 = (bf16[2,256,640]{2,1,0:T(8,128)(2,1)S(1)}, bf16[2,256,640]{2,1,0:T(8,128)(2,1)S(1)}, u32[]{:S(2)}, u32[]{:S(2)}) collective-permute-start(bf16[2,256,640]{2,1,0:T(8,128)(2,1)S(1)} %bitcast.27), channel_id=1, source_target_pairs={{1,0},{2,1},{3,2},{5,4},{6,5},{7,6},{9,8},{10,9},{11,10},{13,12},{... | collective-permute-start | bytes 1966088 | tf_op jit(solution)/shard_map/ppermute | solution.py:699
  102.8 25.1 %collective-permute-start.31 = (bf16[576,640]{1,0:T(8,128)(2,1)S(1)}, bf16[576,640]{1,0:T(8,128)(2,1)S(1)}, u32[]{:S(2)}, u32[]{:S(2)}) collective-permute-start(bf16[576,640]{1,0:T(8,128)(2,1)S(1)} %get-tuple-element.121), channel_id=1, source_target_pairs={{0,8},{4,12},{8,0},{12,4},{16,24},{20,28},{24,16},{28,20},{1,9},{5... | collective-permute-start | bytes 2211848 | tf_op jit(solution)/shard_map/ppermute | solution.py:673
  103.7 33.7 %collective-permute-start.32 = (bf16[576,640]{1,0:T(8,128)(2,1)S(1)}, bf16[576,640]{1,0:T(8,128)(2,1)S(1)}, u32[]{:S(2)}, u32[]{:S(2)}) collective-permute-start(bf16[576,640]{1,0:T(8,128)(2,1)S(1)} %get-tuple-element.122), channel_id=1, source_target_pairs={{0,16},{4,20},{8,24},{12,28},{16,0},{20,4},{24,8},{28,12},{1,17},{... | collective-permute-start | bytes 2211848 | tf_op jit(solution)/shard_map/ppermute | solution.py:673
  105.2 32.2 %collective-permute-start.33 = (bf16[576,640]{1,0:T(8,128)(2,1)S(1)}, bf16[576,640]{1,0:T(8,128)(2,1)S(1)}, u32[]{:S(2)}, u32[]{:S(2)}) collective-permute-start(bf16[576,640]{1,0:T(8,128)(2,1)S(1)} %get-tuple-element.123), channel_id=1, source_target_pairs={{0,24},{4,28},{8,16},{12,20},{16,8},{20,12},{24,0},{28,4},{1,25},{... | collective-permute-start | bytes 2211848 | tf_op jit(solution)/shard_map/ppermute | solution.py:673
  138.3 2.6 %collective-permute-start.34 = (bf16[4,160,768]{2,1,0:T(8,128)(2,1)S(1)}, bf16[4,160,768]{2,1,0:T(8,128)(2,1)S(1)}, u32[]{:S(2)}, u32[]{:S(2)}) collective-permute-start(bf16[4,160,768]{2,1,0:T(8,128)(2,1)S(1)} %get-tuple-element.125), channel_id=1, source_target_pairs={{0,4},{4,0},{8,12},{12,8},{16,20},{20,16},{24,28},{28,24},{1,5},{5... | collective-permute-start | bytes 2949128 | tf_op jit(solution)/shard_map/ppermute | solution.py:673
  141.2 8.1 %collective-permute-start.35 = (bf16[160,768]{1,0:T(8,128)(2,1)S(1)}, bf16[160,768]{1,0:T(8,128)(2,1)S(1)}, u32[]{:S(2)}, u32[]{:S(2)}) collective-permute-start(bf16[160,768]{1,0:T(8,128)(2,1)S(1)} %get-tuple-element.129), channel_id=1, source_target_pairs={{0,8},{4,12},{8,0},{12,4},{16,24},{20,28},{24,16},{28,20},{1,9},{5... | collective-permute-start | bytes 737288 | tf_op jit(solution)/shard_map/ppermute | solution.py:673
  142.5 19.7 %collective-permute-start.41 = (bf16[8,20,640]{2,1,0:T(8,128)(2,1)S(1)}, bf16[8,20,640]{2,1,0:T(8,128)(2,1)S(1)}, u32[]{:S(2)}, u32[]{:S(2)}) collective-permute-start(bf16[8,20,640]{2,1,0:T(8,128)(2,1)S(1)} %get-tuple-element.144), channel_id=1, source_target_pairs={{0,1},{1,2},{2,3},{3,0},{4,5},{5,6},{6,7},{7,4},{8,9},{9,10},{10,1... | collective-permute-start | bytes 614408 | tf_op jit(solution)/shard_map/ppermute | solution.py:678
  144.8 19.1 %collective-permute-start.42 = (bf16[8,20,640]{2,1,0:T(8,128)(2,1)S(1)}, bf16[8,20,640]{2,1,0:T(8,128)(2,1)S(1)}, u32[]{:S(2)}, u32[]{:S(2)}) collective-permute-start(bf16[8,20,640]{2,1,0:T(8,128)(2,1)S(1)} %get-tuple-element.145), channel_id=1, source_target_pairs={{0,2},{1,3},{2,0},{3,1},{4,6},{5,7},{6,4},{7,5},{8,10},{9,11},{10,... | collective-permute-start | bytes 614408 | tf_op jit(solution)/shard_map/ppermute | solution.py:678
  146.4 17.5 %collective-permute-start.43 = (bf16[8,20,640]{2,1,0:T(8,128)(2,1)S(1)}, bf16[8,20,640]{2,1,0:T(8,128)(2,1)S(1)}, u32[]{:S(2)}, u32[]{:S(2)}) collective-permute-start(bf16[8,20,640]{2,1,0:T(8,128)(2,1)S(1)} %get-tuple-element.146), channel_id=1, source_target_pairs={{0,3},{1,0},{2,1},{3,2},{4,7},{5,4},{6,5},{7,6},{8,11},{9,8},{10,9... | collective-permute-start | bytes 614408 | tf_op jit(solution)/shard_map/ppermute | solution.py:678
  147.7 12.1 %collective-permute-start.36 = (bf16[160,768]{1,0:T(8,128)(2,1)S(1)}, bf16[160,768]{1,0:T(8,128)(2,1)S(1)}, u32[]{:S(2)}, u32[]{:S(2)}) collective-permute-start(bf16[160,768]{1,0:T(8,128)(2,1)S(1)} %get-tuple-element.130), channel_id=1, source_target_pairs={{0,16},{4,20},{8,24},{12,28},{16,0},{20,4},{24,8},{28,12},{1,17},{... | collective-permute-start | bytes 737288 | tf_op jit(solution)/shard_map/ppermute | solution.py:673
  149.2 10.6 %collective-permute-start.37 = (bf16[160,768]{1,0:T(8,128)(2,1)S(1)}, bf16[160,768]{1,0:T(8,128)(2,1)S(1)}, u32[]{:S(2)}, u32[]{:S(2)}) collective-permute-start(bf16[160,768]{1,0:T(8,128)(2,1)S(1)} %get-tuple-element.131), channel_id=1, source_target_pairs={{0,24},{4,28},{8,16},{12,20},{16,8},{20,12},{24,0},{28,4},{1,25},{... | collective-permute-start | bytes 737288 | tf_op jit(solution)/shard_map/ppermute | solution.py:673
  160.0 6.4 %collective-permute-start.38 = (bf16[40,768]{1,0:T(8,128)(2,1)S(1)}, bf16[40,768]{1,0:T(8,128)(2,1)S(1)}, u32[]{:S(2)}, u32[]{:S(2)}) collective-permute-start(bf16[40,768]{1,0:T(8,128)(2,1)S(1)} %get-tuple-element.134), channel_id=1, source_target_pairs={{0,1},{1,2},{2,3},{3,0},{4,5},{5,6},{6,7},{7,4},{8,9},{9,10},{10,1... | collective-permute-start | bytes 184328 | tf_op jit(solution)/shard_map/ppermute | solution.py:678
  160.8 11.1 %collective-permute-start.39 = (bf16[40,768]{1,0:T(8,128)(2,1)S(1)}, bf16[40,768]{1,0:T(8,128)(2,1)S(1)}, u32[]{:S(2)}, u32[]{:S(2)}) collective-permute-start(bf16[40,768]{1,0:T(8,128)(2,1)S(1)} %get-tuple-element.135), channel_id=1, source_target_pairs={{0,2},{1,3},{2,0},{3,1},{4,6},{5,7},{6,4},{7,5},{8,10},{9,11},{10,... | collective-permute-start | bytes 184328 | tf_op jit(solution)/shard_map/ppermute | solution.py:678
  162.1 9.7 %collective-permute-start.40 = (bf16[40,768]{1,0:T(8,128)(2,1)S(1)}, bf16[40,768]{1,0:T(8,128)(2,1)S(1)}, u32[]{:S(2)}, u32[]{:S(2)}) collective-permute-start(bf16[40,768]{1,0:T(8,128)(2,1)S(1)} %get-tuple-element.136), channel_id=1, source_target_pairs={{0,3},{1,0},{2,1},{3,2},{4,7},{5,4},{6,5},{7,6},{8,11},{9,8},{10,9... | collective-permute-start | bytes 184328 | tf_op jit(solution)/shard_map/ppermute | solution.py:678
  (4 other events, 34.3 us)

commit v3 on v2

--- a/solution.py
+++ b/solution.py
@@ -16,6 +16,7 @@
 BF = jnp.bfloat16
 F32 = jnp.float32
 LANES = 128
+US_S = 0.1
 WIDE_VECTORS = 3
 NARROW_VECTORS = 6
 MIB = 1024 * 1024
@@ -60,7 +61,7 @@
 
 
 def each_chunk(count, step, body):
-    @pl.loop(0, count // step)
+    @pl.loop(0, count // step, unroll=8 if count // step >= 8 else 4)
     def _(i):
         body(pl.ds(pl.multiple_of(i * step, step), step))
 
@@ -80,6 +81,46 @@
         values = [jnp.where(here, values[m ^ bit], values[m]) for m in range(len(values))]
         bit *= 2
     return values
+
+
+def by_shift(values, me):
+    bit = 1
+    n = len(values)
+    while bit < n:
+        here = (me & bit) != 0
+        values = [jnp.where(here, values[(k + bit) % n], values[k]) for k in range(n)]
+        bit *= 2
+    return values
+
+
+def of_core(values):
+    core = lax.axis_index("dp") & 1
+    return [
+        jnp.where(core == 1, odd, even) for even, odd in zip(values[0::2], values[1::2])
+    ]
+
+
+def beside(value, count):
+    r = value.shape[0] // count
+    return jnp.concatenate([value[g * r : (g + 1) * r] for g in range(count)], axis=1)
+
+
+def below(value):
+    count = value.shape[1] // LANES
+    return jnp.concatenate([value[:, g * LANES : (g + 1) * LANES] for g in range(count)], axis=0)
+
+
+def stats_rows(total, inner):
+    terms = [term.astype(F32) for term in thirds(total)]
+    rest = inner - 3 * LANES
+    return jnp.concatenate(terms + ([jnp.zeros((8, rest), F32)] if rest else []), axis=1)
+
+
+def padded(value, rows):
+    gap = rows - value.shape[0]
+    if gap == 0:
+        return value
+    return jnp.concatenate([value, jnp.zeros((gap, value.shape[1]), F32)], axis=0)
 
 
 def vmem(n):
@@ -140,27 +181,33 @@
 
 def pack_b_kernel(conv, w_out, group, sems, conv_held, out_held):
     fetch((conv, w_out), (conv_held, out_held), sems)
-    inner = group.shape[2]
-    group[0:KERNEL_TAPS] = conv_held[...]
+    inner = group.shape[1]
+    rows = [conv_held[k].astype(F32) for k in range(KERNEL_TAPS)]
     for h in range(w_out.shape[1] // inner):
-        group[KERNEL_TAPS + h] = out_held[:, h * inner : (h + 1) * inner]
-
-
-def place_kernel(axis, n, *refs):
+        rows.append(out_held[:, h * inner : (h + 1) * inner].astype(F32))
+    group[...] = jnp.concatenate(rows, axis=0).astype(BF)
+
+
+def line_a_kernel(n, *refs):
     parts, out = refs[:n], refs[n]
-    me = lax.axis_index(axis)
-    values = [p[...].astype(F32) for p in parts]
-    ordered = []
-    for place in range(n):
-        value = values[0]
-        for k in range(1, n):
-            value = jnp.where(lax.rem(me - place + n, n) == k, values[k], value)
-        ordered.append(value)
-    out[...] = jnp.concatenate(ordered, axis=-2).astype(BF)
-
-
-def first_kernel(tokens, n1, r1):
-    width = tokens.shape[1]
+    ordered = by_shift([parts[-k % n][...].astype(F32) for k in range(n)], -lax.axis_index("seq") % n)
+    out[...] = jnp.concatenate(ordered, axis=0).astype(BF)
+
+
+def line_b_kernel(n, *refs):
+    parts, out = refs[:n], refs[n]
+    slabs = out.shape[0]
+    values = [parts[-k % n][...].astype(F32) for k in range(n)]
+    ordered = by_shift(values, -lax.axis_index("seq") % n)
+    part = values[0].shape[0] // slabs
+    for slab in range(slabs):
+        out[slab] = jnp.concatenate(
+            [value[slab * part : (slab + 1) * part] for value in ordered], axis=0
+        ).astype(BF)
+
+
+def first_kernel(wide, narrow, tokens, n1, r1, spread):
+    spread[...] = spread_matrix(tokens.shape[1], spread.shape[1], wide, narrow)
 
     def body(c):
         n, r = standardize(tokens[c, :].astype(F32))
@@ -178,7 +225,7 @@
     return (lax.broadcasted_iota(jnp.int32, (width, inner), 1) == at).astype(F32).astype(BF)
 
 
-def second_kernel(chips, vocab, wide, narrow, n1, *refs):
+def second_kernel(chips, vocab, n1, spread, *refs):
     pieces = refs[: 2 * chips]
     (w_in, extras, wide_v, narrow_v, act, gp1, n2, gp2, r2, conv_in, proj) = refs[2 * chips :]
     width, inner = w_in.shape
@@ -195,7 +242,7 @@
     wide_v[0:WIDE_VECTORS, :] = turned[vocab : vocab + WIDE_VECTORS]
     first = vocab + WIDE_VECTORS
     narrow_v[0:NARROW_VECTORS, :] = dot(
-        turned.astype(BF), spread_matrix(width, inner, wide, narrow)
+        turned.astype(BF), spread[...]
     )[first : first + NARROW_VECTORS]
     g1, b1 = wide_v[0:1, :], wide_v[1:2, :]
     bias, g2, b2 = narrow_v[0:1, :], narrow_v[1:2, :], narrow_v[2:3, :]
@@ -242,18 +289,17 @@
         taps,
         block_out,
         third_act,
-        out_low,
         logit_grad,
         head_grad,
         conv_low,
         narrow_sums,
-        wide_sums,
         stats,
         ext,
         n3,
         gp3,
         r3,
         work,
+        product,
     ) = refs[2 * hops + 1 + 2 * chips :]
     inner = taps.shape[1]
     width = tokens.shape[1]
@@ -271,7 +317,11 @@
     bias, g3, b3 = narrow_v[3:4, :], narrow_v[4:5, :], narrow_v[5:6, :]
     bias_out = wide_v[2:3, :]
     narrow_sums[...] = jnp.zeros_like(narrow_sums)
-    wide_sums[...] = jnp.zeros_like(wide_sums)
+    value = dot(taps[KERNEL_TAPS], extras[0:inner, :])
+    for h in range(1, width // inner):
+        value += dot(taps[KERNEL_TAPS + h], extras[h * inner : (h + 1) * inner, :])
+    product[:, 0:LANES] = value.astype(BF)
+    product[:, LANES : 2 * LANES] = (value - value.astype(BF).astype(F32)).astype(BF)
     stats[...] = jnp.zeros_like(stats)
     head_grad[...] = jnp.zeros_like(head_grad)
     seat = lax.axis_index("seq")
@@ -337,19 +387,7 @@
             jnp.sum(mask * entropy, axis=0, keepdims=True), (1, LANES)
         )
         head_grad[...] += dot_tn(block_out[whole, :], grad)
-        work[...] = dot_nt(grad, extras[...])
-
-        def lower(c):
-            here = pl.ds(pl.multiple_of(s * length + c.start, c.size), c.size)
-            low = work[c, :].astype(BF)
-            out_low[here, :] = low
-            wide_sums[...] += rows8(low.astype(F32))
-
-        each_chunk(length, 32, lower)
-        back = dot_nt(out_low[whole, 0:inner], taps[KERNEL_TAPS])
-        for h in range(1, width // inner):
-            back += dot_nt(out_low[whole, h * inner : (h + 1) * inner], taps[KERNEL_TAPS + h])
-        work[:, 0:inner] = back
+        work[:, 0:inner] = dot_nt(jnp.concatenate([grad, grad], axis=1), product[...])
 
         def behind(c):
             e = work[c, 0:inner] * gp3[c, :]
@@ -375,28 +413,26 @@
     third_other,
     low_own,
     low_other,
-    out_low,
+    logit_own,
     logit_other,
-    extras,
     stats,
     stats_other,
     *refs,
 ):
     count = 2 * hops + 1
     blocks = (refs[:count], refs[count : 2 * count])
-    own, own_stats = refs[2 * count : 2 * count + 2]
-    sends = refs[2 * count + 2 : 2 * count + 1 + chips]
-    turned, turn, third_t, out_other = refs[2 * count + 1 + chips :]
+    own, own_stats, own_out = refs[2 * count : 2 * count + 3]
+    sends = refs[2 * count + 3 : 2 * count + 2 + chips]
+    turned, turn, third_t = refs[2 * count + 2 + chips :]
     slabs, block, inner = own.shape
     length = low_own.shape[0] // seqs
     me = lax.axis_index("dp") // 2
     core = lax.axis_index("dp") & 1
     total_stats = stats[...] + stats_other[...]
     own_stats[...] = total_stats
+    tail = jnp.concatenate([stats_rows(total_stats, inner), jnp.zeros((8, inner), F32)], axis=0)
     for send in sends:
-        send[slabs * block : slabs * block + 16, :] = jnp.zeros((16, inner), BF)
-        for j, term in enumerate(thirds(total_stats)):
-            send[slabs * block : slabs * block + 8, j * LANES : (j + 1) * LANES] = term
+        send[send.shape[0] - 16 :, :] = tail.astype(BF)
 
     def chosen(ref, q):
         even = ref[2 * q * block : (2 * q + 1) * block, :]
@@ -418,7 +454,6 @@
             turn[...] = jnp.transpose((third_own, third_other)[side][columns, :])
             for q in range(chips):
                 third_t[side, q * block : (q + 1) * block, columns] = chosen(turn, q)
-    out_other[...] = dot_nt(logit_other[...], extras[...]).astype(BF)
 
     def share(slab, value):
         parts = by_mask([value[q * block : (q + 1) * block] for q in range(chips)], me)
@@ -436,12 +471,12 @@
                     low[s * length : (s + 1) * length, :],
                 )
         share(k, value)
-    for h in range(slabs - KERNEL_TAPS):
-        columns = slice(h * inner, (h + 1) * inner)
-        share(
-            KERNEL_TAPS + h,
-            dot(third_t[0], out_low[:, columns]) + dot(third_t[1], out_other[:, columns]),
-        )
+    value = dot(third_t[0], logit_own[...]) + dot(third_t[1], logit_other[...])
+    parts = by_mask([value[q * block : (q + 1) * block] for q in range(chips)], me)
+    own_out[...] = parts[0]
+    for m in range(1, chips):
+        lines = beside(parts[m], inner // LANES)
+        sends[m - 1][slabs * block : slabs * block + lines.shape[0], :] = lines.astype(BF)
 
 
 def sum_terms(ref_value):
@@ -452,62 +487,78 @@
     )
 
 
-def line_b_kernel(count, size, part, own, stats, *refs):
+def line_grad_b_kernel(count, size, part, own, stats, own_out, *refs):
     parts = refs[:count]
-    keep, keep_stats = refs[count : count + 2]
-    sends = refs[count + 2 :]
+    keep, keep_stats, keep_out = refs[count : count + 3]
+    sends = refs[count + 3 :]
     slabs, block, inner = own.shape
     me = lax.axis_index("seq")
+    rows = parts[0].shape[0]
     sums = stats[...]
+    out = own_out[...]
     for p in parts:
-        sums += sum_terms(p[slabs * block : slabs * block + 16, :])
+        sums += sum_terms(p[rows - 16 :, :])
+        out += below(p[slabs * block : rows - 16, :].astype(F32))
     keep_stats[...] = sums
-    for send in sends:
-        send[slabs] = jnp.zeros(send.shape[1:], BF)
-        for j, term in enumerate(thirds(sums)):
-            send[slabs, 0:8, j * LANES : (j + 1) * LANES] = term
+    pieces = [[] for _ in range(size)]
     for slab in range(slabs):
         value = own[slab]
         for p in parts:
             value += p[slab * block : (slab + 1) * block, :].astype(F32)
-        cut = [value[z * part : (z + 1) * part] for z in range(size)]
-        for k in range(size):
-            piece = cut[0]
-            for z in range(1, size):
-                piece = jnp.where(lax.rem(me + k, size) == z, cut[z], piece)
-            if k == 0:
-                keep[slab] = piece
-            else:
-                sends[k - 1][slab, 0:part, :] = piece.astype(BF)
-
-
-def end_b_kernel(count, keep, stats, *refs):
+        cut = by_shift([value[z * part : (z + 1) * part] for z in range(size)], me)
+        keep[slab] = cut[0]
+        for k in range(1, size):
+            pieces[k].append(cut[k])
+    cut = by_shift([out[z * part : (z + 1) * part] for z in range(size)], me)
+    tail_rows = keep_out.shape[0]
+    keep_out[...] = padded(cut[0], tail_rows)
+    terms = padded(stats_rows(sums, 3 * LANES), tail_rows)
+    gap = sends[0].shape[0] - slabs * part - tail_rows
+    for k in range(1, size):
+        rest = inner - 4 * LANES
+        tail = [terms, padded(cut[k], tail_rows), jnp.zeros((tail_rows, rest), F32)]
+        lines = pieces[k] + ([jnp.zeros((gap, inner), F32)] if gap else [])
+        lines.append(jnp.concatenate(tail, axis=1))
+        sends[k - 1][...] = jnp.concatenate(lines, axis=0).astype(BF)
+
+
+def end_b_kernel(count, keep, stats, keep_out, extras, *refs):
     parts = refs[:count]
-    conv, out, sums, = refs[count:]
+    conv, out, sums = refs[count:]
     slabs, part, inner = keep.shape
+    tail_rows = keep_out.shape[0]
+    values = [p[...].astype(F32) for p in parts]
     total = stats[...]
-    for p in parts:
-        total += sum_terms(p[slabs])
+    product = keep_out[...]
+    for value in values:
+        tail = value[value.shape[0] - tail_rows :]
+        total += sum_terms(tail)
+        product += tail[:, 3 * LANES : 4 * LANES]
     sums[...] = total
+    value = 0.0
+    for term in thirds(product):
+        value = value + dot_nt(term, extras[...])
+    out[...] = value[0:part]
     for slab in range(slabs):
         value = keep[slab]
-        for p in parts:
-            value += p[slab, 0:part, :].astype(F32)
-        if slab < KERNEL_TAPS:
-            conv[slab] = value
-        else:
-            out[:, (slab - KERNEL_TAPS) * inner : (slab - KERNEL_TAPS + 1) * inner] = value
-
-
-def split_a_kernel(chips, keep, got, own, token, *sends):
+        for v in values:
+            value += v[slab * part : (slab + 1) * part]
+        conv[slab] = value
+
+
+def split_a_kernel(chips, keep, got_low, got_high, own, token, *sends):
     token[...] = jnp.zeros_like(token)
-    me = lax.axis_index("dp") // 2
-    own[...] = keep[me] + got[me].astype(F32)
+    half = chips // 2
+    sums = [
+        keep[q] + (got_low, got_high)[q // half][q % half].astype(F32) for q in range(chips)
+    ]
+    sums = by_mask(sums, lax.axis_index("dp") // 2)
+    own[...] = sums[0]
     for m in range(1, chips):
-        sends[m - 1][...] = (keep[me ^ m] + got[me ^ m].astype(F32)).astype(BF)
-
-
-def line_a_kernel(count, size, part, own, *refs):
+        sends[m - 1][...] = sums[m].astype(BF)
+
+
+def line_grad_a_kernel(count, size, part, own, *refs):
     parts = refs[:count]
     keep = refs[count]
     sends = refs[count + 1 :]
@@ -563,12 +614,14 @@
     wide_v,
     narrow_v,
     narrow_sums,
-    wide_sums,
+    stats,
+    extras,
     head_grad,
     *refs,
 ):
     blocks = refs[: 2 * hops + 1]
-    keep, send, e1, low, ext, work, act_t, sums1, sums2 = refs[2 * hops + 1 :]
+    keep, send_low, send_high, e1, low, ext, work, act_t, sums1, sums2 = refs[2 * hops + 1 :]
+    half = chips // 2
     width, inner = w_in.shape
     rows = low.shape[0]
     length = rows // seqs
@@ -615,7 +668,10 @@
     def folded(ref, j):
         return jnp.sum(ref[8 * j : 8 * j + 8, :], axis=0, keepdims=True)
 
-    wides = [folded(sums1, 0), folded(sums1, 1), folded(wide_sums, 0)]
+    bias = 0.0
+    for term in thirds(stats[...]):
+        bias = bias + dot_nt(term, extras[...])
+    wides = [folded(sums1, 0), folded(sums1, 1), bias[2:3, :]]
     narrows = [folded(sums2, 2), folded(sums2, 0), folded(sums2, 1)]
     narrows += [folded(narrow_sums, 2), folded(narrow_sums, 0), folded(narrow_sums, 1)]
     row = lax.broadcasted_iota(jnp.int32, (16, inner), 0)
@@ -649,8 +705,9 @@
 
             @pl.when(core != c)
             def _():
-                send[q, :, 0:inner] = value.astype(BF)
-                send[q, :, inner : inner + LANES] = extra[lines].astype(BF)
+                send = (send_low, send_high)[q // half]
+                send[q % half, :, 0:inner] = value.astype(BF)
+                send[q % half, :, inner : inner + LANES] = extra[lines].astype(BF)
 
 
 def input_kernel(e1, n1, r1, wide_v, logit_grad, extras, input_grad, token, work):
@@ -759,7 +816,7 @@
     )
     parts_a = line_parts(block_a)
     (line_a,) = call(
-        functools.partial(place_kernel, "seq", size),
+        functools.partial(line_a_kernel, size),
         parts_a,
         [sds((size * wide, inner + LANES), BF)],
         name="line_a",
@@ -768,7 +825,7 @@
     (block_b,) = call(
         pack_b_kernel,
         ins,
-        [sds((slabs, narrow, inner), BF)],
+        [sds((slabs * narrow, inner), BF)],
         [pltpu.SemaphoreType.DMA((2,))] + [pltpu.VMEM(x.shape, BF) for x in ins],
         limit=8,
         name="pack_b",
@@ -777,10 +834,10 @@
     )
     own_a = [line_a] + [swap(line_a, 2 * m) for m in range(1, chips)]
     parts_b = line_parts(block_b)
-    n1, r1 = call(
-        first_kernel,
+    n1, r1, spread = call(
+        functools.partial(first_kernel, wide, narrow),
         [flat],
-        [sds((rows, width), F32), sds((rows, LANES), F32)],
+        [sds((rows, width), F32), sds((rows, LANES), F32), sds((width, inner), BF)],
         us=6,
         limit=8,
         name="first",
@@ -789,7 +846,7 @@
     *own_a, _ = lax.optimization_barrier((*own_a, r1))
     pieces_a = list(own_a) + [swap(piece, 1) for piece in own_a]
     (line_b,) = call(
-        functools.partial(place_kernel, "seq", size),
+        functools.partial(line_b_kernel, size),
         parts_b,
         [sds((slabs, size * narrow, inner), BF)],
         name="line_b",
@@ -797,8 +854,8 @@
     )
     own_b = [line_b] + [swap(line_b, 2 * m) for m in range(1, chips)]
     w_in, extras, wide_v, narrow_v, act, gp1, n2, gp2, r2, conv_in = call(
-        functools.partial(second_kernel, chips, vocab, wide, narrow),
-        [n1] + pieces_a,
+        functools.partial(second_kernel, chips, vocab),
+        [n1, spread] + pieces_a,
         [
             sds((width, inner), BF),
             sds((width, LANES), BF),
@@ -826,12 +883,10 @@
         taps,
         block_out,
         third_act,
-        out_low,
         logit_grad,
         head_grad,
         conv_low,
         narrow_sums,
-        wide_sums,
         stats,
     ) = call(
         functools.partial(middle_kernel, chips, hops, seqs, vocab),
@@ -851,12 +906,10 @@
             sds((slabs, inner, inner), BF),
             sds((rows, width), BF),
             sds((rows, inner), BF),
-            sds((rows, width), BF),
             sds((rows, LANES), BF),
             sds((width, LANES), F32),
             sds((rows, inner), BF),
             sds((24, inner), F32),
-            sds((8, width), F32),
             sds((8, LANES), F32),
         ],
         [
@@ -865,6 +918,7 @@
             pltpu.VMEM((length, inner), F32),
             pltpu.VMEM((length, LANES), F32),
             pltpu.VMEM((length, width), F32),
+            pltpu.VMEM((inner, 2 * LANES), BF),
         ],
         us=17,
         limit=16,
@@ -875,33 +929,38 @@
     third_other = swap(third_act, 1)
     logit_other = swap(logit_grad, 1)
     stats_other = swap(stats, 1)
+    message = KERNEL_TAPS * size * narrow + size * narrow // (inner // LANES) + 16
     split_b = call(
         functools.partial(conv_grad_kernel, chips, hops, seqs),
-        [third_act, third_other, conv_low, low_other, out_low, logit_other, extras]
+        [third_act, third_other, conv_low, low_other, logit_grad, logit_other]
         + [stats, stats_other]
         + blocks
         + other_blocks,
-        [sds((slabs, size * narrow, inner), F32), sds((8, LANES), F32)]
-        + [sds((slabs * size * narrow + 16, inner), BF)] * (chips - 1),
+        [
+            sds((KERNEL_TAPS, size * narrow, inner), F32),
+            sds((8, LANES), F32),
+            sds((size * narrow, LANES), F32),
+        ]
+        + [sds((message, inner), BF)] * (chips - 1),
         [
             pltpu.VMEM((2 * seqs, inner // 2, (2 * hops + 1) * length), BF),
             pltpu.VMEM((inner, length), BF),
             pltpu.VMEM((2, inner // 2, rows), BF),
-            pltpu.VMEM((rows, width), BF),
         ],
         us=7,
         limit=16,
         name="conv_grad",
     )
-    from_chips_b = [swap(piece, 2 * m) for m, piece in zip(range(1, chips), split_b[2:])]
-    keep_a, send_a, e1 = call(
+    from_chips_b = [swap(piece, 2 * m) for m, piece in zip(range(1, chips), split_b[3:])]
+    keep_a, send_low, send_high, e1 = call(
         functools.partial(back_kernel, chips, hops, seqs, vocab, wide, narrow),
         [taps, n2, gp2, r2, n1, gp1, act, w_in, wide_v, narrow_v]
-        + [narrow_sums, wide_sums, head_grad]
+        + [narrow_sums, stats, extras, head_grad]
         + grad_blocks,
         [
             sds((chips, size * wide, inner + LANES), F32),
-            sds((chips, size * wide, inner + LANES), BF),
+            sds((chips // 2, size * wide, inner + LANES), BF),
+            sds((chips // 2, size * wide, inner + LANES), BF),
             sds((rows, width), F32),
         ],
         [
@@ -912,42 +971,44 @@
             pltpu.VMEM((16, width), F32),
             pltpu.VMEM((24, inner), F32),
         ],
-        us=12,
+        us=US_S,
         limit=20,
         name="back",
         after=[split_b[1]],
     )
-    line_b2 = call(
-        functools.partial(line_b_kernel, chips - 1, size, narrow),
-        [split_b[0], split_b[1]] + from_chips_b,
-        [sds((slabs, narrow, inner), F32), sds((8, LANES), F32)]
-        + [sds((slabs + 1, max(narrow, 8), inner), BF)] * (size - 1),
-        name="line_grad_b",
-    )
-    send_a, _ = lax.optimization_barrier((send_a, line_b2[1]))
-    got_a = swap(send_a, 1)
+    got_low, got_high = swap(send_low, 1), swap(send_high, 1)
     split = call(
         functools.partial(split_a_kernel, chips),
-        [keep_a, got_a],
+        [keep_a, got_low, got_high],
         [sds((size * wide, inner + LANES), F32), sds((8, LANES), F32)]
         + [sds((size * wide, inner + LANES), BF)] * (chips - 1),
+        us=US_S,
         name="split_a",
-        after=[line_b2[1]],
-    )
-    from_chips = [swap(piece, 2 * m) for m, piece in zip(range(1, chips), split[2:])]
-    from_line_b = [shifted(piece, k) for k, piece in zip(range(1, size), line_b2[2:])]
+    )
+    tail = -(-max(narrow, 8) // 8) * 8
+    line_b2 = call(
+        functools.partial(line_grad_b_kernel, chips - 1, size, narrow),
+        list(split_b[:3]) + from_chips_b,
+        [sds((KERNEL_TAPS, narrow, inner), F32), sds((8, LANES), F32), sds((tail, LANES), F32)]
+        + [sds((-(-KERNEL_TAPS * narrow // 8) * 8 + tail, inner), BF)] * (size - 1),
+        name="line_grad_b",
+        after=[split[1]],
+    )
+    *a_sends, _ = lax.optimization_barrier((*split[2:], line_b2[1]))
+    from_chips = [swap(piece, 2 * m) for m, piece in zip(range(1, chips), a_sends)]
 
     input_grad, input_token = call(
         input_kernel,
         [e1, n1, r1, wide_v, logit_grad, extras],
         [sds((rows, width), BF), sds((8, LANES), F32)],
         [pltpu.VMEM((rows, width), F32)],
-        us=5,
+        us=3,
         name="input",
-        after=[split[1]],
-    )
+        after=[line_b2[1]],
+    )
+    from_line_b = [shifted(piece, k) for k, piece in zip(range(1, size), line_b2[3:])]
     line = call(
-        functools.partial(line_a_kernel, chips - 1, size, wide),
+        functools.partial(line_grad_a_kernel, chips - 1, size, wide),
         [split[0]] + from_chips,
         [sds((wide, inner + LANES), F32)] + [sds((wide, inner + LANES), BF)] * (size - 1),
         name="line_grad_a",
@@ -955,7 +1016,7 @@
     )
     conv_share, out_share, sums = call(
         functools.partial(end_b_kernel, size - 1),
-        [line_b2[0], line_b2[1]] + from_line_b,
+        [line_b2[0], line_b2[1], line_b2[2], extras] + from_line_b,
         [sds((KERNEL_TAPS, narrow, inner), F32), sds((narrow, width), F32), sds((8, LANES), F32)],
         name="end_b",
         after=[line[0]],

time: 174 us -> 148 us (0.85)
  Pallas kernels: 59.9 us -> 41.7 us
  waiting for transfers between devices: 56.8 us -> 49.9 us
    pallas_call x15, Pallas kernels: 59.9 us -> 41.7 us  [call(): pl.pallas_call(body, out_shape=list(outs), in_specs=[pl.BlockSpec(memory_...]
    ppermute x28 -> x29, waiting for transfers between devices: 35.9 us -> 32.6 us  [swap(): return lax.ppermute(value, 'dp', [(i, i ^ mask) for i in range(count)])]
    ppermute x2, waiting for transfers between devices: 6.65 us -> 4.17 us  [halo(): lax.ppermute(series, 'seq', [(i + h, i) for i in range(size - h)])]
    ppermute x2, starting transfers between devices: 11 us -> 8.78 us  [halo(): lax.ppermute(series, 'seq', [(i, i + h) for i in range(size - h)])]
    ppermute x12, waiting for transfers between devices: 9.38 us -> 7.18 us  [shifted(): lax.ppermute(value, 'seq', [(i, (i + k) % size) for i in range(size)])]
    ppermute x28 -> x29, starting transfers between devices: 18.5 us -> 19.4 us  [swap(): return lax.ppermute(value, 'dp', [(i, i ^ mask) for i in range(count)])]
  transfers between devices with their start and end apart: 44 -> 45, of which waited for: 19 -> 18; matrix products, arithmetic and copies ran while one was open for 1% -> 1% of each run, Pallas kernels for 32% -> 26%
where the time goes in v3:
time: 148 us
  starting transfers between devices  51.9 us (35%)
  waiting for transfers between devices  49.9 us (34%)
  Pallas kernels  41.7 us (28%)
  between operations  2.72 us (2%)
    pallas_call x15, Pallas kernels, call(): pl.pallas_call(body, out_shape=list(outs), in_specs=[pl.BlockSpec(memory_...  41.7 us
    ppermute x29, waiting for transfers between devices, swap(): return lax.ppermute(value, 'dp', [(i, i ^ mask) for i in range(count)])  32.6 us
    ppermute x12, starting transfers between devices, shifted(): lax.ppermute(value, 'seq', [(i, (i + k) % size) for i in range(size)])  20.8 us
    ppermute x29, starting transfers between devices, swap(): return lax.ppermute(value, 'dp', [(i, i ^ mask) for i in range(count)])  19.4 us
    ppermute x2, starting transfers between devices, halo(): lax.ppermute(series, 'seq', [(i, i + h) for i in range(size - h)])  8.78 us
    ppermute x12, waiting for transfers between devices, shifted(): lax.ppermute(value, 'seq', [(i, (i + k) % size) for i in range(size)])  7.18 us
    ppermute x2, waiting for transfers between devices, halo(): lax.ppermute(series, 'seq', [(i, i + h) for i in range(size - h)])  5.9 us
    ppermute x2, waiting for transfers between devices, halo(): lax.ppermute(series, 'seq', [(i + h, i) for i in range(size - h)])  4.17 us
  transfers between devices with their start and end apart: 45, of which 18 were waited for; matrix products, arithmetic and copies ran while one was open for 1% of the time, Pallas kernels for 26%

profile of v3, /device:TPU:0, one launch (start us, length us, event | category | flops | bytes accessed | tf_op | source)
XLA Modules:
  0.0 148.1 jit_solution(14208892835381602316)
XLA Ops:
  0.7 1.6 %pack_a.1.refs_2_.refs_0_ = bf16[40,768]{1,0:T(8,128)(2,1)} custom-call(bf16[40,640]{1,0:T(8,128)(2,1)} %refs_0_.1, bf16[30,40]{1,0:T(8,128)(2,1)} %bitcast.30, bf16[40]{0:T(256)(128)(2,1)} %refs_2_.1, bf16[40]{0:T(256)(128)(2,1)} %refs_3_.1, bf16[40]{0:T(256)(128)(2,1)} %refs_4_.2, bf16[20]{0:T(256)(128)(2,1)} %refs_5_.2, bf16[20]{0:T(256)(128)(2,1)} %refs_6_.2, ...), custom_call_target="tpu_custom_call" | custom-call | flops 1000000000 | bytes 1000 | tf_op jit(solution)/shard_map/pack_a/pallas_call | solution.py:137
  2.3 3.1 %collective-permute-start = (bf16[40,768]{1,0:T(8,128)(2,1)}, bf16[40,768]{1,0:T(8,128)(2,1)S(1)}, u32[]{:S(2)}, u32[]{:S(2)}) collective-permute-start(bf16[40,768]{1,0:T(8,128)(2,1)} %pack_a.1.refs_2_.refs_0_), channel_id=1, source_target_pairs={{0,1},{1,2},{2,3},{3,0},{4,5},{5,6},{6,7},{7,4},{8,9},{9,10},{10,1... | collective-permute-start | bytes 184328 | tf_op jit(solution)/shard_map/ppermute | solution.py:735
  5.4 2.6 %collective-permute-start.1 = (bf16[40,768]{1,0:T(8,128)(2,1)}, bf16[40,768]{1,0:T(8,128)(2,1)S(1)}, u32[]{:S(2)}, u32[]{:S(2)}) collective-permute-start(bf16[40,768]{1,0:T(8,128)(2,1)} %pack_a.1.refs_2_.refs_0_), channel_id=1, source_target_pairs={{0,2},{1,3},{2,0},{3,1},{4,6},{5,7},{6,4},{7,5},{8,10},{9,11},{10,... | collective-permute-start | bytes 184328 | tf_op jit(solution)/shard_map/ppermute | solution.py:735
  8.0 1.3 collective-permute-start.2
  10.1 2.4 %collective-permute-done.1.refs_2_ = bf16[40,768]{1,0:T(8,128)(2,1)S(1)} collective-permute-done((bf16[40,768]{1,0:T(8,128)(2,1)}, bf16[40,768]{1,0:T(8,128)(2,1)S(1)}, u32[]{:S(2)}, u32[]{:S(2)}) %collective-permute-start.1) | collective-permute-done | bytes 61472 | tf_op jit(solution)/shard_map/ppermute | solution.py:735
  12.8 0.8 copy-done.3
  13.7 1.6 %collective-permute-start.3 = (bf16[160,768]{1,0:T(8,128)(2,1)S(1)}, bf16[160,768]{1,0:T(8,128)(2,1)S(1)}, u32[]{:S(2)}, u32[]{:S(2)}) collective-permute-start(bf16[160,768]{1,0:T(8,128)(2,1)S(1)} %line_a.1.refs_2_), channel_id=1, source_target_pairs={{0,8},{4,12},{8,0},{12,4},{16,24},{20,28},{24,16},{28,20},{1,9},{5... | collective-permute-start | bytes 737288 | tf_op jit(solution)/shard_map/ppermute | solution.py:730
  15.6 1.4 collective-permute-start.10
  17.0 2.1 %collective-permute-start.11 = (bf16[140,640]{1,0:T(8,128)(2,1)S(1)}, bf16[140,640]{1,0:T(8,128)(2,1)S(1)}, u32[]{:S(2)}, u32[]{:S(2)}) collective-permute-start(bf16[140,640]{1,0:T(8,128)(2,1)S(1)} %pack_b.1.refs_1_.refs_0_), channel_id=1, source_target_pairs={{0,2},{1,3},{2,0},{3,1},{4,6},{5,7},{6,4},{7,5},{8,10},{9,11},{10,... | collective-permute-start | bytes 537608 | tf_op jit(solution)/shard_map/ppermute | solution.py:735
  19.5 1.5 %collective-permute-start.4 = (bf16[160,768]{1,0:T(8,128)(2,1)S(1)}, bf16[160,768]{1,0:T(8,128)(2,1)S(1)}, u32[]{:S(2)}, u32[]{:S(2)}) collective-permute-start(bf16[160,768]{1,0:T(8,128)(2,1)S(1)} %line_a.1.refs_2_), channel_id=1, source_target_pairs={{0,16},{4,20},{8,24},{12,28},{16,0},{20,4},{24,8},{28,12},{1,17},{... | collective-permute-start | bytes 737288 | tf_op jit(solution)/shard_map/ppermute | solution.py:730
  21.1 1.8 %collective-permute-start.5 = (bf16[160,768]{1,0:T(8,128)(2,1)S(1)}, bf16[160,768]{1,0:T(8,128)(2,1)S(1)}, u32[]{:S(2)}, u32[]{:S(2)}) collective-permute-start(bf16[160,768]{1,0:T(8,128)(2,1)S(1)} %line_a.1.refs_2_), channel_id=1, source_target_pairs={{0,24},{4,28},{8,16},{12,20},{16,8},{20,12},{24,0},{28,4},{1,25},{... | collective-permute-start | bytes 737288 | tf_op jit(solution)/shard_map/ppermute | solution.py:730
  22.8 1.6 %first.1 = (f32[512,1280]{1,0:T(8,128)S(1)}, f32[512,128]{1,0:T(8,128)S(1)}, bf16[1280,640]{1,0:T(8,128)(2,1)S(1)}) custom-call(bf16[512,1280]{1,0:T(8,128)(2,1)S(1)} %bitcast.22, bf16[140,640]{1,0:T(8,128)(2,1)S(1)} %pack_b.1.refs_1_.refs_0_), custom_call_target="tpu_custom_call" | custom-call | flops 6000000000 | bytes 1000 | tf_op jit(solution)/shard_map/first/pallas_call | solution.py:137
  24.4 7.0 %collective-permute-done.4.refs_4_ = bf16[160,768]{1,0:T(8,128)(2,1)S(1)} collective-permute-done((bf16[160,768]{1,0:T(8,128)(2,1)S(1)}, bf16[160,768]{1,0:T(8,128)(2,1)S(1)}, u32[]{:S(2)}, u32[]{:S(2)}) %collective-permute-start.4) | collective-permute-done | bytes 245792 | tf_op jit(solution)/shard_map/ppermute | solution.py:730
  32.7 0.9 collective-permute-start.15
  33.6 1.2 collective-permute-start.16
  34.9 1.4 collective-permute-start.17
  36.3 6.4 %second.1 = (bf16[1280,640]{1,0:T(8,128)(2,1)S(1)}, bf16[1280,128]{1,0:T(8,128)(2,1)S(1)}, f32[8,1280]{1,0:T(8,128)S(1)}, f32[8,640]{1,0:T(8,128)S(1)}, bf16[512...) custom-call(f32[512,1280]{1,0:T(8,128)S(1)} %get-tuple-element.91.re, ...), custom_call_target="tpu_custom_call" | custom-call | flops 8999999488 | bytes 1000 | tf_op jit(solution)/shard_map/second/pallas_call | solution.py:137
  42.7 4.4 %collective-permute-start.13 = (bf16[2,256,640]{2,1,0:T(8,128)(2,1)S(1)}, bf16[2,256,640]{2,1,0:T(8,128)(2,1)S(1)}, u32[]{:S(2)}, u32[]{:S(2)}) collective-permute-start(bf16[2,256,640]{2,1,0:T(8,128)(2,1)S(1)} %bitcast.24), channel_id=1, source_target_pairs={{0,1},{1,2},{2,3},{4,5},{5,6},{6,7},{8,9},{9,10},{10,11},{12,13},{... | collective-permute-start | bytes 1966088 | tf_op jit(solution)/shard_map/ppermute | solution.py:752
  47.2 1.5 collective-permute-start.14
  48.7 3.1 %collective-permute-done.15.refs_12_ = bf16[7,80,640]{2,1,0:T(8,128)(2,1)S(1)} collective-permute-done((bf16[7,80,640]{2,1,0:T(8,128)(2,1)S(1)}, bf16[7,80,640]{2,1,0:T(8,128)(2,1)S(1)}, u32[]{:S(2)}, u32[]{:S(2)}) %collective-permute-start.15) | collective-permute-done | bytes 716832 | tf_op jit(solution)/shard_map/ppermute | solution.py:730
  51.7 13.8 %collective-permute-done.16.refs_13_ = bf16[7,80,640]{2,1,0:T(8,128)(2,1)S(1)} collective-permute-done((bf16[7,80,640]{2,1,0:T(8,128)(2,1)S(1)}, bf16[7,80,640]{2,1,0:T(8,128)(2,1)S(1)}, u32[]{:S(2)}, u32[]{:S(2)}) %collective-permute-start.16) | collective-permute-done | bytes 716832 | tf_op jit(solution)/shard_map/ppermute | solution.py:730
  65.5 1.6 %collective-permute-done.17.refs_14_ = bf16[7,80,640]{2,1,0:T(8,128)(2,1)S(1)} collective-permute-done((bf16[7,80,640]{2,1,0:T(8,128)(2,1)S(1)}, bf16[7,80,640]{2,1,0:T(8,128)(2,1)S(1)}, u32[]{:S(2)}, u32[]{:S(2)}) %collective-permute-start.17) | collective-permute-done | bytes 716832 | tf_op jit(solution)/shard_map/ppermute | solution.py:730
  68.3 1.1 collective-permute-done.19.refs_16_
  69.5 0.9 collective-permute-done.20.refs_17_
  70.4 1.0 collective-permute-done.21.refs_18_
  71.4 11.5 %middle.1 = (bf16[7,640,640]{2,1,0:T(8,128)(2,1)S(1)}, bf16[512,1280]{1,0:T(8,128)(2,1)}, bf16[512,640]{1,0:T(8,128)(2,1)S(1)}, bf16[512,128]{1,0:T(8,128)(2,1)S...) custom-call(f32[8,1280]{1,0:T(8,128)S(1)} %get-tuple-element.98.refs, ...), custom_call_target="tpu_custom_call" | custom-call | flops 16999999488 | bytes 1000 | tf_op jit(solution)/shard_map/middle/pallas_call | solution.py:137
  83.9 4.4 %collective-permute-start.22 = (bf16[2,256,640]{2,1,0:T(8,128)(2,1)S(1)}, bf16[2,256,640]{2,1,0:T(8,128)(2,1)S(1)}, u32[]{:S(2)}, u32[]{:S(2)}) collective-permute-start(bf16[2,256,640]{2,1,0:T(8,128)(2,1)S(1)} %bitcast.19), channel_id=1, source_target_pairs={{0,1},{1,2},{2,3},{4,5},{5,6},{6,7},{8,9},{9,10},{10,11},{12,13},{... | collective-permute-start | bytes 1966088 | tf_op jit(solution)/shard_map/ppermute | solution.py:752
  88.3 1.5 %collective-permute-start.23 = (bf16[2,256,640]{2,1,0:T(8,128)(2,1)S(1)}, bf16[2,256,640]{2,1,0:T(8,128)(2,1)S(1)}, u32[]{:S(2)}, u32[]{:S(2)}) collective-permute-start(bf16[2,256,640]{2,1,0:T(8,128)(2,1)S(1)} %bitcast.20), channel_id=1, source_target_pairs={{1,0},{2,1},{3,2},{5,4},{6,5},{7,6},{9,8},{10,9},{11,10},{13,12},{... | collective-permute-start | bytes 1966088 | tf_op jit(solution)/shard_map/ppermute | solution.py:756
  89.8 3.2 %conv_grad.1 = (f32[5,80,640]{2,1,0:T(8,128)S(1)}, f32[8,128]{1,0:T(8,128)S(1)}, f32[80,128]{1,0:T(8,128)S(1)}, bf16[432,640]{1,0:T(8,128)(2,1)S(1)}, bf16[432,6...) custom-call(bf16[512,640]{1,0:T(8,128)(2,1)S(1)} %get-tuple-element.117.refs_0_, ...), custom_call_target="tpu_custom_call" | custom-call | flops 7000000000 | bytes 1000 | tf_op jit(solution)/shard_map/conv_grad/pallas_call | solution.py:137
  93.1 0.9 collective-permute-start.31
  94.0 1.5 %collective-permute-start.32 = (bf16[432,640]{1,0:T(8,128)(2,1)S(1)}, bf16[432,640]{1,0:T(8,128)(2,1)S(1)}, u32[]{:S(2)}, u32[]{:S(2)}) collective-permute-start(bf16[432,640]{1,0:T(8,128)(2,1)S(1)} %get-tuple-element.124), channel_id=1, source_target_pairs={{0,16},{4,20},{8,24},{12,28},{16,0},{20,4},{24,8},{28,12},{1,17},{... | collective-permute-start | bytes 1658888 | tf_op jit(solution)/shard_map/ppermute | solution.py:730
  95.5 1.1 collective-permute-start.33
  96.6 5.9 %collective-permute-done.22.refs_14_ = bf16[2,256,640]{2,1,0:T(8,128)(2,1)S(1)} collective-permute-done((bf16[2,256,640]{2,1,0:T(8,128)(2,1)S(1)}, bf16[2,256,640]{2,1,0:T(8,128)(2,1)S(1)}, u32[]{:S(2)}, u32[]{:S(2)}) %collective-permute-start.22) | collective-permute-done | bytes 655392 | tf_op jit(solution)/shard_map/ppermute | solution.py:752
  102.5 4.2 %collective-permute-done.23.refs_16_ = bf16[2,256,640]{2,1,0:T(8,128)(2,1)S(1)} collective-permute-done((bf16[2,256,640]{2,1,0:T(8,128)(2,1)S(1)}, bf16[2,256,640]{2,1,0:T(8,128)(2,1)S(1)}, u32[]{:S(2)}, u32[]{:S(2)}) %collective-permute-start.23) | collective-permute-done | bytes 655392 | tf_op jit(solution)/shard_map/ppermute | solution.py:756
  106.7 10.7 %back.1 = (f32[4,160,768]{2,1,0:T(8,128)S(1)}, bf16[2,160,768]{2,1,0:T(8,128)(2,1)S(1)}, bf16[2,160,768]{2,1,0:T(8,128)(2,1)S(1)}, f32[512,1280]{1,0:T(8,128)S(1)}) custom-call(bf16[7,640,640]{2,1,0:T(8,128)(2,1)S(1)} %get-tuple-element.106.refs_0_, f32[512,640]{1,0:T(8,128)S(1)} %get-tuple-element.107.refs_1_, f32[512,640]{1,0:T(8,128)S(1)} %get-tuple-element.108.refs_2_, ...), custom_call_target="tpu_custom_call" | custom-call | flops 100000000 | bytes 1000 | tf_op jit(solution)/shard_map/back/pallas_call | solution.py:137
  118.0 1.4 collective-permute-done.34.refs_1_
  121.0 0.9 collective-permute-start.36
  121.9 1.5 %collective-permute-start.37 = (bf16[160,768]{1,0:T(8,128)(2,1)S(1)}, bf16[160,768]{1,0:T(8,128)(2,1)S(1)}, u32[]{:S(2)}, u32[]{:S(2)}) collective-permute-start(bf16[160,768]{1,0:T(8,128)(2,1)S(1)} %get-tuple-element.137), channel_id=1, source_target_pairs={{0,16},{4,20},{8,24},{12,28},{16,0},{20,4},{24,8},{28,12},{1,17},{... | collective-permute-start | bytes 737288 | tf_op jit(solution)/shard_map/ppermute | solution.py:730
  123.5 1.1 collective-permute-start.38
  124.6 1.7 %collective-permute-start.42 = (bf16[128,640]{1,0:T(8,128)(2,1)S(1)}, bf16[128,640]{1,0:T(8,128)(2,1)S(1)}, u32[]{:S(2)}, u32[]{:S(2)}) collective-permute-start(bf16[128,640]{1,0:T(8,128)(2,1)S(1)} %get-tuple-element.152), channel_id=1, source_target_pairs={{0,1},{1,2},{2,3},{3,0},{4,5},{5,6},{6,7},{7,4},{8,9},{9,10},{10,1... | collective-permute-start | bytes 491528 | tf_op jit(solution)/shard_map/ppermute | solution.py:735
  126.2 1.6 %collective-permute-start.43 = (bf16[128,640]{1,0:T(8,128)(2,1)S(1)}, bf16[128,640]{1,0:T(8,128)(2,1)S(1)}, u32[]{:S(2)}, u32[]{:S(2)}) collective-permute-start(bf16[128,640]{1,0:T(8,128)(2,1)S(1)} %get-tuple-element.153), channel_id=1, source_target_pairs={{0,2},{1,3},{2,0},{3,1},{4,6},{5,7},{6,4},{7,5},{8,10},{9,11},{10,... | collective-permute-start | bytes 491528 | tf_op jit(solution)/shard_map/ppermute | solution.py:735
  127.8 2.1 %collective-permute-done.36.refs_1_ = bf16[160,768]{1,0:T(8,128)(2,1)S(1)} collective-permute-done((bf16[160,768]{1,0:T(8,128)(2,1)S(1)}, bf16[160,768]{1,0:T(8,128)(2,1)S(1)}, u32[]{:S(2)}, u32[]{:S(2)}) %collective-permute-start.36) | collective-permute-done | bytes 245792 | tf_op jit(solution)/shard_map/ppermute | solution.py:730
  129.9 2.8 %collective-permute-start.44 = (bf16[128,640]{1,0:T(8,128)(2,1)S(1)}, bf16[128,640]{1,0:T(8,128)(2,1)S(1)}, u32[]{:S(2)}, u32[]{:S(2)}) collective-permute-start(bf16[128,640]{1,0:T(8,128)(2,1)S(1)} %get-tuple-element.154), channel_id=1, source_target_pairs={{0,3},{1,0},{2,1},{3,2},{4,7},{5,4},{6,5},{7,6},{8,11},{9,8},{10,9... | collective-permute-start | bytes 491528 | tf_op jit(solution)/shard_map/ppermute | solution.py:735
  132.6 2.9 %input.1 = (bf16[512,1280]{1,0:T(8,128)(2,1)}, f32[8,128]{1,0:T(8,128)S(1)}) custom-call(f32[512,1280]{1,0:T(8,128)S(1)} %get-tuple-element.120.refs_0_, f32[512,1280]{1,0:T(8,128)S(1)} %get-tuple-element.91.refs_0_.refs_4_.refs_1_, f32[512,128]{1,0:T(8,128)S(1)} %get-tuple-element.93.refs_4_.refs_2_, ...), custom_call_target="tpu_custom_call" | custom-call | flops 3000000000 | bytes 1000 | tf_op jit(solution)/shard_map/input/pallas_call | solution.py:137
  135.8 1.4 collective-permute-start.40
  137.3 2.4 %collective-permute-start.41 = (bf16[40,768]{1,0:T(8,128)(2,1)S(1)}, bf16[40,768]{1,0:T(8,128)(2,1)S(1)}, u32[]{:S(2)}, u32[]{:S(2)}) collective-permute-start(bf16[40,768]{1,0:T(8,128)(2,1)S(1)} %get-tuple-element.143), channel_id=1, source_target_pairs={{0,3},{1,0},{2,1},{3,2},{4,7},{5,4},{6,5},{7,6},{8,11},{9,8},{10,9... | collective-permute-start | bytes 184328 | tf_op jit(solution)/shard_map/ppermute | solution.py:735
  140.3 1.2 end_b.1
  143.2 3.1 %collective-permute-done.40.refs_2_ = bf16[40,768]{1,0:T(8,128)(2,1)S(1)} collective-permute-done((bf16[40,768]{1,0:T(8,128)(2,1)S(1)}, bf16[40,768]{1,0:T(8,128)(2,1)S(1)}, u32[]{:S(2)}, u32[]{:S(2)}) %collective-permute-start.40) | collective-permute-done | bytes 61472 | tf_op jit(solution)/shard_map/ppermute | solution.py:735
  (76 shorter events, 10.4 us)
Async XLA Ops:
  2.3 7.8 %collective-permute-start = (bf16[40,768]{1,0:T(8,128)(2,1)}, bf16[40,768]{1,0:T(8,128)(2,1)S(1)}, u32[]{:S(2)}, u32[]{:S(2)}) collective-permute-start(bf16[40,768]{1,0:T(8,128)(2,1)} %pack_a.1.refs_2_.refs_0_), channel_id=1, source_target_pairs={{0,1},{1,2},{2,3},{3,0},{4,5},{5,6},{6,7},{7,4},{8,9},{9,10},{10,1... | collective-permute-start | bytes 184328 | tf_op jit(solution)/shard_map/ppermute | solution.py:735
  5.4 7.1 %collective-permute-start.1 = (bf16[40,768]{1,0:T(8,128)(2,1)}, bf16[40,768]{1,0:T(8,128)(2,1)S(1)}, u32[]{:S(2)}, u32[]{:S(2)}) collective-permute-start(bf16[40,768]{1,0:T(8,128)(2,1)} %pack_a.1.refs_2_.refs_0_), channel_id=1, source_target_pairs={{0,2},{1,3},{2,0},{3,1},{4,6},{5,7},{6,4},{7,5},{8,10},{9,11},{10,... | collective-permute-start | bytes 184328 | tf_op jit(solution)/shard_map/ppermute | solution.py:735
  8.0 4.8 %collective-permute-start.2 = (bf16[40,768]{1,0:T(8,128)(2,1)}, bf16[40,768]{1,0:T(8,128)(2,1)S(1)}, u32[]{:S(2)}, u32[]{:S(2)}) collective-permute-start(bf16[40,768]{1,0:T(8,128)(2,1)} %pack_a.1.refs_2_.refs_0_), channel_id=1, source_target_pairs={{0,3},{1,0},{2,1},{3,2},{4,7},{5,4},{6,5},{7,6},{8,11},{9,8},{10,9... | collective-permute-start | bytes 184328 | tf_op jit(solution)/shard_map/ppermute | solution.py:735
  13.7 7.3 %collective-permute-start.3 = (bf16[160,768]{1,0:T(8,128)(2,1)S(1)}, bf16[160,768]{1,0:T(8,128)(2,1)S(1)}, u32[]{:S(2)}, u32[]{:S(2)}) collective-permute-start(bf16[160,768]{1,0:T(8,128)(2,1)S(1)} %line_a.1.refs_2_), channel_id=1, source_target_pairs={{0,8},{4,12},{8,0},{12,4},{16,24},{20,28},{24,16},{28,20},{1,9},{5... | collective-permute-start | bytes 737288 | tf_op jit(solution)/shard_map/ppermute | solution.py:730
  15.6 16.3 %collective-permute-start.10 = (bf16[140,640]{1,0:T(8,128)(2,1)S(1)}, bf16[140,640]{1,0:T(8,128)(2,1)S(1)}, u32[]{:S(2)}, u32[]{:S(2)}) collective-permute-start(bf16[140,640]{1,0:T(8,128)(2,1)S(1)} %pack_b.1.refs_1_.refs_0_), channel_id=1, source_target_pairs={{0,1},{1,2},{2,3},{3,0},{4,5},{5,6},{6,7},{7,4},{8,9},{9,10},{10,1... | collective-permute-start | bytes 537608 | tf_op jit(solution)/shard_map/ppermute | solution.py:735
  17.0 14.9 %collective-permute-start.11 = (bf16[140,640]{1,0:T(8,128)(2,1)S(1)}, bf16[140,640]{1,0:T(8,128)(2,1)S(1)}, u32[]{:S(2)}, u32[]{:S(2)}) collective-permute-start(bf16[140,640]{1,0:T(8,128)(2,1)S(1)} %pack_b.1.refs_1_.refs_0_), channel_id=1, source_target_pairs={{0,2},{1,3},{2,0},{3,1},{4,6},{5,7},{6,4},{7,5},{8,10},{9,11},{10,... | collective-permute-start | bytes 537608 | tf_op jit(solution)/shard_map/ppermute | solution.py:735
  19.1 13.3 %collective-permute-start.12 = (bf16[140,640]{1,0:T(8,128)(2,1)S(1)}, bf16[140,640]{1,0:T(8,128)(2,1)S(1)}, u32[]{:S(2)}, u32[]{:S(2)}) collective-permute-start(bf16[140,640]{1,0:T(8,128)(2,1)S(1)} %pack_b.1.refs_1_.refs_0_), channel_id=1, source_target_pairs={{0,3},{1,0},{2,1},{3,2},{4,7},{5,4},{6,5},{7,6},{8,11},{9,8},{10,9... | collective-permute-start | bytes 537608 | tf_op jit(solution)/shard_map/ppermute | solution.py:735
  19.5 11.9 %collective-permute-start.4 = (bf16[160,768]{1,0:T(8,128)(2,1)S(1)}, bf16[160,768]{1,0:T(8,128)(2,1)S(1)}, u32[]{:S(2)}, u32[]{:S(2)}) collective-permute-start(bf16[160,768]{1,0:T(8,128)(2,1)S(1)} %line_a.1.refs_2_), channel_id=1, source_target_pairs={{0,16},{4,20},{8,24},{12,28},{16,0},{20,4},{24,8},{28,12},{1,17},{... | collective-permute-start | bytes 737288 | tf_op jit(solution)/shard_map/ppermute | solution.py:730
  21.1 10.3 %collective-permute-start.5 = (bf16[160,768]{1,0:T(8,128)(2,1)S(1)}, bf16[160,768]{1,0:T(8,128)(2,1)S(1)}, u32[]{:S(2)}, u32[]{:S(2)}) collective-permute-start(bf16[160,768]{1,0:T(8,128)(2,1)S(1)} %line_a.1.refs_2_), channel_id=1, source_target_pairs={{0,24},{4,28},{8,16},{12,20},{16,8},{20,12},{24,0},{28,4},{1,25},{... | collective-permute-start | bytes 737288 | tf_op jit(solution)/shard_map/ppermute | solution.py:730
  31.4 2.2 %collective-permute-start.6 = (bf16[160,768]{1,0:T(8,128)(2,1)S(1)}, bf16[160,768]{1,0:T(8,128)(2,1)S(1)}, u32[]{:S(2)}, u32[]{:S(2)}) collective-permute-start(bf16[160,768]{1,0:T(8,128)(2,1)S(1)} %line_a.1.refs_2_), channel_id=1, source_target_pairs={{0,4},{4,0},{8,12},{12,8},{16,20},{20,16},{24,28},{28,24},{1,5},{5... | collective-permute-start | bytes 737288 | tf_op jit(solution)/shard_map/ppermute | solution.py:730
  31.4 3.5 %collective-permute-start.7 = (bf16[160,768]{1,0:T(8,128)(2,1)S(1)}, bf16[160,768]{1,0:T(8,128)(2,1)S(1)}, u32[]{:S(2)}, u32[]{:S(2)}) collective-permute-start(bf16[160,768]{1,0:T(8,128)(2,1)S(1)} %collective-permute-done.3.refs_3_), channel_id=1, source_target_pairs={{0,4},{4,0},{8,12},{12,8},{16,20},{20,16},{24,28},{28,24},{1,5},{5... | collective-permute-start | bytes 737288 | tf_op jit(solution)/shard_map/ppermute | solution.py:730
  31.9 4.4 %collective-permute-start.8 = (bf16[160,768]{1,0:T(8,128)(2,1)S(1)}, bf16[160,768]{1,0:T(8,128)(2,1)S(1)}, u32[]{:S(2)}, u32[]{:S(2)}) collective-permute-start(bf16[160,768]{1,0:T(8,128)(2,1)S(1)} %collective-permute-done.4.refs_4_), channel_id=1, source_target_pairs={{0,4},{4,0},{8,12},{12,8},{16,20},{20,16},{24,28},{28,24},{1,5},{5... | collective-permute-start | bytes 737288 | tf_op jit(solution)/shard_map/ppermute | solution.py:730
  31.9 4.4 %collective-permute-start.9 = (bf16[160,768]{1,0:T(8,128)(2,1)S(1)}, bf16[160,768]{1,0:T(8,128)(2,1)S(1)}, u32[]{:S(2)}, u32[]{:S(2)}) collective-permute-start(bf16[160,768]{1,0:T(8,128)(2,1)S(1)} %collective-permute-done.5.refs_5_), channel_id=1, source_target_pairs={{0,4},{4,0},{8,12},{12,8},{16,20},{20,16},{24,28},{28,24},{1,5},{5... | collective-permute-start | bytes 737288 | tf_op jit(solution)/shard_map/ppermute | solution.py:730
  32.7 19.0 %collective-permute-start.15 = (bf16[7,80,640]{2,1,0:T(8,128)(2,1)S(1)}, bf16[7,80,640]{2,1,0:T(8,128)(2,1)S(1)}, u32[]{:S(2)}, u32[]{:S(2)}) collective-permute-start(bf16[7,80,640]{2,1,0:T(8,128)(2,1)S(1)} %line_b.1.refs_10_.refs_11_), channel_id=1, source_target_pairs={{0,8},{4,12},{8,0},{12,4},{16,24},{20,28},{24,16},{28,20},{1,9},{5... | collective-permute-start | bytes 2150408 | tf_op jit(solution)/shard_map/ppermute | solution.py:730
  33.6 31.9 %collective-permute-start.16 = (bf16[7,80,640]{2,1,0:T(8,128)(2,1)S(1)}, bf16[7,80,640]{2,1,0:T(8,128)(2,1)S(1)}, u32[]{:S(2)}, u32[]{:S(2)}) collective-permute-start(bf16[7,80,640]{2,1,0:T(8,128)(2,1)S(1)} %line_b.1.refs_10_.refs_11_), channel_id=1, source_target_pairs={{0,16},{4,20},{8,24},{12,28},{16,0},{20,4},{24,8},{28,12},{1,17},{... | collective-permute-start | bytes 2150408 | tf_op jit(solution)/shard_map/ppermute | solution.py:730
  34.9 32.3 %collective-permute-start.17 = (bf16[7,80,640]{2,1,0:T(8,128)(2,1)S(1)}, bf16[7,80,640]{2,1,0:T(8,128)(2,1)S(1)}, u32[]{:S(2)}, u32[]{:S(2)}) collective-permute-start(bf16[7,80,640]{2,1,0:T(8,128)(2,1)S(1)} %line_b.1.refs_10_.refs_11_), channel_id=1, source_target_pairs={{0,24},{4,28},{8,16},{12,20},{16,8},{20,12},{24,0},{28,4},{1,25},{... | collective-permute-start | bytes 2150408 | tf_op jit(solution)/shard_map/ppermute | solution.py:730
  36.3 35.1 %copy-start.4 = (s32[2,256]{1,0:T(2,128)S(1)}, s32[2,256]{1,0:T(2,128)}, u32[]{:S(2)}) copy-start(s32[2,256]{1,0:T(2,128)} %refs_4_.3) | copy-start | bytes 6148
  36.3 35.1 %copy-start.5 = (s32[2,153]{1,0:T(2,128)S(1)}, s32[2,153]{1,0:T(2,128)}, u32[]{:S(2)}) copy-start(s32[2,153]{1,0:T(2,128)} %refs_5_.3) | copy-start | bytes 3676
  36.3 35.1 %copy-start.6 = (s32[2,153]{1,0:T(2,128)S(1)}, s32[2,153]{1,0:T(2,128)}, u32[]{:S(2)}) copy-start(s32[2,153]{1,0:T(2,128)} %refs_6_.3) | copy-start | bytes 3676
  42.7 24.4 %collective-permute-start.13 = (bf16[2,256,640]{2,1,0:T(8,128)(2,1)S(1)}, bf16[2,256,640]{2,1,0:T(8,128)(2,1)S(1)}, u32[]{:S(2)}, u32[]{:S(2)}) collective-permute-start(bf16[2,256,640]{2,1,0:T(8,128)(2,1)S(1)} %bitcast.24), channel_id=1, source_target_pairs={{0,1},{1,2},{2,3},{4,5},{5,6},{6,7},{8,9},{9,10},{10,11},{12,13},{... | collective-permute-start | bytes 1966088 | tf_op jit(solution)/shard_map/ppermute | solution.py:752
  47.2 20.0 %collective-permute-start.14 = (bf16[2,256,640]{2,1,0:T(8,128)(2,1)S(1)}, bf16[2,256,640]{2,1,0:T(8,128)(2,1)S(1)}, u32[]{:S(2)}, u32[]{:S(2)}) collective-permute-start(bf16[2,256,640]{2,1,0:T(8,128)(2,1)S(1)} %bitcast.25), channel_id=1, source_target_pairs={{1,0},{2,1},{3,2},{5,4},{6,5},{7,6},{9,8},{10,9},{11,10},{13,12},{... | collective-permute-start | bytes 1966088 | tf_op jit(solution)/shard_map/ppermute | solution.py:756
  51.7 16.5 %collective-permute-start.18 = (bf16[7,80,640]{2,1,0:T(8,128)(2,1)S(1)}, bf16[7,80,640]{2,1,0:T(8,128)(2,1)S(1)}, u32[]{:S(2)}, u32[]{:S(2)}) collective-permute-start(bf16[7,80,640]{2,1,0:T(8,128)(2,1)S(1)} %line_b.1.refs_10_.refs_11_), channel_id=1, source_target_pairs={{0,4},{4,0},{8,12},{12,8},{16,20},{20,16},{24,28},{28,24},{1,5},{5... | collective-permute-start | bytes 2150408 | tf_op jit(solution)/shard_map/ppermute | solution.py:730
  67.2 2.2 %collective-permute-start.19 = (bf16[7,80,640]{2,1,0:T(8,128)(2,1)S(1)}, bf16[7,80,640]{2,1,0:T(8,128)(2,1)S(1)}, u32[]{:S(2)}, u32[]{:S(2)}) collective-permute-start(bf16[7,80,640]{2,1,0:T(8,128)(2,1)S(1)} %collective-permute-done.15.refs_12_), channel_id=1, source_target_pairs={{0,4},{4,0},{8,12},{12,8},{16,20},{20,16},{24,28},{28,24},{1,5},{5... | collective-permute-start | bytes 2150408 | tf_op jit(solution)/shard_map/ppermute | solution.py:730
  67.2 3.2 %collective-permute-start.20 = (bf16[7,80,640]{2,1,0:T(8,128)(2,1)S(1)}, bf16[7,80,640]{2,1,0:T(8,128)(2,1)S(1)}, u32[]{:S(2)}, u32[]{:S(2)}) collective-permute-start(bf16[7,80,640]{2,1,0:T(8,128)(2,1)S(1)} %collective-permute-done.16.refs_13_), channel_id=1, source_target_pairs={{0,4},{4,0},{8,12},{12,8},{16,20},{20,16},{24,28},{28,24},{1,5},{5... | collective-permute-start | bytes 2150408 | tf_op jit(solution)/shard_map/ppermute | solution.py:730
  67.7 3.7 %collective-permute-start.21 = (bf16[7,80,640]{2,1,0:T(8,128)(2,1)S(1)}, bf16[7,80,640]{2,1,0:T(8,128)(2,1)S(1)}, u32[]{:S(2)}, u32[]{:S(2)}) collective-permute-start(bf16[7,80,640]{2,1,0:T(8,128)(2,1)S(1)} %collective-permute-done.17.refs_14_), channel_id=1, source_target_pairs={{0,4},{4,0},{8,12},{12,8},{16,20},{20,16},{24,28},{28,24},{1,5},{5... | collective-permute-start | bytes 2150408 | tf_op jit(solution)/shard_map/ppermute | solution.py:730
  67.7 15.7 %collective-permute-start.29 = (bf16[2,256,640]{2,1,0:T(8,128)(2,1)S(1)}, bf16[2,256,640]{2,1,0:T(8,128)(2,1)S(1)}, u32[]{:S(2)}, u32[]{:S(2)}) collective-permute-start(bf16[2,256,640]{2,1,0:T(8,128)(2,1)S(1)} %bitcast.26), channel_id=1, source_target_pairs={{0,4},{4,0},{8,12},{12,8},{16,20},{20,16},{24,28},{28,24},{1,5},{5... | collective-permute-start | bytes 1966088 | tf_op jit(solution)/shard_map/ppermute | solution.py:730
  68.2 15.3 %collective-permute-start.28 = (bf16[2,256,640]{2,1,0:T(8,128)(2,1)S(1)}, bf16[2,256,640]{2,1,0:T(8,128)(2,1)S(1)}, u32[]{:S(2)}, u32[]{:S(2)}) collective-permute-start(bf16[2,256,640]{2,1,0:T(8,128)(2,1)S(1)} %collective-permute-done.13.refs_8_), channel_id=1, source_target_pairs={{0,4},{4,0},{8,12},{12,8},{16,20},{20,16},{24,28},{28,24},{1,5},{5... | collective-permute-start | bytes 1966088 | tf_op jit(solution)/shard_map/ppermute | solution.py:730
  69.3 14.6 %collective-permute-start.30 = (bf16[2,256,640]{2,1,0:T(8,128)(2,1)S(1)}, bf16[2,256,640]{2,1,0:T(8,128)(2,1)S(1)}, u32[]{:S(2)}, u32[]{:S(2)}) collective-permute-start(bf16[2,256,640]{2,1,0:T(8,128)(2,1)S(1)} %collective-permute-done.14.refs_10_), channel_id=1, source_target_pairs={{0,4},{4,0},{8,12},{12,8},{16,20},{20,16},{24,28},{28,24},{1,5},{5... | collective-permute-start | bytes 1966088 | tf_op jit(solution)/shard_map/ppermute | solution.py:730
  82.9 6.9 %collective-permute-start.24 = (bf16[512,640]{1,0:T(8,128)(2,1)S(1)}, bf16[512,640]{1,0:T(8,128)(2,1)S(1)}, u32[]{:S(2)}, u32[]{:S(2)}) collective-permute-start(bf16[512,640]{1,0:T(8,128)(2,1)S(1)} %get-tuple-element.117.refs_0_), channel_id=1, source_target_pairs={{0,4},{4,0},{8,12},{12,8},{16,20},{20,16},{24,28},{28,24},{1,5},{5... | collective-permute-start | bytes 1966088 | tf_op jit(solution)/shard_map/ppermute | solution.py:730
  83.0 6.8 %collective-permute-start.25 = (bf16[512,640]{1,0:T(8,128)(2,1)S(1)}, bf16[512,640]{1,0:T(8,128)(2,1)S(1)}, u32[]{:S(2)}, u32[]{:S(2)}) collective-permute-start(bf16[512,640]{1,0:T(8,128)(2,1)S(1)} %get-tuple-element.116.refs_2_), channel_id=1, source_target_pairs={{0,4},{4,0},{8,12},{12,8},{16,20},{20,16},{24,28},{28,24},{1,5},{5... | collective-permute-start | bytes 1966088 | tf_op jit(solution)/shard_map/ppermute | solution.py:730
  83.4 6.4 %collective-permute-start.26 = (bf16[512,128]{1,0:T(8,128)(2,1)S(1)}, bf16[512,128]{1,0:T(8,128)(2,1)S(1)}, u32[]{:S(2)}, u32[]{:S(2)}) collective-permute-start(bf16[512,128]{1,0:T(8,128)(2,1)S(1)} %get-tuple-element.118.refs_4_), channel_id=1, source_target_pairs={{0,4},{4,0},{8,12},{12,8},{16,20},{20,16},{24,28},{28,24},{1,5},{5... | collective-permute-start | bytes 393224 | tf_op jit(solution)/shard_map/ppermute | solution.py:730
  83.5 4.8 %collective-permute-start.27 = (f32[8,128]{1,0:T(8,128)S(1)}, f32[8,128]{1,0:T(8,128)S(1)}, u32[]{:S(2)}, u32[]{:S(2)}) collective-permute-start(f32[8,128]{1,0:T(8,128)S(1)} %get-tuple-element.114.refs_6_.refs_11_), channel_id=1, source_target_pairs={{0,4},{4,0},{8,12},{12,8},{16,20},{20,16},{24,28},{28,24},{1,5},{5... | collective-permute-start | bytes 12296 | tf_op jit(solution)/shard_map/ppermute | solution.py:730
  83.9 18.6 %collective-permute-start.22 = (bf16[2,256,640]{2,1,0:T(8,128)(2,1)S(1)}, bf16[2,256,640]{2,1,0:T(8,128)(2,1)S(1)}, u32[]{:S(2)}, u32[]{:S(2)}) collective-permute-start(bf16[2,256,640]{2,1,0:T(8,128)(2,1)S(1)} %bitcast.19), channel_id=1, source_target_pairs={{0,1},{1,2},{2,3},{4,5},{5,6},{6,7},{8,9},{9,10},{10,11},{12,13},{... | collective-permute-start | bytes 1966088 | tf_op jit(solution)/shard_map/ppermute | solution.py:752
  88.3 18.4 %collective-permute-start.23 = (bf16[2,256,640]{2,1,0:T(8,128)(2,1)S(1)}, bf16[2,256,640]{2,1,0:T(8,128)(2,1)S(1)}, u32[]{:S(2)}, u32[]{:S(2)}) collective-permute-start(bf16[2,256,640]{2,1,0:T(8,128)(2,1)S(1)} %bitcast.20), channel_id=1, source_target_pairs={{1,0},{2,1},{3,2},{5,4},{6,5},{7,6},{9,8},{10,9},{11,10},{13,12},{... | collective-permute-start | bytes 1966088 | tf_op jit(solution)/shard_map/ppermute | solution.py:756
  93.1 27.4 %collective-permute-start.31 = (bf16[432,640]{1,0:T(8,128)(2,1)S(1)}, bf16[432,640]{1,0:T(8,128)(2,1)S(1)}, u32[]{:S(2)}, u32[]{:S(2)}) collective-permute-start(bf16[432,640]{1,0:T(8,128)(2,1)S(1)} %get-tuple-element.123), channel_id=1, source_target_pairs={{0,8},{4,12},{8,0},{12,4},{16,24},{20,28},{24,16},{28,20},{1,9},{5... | collective-permute-start | bytes 1658888 | tf_op jit(solution)/shard_map/ppermute | solution.py:730
  94.0 26.5 %collective-permute-start.32 = (bf16[432,640]{1,0:T(8,128)(2,1)S(1)}, bf16[432,640]{1,0:T(8,128)(2,1)S(1)}, u32[]{:S(2)}, u32[]{:S(2)}) collective-permute-start(bf16[432,640]{1,0:T(8,128)(2,1)S(1)} %get-tuple-element.124), channel_id=1, source_target_pairs={{0,16},{4,20},{8,24},{12,28},{16,0},{20,4},{24,8},{28,12},{1,17},{... | collective-permute-start | bytes 1658888 | tf_op jit(solution)/shard_map/ppermute | solution.py:730
  95.5 25.0 %collective-permute-start.33 = (bf16[432,640]{1,0:T(8,128)(2,1)S(1)}, bf16[432,640]{1,0:T(8,128)(2,1)S(1)}, u32[]{:S(2)}, u32[]{:S(2)}) collective-permute-start(bf16[432,640]{1,0:T(8,128)(2,1)S(1)} %get-tuple-element.125), channel_id=1, source_target_pairs={{0,24},{4,28},{8,16},{12,20},{16,8},{20,12},{24,0},{28,4},{1,25},{... | collective-permute-start | bytes 1658888 | tf_op jit(solution)/shard_map/ppermute | solution.py:730
  117.4 1.9 %collective-permute-start.34 = (bf16[2,160,768]{2,1,0:T(8,128)(2,1)S(1)}, bf16[2,160,768]{2,1,0:T(8,128)(2,1)S(1)}, u32[]{:S(2)}, u32[]{:S(2)}) collective-permute-start(bf16[2,160,768]{2,1,0:T(8,128)(2,1)S(1)} %get-tuple-element.127), channel_id=1, source_target_pairs={{0,4},{4,0},{8,12},{12,8},{16,20},{20,16},{24,28},{28,24},{1,5},{5... | collective-permute-start | bytes 1474568 | tf_op jit(solution)/shard_map/ppermute | solution.py:730
  117.5 2.6 %collective-permute-start.35 = (bf16[2,160,768]{2,1,0:T(8,128)(2,1)S(1)}, bf16[2,160,768]{2,1,0:T(8,128)(2,1)S(1)}, u32[]{:S(2)}, u32[]{:S(2)}) collective-permute-start(bf16[2,160,768]{2,1,0:T(8,128)(2,1)S(1)} %get-tuple-element.128), channel_id=1, source_target_pairs={{0,4},{4,0},{8,12},{12,8},{16,20},{20,16},{24,28},{28,24},{1,5},{5... | collective-permute-start | bytes 1474568 | tf_op jit(solution)/shard_map/ppermute | solution.py:730
  121.0 8.9 %collective-permute-start.36 = (bf16[160,768]{1,0:T(8,128)(2,1)S(1)}, bf16[160,768]{1,0:T(8,128)(2,1)S(1)}, u32[]{:S(2)}, u32[]{:S(2)}) collective-permute-start(bf16[160,768]{1,0:T(8,128)(2,1)S(1)} %get-tuple-element.136), channel_id=1, source_target_pairs={{0,8},{4,12},{8,0},{12,4},{16,24},{20,28},{24,16},{28,20},{1,9},{5... | collective-permute-start | bytes 737288 | tf_op jit(solution)/shard_map/ppermute | solution.py:730
  121.9 13.7 %collective-permute-start.37 = (bf16[160,768]{1,0:T(8,128)(2,1)S(1)}, bf16[160,768]{1,0:T(8,128)(2,1)S(1)}, u32[]{:S(2)}, u32[]{:S(2)}) collective-permute-start(bf16[160,768]{1,0:T(8,128)(2,1)S(1)} %get-tuple-element.137), channel_id=1, source_target_pairs={{0,16},{4,20},{8,24},{12,28},{16,0},{20,4},{24,8},{28,12},{1,17},{... | collective-permute-start | bytes 737288 | tf_op jit(solution)/shard_map/ppermute | solution.py:730
  123.5 12.1 %collective-permute-start.38 = (bf16[160,768]{1,0:T(8,128)(2,1)S(1)}, bf16[160,768]{1,0:T(8,128)(2,1)S(1)}, u32[]{:S(2)}, u32[]{:S(2)}) collective-permute-start(bf16[160,768]{1,0:T(8,128)(2,1)S(1)} %get-tuple-element.138), channel_id=1, source_target_pairs={{0,24},{4,28},{8,16},{12,20},{16,8},{20,12},{24,0},{28,4},{1,25},{... | collective-permute-start | bytes 737288 | tf_op jit(solution)/shard_map/ppermute | solution.py:730
  124.6 12.7 %collective-permute-start.42 = (bf16[128,640]{1,0:T(8,128)(2,1)S(1)}, bf16[128,640]{1,0:T(8,128)(2,1)S(1)}, u32[]{:S(2)}, u32[]{:S(2)}) collective-permute-start(bf16[128,640]{1,0:T(8,128)(2,1)S(1)} %get-tuple-element.152), channel_id=1, source_target_pairs={{0,1},{1,2},{2,3},{3,0},{4,5},{5,6},{6,7},{7,4},{8,9},{9,10},{10,1... | collective-permute-start | bytes 491528 | tf_op jit(solution)/shard_map/ppermute | solution.py:735
  126.2 14.0 %collective-permute-start.43 = (bf16[128,640]{1,0:T(8,128)(2,1)S(1)}, bf16[128,640]{1,0:T(8,128)(2,1)S(1)}, u32[]{:S(2)}, u32[]{:S(2)}) collective-permute-start(bf16[128,640]{1,0:T(8,128)(2,1)S(1)} %get-tuple-element.153), channel_id=1, source_target_pairs={{0,2},{1,3},{2,0},{3,1},{4,6},{5,7},{6,4},{7,5},{8,10},{9,11},{10,... | collective-permute-start | bytes 491528 | tf_op jit(solution)/shard_map/ppermute | solution.py:735
  129.9 10.4 %collective-permute-start.44 = (bf16[128,640]{1,0:T(8,128)(2,1)S(1)}, bf16[128,640]{1,0:T(8,128)(2,1)S(1)}, u32[]{:S(2)}, u32[]{:S(2)}) collective-permute-start(bf16[128,640]{1,0:T(8,128)(2,1)S(1)} %get-tuple-element.154), channel_id=1, source_target_pairs={{0,3},{1,0},{2,1},{3,2},{4,7},{5,4},{6,5},{7,6},{8,11},{9,8},{10,9... | collective-permute-start | bytes 491528 | tf_op jit(solution)/shard_map/ppermute | solution.py:735
  135.8 7.4 %collective-permute-start.39 = (bf16[40,768]{1,0:T(8,128)(2,1)S(1)}, bf16[40,768]{1,0:T(8,128)(2,1)S(1)}, u32[]{:S(2)}, u32[]{:S(2)}) collective-permute-start(bf16[40,768]{1,0:T(8,128)(2,1)S(1)} %get-tuple-element.141), channel_id=1, source_target_pairs={{0,1},{1,2},{2,3},{3,0},{4,5},{5,6},{6,7},{7,4},{8,9},{9,10},{10,1... | collective-permute-start | bytes 184328 | tf_op jit(solution)/shard_map/ppermute | solution.py:735
  135.8 10.5 %collective-permute-start.40 = (bf16[40,768]{1,0:T(8,128)(2,1)S(1)}, bf16[40,768]{1,0:T(8,128)(2,1)S(1)}, u32[]{:S(2)}, u32[]{:S(2)}) collective-permute-start(bf16[40,768]{1,0:T(8,128)(2,1)S(1)} %get-tuple-element.142), channel_id=1, source_target_pairs={{0,2},{1,3},{2,0},{3,1},{4,6},{5,7},{6,4},{7,5},{8,10},{9,11},{10,... | collective-permute-start | bytes 184328 | tf_op jit(solution)/shard_map/ppermute | solution.py:735
  137.3 9.0 %collective-permute-start.41 = (bf16[40,768]{1,0:T(8,128)(2,1)S(1)}, bf16[40,768]{1,0:T(8,128)(2,1)S(1)}, u32[]{:S(2)}, u32[]{:S(2)}) collective-permute-start(bf16[40,768]{1,0:T(8,128)(2,1)S(1)} %get-tuple-element.143), channel_id=1, source_target_pairs={{0,3},{1,0},{2,1},{3,2},{4,7},{5,4},{6,5},{7,6},{8,11},{9,8},{10,9... | collective-permute-start | bytes 184328 | tf_op jit(solution)/shard_map/ppermute | solution.py:735
  (5 other events, 65.7 us)

commit v4 on v3

--- a/solution.py
+++ b/solution.py
@@ -269,7 +269,7 @@
 
 
 def middle_kernel(
-    chips,
+    layout,
     hops,
     seqs,
     vocab,
@@ -284,12 +284,11 @@
     *refs,
 ):
     blocks = refs[: 2 * hops + 1]
-    pieces = refs[2 * hops + 1 : 2 * hops + 1 + 2 * chips]
+    pieces = refs[2 * hops + 1 : 2 * hops + 1 + len(layout)]
     (
         taps,
         block_out,
-        third_act,
-        logit_grad,
+        bundle,
         head_grad,
         conv_low,
         narrow_sums,
@@ -300,18 +299,17 @@
         r3,
         work,
         product,
-    ) = refs[2 * hops + 1 + 2 * chips :]
+    ) = refs[2 * hops + 1 + len(layout) :]
     inner = taps.shape[1]
     width = tokens.shape[1]
     rows = tokens.shape[0]
     length = rows // seqs
     me = lax.axis_index("dp")
     block = pieces[0].shape[1]
-    for c in range(2):
-        for m in range(chips):
-            at = pl.multiple_of((me ^ (2 * m + c)) * block, block)
-            for slab in range(taps.shape[0]):
-                taps[slab, pl.ds(at, block), :] = pieces[c * chips + m][slab]
+    for (mask, first), piece in zip(layout, pieces):
+        at = pl.multiple_of((me ^ mask) * block, block)
+        for slab in range(piece.shape[0]):
+            taps[first + slab, pl.ds(at, block), :] = piece[slab]
     for b, ref in enumerate(blocks):
         ext[:, b * length : (b + 1) * length, :] = ref[...]
     bias, g3, b3 = narrow_v[3:4, :], narrow_v[4:5, :], narrow_v[5:6, :]
@@ -341,14 +339,16 @@
             u = n * g3 + b3
             cdf, pdf = gauss(u)
             here = pl.ds(pl.multiple_of(s * length + c.start, c.size), c.size)
-            third_act[here, :] = (u * cdf).astype(BF)
+            bundle[here, inner : 2 * inner] = (u * cdf).astype(BF)
             gp3[c, :] = cdf + u * pdf
             n3[c, :] = n
             r3[c, :] = jnp.broadcast_to(r, (r.shape[0], LANES))
 
         each_chunk(length, 32, ahead)
         for h in range(width // inner):
-            work[:, h * inner : (h + 1) * inner] = dot(third_act[whole, :], taps[KERNEL_TAPS + h])
+            work[:, h * inner : (h + 1) * inner] = dot(
+                bundle[whole, inner : 2 * inner], taps[KERNEL_TAPS + h]
+            )
 
         def add(c):
             here = pl.ds(pl.multiple_of(s * length + c.start, c.size), c.size)
@@ -372,7 +372,7 @@
         entropy = log_total - picked
         chance = jnp.exp(picked - log_total)
         grad = (LOSS_SCALE * mask * (jnp.exp(logits - log_total) - hot)).astype(BF)
-        logit_grad[whole, :] = grad
+        bundle[whole, 2 * inner :] = grad
         columns = jnp.where(lane == 0, mask, jnp.where(lane == 1, mask * chance, 0.0))
         kinds = lax.broadcasted_iota(jnp.int32, (LANES, length), 0) == types[pl.ds(s, 1), :]
         tallies = jnp.dot(
@@ -400,23 +400,23 @@
             low = (r3[c, 0:1] * (eg - mean_e - n * mean_en)).astype(BF)
             here = pl.ds(pl.multiple_of(s * length + c.start, c.size), c.size)
             conv_low[here, :] = low
+            bundle[here, 0:inner] = low
             narrow_sums[16:24, :] += rows8(low.astype(F32))
 
         each_chunk(length, 32, behind)
+
+    bundle[rows:, :] = jnp.zeros((16, bundle.shape[1]), BF)
+    for j, term in enumerate(thirds(stats[...])):
+        bundle[rows : rows + 8, j * LANES : (j + 1) * LANES] = term
 
 
 def conv_grad_kernel(
     chips,
     hops,
     seqs,
-    third_own,
-    third_other,
-    low_own,
-    low_other,
-    logit_own,
-    logit_other,
+    bundle_own,
+    bundle_other,
     stats,
-    stats_other,
     *refs,
 ):
     count = 2 * hops + 1
@@ -425,10 +425,11 @@
     sends = refs[2 * count + 3 : 2 * count + 2 + chips]
     turned, turn, third_t = refs[2 * count + 2 + chips :]
     slabs, block, inner = own.shape
-    length = low_own.shape[0] // seqs
+    rows = bundle_own.shape[0] - 16
+    length = rows // seqs
     me = lax.axis_index("dp") // 2
     core = lax.axis_index("dp") & 1
-    total_stats = stats[...] + stats_other[...]
+    total_stats = stats[...] + sum_terms(bundle_other[rows:, :])
     own_stats[...] = total_stats
     tail = jnp.concatenate([stats_rows(total_stats, inner), jnp.zeros((8, inner), F32)], axis=0)
     for send in sends:
@@ -451,7 +452,8 @@
                     ] = chosen(turn, q)
         for s in range(seqs):
             columns = slice(s * length, (s + 1) * length)
-            turn[...] = jnp.transpose((third_own, third_other)[side][columns, :])
+            source = (bundle_own, bundle_other)[side]
+            turn[...] = jnp.transpose(source[columns, inner : 2 * inner])
             for q in range(chips):
                 third_t[side, q * block : (q + 1) * block, columns] = chosen(turn, q)
 
@@ -464,14 +466,15 @@
     for k in range(KERNEL_TAPS):
         at = hops * length + (k - CENTRE) * DILATION_RATE
         value = 0.0
-        for side, low in enumerate((low_own, low_other)):
+        for side, low in enumerate((bundle_own, bundle_other)):
             for s in range(seqs):
                 value = value + dot(
                     turned[side * seqs + s, :, at : at + length],
-                    low[s * length : (s + 1) * length, :],
+                    low[s * length : (s + 1) * length, 0:inner],
                 )
         share(k, value)
-    value = dot(third_t[0], logit_own[...]) + dot(third_t[1], logit_other[...])
+    value = dot(third_t[0], bundle_own[0:rows, 2 * inner :])
+    value += dot(third_t[1], bundle_other[0:rows, 2 * inner :])
     parts = by_mask([value[q * block : (q + 1) * block] for q in range(chips)], me)
     own_out[...] = parts[0]
     for m in range(1, chips):
@@ -710,9 +713,10 @@
                 send[q % half, :, inner : inner + LANES] = extra[lines].astype(BF)
 
 
-def input_kernel(e1, n1, r1, wide_v, logit_grad, extras, input_grad, token, work):
+def input_kernel(e1, n1, r1, wide_v, bundle, extras, input_grad, token, work):
     token[...] = jnp.zeros_like(token)
-    work[...] = dot_nt(logit_grad[...], extras[...])
+    logit_grad = bundle[0 : e1.shape[0], bundle.shape[1] - LANES :]
+    work[...] = dot_nt(logit_grad, extras[...])
     g1 = wide_v[0:1, :]
 
     def body(c):
@@ -852,7 +856,15 @@
         name="line_b",
         after=[r1],
     )
-    own_b = [line_b] + [swap(line_b, 2 * m) for m in range(1, chips)]
+    if chips == 4:
+        half = slabs // 2
+        by_x, by_y = swap(line_b, 2), swap(line_b, 4)
+        own_b = [line_b, by_x, by_y, swap(by_x[:half], 4), swap(by_y[half:], 2)]
+        layout = [(0, 0), (2, 0), (4, 0), (6, 0), (6, half)]
+    else:
+        own_b = [line_b] + [swap(line_b, 2 * m) for m in range(1, chips)]
+        layout = [(2 * m, 0) for m in range(chips)]
+    layout = layout + [(mask + 1, first) for mask, first in layout]
     w_in, extras, wide_v, narrow_v, act, gp1, n2, gp2, r2, conv_in = call(
         functools.partial(second_kernel, chips, vocab),
         [n1, spread] + pieces_a,
@@ -876,20 +888,21 @@
     )
     blocks = halo(conv_in.reshape(seqs, length, inner))
     other_line = swap(line_b, 1)
-    *chip_b, _, _ = lax.optimization_barrier((*own_b[1:], blocks[0], blocks[-1]))
-    pieces_b = [line_b] + list(chip_b) + [other_line] + [swap(piece, 1) for piece in chip_b]
+    early = 3 if chips == 4 else 1
+    near = [swap(piece, 1) for piece in own_b[1:early]]
+    *late, _, _ = lax.optimization_barrier((*own_b[early:], blocks[0], blocks[-1]))
+    pieces_b = own_b[:early] + list(late) + [other_line] + near + [swap(piece, 1) for piece in late]
     other_blocks = [swap(piece, 1) for piece in blocks]
     (
         taps,
         block_out,
-        third_act,
-        logit_grad,
+        bundle,
         head_grad,
         conv_low,
         narrow_sums,
         stats,
     ) = call(
-        functools.partial(middle_kernel, chips, hops, seqs, vocab),
+        functools.partial(middle_kernel, layout, hops, seqs, vocab),
         [
             wide_v,
             narrow_v,
@@ -905,8 +918,7 @@
         [
             sds((slabs, inner, inner), BF),
             sds((rows, width), BF),
-            sds((rows, inner), BF),
-            sds((rows, LANES), BF),
+            sds((rows + 16, 2 * inner + LANES), BF),
             sds((width, LANES), F32),
             sds((rows, inner), BF),
             sds((24, inner), F32),
@@ -925,15 +937,11 @@
         name="middle",
     )
     grad_blocks = halo(conv_low.reshape(seqs, length, inner))
-    low_other = swap(conv_low, 1)
-    third_other = swap(third_act, 1)
-    logit_other = swap(logit_grad, 1)
-    stats_other = swap(stats, 1)
+    other_bundle = swap(bundle, 1)
     message = KERNEL_TAPS * size * narrow + size * narrow // (inner // LANES) + 16
     split_b = call(
         functools.partial(conv_grad_kernel, chips, hops, seqs),
-        [third_act, third_other, conv_low, low_other, logit_grad, logit_other]
-        + [stats, stats_other]
+        [bundle, other_bundle, stats]
         + blocks
         + other_blocks,
         [
@@ -999,7 +1007,7 @@
 
     input_grad, input_token = call(
         input_kernel,
-        [e1, n1, r1, wide_v, logit_grad, extras],
+        [e1, n1, r1, wide_v, bundle, extras],
         [sds((rows, width), BF), sds((8, LANES), F32)],
         [pltpu.VMEM((rows, width), F32)],
         us=3,

time: 148 us -> 142 us (0.959)
  waiting for transfers between devices: 49.9 us -> 43.1 us
    ppermute x29 -> x28, waiting for transfers between devices: 32.6 us -> 22.4 us  [swap(): return lax.ppermute(value, 'dp', [(i, i ^ mask) for i in range(count)])]
    ppermute x2, waiting for transfers between devices: 4.17 us -> 7.78 us  [halo(): lax.ppermute(series, 'seq', [(i + h, i) for i in range(size - h)])]
    ppermute x29 -> x28, starting transfers between devices: 19.4 us -> 19.9 us  [swap(): return lax.ppermute(value, 'dp', [(i, i ^ mask) for i in range(count)])]
  transfers between devices with their start and end apart: 45 -> 44, of which waited for: 18 -> 16; matrix products, arithmetic and copies ran while one was open for 1% -> 1% of each run, Pallas kernels for 26% -> 19%
where the time goes in v4:
time: 142 us
  starting transfers between devices  52.6 us (37%)
  waiting for transfers between devices  43.1 us (30%)
  Pallas kernels  41.3 us (29%)
  between operations  2.75 us (2%)
  local copies, waits for them, and re-layouts  1.45 us (1%)
    pallas_call x15, Pallas kernels, call(): pl.pallas_call(body, out_shape=list(outs), in_specs=[pl.BlockSpec(memory_...  41.3 us
    ppermute x28, waiting for transfers between devices, swap(): return lax.ppermute(value, 'dp', [(i, i ^ mask) for i in range(count)])  22.4 us
    ppermute x12, starting transfers between devices, shifted(): lax.ppermute(value, 'seq', [(i, (i + k) % size) for i in range(size)])  21.6 us
    ppermute x28, starting transfers between devices, swap(): return lax.ppermute(value, 'dp', [(i, i ^ mask) for i in range(count)])  19.9 us
    ppermute x2, starting transfers between devices, halo(): lax.ppermute(series, 'seq', [(i, i + h) for i in range(size - h)])  8.12 us
    ppermute x2, waiting for transfers between devices, halo(): lax.ppermute(series, 'seq', [(i + h, i) for i in range(size - h)])  7.78 us
    ppermute x12, waiting for transfers between devices, shifted(): lax.ppermute(value, 'seq', [(i, (i + k) % size) for i in range(size)])  6.96 us
    ppermute x2, waiting for transfers between devices, halo(): lax.ppermute(series, 'seq', [(i, i + h) for i in range(size - h)])  5.98 us
  transfers between devices with their start and end apart: 44, of which 16 were waited for; matrix products, arithmetic and copies ran while one was open for 1% of the time, Pallas kernels for 19%

profile of v4, /device:TPU:0, one launch (start us, length us, event | category | flops | bytes accessed | tf_op | source)
XLA Modules:
  0.0 141.6 jit_solution(1986421092183956723)
XLA Ops:
  0.7 1.6 %pack_a.1.refs_2_.refs_0_ = bf16[40,768]{1,0:T(8,128)(2,1)} custom-call(bf16[40,640]{1,0:T(8,128)(2,1)} %refs_0_.1, bf16[30,40]{1,0:T(8,128)(2,1)} %bitcast.30, bf16[40]{0:T(256)(128)(2,1)} %refs_2_.1, bf16[40]{0:T(256)(128)(2,1)} %refs_3_.1, bf16[40]{0:T(256)(128)(2,1)} %refs_4_.2, bf16[20]{0:T(256)(128)(2,1)} %refs_5_.2, bf16[20]{0:T(256)(128)(2,1)} %refs_6_.2, ...), custom_call_target="tpu_custom_call" | custom-call | flops 1000000000 | bytes 1000 | tf_op jit(solution)/shard_map/pack_a/pallas_call | solution.py:137
  2.3 3.1 %collective-permute-start = (bf16[40,768]{1,0:T(8,128)(2,1)}, bf16[40,768]{1,0:T(8,128)(2,1)S(1)}, u32[]{:S(2)}, u32[]{:S(2)}) collective-permute-start(bf16[40,768]{1,0:T(8,128)(2,1)} %pack_a.1.refs_2_.refs_0_), channel_id=1, source_target_pairs={{0,1},{1,2},{2,3},{3,0},{4,5},{5,6},{6,7},{7,4},{8,9},{9,10},{10,1... | collective-permute-start | bytes 184328 | tf_op jit(solution)/shard_map/ppermute | solution.py:739
  5.4 2.6 %collective-permute-start.1 = (bf16[40,768]{1,0:T(8,128)(2,1)}, bf16[40,768]{1,0:T(8,128)(2,1)S(1)}, u32[]{:S(2)}, u32[]{:S(2)}) collective-permute-start(bf16[40,768]{1,0:T(8,128)(2,1)} %pack_a.1.refs_2_.refs_0_), channel_id=1, source_target_pairs={{0,2},{1,3},{2,0},{3,1},{4,6},{5,7},{6,4},{7,5},{8,10},{9,11},{10,... | collective-permute-start | bytes 184328 | tf_op jit(solution)/shard_map/ppermute | solution.py:739
  8.0 1.3 collective-permute-start.2
  9.3 0.7 collective-permute-done.refs_1_
  10.1 2.4 %collective-permute-done.1.refs_2_ = bf16[40,768]{1,0:T(8,128)(2,1)S(1)} collective-permute-done((bf16[40,768]{1,0:T(8,128)(2,1)}, bf16[40,768]{1,0:T(8,128)(2,1)S(1)}, u32[]{:S(2)}, u32[]{:S(2)}) %collective-permute-start.1) | collective-permute-done | bytes 61472 | tf_op jit(solution)/shard_map/ppermute | solution.py:739
  12.8 0.8 copy-done.3
  13.7 1.6 %collective-permute-start.3 = (bf16[160,768]{1,0:T(8,128)(2,1)S(1)}, bf16[160,768]{1,0:T(8,128)(2,1)S(1)}, u32[]{:S(2)}, u32[]{:S(2)}) collective-permute-start(bf16[160,768]{1,0:T(8,128)(2,1)S(1)} %line_a.1.refs_2_), channel_id=1, source_target_pairs={{0,8},{4,12},{8,0},{12,4},{16,24},{20,28},{24,16},{28,20},{1,9},{5... | collective-permute-start | bytes 737288 | tf_op jit(solution)/shard_map/ppermute | solution.py:734
  15.6 1.4 %collective-permute-start.10 = (bf16[140,640]{1,0:T(8,128)(2,1)S(1)}, bf16[140,640]{1,0:T(8,128)(2,1)S(1)}, u32[]{:S(2)}, u32[]{:S(2)}) collective-permute-start(bf16[140,640]{1,0:T(8,128)(2,1)S(1)} %pack_b.1.refs_1_.refs_0_), channel_id=1, source_target_pairs={{0,1},{1,2},{2,3},{3,0},{4,5},{5,6},{6,7},{7,4},{8,9},{9,10},{10,1... | collective-permute-start | bytes 537608 | tf_op jit(solution)/shard_map/ppermute | solution.py:739
  17.0 2.1 %collective-permute-start.11 = (bf16[140,640]{1,0:T(8,128)(2,1)S(1)}, bf16[140,640]{1,0:T(8,128)(2,1)S(1)}, u32[]{:S(2)}, u32[]{:S(2)}) collective-permute-start(bf16[140,640]{1,0:T(8,128)(2,1)S(1)} %pack_b.1.refs_1_.refs_0_), channel_id=1, source_target_pairs={{0,2},{1,3},{2,0},{3,1},{4,6},{5,7},{6,4},{7,5},{8,10},{9,11},{10,... | collective-permute-start | bytes 537608 | tf_op jit(solution)/shard_map/ppermute | solution.py:739
  19.5 1.5 %collective-permute-start.4 = (bf16[160,768]{1,0:T(8,128)(2,1)S(1)}, bf16[160,768]{1,0:T(8,128)(2,1)S(1)}, u32[]{:S(2)}, u32[]{:S(2)}) collective-permute-start(bf16[160,768]{1,0:T(8,128)(2,1)S(1)} %line_a.1.refs_2_), channel_id=1, source_target_pairs={{0,16},{4,20},{8,24},{12,28},{16,0},{20,4},{24,8},{28,12},{1,17},{... | collective-permute-start | bytes 737288 | tf_op jit(solution)/shard_map/ppermute | solution.py:734
  21.1 1.8 %collective-permute-start.5 = (bf16[160,768]{1,0:T(8,128)(2,1)S(1)}, bf16[160,768]{1,0:T(8,128)(2,1)S(1)}, u32[]{:S(2)}, u32[]{:S(2)}) collective-permute-start(bf16[160,768]{1,0:T(8,128)(2,1)S(1)} %line_a.1.refs_2_), channel_id=1, source_target_pairs={{0,24},{4,28},{8,16},{12,20},{16,8},{20,12},{24,0},{28,4},{1,25},{... | collective-permute-start | bytes 737288 | tf_op jit(solution)/shard_map/ppermute | solution.py:734
  22.8 1.6 %first.1 = (f32[512,1280]{1,0:T(8,128)S(1)}, f32[512,128]{1,0:T(8,128)S(1)}, bf16[1280,640]{1,0:T(8,128)(2,1)S(1)}) custom-call(bf16[512,1280]{1,0:T(8,128)(2,1)S(1)} %bitcast.22, bf16[140,640]{1,0:T(8,128)(2,1)S(1)} %pack_b.1.refs_1_.refs_0_), custom_call_target="tpu_custom_call" | custom-call | flops 6000000000 | bytes 1000 | tf_op jit(solution)/shard_map/first/pallas_call | solution.py:137
  24.4 7.0 %collective-permute-done.4.refs_4_ = bf16[160,768]{1,0:T(8,128)(2,1)S(1)} collective-permute-done((bf16[160,768]{1,0:T(8,128)(2,1)S(1)}, bf16[160,768]{1,0:T(8,128)(2,1)S(1)}, u32[]{:S(2)}, u32[]{:S(2)}) %collective-permute-start.4) | collective-permute-done | bytes 245792 | tf_op jit(solution)/shard_map/ppermute | solution.py:734
  32.7 0.9 collective-permute-start.15
  33.6 1.2 collective-permute-start.16
  34.9 6.4 %second.1 = (bf16[1280,640]{1,0:T(8,128)(2,1)S(1)}, bf16[1280,128]{1,0:T(8,128)(2,1)S(1)}, f32[8,1280]{1,0:T(8,128)S(1)}, f32[8,640]{1,0:T(8,128)S(1)}, bf16[512...) custom-call(f32[512,1280]{1,0:T(8,128)S(1)} %get-tuple-element.89.re, ...), custom_call_target="tpu_custom_call" | custom-call | flops 8999999488 | bytes 1000 | tf_op jit(solution)/shard_map/second/pallas_call | solution.py:137
  41.3 4.4 %collective-permute-start.13 = (bf16[2,256,640]{2,1,0:T(8,128)(2,1)S(1)}, bf16[2,256,640]{2,1,0:T(8,128)(2,1)S(1)}, u32[]{:S(2)}, u32[]{:S(2)}) collective-permute-start(bf16[2,256,640]{2,1,0:T(8,128)(2,1)S(1)} %bitcast.24), channel_id=1, source_target_pairs={{0,1},{1,2},{2,3},{4,5},{5,6},{6,7},{8,9},{9,10},{10,11},{12,13},{... | collective-permute-start | bytes 1966088 | tf_op jit(solution)/shard_map/ppermute | solution.py:756
  45.7 1.5 %collective-permute-start.14 = (bf16[2,256,640]{2,1,0:T(8,128)(2,1)S(1)}, bf16[2,256,640]{2,1,0:T(8,128)(2,1)S(1)}, u32[]{:S(2)}, u32[]{:S(2)}) collective-permute-start(bf16[2,256,640]{2,1,0:T(8,128)(2,1)S(1)} %bitcast.25), channel_id=1, source_target_pairs={{1,0},{2,1},{3,2},{5,4},{6,5},{7,6},{9,8},{10,9},{11,10},{13,12},{... | collective-permute-start | bytes 1966088 | tf_op jit(solution)/shard_map/ppermute | solution.py:760
  47.2 3.6 %collective-permute-done.15.refs_12_ = bf16[7,80,640]{2,1,0:T(8,128)(2,1)S(1)} collective-permute-done((bf16[7,80,640]{2,1,0:T(8,128)(2,1)S(1)}, bf16[7,80,640]{2,1,0:T(8,128)(2,1)S(1)}, u32[]{:S(2)}, u32[]{:S(2)}) %collective-permute-start.15) | collective-permute-done | bytes 716832 | tf_op jit(solution)/shard_map/ppermute | solution.py:734
  50.9 1.6 %collective-permute-start.17 = (bf16[3,80,640]{2,1,0:T(8,128)(2,1)S(1)}, bf16[3,80,640]{2,1,0:T(8,128)(2,1)S(1)}, u32[]{:S(2)}, u32[]{:S(2)}) collective-permute-start(bf16[3,80,640]{2,1,0:T(8,128)(2,1)S(1)} %slice.24), channel_id=1, source_target_pairs={{0,16},{4,20},{8,24},{12,28},{16,0},{20,4},{24,8},{28,12},{1,17},{... | collective-permute-start | bytes 921608 | tf_op jit(solution)/shard_map/ppermute | solution.py:734
  52.5 0.6 collective-permute-start.18
  53.1 6.2 %collective-permute-done.17.refs_14_ = bf16[3,80,640]{2,1,0:T(8,128)(2,1)S(1)} collective-permute-done((bf16[3,80,640]{2,1,0:T(8,128)(2,1)S(1)}, bf16[3,80,640]{2,1,0:T(8,128)(2,1)S(1)}, u32[]{:S(2)}, u32[]{:S(2)}) %collective-permute-start.17) | collective-permute-done | bytes 307232 | tf_op jit(solution)/shard_map/ppermute | solution.py:734
  59.8 3.6 %collective-permute-done.14.refs_10_.refs_5_ = bf16[2,256,640]{2,1,0:T(8,128)(2,1)S(1)} collective-permute-done((bf16[2,256,640]{2,1,0:T(8,128)(2,1)S(1)}, bf16[2,256,640]{2,1,0:T(8,128)(2,1)S(1)}, u32[]{:S(2)}, u32[]{:S(2)}) %collective-permute-start.14) | collective-permute-done | bytes 655392 | tf_op jit(solution)/shard_map/ppermute | solution.py:760
  64.0 1.6 %collective-permute-done.22.refs_19_ = bf16[3,80,640]{2,1,0:T(8,128)(2,1)S(1)} collective-permute-done((bf16[3,80,640]{2,1,0:T(8,128)(2,1)S(1)}, bf16[3,80,640]{2,1,0:T(8,128)(2,1)S(1)}, u32[]{:S(2)}, u32[]{:S(2)}) %collective-permute-start.22) | collective-permute-done | bytes 307232 | tf_op jit(solution)/shard_map/ppermute | solution.py:734
  65.7 11.3 %middle.1 = (bf16[7,640,640]{2,1,0:T(8,128)(2,1)S(1)}, bf16[512,1280]{1,0:T(8,128)(2,1)}, bf16[528,1408]{1,0:T(8,128)(2,1)S(1)}, f32[1280,128]{1,0:T(8,128)S(1)}...) custom-call(f32[8,1280]{1,0:T(8,128)S(1)} %get-tuple-element.96.refs_0_.refs_8_.refs_3_, ...), custom_call_target="tpu_custom_call" | custom-call | flops 16999999488 | bytes 1000 | tf_op jit(solution)/shard_map/middle/pallas_call | solution.py:137
  78.0 3.7 %collective-permute-start.24 = (bf16[2,256,640]{2,1,0:T(8,128)(2,1)S(1)}, bf16[2,256,640]{2,1,0:T(8,128)(2,1)S(1)}, u32[]{:S(2)}, u32[]{:S(2)}) collective-permute-start(bf16[2,256,640]{2,1,0:T(8,128)(2,1)S(1)} %bitcast.19), channel_id=1, source_target_pairs={{0,1},{1,2},{2,3},{4,5},{5,6},{6,7},{8,9},{9,10},{10,11},{12,13},{... | collective-permute-start | bytes 1966088 | tf_op jit(solution)/shard_map/ppermute | solution.py:756
  81.7 1.5 %collective-permute-start.25 = (bf16[2,256,640]{2,1,0:T(8,128)(2,1)S(1)}, bf16[2,256,640]{2,1,0:T(8,128)(2,1)S(1)}, u32[]{:S(2)}, u32[]{:S(2)}) collective-permute-start(bf16[2,256,640]{2,1,0:T(8,128)(2,1)S(1)} %bitcast.20), channel_id=1, source_target_pairs={{1,0},{2,1},{3,2},{5,4},{6,5},{7,6},{9,8},{10,9},{11,10},{13,12},{... | collective-permute-start | bytes 1966088 | tf_op jit(solution)/shard_map/ppermute | solution.py:760
  83.2 3.1 %conv_grad.1 = (f32[5,80,640]{2,1,0:T(8,128)S(1)}, f32[8,128]{1,0:T(8,128)S(1)}, f32[80,128]{1,0:T(8,128)S(1)}, bf16[432,640]{1,0:T(8,128)(2,1)S(1)}, bf16[432,6...) custom-call(bf16[528,1408]{1,0:T(8,128)(2,1)S(1)} %get-tuple-element.114.refs_0_.refs_4_, ...), custom_call_target="tpu_custom_call" | custom-call | flops 7000000000 | bytes 1000 | tf_op jit(solution)/shard_map/conv_grad/pallas_call | solution.py:137
  86.4 1.3 collective-permute-start.30
  88.2 1.7 %collective-permute-start.32 = (bf16[432,640]{1,0:T(8,128)(2,1)S(1)}, bf16[432,640]{1,0:T(8,128)(2,1)S(1)}, u32[]{:S(2)}, u32[]{:S(2)}) collective-permute-start(bf16[432,640]{1,0:T(8,128)(2,1)S(1)} %get-tuple-element.121), channel_id=1, source_target_pairs={{0,24},{4,28},{8,16},{12,20},{16,8},{20,12},{24,0},{28,4},{1,25},{... | collective-permute-start | bytes 1658888 | tf_op jit(solution)/shard_map/ppermute | solution.py:734
  89.9 6.0 %collective-permute-done.24.refs_14_ = bf16[2,256,640]{2,1,0:T(8,128)(2,1)S(1)} collective-permute-done((bf16[2,256,640]{2,1,0:T(8,128)(2,1)S(1)}, bf16[2,256,640]{2,1,0:T(8,128)(2,1)S(1)}, u32[]{:S(2)}, u32[]{:S(2)}) %collective-permute-start.24) | collective-permute-done | bytes 655392 | tf_op jit(solution)/shard_map/ppermute | solution.py:756
  95.9 4.2 %collective-permute-done.25.refs_16_ = bf16[2,256,640]{2,1,0:T(8,128)(2,1)S(1)} collective-permute-done((bf16[2,256,640]{2,1,0:T(8,128)(2,1)S(1)}, bf16[2,256,640]{2,1,0:T(8,128)(2,1)S(1)}, u32[]{:S(2)}, u32[]{:S(2)}) %collective-permute-start.25) | collective-permute-done | bytes 655392 | tf_op jit(solution)/shard_map/ppermute | solution.py:760
  100.1 10.8 %back.1 = (f32[4,160,768]{2,1,0:T(8,128)S(1)}, bf16[2,160,768]{2,1,0:T(8,128)(2,1)S(1)}, bf16[2,160,768]{2,1,0:T(8,128)(2,1)S(1)}, f32[512,1280]{1,0:T(8,128)S(1)}) custom-call(bf16[7,640,640]{2,1,0:T(8,128)(2,1)S(1)} %get-tuple-element.103.refs_0_, f32[512,640]{1,0:T(8,128)S(1)} %get-tuple-element.104.refs_1_, f32[512,640]{1,0:T(8,128)S(1)} %get-tuple-element.105.refs_2_, ...), custom_call_target="tpu_custom_call" | custom-call | flops 100000000 | bytes 1000 | tf_op jit(solution)/shard_map/back/pallas_call | solution.py:137
  111.4 1.4 collective-permute-done.33.refs_1_
  112.8 0.7 collective-permute-done.34.refs_2_
  114.4 1.3 collective-permute-start.35
  116.2 1.8 %collective-permute-start.37 = (bf16[160,768]{1,0:T(8,128)(2,1)S(1)}, bf16[160,768]{1,0:T(8,128)(2,1)S(1)}, u32[]{:S(2)}, u32[]{:S(2)}) collective-permute-start(bf16[160,768]{1,0:T(8,128)(2,1)S(1)} %get-tuple-element.134), channel_id=1, source_target_pairs={{0,24},{4,28},{8,16},{12,20},{16,8},{20,12},{24,0},{28,4},{1,25},{... | collective-permute-start | bytes 737288 | tf_op jit(solution)/shard_map/ppermute | solution.py:734
  117.9 2.0 %collective-permute-start.41 = (bf16[128,640]{1,0:T(8,128)(2,1)S(1)}, bf16[128,640]{1,0:T(8,128)(2,1)S(1)}, u32[]{:S(2)}, u32[]{:S(2)}) collective-permute-start(bf16[128,640]{1,0:T(8,128)(2,1)S(1)} %get-tuple-element.148), channel_id=1, source_target_pairs={{0,1},{1,2},{2,3},{3,0},{4,5},{5,6},{6,7},{7,4},{8,9},{9,10},{10,1... | collective-permute-start | bytes 491528 | tf_op jit(solution)/shard_map/ppermute | solution.py:739
  119.9 1.6 %collective-permute-start.42 = (bf16[128,640]{1,0:T(8,128)(2,1)S(1)}, bf16[128,640]{1,0:T(8,128)(2,1)S(1)}, u32[]{:S(2)}, u32[]{:S(2)}) collective-permute-start(bf16[128,640]{1,0:T(8,128)(2,1)S(1)} %get-tuple-element.149), channel_id=1, source_target_pairs={{0,2},{1,3},{2,0},{3,1},{4,6},{5,7},{6,4},{7,5},{8,10},{9,11},{10,... | collective-permute-start | bytes 491528 | tf_op jit(solution)/shard_map/ppermute | solution.py:739
  121.5 1.8 %collective-permute-done.35.refs_1_ = bf16[160,768]{1,0:T(8,128)(2,1)S(1)} collective-permute-done((bf16[160,768]{1,0:T(8,128)(2,1)S(1)}, bf16[160,768]{1,0:T(8,128)(2,1)S(1)}, u32[]{:S(2)}, u32[]{:S(2)}) %collective-permute-start.35) | collective-permute-done | bytes 245792 | tf_op jit(solution)/shard_map/ppermute | solution.py:734
  123.3 2.9 %collective-permute-start.43 = (bf16[128,640]{1,0:T(8,128)(2,1)S(1)}, bf16[128,640]{1,0:T(8,128)(2,1)S(1)}, u32[]{:S(2)}, u32[]{:S(2)}) collective-permute-start(bf16[128,640]{1,0:T(8,128)(2,1)S(1)} %get-tuple-element.150), channel_id=1, source_target_pairs={{0,3},{1,0},{2,1},{3,2},{4,7},{5,4},{6,5},{7,6},{8,11},{9,8},{10,9... | collective-permute-start | bytes 491528 | tf_op jit(solution)/shard_map/ppermute | solution.py:739
  126.2 2.8 %input.1 = (bf16[512,1280]{1,0:T(8,128)(2,1)}, f32[8,128]{1,0:T(8,128)S(1)}) custom-call(f32[512,1280]{1,0:T(8,128)S(1)} %get-tuple-element.116.refs_0_, f32[512,1280]{1,0:T(8,128)S(1)} %get-tuple-element.89.refs_0_.refs_4_.refs_1_, f32[512,128]{1,0:T(8,128)S(1)} %get-tuple-element.91.refs_4_.refs_2_, ...), custom_call_target="tpu_custom_call" | custom-call | flops 3000000000 | bytes 1000 | tf_op jit(solution)/shard_map/input/pallas_call | solution.py:137
  129.7 1.2 collective-permute-start.39
  130.9 2.4 %collective-permute-start.40 = (bf16[40,768]{1,0:T(8,128)(2,1)S(1)}, bf16[40,768]{1,0:T(8,128)(2,1)S(1)}, u32[]{:S(2)}, u32[]{:S(2)}) collective-permute-start(bf16[40,768]{1,0:T(8,128)(2,1)S(1)} %get-tuple-element.139), channel_id=1, source_target_pairs={{0,3},{1,0},{2,1},{3,2},{4,7},{5,4},{6,5},{7,6},{8,11},{9,8},{10,9... | collective-permute-start | bytes 184328 | tf_op jit(solution)/shard_map/ppermute | solution.py:739
  133.5 1.2 end_b.1
  136.4 3.3 %collective-permute-done.39.refs_2_ = bf16[40,768]{1,0:T(8,128)(2,1)S(1)} collective-permute-done((bf16[40,768]{1,0:T(8,128)(2,1)S(1)}, bf16[40,768]{1,0:T(8,128)(2,1)S(1)}, u32[]{:S(2)}, u32[]{:S(2)}) %collective-permute-start.39) | collective-permute-done | bytes 61472 | tf_op jit(solution)/shard_map/ppermute | solution.py:739
  139.8 0.7 end_a.1
  (76 shorter events, 9.1 us)
Async XLA Ops:
  2.3 7.8 %collective-permute-start = (bf16[40,768]{1,0:T(8,128)(2,1)}, bf16[40,768]{1,0:T(8,128)(2,1)S(1)}, u32[]{:S(2)}, u32[]{:S(2)}) collective-permute-start(bf16[40,768]{1,0:T(8,128)(2,1)} %pack_a.1.refs_2_.refs_0_), channel_id=1, source_target_pairs={{0,1},{1,2},{2,3},{3,0},{4,5},{5,6},{6,7},{7,4},{8,9},{9,10},{10,1... | collective-permute-start | bytes 184328 | tf_op jit(solution)/shard_map/ppermute | solution.py:739
  5.4 7.1 %collective-permute-start.1 = (bf16[40,768]{1,0:T(8,128)(2,1)}, bf16[40,768]{1,0:T(8,128)(2,1)S(1)}, u32[]{:S(2)}, u32[]{:S(2)}) collective-permute-start(bf16[40,768]{1,0:T(8,128)(2,1)} %pack_a.1.refs_2_.refs_0_), channel_id=1, source_target_pairs={{0,2},{1,3},{2,0},{3,1},{4,6},{5,7},{6,4},{7,5},{8,10},{9,11},{10,... | collective-permute-start | bytes 184328 | tf_op jit(solution)/shard_map/ppermute | solution.py:739
  8.0 4.8 %collective-permute-start.2 = (bf16[40,768]{1,0:T(8,128)(2,1)}, bf16[40,768]{1,0:T(8,128)(2,1)S(1)}, u32[]{:S(2)}, u32[]{:S(2)}) collective-permute-start(bf16[40,768]{1,0:T(8,128)(2,1)} %pack_a.1.refs_2_.refs_0_), channel_id=1, source_target_pairs={{0,3},{1,0},{2,1},{3,2},{4,7},{5,4},{6,5},{7,6},{8,11},{9,8},{10,9... | collective-permute-start | bytes 184328 | tf_op jit(solution)/shard_map/ppermute | solution.py:739
  13.7 7.3 %collective-permute-start.3 = (bf16[160,768]{1,0:T(8,128)(2,1)S(1)}, bf16[160,768]{1,0:T(8,128)(2,1)S(1)}, u32[]{:S(2)}, u32[]{:S(2)}) collective-permute-start(bf16[160,768]{1,0:T(8,128)(2,1)S(1)} %line_a.1.refs_2_), channel_id=1, source_target_pairs={{0,8},{4,12},{8,0},{12,4},{16,24},{20,28},{24,16},{28,20},{1,9},{5... | collective-permute-start | bytes 737288 | tf_op jit(solution)/shard_map/ppermute | solution.py:734
  15.6 16.3 %collective-permute-start.10 = (bf16[140,640]{1,0:T(8,128)(2,1)S(1)}, bf16[140,640]{1,0:T(8,128)(2,1)S(1)}, u32[]{:S(2)}, u32[]{:S(2)}) collective-permute-start(bf16[140,640]{1,0:T(8,128)(2,1)S(1)} %pack_b.1.refs_1_.refs_0_), channel_id=1, source_target_pairs={{0,1},{1,2},{2,3},{3,0},{4,5},{5,6},{6,7},{7,4},{8,9},{9,10},{10,1... | collective-permute-start | bytes 537608 | tf_op jit(solution)/shard_map/ppermute | solution.py:739
  17.0 14.9 %collective-permute-start.11 = (bf16[140,640]{1,0:T(8,128)(2,1)S(1)}, bf16[140,640]{1,0:T(8,128)(2,1)S(1)}, u32[]{:S(2)}, u32[]{:S(2)}) collective-permute-start(bf16[140,640]{1,0:T(8,128)(2,1)S(1)} %pack_b.1.refs_1_.refs_0_), channel_id=1, source_target_pairs={{0,2},{1,3},{2,0},{3,1},{4,6},{5,7},{6,4},{7,5},{8,10},{9,11},{10,... | collective-permute-start | bytes 537608 | tf_op jit(solution)/shard_map/ppermute | solution.py:739
  19.1 13.3 %collective-permute-start.12 = (bf16[140,640]{1,0:T(8,128)(2,1)S(1)}, bf16[140,640]{1,0:T(8,128)(2,1)S(1)}, u32[]{:S(2)}, u32[]{:S(2)}) collective-permute-start(bf16[140,640]{1,0:T(8,128)(2,1)S(1)} %pack_b.1.refs_1_.refs_0_), channel_id=1, source_target_pairs={{0,3},{1,0},{2,1},{3,2},{4,7},{5,4},{6,5},{7,6},{8,11},{9,8},{10,9... | collective-permute-start | bytes 537608 | tf_op jit(solution)/shard_map/ppermute | solution.py:739
  19.5 11.9 %collective-permute-start.4 = (bf16[160,768]{1,0:T(8,128)(2,1)S(1)}, bf16[160,768]{1,0:T(8,128)(2,1)S(1)}, u32[]{:S(2)}, u32[]{:S(2)}) collective-permute-start(bf16[160,768]{1,0:T(8,128)(2,1)S(1)} %line_a.1.refs_2_), channel_id=1, source_target_pairs={{0,16},{4,20},{8,24},{12,28},{16,0},{20,4},{24,8},{28,12},{1,17},{... | collective-permute-start | bytes 737288 | tf_op jit(solution)/shard_map/ppermute | solution.py:734
  21.1 10.3 %collective-permute-start.5 = (bf16[160,768]{1,0:T(8,128)(2,1)S(1)}, bf16[160,768]{1,0:T(8,128)(2,1)S(1)}, u32[]{:S(2)}, u32[]{:S(2)}) collective-permute-start(bf16[160,768]{1,0:T(8,128)(2,1)S(1)} %line_a.1.refs_2_), channel_id=1, source_target_pairs={{0,24},{4,28},{8,16},{12,20},{16,8},{20,12},{24,0},{28,4},{1,25},{... | collective-permute-start | bytes 737288 | tf_op jit(solution)/shard_map/ppermute | solution.py:734
  31.4 2.2 %collective-permute-start.6 = (bf16[160,768]{1,0:T(8,128)(2,1)S(1)}, bf16[160,768]{1,0:T(8,128)(2,1)S(1)}, u32[]{:S(2)}, u32[]{:S(2)}) collective-permute-start(bf16[160,768]{1,0:T(8,128)(2,1)S(1)} %line_a.1.refs_2_), channel_id=1, source_target_pairs={{0,4},{4,0},{8,12},{12,8},{16,20},{20,16},{24,28},{28,24},{1,5},{5... | collective-permute-start | bytes 737288 | tf_op jit(solution)/shard_map/ppermute | solution.py:734
  31.4 3.5 %collective-permute-start.7 = (bf16[160,768]{1,0:T(8,128)(2,1)S(1)}, bf16[160,768]{1,0:T(8,128)(2,1)S(1)}, u32[]{:S(2)}, u32[]{:S(2)}) collective-permute-start(bf16[160,768]{1,0:T(8,128)(2,1)S(1)} %collective-permute-done.3.refs_3_), channel_id=1, source_target_pairs={{0,4},{4,0},{8,12},{12,8},{16,20},{20,16},{24,28},{28,24},{1,5},{5... | collective-permute-start | bytes 737288 | tf_op jit(solution)/shard_map/ppermute | solution.py:734
  31.9 3.0 %collective-permute-start.8 = (bf16[160,768]{1,0:T(8,128)(2,1)S(1)}, bf16[160,768]{1,0:T(8,128)(2,1)S(1)}, u32[]{:S(2)}, u32[]{:S(2)}) collective-permute-start(bf16[160,768]{1,0:T(8,128)(2,1)S(1)} %collective-permute-done.4.refs_4_), channel_id=1, source_target_pairs={{0,4},{4,0},{8,12},{12,8},{16,20},{20,16},{24,28},{28,24},{1,5},{5... | collective-permute-start | bytes 737288 | tf_op jit(solution)/shard_map/ppermute | solution.py:734
  31.9 2.9 %collective-permute-start.9 = (bf16[160,768]{1,0:T(8,128)(2,1)S(1)}, bf16[160,768]{1,0:T(8,128)(2,1)S(1)}, u32[]{:S(2)}, u32[]{:S(2)}) collective-permute-start(bf16[160,768]{1,0:T(8,128)(2,1)S(1)} %collective-permute-done.5.refs_5_), channel_id=1, source_target_pairs={{0,4},{4,0},{8,12},{12,8},{16,20},{20,16},{24,28},{28,24},{1,5},{5... | collective-permute-start | bytes 737288 | tf_op jit(solution)/shard_map/ppermute | solution.py:734
  32.7 18.1 %collective-permute-start.15 = (bf16[7,80,640]{2,1,0:T(8,128)(2,1)S(1)}, bf16[7,80,640]{2,1,0:T(8,128)(2,1)S(1)}, u32[]{:S(2)}, u32[]{:S(2)}) collective-permute-start(bf16[7,80,640]{2,1,0:T(8,128)(2,1)S(1)} %line_b.1.refs_10_.refs_11_), channel_id=1, source_target_pairs={{0,8},{4,12},{8,0},{12,4},{16,24},{20,28},{24,16},{28,20},{1,9},{5... | collective-permute-start | bytes 2150408 | tf_op jit(solution)/shard_map/ppermute | solution.py:734
  33.6 18.8 %collective-permute-start.16 = (bf16[7,80,640]{2,1,0:T(8,128)(2,1)S(1)}, bf16[7,80,640]{2,1,0:T(8,128)(2,1)S(1)}, u32[]{:S(2)}, u32[]{:S(2)}) collective-permute-start(bf16[7,80,640]{2,1,0:T(8,128)(2,1)S(1)} %line_b.1.refs_10_.refs_11_), channel_id=1, source_target_pairs={{0,16},{4,20},{8,24},{12,28},{16,0},{20,4},{24,8},{28,12},{1,17},{... | collective-permute-start | bytes 2150408 | tf_op jit(solution)/shard_map/ppermute | solution.py:734
  34.9 29.1 %copy-start.7 = (bf16[30]{0:T(256)(128)(2,1)S(1)}, bf16[30]{0:T(256)(128)(2,1)}, u32[]{:S(2)}) copy-start(bf16[30]{0:T(256)(128)(2,1)} %param.32) | copy-start | bytes 184
  34.9 30.8 %copy-start.4 = (s32[2,256]{1,0:T(2,128)S(1)}, s32[2,256]{1,0:T(2,128)}, u32[]{:S(2)}) copy-start(s32[2,256]{1,0:T(2,128)} %refs_4_.3) | copy-start | bytes 6148
  34.9 30.8 %copy-start.5 = (s32[2,153]{1,0:T(2,128)S(1)}, s32[2,153]{1,0:T(2,128)}, u32[]{:S(2)}) copy-start(s32[2,153]{1,0:T(2,128)} %refs_5_.3) | copy-start | bytes 3676
  34.9 30.7 %copy-start.6 = (s32[2,153]{1,0:T(2,128)S(1)}, s32[2,153]{1,0:T(2,128)}, u32[]{:S(2)}) copy-start(s32[2,153]{1,0:T(2,128)} %refs_6_.3) | copy-start | bytes 3676
  41.3 18.0 %collective-permute-start.13 = (bf16[2,256,640]{2,1,0:T(8,128)(2,1)S(1)}, bf16[2,256,640]{2,1,0:T(8,128)(2,1)S(1)}, u32[]{:S(2)}, u32[]{:S(2)}) collective-permute-start(bf16[2,256,640]{2,1,0:T(8,128)(2,1)S(1)} %bitcast.24), channel_id=1, source_target_pairs={{0,1},{1,2},{2,3},{4,5},{5,6},{6,7},{8,9},{9,10},{10,11},{12,13},{... | collective-permute-start | bytes 1966088 | tf_op jit(solution)/shard_map/ppermute | solution.py:756
  45.7 17.7 %collective-permute-start.14 = (bf16[2,256,640]{2,1,0:T(8,128)(2,1)S(1)}, bf16[2,256,640]{2,1,0:T(8,128)(2,1)S(1)}, u32[]{:S(2)}, u32[]{:S(2)}) collective-permute-start(bf16[2,256,640]{2,1,0:T(8,128)(2,1)S(1)} %bitcast.25), channel_id=1, source_target_pairs={{1,0},{2,1},{3,2},{5,4},{6,5},{7,6},{9,8},{10,9},{11,10},{13,12},{... | collective-permute-start | bytes 1966088 | tf_op jit(solution)/shard_map/ppermute | solution.py:760
  50.9 8.5 %collective-permute-start.17 = (bf16[3,80,640]{2,1,0:T(8,128)(2,1)S(1)}, bf16[3,80,640]{2,1,0:T(8,128)(2,1)S(1)}, u32[]{:S(2)}, u32[]{:S(2)}) collective-permute-start(bf16[3,80,640]{2,1,0:T(8,128)(2,1)S(1)} %slice.24), channel_id=1, source_target_pairs={{0,16},{4,20},{8,24},{12,28},{16,0},{20,4},{24,8},{28,12},{1,17},{... | collective-permute-start | bytes 921608 | tf_op jit(solution)/shard_map/ppermute | solution.py:734
  52.5 11.0 %collective-permute-start.18 = (bf16[4,80,640]{2,1,0:T(8,128)(2,1)S(1)}, bf16[4,80,640]{2,1,0:T(8,128)(2,1)S(1)}, u32[]{:S(2)}, u32[]{:S(2)}) collective-permute-start(bf16[4,80,640]{2,1,0:T(8,128)(2,1)S(1)} %slice.25), channel_id=1, source_target_pairs={{0,8},{4,12},{8,0},{12,4},{16,24},{20,28},{24,16},{28,20},{1,9},{5... | collective-permute-start | bytes 1228808 | tf_op jit(solution)/shard_map/ppermute | solution.py:734
  53.1 10.9 %collective-permute-start.19 = (bf16[7,80,640]{2,1,0:T(8,128)(2,1)S(1)}, bf16[7,80,640]{2,1,0:T(8,128)(2,1)S(1)}, u32[]{:S(2)}, u32[]{:S(2)}) collective-permute-start(bf16[7,80,640]{2,1,0:T(8,128)(2,1)S(1)} %line_b.1.refs_10_.refs_11_), channel_id=1, source_target_pairs={{0,4},{4,0},{8,12},{12,8},{16,20},{20,16},{24,28},{28,24},{1,5},{5... | collective-permute-start | bytes 2150408 | tf_op jit(solution)/shard_map/ppermute | solution.py:734
  59.3 4.7 %collective-permute-start.20 = (bf16[7,80,640]{2,1,0:T(8,128)(2,1)S(1)}, bf16[7,80,640]{2,1,0:T(8,128)(2,1)S(1)}, u32[]{:S(2)}, u32[]{:S(2)}) collective-permute-start(bf16[7,80,640]{2,1,0:T(8,128)(2,1)S(1)} %collective-permute-done.15.refs_12_), channel_id=1, source_target_pairs={{0,4},{4,0},{8,12},{12,8},{16,20},{20,16},{24,28},{28,24},{1,5},{5... | collective-permute-start | bytes 2150408 | tf_op jit(solution)/shard_map/ppermute | solution.py:734
  59.3 4.7 %collective-permute-start.21 = (bf16[7,80,640]{2,1,0:T(8,128)(2,1)S(1)}, bf16[7,80,640]{2,1,0:T(8,128)(2,1)S(1)}, u32[]{:S(2)}, u32[]{:S(2)}) collective-permute-start(bf16[7,80,640]{2,1,0:T(8,128)(2,1)S(1)} %collective-permute-done.16.refs_13_), channel_id=1, source_target_pairs={{0,4},{4,0},{8,12},{12,8},{16,20},{20,16},{24,28},{28,24},{1,5},{5... | collective-permute-start | bytes 2150408 | tf_op jit(solution)/shard_map/ppermute | solution.py:734
  63.5 2.2 %collective-permute-start.23 = (bf16[4,80,640]{2,1,0:T(8,128)(2,1)S(1)}, bf16[4,80,640]{2,1,0:T(8,128)(2,1)S(1)}, u32[]{:S(2)}, u32[]{:S(2)}) collective-permute-start(bf16[4,80,640]{2,1,0:T(8,128)(2,1)S(1)} %collective-permute-done.18.refs_15_), channel_id=1, source_target_pairs={{0,4},{4,0},{8,12},{12,8},{16,20},{20,16},{24,28},{28,24},{1,5},{5... | collective-permute-start | bytes 1228808 | tf_op jit(solution)/shard_map/ppermute | solution.py:734
  63.5 2.2 %collective-permute-start.22 = (bf16[3,80,640]{2,1,0:T(8,128)(2,1)S(1)}, bf16[3,80,640]{2,1,0:T(8,128)(2,1)S(1)}, u32[]{:S(2)}, u32[]{:S(2)}) collective-permute-start(bf16[3,80,640]{2,1,0:T(8,128)(2,1)S(1)} %collective-permute-done.17.refs_14_), channel_id=1, source_target_pairs={{0,4},{4,0},{8,12},{12,8},{16,20},{20,16},{24,28},{28,24},{1,5},{5... | collective-permute-start | bytes 921608 | tf_op jit(solution)/shard_map/ppermute | solution.py:734
  76.9 6.3 %collective-permute-start.26 = (bf16[528,1408]{1,0:T(8,128)(2,1)S(1)}, bf16[528,1408]{1,0:T(8,128)(2,1)S(1)}, u32[]{:S(2)}, u32[]{:S(2)}) collective-permute-start(bf16[528,1408]{1,0:T(8,128)(2,1)S(1)} %get-tuple-element.114.refs_0_.refs_4_), channel_id=1, source_target_pairs={{0,4},{4,0},{8,12},{12,8},{16,20},{20,16},{24,28},{28,24},{1,5},{5... | collective-permute-start | bytes 4460552 | tf_op jit(solution)/shard_map/ppermute | solution.py:734
  77.1 4.6 %collective-permute-start.28 = (bf16[2,256,640]{2,1,0:T(8,128)(2,1)S(1)}, bf16[2,256,640]{2,1,0:T(8,128)(2,1)S(1)}, u32[]{:S(2)}, u32[]{:S(2)}) collective-permute-start(bf16[2,256,640]{2,1,0:T(8,128)(2,1)S(1)} %bitcast.27), channel_id=1, source_target_pairs={{0,4},{4,0},{8,12},{12,8},{16,20},{20,16},{24,28},{28,24},{1,5},{5... | collective-permute-start | bytes 1966088 | tf_op jit(solution)/shard_map/ppermute | solution.py:734
  77.4 5.8 %collective-permute-start.27 = (bf16[2,256,640]{2,1,0:T(8,128)(2,1)S(1)}, bf16[2,256,640]{2,1,0:T(8,128)(2,1)S(1)}, u32[]{:S(2)}, u32[]{:S(2)}) collective-permute-start(bf16[2,256,640]{2,1,0:T(8,128)(2,1)S(1)} %collective-permute-done.13.refs_8_.refs_3_), channel_id=1, source_target_pairs={{0,4},{4,0},{8,12},{12,8},{16,20},{20,16},{24,28},{28,24},{1,5},{5... | collective-permute-start | bytes 1966088 | tf_op jit(solution)/shard_map/ppermute | solution.py:734
  77.6 5.6 %collective-permute-start.29 = (bf16[2,256,640]{2,1,0:T(8,128)(2,1)S(1)}, bf16[2,256,640]{2,1,0:T(8,128)(2,1)S(1)}, u32[]{:S(2)}, u32[]{:S(2)}) collective-permute-start(bf16[2,256,640]{2,1,0:T(8,128)(2,1)S(1)} %collective-permute-done.14.refs_10_.refs_5_), channel_id=1, source_target_pairs={{0,4},{4,0},{8,12},{12,8},{16,20},{20,16},{24,28},{28,24},{1,5},{5... | collective-permute-start | bytes 1966088 | tf_op jit(solution)/shard_map/ppermute | solution.py:734
  78.0 17.9 %collective-permute-start.24 = (bf16[2,256,640]{2,1,0:T(8,128)(2,1)S(1)}, bf16[2,256,640]{2,1,0:T(8,128)(2,1)S(1)}, u32[]{:S(2)}, u32[]{:S(2)}) collective-permute-start(bf16[2,256,640]{2,1,0:T(8,128)(2,1)S(1)} %bitcast.19), channel_id=1, source_target_pairs={{0,1},{1,2},{2,3},{4,5},{5,6},{6,7},{8,9},{9,10},{10,11},{12,13},{... | collective-permute-start | bytes 1966088 | tf_op jit(solution)/shard_map/ppermute | solution.py:756
  81.7 18.4 %collective-permute-start.25 = (bf16[2,256,640]{2,1,0:T(8,128)(2,1)S(1)}, bf16[2,256,640]{2,1,0:T(8,128)(2,1)S(1)}, u32[]{:S(2)}, u32[]{:S(2)}) collective-permute-start(bf16[2,256,640]{2,1,0:T(8,128)(2,1)S(1)} %bitcast.20), channel_id=1, source_target_pairs={{1,0},{2,1},{3,2},{5,4},{6,5},{7,6},{9,8},{10,9},{11,10},{13,12},{... | collective-permute-start | bytes 1966088 | tf_op jit(solution)/shard_map/ppermute | solution.py:760
  86.4 27.5 %collective-permute-start.30 = (bf16[432,640]{1,0:T(8,128)(2,1)S(1)}, bf16[432,640]{1,0:T(8,128)(2,1)S(1)}, u32[]{:S(2)}, u32[]{:S(2)}) collective-permute-start(bf16[432,640]{1,0:T(8,128)(2,1)S(1)} %get-tuple-element.119), channel_id=1, source_target_pairs={{0,8},{4,12},{8,0},{12,4},{16,24},{20,28},{24,16},{28,20},{1,9},{5... | collective-permute-start | bytes 1658888 | tf_op jit(solution)/shard_map/ppermute | solution.py:734
  87.7 26.2 %collective-permute-start.31 = (bf16[432,640]{1,0:T(8,128)(2,1)S(1)}, bf16[432,640]{1,0:T(8,128)(2,1)S(1)}, u32[]{:S(2)}, u32[]{:S(2)}) collective-permute-start(bf16[432,640]{1,0:T(8,128)(2,1)S(1)} %get-tuple-element.120), channel_id=1, source_target_pairs={{0,16},{4,20},{8,24},{12,28},{16,0},{20,4},{24,8},{28,12},{1,17},{... | collective-permute-start | bytes 1658888 | tf_op jit(solution)/shard_map/ppermute | solution.py:734
  88.2 25.7 %collective-permute-start.32 = (bf16[432,640]{1,0:T(8,128)(2,1)S(1)}, bf16[432,640]{1,0:T(8,128)(2,1)S(1)}, u32[]{:S(2)}, u32[]{:S(2)}) collective-permute-start(bf16[432,640]{1,0:T(8,128)(2,1)S(1)} %get-tuple-element.121), channel_id=1, source_target_pairs={{0,24},{4,28},{8,16},{12,20},{16,8},{20,12},{24,0},{28,4},{1,25},{... | collective-permute-start | bytes 1658888 | tf_op jit(solution)/shard_map/ppermute | solution.py:734
  110.8 1.9 %collective-permute-start.33 = (bf16[2,160,768]{2,1,0:T(8,128)(2,1)S(1)}, bf16[2,160,768]{2,1,0:T(8,128)(2,1)S(1)}, u32[]{:S(2)}, u32[]{:S(2)}) collective-permute-start(bf16[2,160,768]{2,1,0:T(8,128)(2,1)S(1)} %get-tuple-element.123), channel_id=1, source_target_pairs={{0,4},{4,0},{8,12},{12,8},{16,20},{20,16},{24,28},{28,24},{1,5},{5... | collective-permute-start | bytes 1474568 | tf_op jit(solution)/shard_map/ppermute | solution.py:734
  110.9 2.6 %collective-permute-start.34 = (bf16[2,160,768]{2,1,0:T(8,128)(2,1)S(1)}, bf16[2,160,768]{2,1,0:T(8,128)(2,1)S(1)}, u32[]{:S(2)}, u32[]{:S(2)}) collective-permute-start(bf16[2,160,768]{2,1,0:T(8,128)(2,1)S(1)} %get-tuple-element.124), channel_id=1, source_target_pairs={{0,4},{4,0},{8,12},{12,8},{16,20},{20,16},{24,28},{28,24},{1,5},{5... | collective-permute-start | bytes 1474568 | tf_op jit(solution)/shard_map/ppermute | solution.py:734
  114.4 8.9 %collective-permute-start.35 = (bf16[160,768]{1,0:T(8,128)(2,1)S(1)}, bf16[160,768]{1,0:T(8,128)(2,1)S(1)}, u32[]{:S(2)}, u32[]{:S(2)}) collective-permute-start(bf16[160,768]{1,0:T(8,128)(2,1)S(1)} %get-tuple-element.132), channel_id=1, source_target_pairs={{0,8},{4,12},{8,0},{12,4},{16,24},{20,28},{24,16},{28,20},{1,9},{5... | collective-permute-start | bytes 737288 | tf_op jit(solution)/shard_map/ppermute | solution.py:734
  115.7 13.3 %collective-permute-start.36 = (bf16[160,768]{1,0:T(8,128)(2,1)S(1)}, bf16[160,768]{1,0:T(8,128)(2,1)S(1)}, u32[]{:S(2)}, u32[]{:S(2)}) collective-permute-start(bf16[160,768]{1,0:T(8,128)(2,1)S(1)} %get-tuple-element.133), channel_id=1, source_target_pairs={{0,16},{4,20},{8,24},{12,28},{16,0},{20,4},{24,8},{28,12},{1,17},{... | collective-permute-start | bytes 737288 | tf_op jit(solution)/shard_map/ppermute | solution.py:734
  116.2 12.8 %collective-permute-start.37 = (bf16[160,768]{1,0:T(8,128)(2,1)S(1)}, bf16[160,768]{1,0:T(8,128)(2,1)S(1)}, u32[]{:S(2)}, u32[]{:S(2)}) collective-permute-start(bf16[160,768]{1,0:T(8,128)(2,1)S(1)} %get-tuple-element.134), channel_id=1, source_target_pairs={{0,24},{4,28},{8,16},{12,20},{16,8},{20,12},{24,0},{28,4},{1,25},{... | collective-permute-start | bytes 737288 | tf_op jit(solution)/shard_map/ppermute | solution.py:734
  117.9 13.0 %collective-permute-start.41 = (bf16[128,640]{1,0:T(8,128)(2,1)S(1)}, bf16[128,640]{1,0:T(8,128)(2,1)S(1)}, u32[]{:S(2)}, u32[]{:S(2)}) collective-permute-start(bf16[128,640]{1,0:T(8,128)(2,1)S(1)} %get-tuple-element.148), channel_id=1, source_target_pairs={{0,1},{1,2},{2,3},{3,0},{4,5},{5,6},{6,7},{7,4},{8,9},{9,10},{10,1... | collective-permute-start | bytes 491528 | tf_op jit(solution)/shard_map/ppermute | solution.py:739
  119.9 13.4 %collective-permute-start.42 = (bf16[128,640]{1,0:T(8,128)(2,1)S(1)}, bf16[128,640]{1,0:T(8,128)(2,1)S(1)}, u32[]{:S(2)}, u32[]{:S(2)}) collective-permute-start(bf16[128,640]{1,0:T(8,128)(2,1)S(1)} %get-tuple-element.149), channel_id=1, source_target_pairs={{0,2},{1,3},{2,0},{3,1},{4,6},{5,7},{6,4},{7,5},{8,10},{9,11},{10,... | collective-permute-start | bytes 491528 | tf_op jit(solution)/shard_map/ppermute | solution.py:739
  123.3 10.2 %collective-permute-start.43 = (bf16[128,640]{1,0:T(8,128)(2,1)S(1)}, bf16[128,640]{1,0:T(8,128)(2,1)S(1)}, u32[]{:S(2)}, u32[]{:S(2)}) collective-permute-start(bf16[128,640]{1,0:T(8,128)(2,1)S(1)} %get-tuple-element.150), channel_id=1, source_target_pairs={{0,3},{1,0},{2,1},{3,2},{4,7},{5,4},{6,5},{7,6},{8,11},{9,8},{10,9... | collective-permute-start | bytes 491528 | tf_op jit(solution)/shard_map/ppermute | solution.py:739
  129.1 7.3 %collective-permute-start.38 = (bf16[40,768]{1,0:T(8,128)(2,1)S(1)}, bf16[40,768]{1,0:T(8,128)(2,1)S(1)}, u32[]{:S(2)}, u32[]{:S(2)}) collective-permute-start(bf16[40,768]{1,0:T(8,128)(2,1)S(1)} %get-tuple-element.137), channel_id=1, source_target_pairs={{0,1},{1,2},{2,3},{3,0},{4,5},{5,6},{6,7},{7,4},{8,9},{9,10},{10,1... | collective-permute-start | bytes 184328 | tf_op jit(solution)/shard_map/ppermute | solution.py:739
  129.7 10.0 %collective-permute-start.39 = (bf16[40,768]{1,0:T(8,128)(2,1)S(1)}, bf16[40,768]{1,0:T(8,128)(2,1)S(1)}, u32[]{:S(2)}, u32[]{:S(2)}) collective-permute-start(bf16[40,768]{1,0:T(8,128)(2,1)S(1)} %get-tuple-element.138), channel_id=1, source_target_pairs={{0,2},{1,3},{2,0},{3,1},{4,6},{5,7},{6,4},{7,5},{8,10},{9,11},{10,... | collective-permute-start | bytes 184328 | tf_op jit(solution)/shard_map/ppermute | solution.py:739
  130.9 8.9 %collective-permute-start.40 = (bf16[40,768]{1,0:T(8,128)(2,1)S(1)}, bf16[40,768]{1,0:T(8,128)(2,1)S(1)}, u32[]{:S(2)}, u32[]{:S(2)}) collective-permute-start(bf16[40,768]{1,0:T(8,128)(2,1)S(1)} %get-tuple-element.139), channel_id=1, source_target_pairs={{0,3},{1,0},{2,1},{3,2},{4,7},{5,4},{6,5},{7,6},{8,11},{9,8},{10,9... | collective-permute-start | bytes 184328 | tf_op jit(solution)/shard_map/ppermute | solution.py:739
  (4 other events, 34.3 us)

commit v5 on v4

--- a/solution.py
+++ b/solution.py
@@ -25,14 +25,13 @@
 
 
 def gauss(u):
-    z = jnp.abs(u) * HALF_ROOT
-    t = pl.reciprocal(1.0 + 0.3275911 * z, approx=False)
-    e = jnp.exp(-0.5 * u * u)
+    t = pl.reciprocal(1.0 + (0.3275911 * HALF_ROOT) * jnp.abs(u), approx=False)
+    e = jnp.exp2(u * u * -0.7213475204444817)
     poly = t * (
-        0.254829592
-        + t * (-0.284496736 + t * (1.421413741 + t * (-1.453152027 + t * 1.061405429)))
-    )
-    tail = 0.5 * poly * e
+        0.127414796
+        + t * (-0.142248368 + t * (0.7107068705 + t * (-0.7265760135 + t * 0.5307027145)))
+    )
+    tail = poly * e
     return jnp.where(u < 0, tail, 1.0 - tail), e * INV_ROOT_TWO_PI
 
 
@@ -253,8 +252,11 @@
         act[c, :] = (u * cdf).astype(BF)
         gp1[c, :] = cdf + u * pdf
 
-    each_chunk(rows, 16, body)
-    proj[...] = dot(act[...], w_in[...])
+    half = rows // 2
+    for at in range(0, rows, half):
+        for j in range(at, at + half, 16):
+            body(pl.ds(j, 16))
+        proj[at : at + half, :] = dot(act[at : at + half, :], w_in[...])
 
     def later(c):
         n, r = standardize(proj[c, :] + bias)
@@ -265,7 +267,8 @@
         n2[c, :] = n
         r2[c, :] = jnp.broadcast_to(r, (r.shape[0], LANES))
 
-    each_chunk(rows, 32, later)
+    for j in range(0, rows, 32):
+        later(pl.ds(j, 32))
 
 
 def middle_kernel(
@@ -324,7 +327,7 @@
     head_grad[...] = jnp.zeros_like(head_grad)
     seat = lax.axis_index("seq")
 
-    @pl.loop(0, seqs)
+    @pl.loop(0, seqs, unroll=True)
     def _(s):
         whole = pl.ds(pl.multiple_of(s * length, length), length)
         total = dot(ext[s, pl.ds(hops * length - REACH, length), :], taps[0])

time: 142 us -> 140 us (0.986)
  Pallas kernels: 41.3 us -> 37.3 us
    pallas_call x15, Pallas kernels: 41.3 us -> 37.3 us  [call(): pl.pallas_call(body, out_shape=list(outs), in_specs=[pl.BlockSpec(memory_...]
    ppermute x28, waiting for transfers between devices: 22.4 us -> 25.3 us  [swap(): return lax.ppermute(value, 'dp', [(i, i ^ mask) for i in range(count)])]
    ppermute x2, waiting for transfers between devices: 7.78 us -> 6.06 us  [halo(): lax.ppermute(series, 'seq', [(i + h, i) for i in range(size - h)])]
  transfers between devices with their start and end apart: 44 -> 44, of which waited for: 16 -> 17; matrix products, arithmetic and copies ran while one was open for 1% -> 1% of each run, Pallas kernels for 19% -> 18%
where the time goes in v5:
time: 140 us; the launch traced here: 139 us
  starting transfers between devices  52.9 us (38%)
  waiting for transfers between devices  44.5 us (32%)
  Pallas kernels  37.3 us (27%)
  between operations  2.76 us (2%)
  local copies, waits for them, and re-layouts  1.45 us (1%)
    pallas_call x15, Pallas kernels, call(): pl.pallas_call(body, out_shape=list(outs), in_specs=[pl.BlockSpec(memory_...  37.3 us
    ppermute x28, waiting for transfers between devices, swap(): return lax.ppermute(value, 'dp', [(i, i ^ mask) for i in range(count)])  25.3 us
    ppermute x12, starting transfers between devices, shifted(): lax.ppermute(value, 'seq', [(i, (i + k) % size) for i in range(size)])  21.3 us
    ppermute x28, starting transfers between devices, swap(): return lax.ppermute(value, 'dp', [(i, i ^ mask) for i in range(count)])  20 us
    ppermute x2, starting transfers between devices, halo(): lax.ppermute(series, 'seq', [(i, i + h) for i in range(size - h)])  8.72 us
    ppermute x12, waiting for transfers between devices, shifted(): lax.ppermute(value, 'seq', [(i, (i + k) % size) for i in range(size)])  7.12 us
    ppermute x2, waiting for transfers between devices, halo(): lax.ppermute(series, 'seq', [(i + h, i) for i in range(size - h)])  6.06 us
    ppermute x2, waiting for transfers between devices, halo(): lax.ppermute(series, 'seq', [(i, i + h) for i in range(size - h)])  5.98 us
  transfers between devices with their start and end apart: 44, of which 17 were waited for; matrix products, arithmetic and copies ran while one was open for 1% of the time, Pallas kernels for 18%

profile of v5, /device:TPU:0, one launch (start us, length us, event | category | flops | bytes accessed | tf_op | source)
XLA Modules:
  0.0 139.4 jit_solution(6880046960178935148)
XLA Ops:
  0.7 1.6 %pack_a.1.refs_2_.refs_0_ = bf16[40,768]{1,0:T(8,128)(2,1)} custom-call(bf16[40,640]{1,0:T(8,128)(2,1)} %refs_0_.1, bf16[30,40]{1,0:T(8,128)(2,1)} %bitcast.30, bf16[40]{0:T(256)(128)(2,1)} %refs_2_.1, bf16[40]{0:T(256)(128)(2,1)} %refs_3_.1, bf16[40]{0:T(256)(128)(2,1)} %refs_4_.2, bf16[20]{0:T(256)(128)(2,1)} %refs_5_.2, bf16[20]{0:T(256)(128)(2,1)} %refs_6_.2, ...), custom_call_target="tpu_custom_call" | custom-call | flops 1000000000 | bytes 1000 | tf_op jit(solution)/shard_map/pack_a/pallas_call | solution.py:136
  2.3 3.1 %collective-permute-start = (bf16[40,768]{1,0:T(8,128)(2,1)}, bf16[40,768]{1,0:T(8,128)(2,1)S(1)}, u32[]{:S(2)}, u32[]{:S(2)}) collective-permute-start(bf16[40,768]{1,0:T(8,128)(2,1)} %pack_a.1.refs_2_.refs_0_), channel_id=1, source_target_pairs={{0,1},{1,2},{2,3},{3,0},{4,5},{5,6},{6,7},{7,4},{8,9},{9,10},{10,1... | collective-permute-start | bytes 184328 | tf_op jit(solution)/shard_map/ppermute | solution.py:742
  5.4 2.6 %collective-permute-start.1 = (bf16[40,768]{1,0:T(8,128)(2,1)}, bf16[40,768]{1,0:T(8,128)(2,1)S(1)}, u32[]{:S(2)}, u32[]{:S(2)}) collective-permute-start(bf16[40,768]{1,0:T(8,128)(2,1)} %pack_a.1.refs_2_.refs_0_), channel_id=1, source_target_pairs={{0,2},{1,3},{2,0},{3,1},{4,6},{5,7},{6,4},{7,5},{8,10},{9,11},{10,... | collective-permute-start | bytes 184328 | tf_op jit(solution)/shard_map/ppermute | solution.py:742
  8.0 1.3 collective-permute-start.2
  9.3 0.7 collective-permute-done.refs_1_
  10.1 2.4 %collective-permute-done.1.refs_2_ = bf16[40,768]{1,0:T(8,128)(2,1)S(1)} collective-permute-done((bf16[40,768]{1,0:T(8,128)(2,1)}, bf16[40,768]{1,0:T(8,128)(2,1)S(1)}, u32[]{:S(2)}, u32[]{:S(2)}) %collective-permute-start.1) | collective-permute-done | bytes 61472 | tf_op jit(solution)/shard_map/ppermute | solution.py:742
  12.8 0.8 copy-done.3
  13.7 1.6 %collective-permute-start.3 = (bf16[160,768]{1,0:T(8,128)(2,1)S(1)}, bf16[160,768]{1,0:T(8,128)(2,1)S(1)}, u32[]{:S(2)}, u32[]{:S(2)}) collective-permute-start(bf16[160,768]{1,0:T(8,128)(2,1)S(1)} %line_a.1.refs_2_), channel_id=1, source_target_pairs={{0,8},{4,12},{8,0},{12,4},{16,24},{20,28},{24,16},{28,20},{1,9},{5... | collective-permute-start | bytes 737288 | tf_op jit(solution)/shard_map/ppermute | solution.py:737
  15.6 1.4 %collective-permute-start.10 = (bf16[140,640]{1,0:T(8,128)(2,1)S(1)}, bf16[140,640]{1,0:T(8,128)(2,1)S(1)}, u32[]{:S(2)}, u32[]{:S(2)}) collective-permute-start(bf16[140,640]{1,0:T(8,128)(2,1)S(1)} %pack_b.1.refs_1_.refs_0_), channel_id=1, source_target_pairs={{0,1},{1,2},{2,3},{3,0},{4,5},{5,6},{6,7},{7,4},{8,9},{9,10},{10,1... | collective-permute-start | bytes 537608 | tf_op jit(solution)/shard_map/ppermute | solution.py:742
  17.0 2.1 %collective-permute-start.11 = (bf16[140,640]{1,0:T(8,128)(2,1)S(1)}, bf16[140,640]{1,0:T(8,128)(2,1)S(1)}, u32[]{:S(2)}, u32[]{:S(2)}) collective-permute-start(bf16[140,640]{1,0:T(8,128)(2,1)S(1)} %pack_b.1.refs_1_.refs_0_), channel_id=1, source_target_pairs={{0,2},{1,3},{2,0},{3,1},{4,6},{5,7},{6,4},{7,5},{8,10},{9,11},{10,... | collective-permute-start | bytes 537608 | tf_op jit(solution)/shard_map/ppermute | solution.py:742
  19.5 1.5 %collective-permute-start.4 = (bf16[160,768]{1,0:T(8,128)(2,1)S(1)}, bf16[160,768]{1,0:T(8,128)(2,1)S(1)}, u32[]{:S(2)}, u32[]{:S(2)}) collective-permute-start(bf16[160,768]{1,0:T(8,128)(2,1)S(1)} %line_a.1.refs_2_), channel_id=1, source_target_pairs={{0,16},{4,20},{8,24},{12,28},{16,0},{20,4},{24,8},{28,12},{1,17},{... | collective-permute-start | bytes 737288 | tf_op jit(solution)/shard_map/ppermute | solution.py:737
  21.1 1.8 %collective-permute-start.5 = (bf16[160,768]{1,0:T(8,128)(2,1)S(1)}, bf16[160,768]{1,0:T(8,128)(2,1)S(1)}, u32[]{:S(2)}, u32[]{:S(2)}) collective-permute-start(bf16[160,768]{1,0:T(8,128)(2,1)S(1)} %line_a.1.refs_2_), channel_id=1, source_target_pairs={{0,24},{4,28},{8,16},{12,20},{16,8},{20,12},{24,0},{28,4},{1,25},{... | collective-permute-start | bytes 737288 | tf_op jit(solution)/shard_map/ppermute | solution.py:737
  22.8 1.6 %first.1 = (f32[512,1280]{1,0:T(8,128)S(1)}, f32[512,128]{1,0:T(8,128)S(1)}, bf16[1280,640]{1,0:T(8,128)(2,1)S(1)}) custom-call(bf16[512,1280]{1,0:T(8,128)(2,1)S(1)} %bitcast.22, bf16[140,640]{1,0:T(8,128)(2,1)S(1)} %pack_b.1.refs_1_.refs_0_), custom_call_target="tpu_custom_call" | custom-call | flops 6000000000 | bytes 1000 | tf_op jit(solution)/shard_map/first/pallas_call | solution.py:136
  24.4 7.0 %collective-permute-done.4.refs_4_ = bf16[160,768]{1,0:T(8,128)(2,1)S(1)} collective-permute-done((bf16[160,768]{1,0:T(8,128)(2,1)S(1)}, bf16[160,768]{1,0:T(8,128)(2,1)S(1)}, u32[]{:S(2)}, u32[]{:S(2)}) %collective-permute-start.4) | collective-permute-done | bytes 245792 | tf_op jit(solution)/shard_map/ppermute | solution.py:737
  32.7 0.9 collective-permute-start.15
  33.6 1.2 collective-permute-start.16
  34.9 4.7 %second.1 = (bf16[1280,640]{1,0:T(8,128)(2,1)S(1)}, bf16[1280,128]{1,0:T(8,128)(2,1)S(1)}, f32[8,1280]{1,0:T(8,128)S(1)}, f32[8,640]{1,0:T(8,128)S(1)}, bf16[512...) custom-call(f32[512,1280]{1,0:T(8,128)S(1)} %get-tuple-element.89.re, ...), custom_call_target="tpu_custom_call" | custom-call | flops 8999999488 | bytes 1000 | tf_op jit(solution)/shard_map/second/pallas_call | solution.py:136
  39.6 4.4 %collective-permute-start.13 = (bf16[2,256,640]{2,1,0:T(8,128)(2,1)S(1)}, bf16[2,256,640]{2,1,0:T(8,128)(2,1)S(1)}, u32[]{:S(2)}, u32[]{:S(2)}) collective-permute-start(bf16[2,256,640]{2,1,0:T(8,128)(2,1)S(1)} %bitcast.24), channel_id=1, source_target_pairs={{0,1},{1,2},{2,3},{4,5},{5,6},{6,7},{8,9},{9,10},{10,11},{12,13},{... | collective-permute-start | bytes 1966088 | tf_op jit(solution)/shard_map/ppermute | solution.py:759
  44.0 1.5 %collective-permute-start.14 = (bf16[2,256,640]{2,1,0:T(8,128)(2,1)S(1)}, bf16[2,256,640]{2,1,0:T(8,128)(2,1)S(1)}, u32[]{:S(2)}, u32[]{:S(2)}) collective-permute-start(bf16[2,256,640]{2,1,0:T(8,128)(2,1)S(1)} %bitcast.25), channel_id=1, source_target_pairs={{1,0},{2,1},{3,2},{5,4},{6,5},{7,6},{9,8},{10,9},{11,10},{13,12},{... | collective-permute-start | bytes 1966088 | tf_op jit(solution)/shard_map/ppermute | solution.py:763
  45.5 5.3 %collective-permute-done.15.refs_12_ = bf16[7,80,640]{2,1,0:T(8,128)(2,1)S(1)} collective-permute-done((bf16[7,80,640]{2,1,0:T(8,128)(2,1)S(1)}, bf16[7,80,640]{2,1,0:T(8,128)(2,1)S(1)}, u32[]{:S(2)}, u32[]{:S(2)}) %collective-permute-start.15) | collective-permute-done | bytes 716832 | tf_op jit(solution)/shard_map/ppermute | solution.py:737
  50.9 1.6 %collective-permute-start.17 = (bf16[3,80,640]{2,1,0:T(8,128)(2,1)S(1)}, bf16[3,80,640]{2,1,0:T(8,128)(2,1)S(1)}, u32[]{:S(2)}, u32[]{:S(2)}) collective-permute-start(bf16[3,80,640]{2,1,0:T(8,128)(2,1)S(1)} %slice.24), channel_id=1, source_target_pairs={{0,16},{4,20},{8,24},{12,28},{16,0},{20,4},{24,8},{28,12},{1,17},{... | collective-permute-start | bytes 921608 | tf_op jit(solution)/shard_map/ppermute | solution.py:737
  53.1 6.2 %collective-permute-done.17.refs_14_ = bf16[3,80,640]{2,1,0:T(8,128)(2,1)S(1)} collective-permute-done((bf16[3,80,640]{2,1,0:T(8,128)(2,1)S(1)}, bf16[3,80,640]{2,1,0:T(8,128)(2,1)S(1)}, u32[]{:S(2)}, u32[]{:S(2)}) %collective-permute-start.17) | collective-permute-done | bytes 307232 | tf_op jit(solution)/shard_map/ppermute | solution.py:737
  59.8 1.9 %collective-permute-done.14.refs_10_.refs_5_ = bf16[2,256,640]{2,1,0:T(8,128)(2,1)S(1)} collective-permute-done((bf16[2,256,640]{2,1,0:T(8,128)(2,1)S(1)}, bf16[2,256,640]{2,1,0:T(8,128)(2,1)S(1)}, u32[]{:S(2)}, u32[]{:S(2)}) %collective-permute-start.14) | collective-permute-done | bytes 655392 | tf_op jit(solution)/shard_map/ppermute | solution.py:763
  61.7 1.1 collective-permute-done.18.refs_15_
  63.4 1.6 %collective-permute-done.22.refs_19_ = bf16[3,80,640]{2,1,0:T(8,128)(2,1)S(1)} collective-permute-done((bf16[3,80,640]{2,1,0:T(8,128)(2,1)S(1)}, bf16[3,80,640]{2,1,0:T(8,128)(2,1)S(1)}, u32[]{:S(2)}, u32[]{:S(2)}) %collective-permute-start.22) | collective-permute-done | bytes 307232 | tf_op jit(solution)/shard_map/ppermute | solution.py:737
  65.1 9.0 %middle.1 = (bf16[7,640,640]{2,1,0:T(8,128)(2,1)S(1)}, bf16[512,1280]{1,0:T(8,128)(2,1)}, bf16[528,1408]{1,0:T(8,128)(2,1)S(1)}, f32[1280,128]{1,0:T(8,128)S(1)}...) custom-call(f32[8,1280]{1,0:T(8,128)S(1)} %get-tuple-element.96.refs_0_.refs_8_.refs_3_, ...), custom_call_target="tpu_custom_call" | custom-call | flops 16999999488 | bytes 1000 | tf_op jit(solution)/shard_map/middle/pallas_call | solution.py:136
  75.2 4.3 %collective-permute-start.24 = (bf16[2,256,640]{2,1,0:T(8,128)(2,1)S(1)}, bf16[2,256,640]{2,1,0:T(8,128)(2,1)S(1)}, u32[]{:S(2)}, u32[]{:S(2)}) collective-permute-start(bf16[2,256,640]{2,1,0:T(8,128)(2,1)S(1)} %bitcast.19), channel_id=1, source_target_pairs={{0,1},{1,2},{2,3},{4,5},{5,6},{6,7},{8,9},{9,10},{10,11},{12,13},{... | collective-permute-start | bytes 1966088 | tf_op jit(solution)/shard_map/ppermute | solution.py:759
  79.5 1.5 %collective-permute-start.25 = (bf16[2,256,640]{2,1,0:T(8,128)(2,1)S(1)}, bf16[2,256,640]{2,1,0:T(8,128)(2,1)S(1)}, u32[]{:S(2)}, u32[]{:S(2)}) collective-permute-start(bf16[2,256,640]{2,1,0:T(8,128)(2,1)S(1)} %bitcast.20), channel_id=1, source_target_pairs={{1,0},{2,1},{3,2},{5,4},{6,5},{7,6},{9,8},{10,9},{11,10},{13,12},{... | collective-permute-start | bytes 1966088 | tf_op jit(solution)/shard_map/ppermute | solution.py:763
  81.0 3.1 %conv_grad.1 = (f32[5,80,640]{2,1,0:T(8,128)S(1)}, f32[8,128]{1,0:T(8,128)S(1)}, f32[80,128]{1,0:T(8,128)S(1)}, bf16[432,640]{1,0:T(8,128)(2,1)S(1)}, bf16[432,6...) custom-call(bf16[528,1408]{1,0:T(8,128)(2,1)S(1)} %get-tuple-element.114.refs_0_.refs_4_, ...), custom_call_target="tpu_custom_call" | custom-call | flops 7000000000 | bytes 1000 | tf_op jit(solution)/shard_map/conv_grad/pallas_call | solution.py:136
  84.8 1.2 collective-permute-start.31
  86.0 1.8 %collective-permute-start.32 = (bf16[432,640]{1,0:T(8,128)(2,1)S(1)}, bf16[432,640]{1,0:T(8,128)(2,1)S(1)}, u32[]{:S(2)}, u32[]{:S(2)}) collective-permute-start(bf16[432,640]{1,0:T(8,128)(2,1)S(1)} %get-tuple-element.121), channel_id=1, source_target_pairs={{0,24},{4,28},{8,16},{12,20},{16,8},{20,12},{24,0},{28,4},{1,25},{... | collective-permute-start | bytes 1658888 | tf_op jit(solution)/shard_map/ppermute | solution.py:737
  87.7 6.0 %collective-permute-done.24.refs_14_ = bf16[2,256,640]{2,1,0:T(8,128)(2,1)S(1)} collective-permute-done((bf16[2,256,640]{2,1,0:T(8,128)(2,1)S(1)}, bf16[2,256,640]{2,1,0:T(8,128)(2,1)S(1)}, u32[]{:S(2)}, u32[]{:S(2)}) %collective-permute-start.24) | collective-permute-done | bytes 655392 | tf_op jit(solution)/shard_map/ppermute | solution.py:759
  93.7 4.2 %collective-permute-done.25.refs_16_ = bf16[2,256,640]{2,1,0:T(8,128)(2,1)S(1)} collective-permute-done((bf16[2,256,640]{2,1,0:T(8,128)(2,1)S(1)}, bf16[2,256,640]{2,1,0:T(8,128)(2,1)S(1)}, u32[]{:S(2)}, u32[]{:S(2)}) %collective-permute-start.25) | collective-permute-done | bytes 655392 | tf_op jit(solution)/shard_map/ppermute | solution.py:763
  97.9 10.8 %back.1 = (f32[4,160,768]{2,1,0:T(8,128)S(1)}, bf16[2,160,768]{2,1,0:T(8,128)(2,1)S(1)}, bf16[2,160,768]{2,1,0:T(8,128)(2,1)S(1)}, f32[512,1280]{1,0:T(8,128)S(1)}) custom-call(bf16[7,640,640]{2,1,0:T(8,128)(2,1)S(1)} %get-tuple-element.103.refs_0_, f32[512,640]{1,0:T(8,128)S(1)} %get-tuple-element.104.refs_1_, f32[512,640]{1,0:T(8,128)S(1)} %get-tuple-element.105.refs_2_, ...), custom_call_target="tpu_custom_call" | custom-call | flops 100000000 | bytes 1000 | tf_op jit(solution)/shard_map/back/pallas_call | solution.py:136
  109.2 1.4 collective-permute-done.33.refs_1_
  110.6 0.7 collective-permute-done.34.refs_2_
  112.8 1.2 collective-permute-start.36
  114.0 1.8 %collective-permute-start.37 = (bf16[160,768]{1,0:T(8,128)(2,1)S(1)}, bf16[160,768]{1,0:T(8,128)(2,1)S(1)}, u32[]{:S(2)}, u32[]{:S(2)}) collective-permute-start(bf16[160,768]{1,0:T(8,128)(2,1)S(1)} %get-tuple-element.134), channel_id=1, source_target_pairs={{0,24},{4,28},{8,16},{12,20},{16,8},{20,12},{24,0},{28,4},{1,25},{... | collective-permute-start | bytes 737288 | tf_op jit(solution)/shard_map/ppermute | solution.py:737
  115.7 1.5 %collective-permute-start.41 = (bf16[128,640]{1,0:T(8,128)(2,1)S(1)}, bf16[128,640]{1,0:T(8,128)(2,1)S(1)}, u32[]{:S(2)}, u32[]{:S(2)}) collective-permute-start(bf16[128,640]{1,0:T(8,128)(2,1)S(1)} %get-tuple-element.148), channel_id=1, source_target_pairs={{0,1},{1,2},{2,3},{3,0},{4,5},{5,6},{6,7},{7,4},{8,9},{9,10},{10,1... | collective-permute-start | bytes 491528 | tf_op jit(solution)/shard_map/ppermute | solution.py:742
  117.3 1.9 %collective-permute-start.42 = (bf16[128,640]{1,0:T(8,128)(2,1)S(1)}, bf16[128,640]{1,0:T(8,128)(2,1)S(1)}, u32[]{:S(2)}, u32[]{:S(2)}) collective-permute-start(bf16[128,640]{1,0:T(8,128)(2,1)S(1)} %get-tuple-element.149), channel_id=1, source_target_pairs={{0,2},{1,3},{2,0},{3,1},{4,6},{5,7},{6,4},{7,5},{8,10},{9,11},{10,... | collective-permute-start | bytes 491528 | tf_op jit(solution)/shard_map/ppermute | solution.py:742
  119.2 1.9 %collective-permute-done.35.refs_1_ = bf16[160,768]{1,0:T(8,128)(2,1)S(1)} collective-permute-done((bf16[160,768]{1,0:T(8,128)(2,1)S(1)}, bf16[160,768]{1,0:T(8,128)(2,1)S(1)}, u32[]{:S(2)}, u32[]{:S(2)}) %collective-permute-start.35) | collective-permute-done | bytes 245792 | tf_op jit(solution)/shard_map/ppermute | solution.py:737
  121.1 2.9 %collective-permute-start.43 = (bf16[128,640]{1,0:T(8,128)(2,1)S(1)}, bf16[128,640]{1,0:T(8,128)(2,1)S(1)}, u32[]{:S(2)}, u32[]{:S(2)}) collective-permute-start(bf16[128,640]{1,0:T(8,128)(2,1)S(1)} %get-tuple-element.150), channel_id=1, source_target_pairs={{0,3},{1,0},{2,1},{3,2},{4,7},{5,4},{6,5},{7,6},{8,11},{9,8},{10,9... | collective-permute-start | bytes 491528 | tf_op jit(solution)/shard_map/ppermute | solution.py:742
  124.0 2.8 %input.1 = (bf16[512,1280]{1,0:T(8,128)(2,1)}, f32[8,128]{1,0:T(8,128)S(1)}) custom-call(f32[512,1280]{1,0:T(8,128)S(1)} %get-tuple-element.116.refs_0_, f32[512,1280]{1,0:T(8,128)S(1)} %get-tuple-element.89.refs_0_.refs_4_.refs_1_, f32[512,128]{1,0:T(8,128)S(1)} %get-tuple-element.91.refs_4_.refs_2_, ...), custom_call_target="tpu_custom_call" | custom-call | flops 3000000000 | bytes 1000 | tf_op jit(solution)/shard_map/input/pallas_call | solution.py:136
  127.5 1.2 collective-permute-start.39
  128.7 2.3 %collective-permute-start.40 = (bf16[40,768]{1,0:T(8,128)(2,1)S(1)}, bf16[40,768]{1,0:T(8,128)(2,1)S(1)}, u32[]{:S(2)}, u32[]{:S(2)}) collective-permute-start(bf16[40,768]{1,0:T(8,128)(2,1)S(1)} %get-tuple-element.139), channel_id=1, source_target_pairs={{0,3},{1,0},{2,1},{3,2},{4,7},{5,4},{6,5},{7,6},{8,11},{9,8},{10,9... | collective-permute-start | bytes 184328 | tf_op jit(solution)/shard_map/ppermute | solution.py:742
  131.3 1.2 end_b.1
  134.2 3.3 %collective-permute-done.39.refs_2_ = bf16[40,768]{1,0:T(8,128)(2,1)S(1)} collective-permute-done((bf16[40,768]{1,0:T(8,128)(2,1)S(1)}, bf16[40,768]{1,0:T(8,128)(2,1)S(1)}, u32[]{:S(2)}, u32[]{:S(2)}) %collective-permute-start.39) | collective-permute-done | bytes 61472 | tf_op jit(solution)/shard_map/ppermute | solution.py:742
  137.6 0.7 end_a.1
  (76 shorter events, 10.1 us)
Async XLA Ops:
  2.3 7.8 %collective-permute-start = (bf16[40,768]{1,0:T(8,128)(2,1)}, bf16[40,768]{1,0:T(8,128)(2,1)S(1)}, u32[]{:S(2)}, u32[]{:S(2)}) collective-permute-start(bf16[40,768]{1,0:T(8,128)(2,1)} %pack_a.1.refs_2_.refs_0_), channel_id=1, source_target_pairs={{0,1},{1,2},{2,3},{3,0},{4,5},{5,6},{6,7},{7,4},{8,9},{9,10},{10,1... | collective-permute-start | bytes 184328 | tf_op jit(solution)/shard_map/ppermute | solution.py:742
  5.4 7.1 %collective-permute-start.1 = (bf16[40,768]{1,0:T(8,128)(2,1)}, bf16[40,768]{1,0:T(8,128)(2,1)S(1)}, u32[]{:S(2)}, u32[]{:S(2)}) collective-permute-start(bf16[40,768]{1,0:T(8,128)(2,1)} %pack_a.1.refs_2_.refs_0_), channel_id=1, source_target_pairs={{0,2},{1,3},{2,0},{3,1},{4,6},{5,7},{6,4},{7,5},{8,10},{9,11},{10,... | collective-permute-start | bytes 184328 | tf_op jit(solution)/shard_map/ppermute | solution.py:742
  8.0 4.8 %collective-permute-start.2 = (bf16[40,768]{1,0:T(8,128)(2,1)}, bf16[40,768]{1,0:T(8,128)(2,1)S(1)}, u32[]{:S(2)}, u32[]{:S(2)}) collective-permute-start(bf16[40,768]{1,0:T(8,128)(2,1)} %pack_a.1.refs_2_.refs_0_), channel_id=1, source_target_pairs={{0,3},{1,0},{2,1},{3,2},{4,7},{5,4},{6,5},{7,6},{8,11},{9,8},{10,9... | collective-permute-start | bytes 184328 | tf_op jit(solution)/shard_map/ppermute | solution.py:742
  13.7 7.3 %collective-permute-start.3 = (bf16[160,768]{1,0:T(8,128)(2,1)S(1)}, bf16[160,768]{1,0:T(8,128)(2,1)S(1)}, u32[]{:S(2)}, u32[]{:S(2)}) collective-permute-start(bf16[160,768]{1,0:T(8,128)(2,1)S(1)} %line_a.1.refs_2_), channel_id=1, source_target_pairs={{0,8},{4,12},{8,0},{12,4},{16,24},{20,28},{24,16},{28,20},{1,9},{5... | collective-permute-start | bytes 737288 | tf_op jit(solution)/shard_map/ppermute | solution.py:737
  15.6 16.3 %collective-permute-start.10 = (bf16[140,640]{1,0:T(8,128)(2,1)S(1)}, bf16[140,640]{1,0:T(8,128)(2,1)S(1)}, u32[]{:S(2)}, u32[]{:S(2)}) collective-permute-start(bf16[140,640]{1,0:T(8,128)(2,1)S(1)} %pack_b.1.refs_1_.refs_0_), channel_id=1, source_target_pairs={{0,1},{1,2},{2,3},{3,0},{4,5},{5,6},{6,7},{7,4},{8,9},{9,10},{10,1... | collective-permute-start | bytes 537608 | tf_op jit(solution)/shard_map/ppermute | solution.py:742
  17.0 14.9 %collective-permute-start.11 = (bf16[140,640]{1,0:T(8,128)(2,1)S(1)}, bf16[140,640]{1,0:T(8,128)(2,1)S(1)}, u32[]{:S(2)}, u32[]{:S(2)}) collective-permute-start(bf16[140,640]{1,0:T(8,128)(2,1)S(1)} %pack_b.1.refs_1_.refs_0_), channel_id=1, source_target_pairs={{0,2},{1,3},{2,0},{3,1},{4,6},{5,7},{6,4},{7,5},{8,10},{9,11},{10,... | collective-permute-start | bytes 537608 | tf_op jit(solution)/shard_map/ppermute | solution.py:742
  19.1 13.3 %collective-permute-start.12 = (bf16[140,640]{1,0:T(8,128)(2,1)S(1)}, bf16[140,640]{1,0:T(8,128)(2,1)S(1)}, u32[]{:S(2)}, u32[]{:S(2)}) collective-permute-start(bf16[140,640]{1,0:T(8,128)(2,1)S(1)} %pack_b.1.refs_1_.refs_0_), channel_id=1, source_target_pairs={{0,3},{1,0},{2,1},{3,2},{4,7},{5,4},{6,5},{7,6},{8,11},{9,8},{10,9... | collective-permute-start | bytes 537608 | tf_op jit(solution)/shard_map/ppermute | solution.py:742
  19.5 11.9 %collective-permute-start.4 = (bf16[160,768]{1,0:T(8,128)(2,1)S(1)}, bf16[160,768]{1,0:T(8,128)(2,1)S(1)}, u32[]{:S(2)}, u32[]{:S(2)}) collective-permute-start(bf16[160,768]{1,0:T(8,128)(2,1)S(1)} %line_a.1.refs_2_), channel_id=1, source_target_pairs={{0,16},{4,20},{8,24},{12,28},{16,0},{20,4},{24,8},{28,12},{1,17},{... | collective-permute-start | bytes 737288 | tf_op jit(solution)/shard_map/ppermute | solution.py:737
  21.1 10.3 %collective-permute-start.5 = (bf16[160,768]{1,0:T(8,128)(2,1)S(1)}, bf16[160,768]{1,0:T(8,128)(2,1)S(1)}, u32[]{:S(2)}, u32[]{:S(2)}) collective-permute-start(bf16[160,768]{1,0:T(8,128)(2,1)S(1)} %line_a.1.refs_2_), channel_id=1, source_target_pairs={{0,24},{4,28},{8,16},{12,20},{16,8},{20,12},{24,0},{28,4},{1,25},{... | collective-permute-start | bytes 737288 | tf_op jit(solution)/shard_map/ppermute | solution.py:737
  31.4 2.2 %collective-permute-start.6 = (bf16[160,768]{1,0:T(8,128)(2,1)S(1)}, bf16[160,768]{1,0:T(8,128)(2,1)S(1)}, u32[]{:S(2)}, u32[]{:S(2)}) collective-permute-start(bf16[160,768]{1,0:T(8,128)(2,1)S(1)} %line_a.1.refs_2_), channel_id=1, source_target_pairs={{0,4},{4,0},{8,12},{12,8},{16,20},{20,16},{24,28},{28,24},{1,5},{5... | collective-permute-start | bytes 737288 | tf_op jit(solution)/shard_map/ppermute | solution.py:737
  31.4 3.5 %collective-permute-start.7 = (bf16[160,768]{1,0:T(8,128)(2,1)S(1)}, bf16[160,768]{1,0:T(8,128)(2,1)S(1)}, u32[]{:S(2)}, u32[]{:S(2)}) collective-permute-start(bf16[160,768]{1,0:T(8,128)(2,1)S(1)} %collective-permute-done.3.refs_3_), channel_id=1, source_target_pairs={{0,4},{4,0},{8,12},{12,8},{16,20},{20,16},{24,28},{28,24},{1,5},{5... | collective-permute-start | bytes 737288 | tf_op jit(solution)/shard_map/ppermute | solution.py:737
  31.9 3.0 %collective-permute-start.8 = (bf16[160,768]{1,0:T(8,128)(2,1)S(1)}, bf16[160,768]{1,0:T(8,128)(2,1)S(1)}, u32[]{:S(2)}, u32[]{:S(2)}) collective-permute-start(bf16[160,768]{1,0:T(8,128)(2,1)S(1)} %collective-permute-done.4.refs_4_), channel_id=1, source_target_pairs={{0,4},{4,0},{8,12},{12,8},{16,20},{20,16},{24,28},{28,24},{1,5},{5... | collective-permute-start | bytes 737288 | tf_op jit(solution)/shard_map/ppermute | solution.py:737
  31.9 2.9 %collective-permute-start.9 = (bf16[160,768]{1,0:T(8,128)(2,1)S(1)}, bf16[160,768]{1,0:T(8,128)(2,1)S(1)}, u32[]{:S(2)}, u32[]{:S(2)}) collective-permute-start(bf16[160,768]{1,0:T(8,128)(2,1)S(1)} %collective-permute-done.5.refs_5_), channel_id=1, source_target_pairs={{0,4},{4,0},{8,12},{12,8},{16,20},{20,16},{24,28},{28,24},{1,5},{5... | collective-permute-start | bytes 737288 | tf_op jit(solution)/shard_map/ppermute | solution.py:737
  32.7 18.1 %collective-permute-start.15 = (bf16[7,80,640]{2,1,0:T(8,128)(2,1)S(1)}, bf16[7,80,640]{2,1,0:T(8,128)(2,1)S(1)}, u32[]{:S(2)}, u32[]{:S(2)}) collective-permute-start(bf16[7,80,640]{2,1,0:T(8,128)(2,1)S(1)} %line_b.1.refs_10_.refs_11_), channel_id=1, source_target_pairs={{0,8},{4,12},{8,0},{12,4},{16,24},{20,28},{24,16},{28,20},{1,9},{5... | collective-permute-start | bytes 2150408 | tf_op jit(solution)/shard_map/ppermute | solution.py:737
  33.6 18.8 %collective-permute-start.16 = (bf16[7,80,640]{2,1,0:T(8,128)(2,1)S(1)}, bf16[7,80,640]{2,1,0:T(8,128)(2,1)S(1)}, u32[]{:S(2)}, u32[]{:S(2)}) collective-permute-start(bf16[7,80,640]{2,1,0:T(8,128)(2,1)S(1)} %line_b.1.refs_10_.refs_11_), channel_id=1, source_target_pairs={{0,16},{4,20},{8,24},{12,28},{16,0},{20,4},{24,8},{28,12},{1,17},{... | collective-permute-start | bytes 2150408 | tf_op jit(solution)/shard_map/ppermute | solution.py:737
  34.9 28.5 %copy-start.7 = (bf16[30]{0:T(256)(128)(2,1)S(1)}, bf16[30]{0:T(256)(128)(2,1)}, u32[]{:S(2)}) copy-start(bf16[30]{0:T(256)(128)(2,1)} %param.32) | copy-start | bytes 184
  34.9 30.2 %copy-start.4 = (s32[2,256]{1,0:T(2,128)S(1)}, s32[2,256]{1,0:T(2,128)}, u32[]{:S(2)}) copy-start(s32[2,256]{1,0:T(2,128)} %refs_4_.3) | copy-start | bytes 6148
  34.9 30.2 %copy-start.5 = (s32[2,153]{1,0:T(2,128)S(1)}, s32[2,153]{1,0:T(2,128)}, u32[]{:S(2)}) copy-start(s32[2,153]{1,0:T(2,128)} %refs_5_.3) | copy-start | bytes 3676
  34.9 30.2 %copy-start.6 = (s32[2,153]{1,0:T(2,128)S(1)}, s32[2,153]{1,0:T(2,128)}, u32[]{:S(2)}) copy-start(s32[2,153]{1,0:T(2,128)} %refs_6_.3) | copy-start | bytes 3676
  39.6 19.7 %collective-permute-start.13 = (bf16[2,256,640]{2,1,0:T(8,128)(2,1)S(1)}, bf16[2,256,640]{2,1,0:T(8,128)(2,1)S(1)}, u32[]{:S(2)}, u32[]{:S(2)}) collective-permute-start(bf16[2,256,640]{2,1,0:T(8,128)(2,1)S(1)} %bitcast.24), channel_id=1, source_target_pairs={{0,1},{1,2},{2,3},{4,5},{5,6},{6,7},{8,9},{9,10},{10,11},{12,13},{... | collective-permute-start | bytes 1966088 | tf_op jit(solution)/shard_map/ppermute | solution.py:759
  44.0 17.7 %collective-permute-start.14 = (bf16[2,256,640]{2,1,0:T(8,128)(2,1)S(1)}, bf16[2,256,640]{2,1,0:T(8,128)(2,1)S(1)}, u32[]{:S(2)}, u32[]{:S(2)}) collective-permute-start(bf16[2,256,640]{2,1,0:T(8,128)(2,1)S(1)} %bitcast.25), channel_id=1, source_target_pairs={{1,0},{2,1},{3,2},{5,4},{6,5},{7,6},{9,8},{10,9},{11,10},{13,12},{... | collective-permute-start | bytes 1966088 | tf_op jit(solution)/shard_map/ppermute | solution.py:763
  50.9 8.5 %collective-permute-start.17 = (bf16[3,80,640]{2,1,0:T(8,128)(2,1)S(1)}, bf16[3,80,640]{2,1,0:T(8,128)(2,1)S(1)}, u32[]{:S(2)}, u32[]{:S(2)}) collective-permute-start(bf16[3,80,640]{2,1,0:T(8,128)(2,1)S(1)} %slice.24), channel_id=1, source_target_pairs={{0,16},{4,20},{8,24},{12,28},{16,0},{20,4},{24,8},{28,12},{1,17},{... | collective-permute-start | bytes 921608 | tf_op jit(solution)/shard_map/ppermute | solution.py:737
  52.5 10.4 %collective-permute-start.18 = (bf16[4,80,640]{2,1,0:T(8,128)(2,1)S(1)}, bf16[4,80,640]{2,1,0:T(8,128)(2,1)S(1)}, u32[]{:S(2)}, u32[]{:S(2)}) collective-permute-start(bf16[4,80,640]{2,1,0:T(8,128)(2,1)S(1)} %slice.25), channel_id=1, source_target_pairs={{0,8},{4,12},{8,0},{12,4},{16,24},{20,28},{24,16},{28,20},{1,9},{5... | collective-permute-start | bytes 1228808 | tf_op jit(solution)/shard_map/ppermute | solution.py:737
  53.1 10.3 %collective-permute-start.19 = (bf16[7,80,640]{2,1,0:T(8,128)(2,1)S(1)}, bf16[7,80,640]{2,1,0:T(8,128)(2,1)S(1)}, u32[]{:S(2)}, u32[]{:S(2)}) collective-permute-start(bf16[7,80,640]{2,1,0:T(8,128)(2,1)S(1)} %line_b.1.refs_10_.refs_11_), channel_id=1, source_target_pairs={{0,4},{4,0},{8,12},{12,8},{16,20},{20,16},{24,28},{28,24},{1,5},{5... | collective-permute-start | bytes 2150408 | tf_op jit(solution)/shard_map/ppermute | solution.py:737
  59.3 4.1 %collective-permute-start.20 = (bf16[7,80,640]{2,1,0:T(8,128)(2,1)S(1)}, bf16[7,80,640]{2,1,0:T(8,128)(2,1)S(1)}, u32[]{:S(2)}, u32[]{:S(2)}) collective-permute-start(bf16[7,80,640]{2,1,0:T(8,128)(2,1)S(1)} %collective-permute-done.15.refs_12_), channel_id=1, source_target_pairs={{0,4},{4,0},{8,12},{12,8},{16,20},{20,16},{24,28},{28,24},{1,5},{5... | collective-permute-start | bytes 2150408 | tf_op jit(solution)/shard_map/ppermute | solution.py:737
  59.3 4.1 %collective-permute-start.21 = (bf16[7,80,640]{2,1,0:T(8,128)(2,1)S(1)}, bf16[7,80,640]{2,1,0:T(8,128)(2,1)S(1)}, u32[]{:S(2)}, u32[]{:S(2)}) collective-permute-start(bf16[7,80,640]{2,1,0:T(8,128)(2,1)S(1)} %collective-permute-done.16.refs_13_), channel_id=1, source_target_pairs={{0,4},{4,0},{8,12},{12,8},{16,20},{20,16},{24,28},{28,24},{1,5},{5... | collective-permute-start | bytes 2150408 | tf_op jit(solution)/shard_map/ppermute | solution.py:737
  62.9 2.2 %collective-permute-start.23 = (bf16[4,80,640]{2,1,0:T(8,128)(2,1)S(1)}, bf16[4,80,640]{2,1,0:T(8,128)(2,1)S(1)}, u32[]{:S(2)}, u32[]{:S(2)}) collective-permute-start(bf16[4,80,640]{2,1,0:T(8,128)(2,1)S(1)} %collective-permute-done.18.refs_15_), channel_id=1, source_target_pairs={{0,4},{4,0},{8,12},{12,8},{16,20},{20,16},{24,28},{28,24},{1,5},{5... | collective-permute-start | bytes 1228808 | tf_op jit(solution)/shard_map/ppermute | solution.py:737
  62.9 2.2 %collective-permute-start.22 = (bf16[3,80,640]{2,1,0:T(8,128)(2,1)S(1)}, bf16[3,80,640]{2,1,0:T(8,128)(2,1)S(1)}, u32[]{:S(2)}, u32[]{:S(2)}) collective-permute-start(bf16[3,80,640]{2,1,0:T(8,128)(2,1)S(1)} %collective-permute-done.17.refs_14_), channel_id=1, source_target_pairs={{0,4},{4,0},{8,12},{12,8},{16,20},{20,16},{24,28},{28,24},{1,5},{5... | collective-permute-start | bytes 921608 | tf_op jit(solution)/shard_map/ppermute | solution.py:737
  74.1 7.0 %collective-permute-start.26 = (bf16[528,1408]{1,0:T(8,128)(2,1)S(1)}, bf16[528,1408]{1,0:T(8,128)(2,1)S(1)}, u32[]{:S(2)}, u32[]{:S(2)}) collective-permute-start(bf16[528,1408]{1,0:T(8,128)(2,1)S(1)} %get-tuple-element.114.refs_0_.refs_4_), channel_id=1, source_target_pairs={{0,4},{4,0},{8,12},{12,8},{16,20},{20,16},{24,28},{28,24},{1,5},{5... | collective-permute-start | bytes 4460552 | tf_op jit(solution)/shard_map/ppermute | solution.py:737
  74.3 5.2 %collective-permute-start.28 = (bf16[2,256,640]{2,1,0:T(8,128)(2,1)S(1)}, bf16[2,256,640]{2,1,0:T(8,128)(2,1)S(1)}, u32[]{:S(2)}, u32[]{:S(2)}) collective-permute-start(bf16[2,256,640]{2,1,0:T(8,128)(2,1)S(1)} %bitcast.27), channel_id=1, source_target_pairs={{0,4},{4,0},{8,12},{12,8},{16,20},{20,16},{24,28},{28,24},{1,5},{5... | collective-permute-start | bytes 1966088 | tf_op jit(solution)/shard_map/ppermute | solution.py:737
  74.7 6.4 %collective-permute-start.27 = (bf16[2,256,640]{2,1,0:T(8,128)(2,1)S(1)}, bf16[2,256,640]{2,1,0:T(8,128)(2,1)S(1)}, u32[]{:S(2)}, u32[]{:S(2)}) collective-permute-start(bf16[2,256,640]{2,1,0:T(8,128)(2,1)S(1)} %collective-permute-done.13.refs_8_.refs_3_), channel_id=1, source_target_pairs={{0,4},{4,0},{8,12},{12,8},{16,20},{20,16},{24,28},{28,24},{1,5},{5... | collective-permute-start | bytes 1966088 | tf_op jit(solution)/shard_map/ppermute | solution.py:737
  74.8 6.2 %collective-permute-start.29 = (bf16[2,256,640]{2,1,0:T(8,128)(2,1)S(1)}, bf16[2,256,640]{2,1,0:T(8,128)(2,1)S(1)}, u32[]{:S(2)}, u32[]{:S(2)}) collective-permute-start(bf16[2,256,640]{2,1,0:T(8,128)(2,1)S(1)} %collective-permute-done.14.refs_10_.refs_5_), channel_id=1, source_target_pairs={{0,4},{4,0},{8,12},{12,8},{16,20},{20,16},{24,28},{28,24},{1,5},{5... | collective-permute-start | bytes 1966088 | tf_op jit(solution)/shard_map/ppermute | solution.py:737
  75.2 18.5 %collective-permute-start.24 = (bf16[2,256,640]{2,1,0:T(8,128)(2,1)S(1)}, bf16[2,256,640]{2,1,0:T(8,128)(2,1)S(1)}, u32[]{:S(2)}, u32[]{:S(2)}) collective-permute-start(bf16[2,256,640]{2,1,0:T(8,128)(2,1)S(1)} %bitcast.19), channel_id=1, source_target_pairs={{0,1},{1,2},{2,3},{4,5},{5,6},{6,7},{8,9},{9,10},{10,11},{12,13},{... | collective-permute-start | bytes 1966088 | tf_op jit(solution)/shard_map/ppermute | solution.py:759
  79.5 18.4 %collective-permute-start.25 = (bf16[2,256,640]{2,1,0:T(8,128)(2,1)S(1)}, bf16[2,256,640]{2,1,0:T(8,128)(2,1)S(1)}, u32[]{:S(2)}, u32[]{:S(2)}) collective-permute-start(bf16[2,256,640]{2,1,0:T(8,128)(2,1)S(1)} %bitcast.20), channel_id=1, source_target_pairs={{1,0},{2,1},{3,2},{5,4},{6,5},{7,6},{9,8},{10,9},{11,10},{13,12},{... | collective-permute-start | bytes 1966088 | tf_op jit(solution)/shard_map/ppermute | solution.py:763
  84.2 27.5 %collective-permute-start.30 = (bf16[432,640]{1,0:T(8,128)(2,1)S(1)}, bf16[432,640]{1,0:T(8,128)(2,1)S(1)}, u32[]{:S(2)}, u32[]{:S(2)}) collective-permute-start(bf16[432,640]{1,0:T(8,128)(2,1)S(1)} %get-tuple-element.119), channel_id=1, source_target_pairs={{0,8},{4,12},{8,0},{12,4},{16,24},{20,28},{24,16},{28,20},{1,9},{5... | collective-permute-start | bytes 1658888 | tf_op jit(solution)/shard_map/ppermute | solution.py:737
  84.8 26.9 %collective-permute-start.31 = (bf16[432,640]{1,0:T(8,128)(2,1)S(1)}, bf16[432,640]{1,0:T(8,128)(2,1)S(1)}, u32[]{:S(2)}, u32[]{:S(2)}) collective-permute-start(bf16[432,640]{1,0:T(8,128)(2,1)S(1)} %get-tuple-element.120), channel_id=1, source_target_pairs={{0,16},{4,20},{8,24},{12,28},{16,0},{20,4},{24,8},{28,12},{1,17},{... | collective-permute-start | bytes 1658888 | tf_op jit(solution)/shard_map/ppermute | solution.py:737
  86.0 25.7 %collective-permute-start.32 = (bf16[432,640]{1,0:T(8,128)(2,1)S(1)}, bf16[432,640]{1,0:T(8,128)(2,1)S(1)}, u32[]{:S(2)}, u32[]{:S(2)}) collective-permute-start(bf16[432,640]{1,0:T(8,128)(2,1)S(1)} %get-tuple-element.121), channel_id=1, source_target_pairs={{0,24},{4,28},{8,16},{12,20},{16,8},{20,12},{24,0},{28,4},{1,25},{... | collective-permute-start | bytes 1658888 | tf_op jit(solution)/shard_map/ppermute | solution.py:737
  108.6 1.9 %collective-permute-start.33 = (bf16[2,160,768]{2,1,0:T(8,128)(2,1)S(1)}, bf16[2,160,768]{2,1,0:T(8,128)(2,1)S(1)}, u32[]{:S(2)}, u32[]{:S(2)}) collective-permute-start(bf16[2,160,768]{2,1,0:T(8,128)(2,1)S(1)} %get-tuple-element.123), channel_id=1, source_target_pairs={{0,4},{4,0},{8,12},{12,8},{16,20},{20,16},{24,28},{28,24},{1,5},{5... | collective-permute-start | bytes 1474568 | tf_op jit(solution)/shard_map/ppermute | solution.py:737
  108.7 2.6 %collective-permute-start.34 = (bf16[2,160,768]{2,1,0:T(8,128)(2,1)S(1)}, bf16[2,160,768]{2,1,0:T(8,128)(2,1)S(1)}, u32[]{:S(2)}, u32[]{:S(2)}) collective-permute-start(bf16[2,160,768]{2,1,0:T(8,128)(2,1)S(1)} %get-tuple-element.124), channel_id=1, source_target_pairs={{0,4},{4,0},{8,12},{12,8},{16,20},{20,16},{24,28},{28,24},{1,5},{5... | collective-permute-start | bytes 1474568 | tf_op jit(solution)/shard_map/ppermute | solution.py:737
  112.2 8.9 %collective-permute-start.35 = (bf16[160,768]{1,0:T(8,128)(2,1)S(1)}, bf16[160,768]{1,0:T(8,128)(2,1)S(1)}, u32[]{:S(2)}, u32[]{:S(2)}) collective-permute-start(bf16[160,768]{1,0:T(8,128)(2,1)S(1)} %get-tuple-element.132), channel_id=1, source_target_pairs={{0,8},{4,12},{8,0},{12,4},{16,24},{20,28},{24,16},{28,20},{1,9},{5... | collective-permute-start | bytes 737288 | tf_op jit(solution)/shard_map/ppermute | solution.py:737
  112.8 14.0 %collective-permute-start.36 = (bf16[160,768]{1,0:T(8,128)(2,1)S(1)}, bf16[160,768]{1,0:T(8,128)(2,1)S(1)}, u32[]{:S(2)}, u32[]{:S(2)}) collective-permute-start(bf16[160,768]{1,0:T(8,128)(2,1)S(1)} %get-tuple-element.133), channel_id=1, source_target_pairs={{0,16},{4,20},{8,24},{12,28},{16,0},{20,4},{24,8},{28,12},{1,17},{... | collective-permute-start | bytes 737288 | tf_op jit(solution)/shard_map/ppermute | solution.py:737
  114.0 12.8 %collective-permute-start.37 = (bf16[160,768]{1,0:T(8,128)(2,1)S(1)}, bf16[160,768]{1,0:T(8,128)(2,1)S(1)}, u32[]{:S(2)}, u32[]{:S(2)}) collective-permute-start(bf16[160,768]{1,0:T(8,128)(2,1)S(1)} %get-tuple-element.134), channel_id=1, source_target_pairs={{0,24},{4,28},{8,16},{12,20},{16,8},{20,12},{24,0},{28,4},{1,25},{... | collective-permute-start | bytes 737288 | tf_op jit(solution)/shard_map/ppermute | solution.py:737
  115.7 13.0 %collective-permute-start.41 = (bf16[128,640]{1,0:T(8,128)(2,1)S(1)}, bf16[128,640]{1,0:T(8,128)(2,1)S(1)}, u32[]{:S(2)}, u32[]{:S(2)}) collective-permute-start(bf16[128,640]{1,0:T(8,128)(2,1)S(1)} %get-tuple-element.148), channel_id=1, source_target_pairs={{0,1},{1,2},{2,3},{3,0},{4,5},{5,6},{6,7},{7,4},{8,9},{9,10},{10,1... | collective-permute-start | bytes 491528 | tf_op jit(solution)/shard_map/ppermute | solution.py:742
  117.3 13.7 %collective-permute-start.42 = (bf16[128,640]{1,0:T(8,128)(2,1)S(1)}, bf16[128,640]{1,0:T(8,128)(2,1)S(1)}, u32[]{:S(2)}, u32[]{:S(2)}) collective-permute-start(bf16[128,640]{1,0:T(8,128)(2,1)S(1)} %get-tuple-element.149), channel_id=1, source_target_pairs={{0,2},{1,3},{2,0},{3,1},{4,6},{5,7},{6,4},{7,5},{8,10},{9,11},{10,... | collective-permute-start | bytes 491528 | tf_op jit(solution)/shard_map/ppermute | solution.py:742
  121.1 10.3 %collective-permute-start.43 = (bf16[128,640]{1,0:T(8,128)(2,1)S(1)}, bf16[128,640]{1,0:T(8,128)(2,1)S(1)}, u32[]{:S(2)}, u32[]{:S(2)}) collective-permute-start(bf16[128,640]{1,0:T(8,128)(2,1)S(1)} %get-tuple-element.150), channel_id=1, source_target_pairs={{0,3},{1,0},{2,1},{3,2},{4,7},{5,4},{6,5},{7,6},{8,11},{9,8},{10,9... | collective-permute-start | bytes 491528 | tf_op jit(solution)/shard_map/ppermute | solution.py:742
  126.9 7.3 %collective-permute-start.38 = (bf16[40,768]{1,0:T(8,128)(2,1)S(1)}, bf16[40,768]{1,0:T(8,128)(2,1)S(1)}, u32[]{:S(2)}, u32[]{:S(2)}) collective-permute-start(bf16[40,768]{1,0:T(8,128)(2,1)S(1)} %get-tuple-element.137), channel_id=1, source_target_pairs={{0,1},{1,2},{2,3},{3,0},{4,5},{5,6},{6,7},{7,4},{8,9},{9,10},{10,1... | collective-permute-start | bytes 184328 | tf_op jit(solution)/shard_map/ppermute | solution.py:742
  127.5 10.1 %collective-permute-start.39 = (bf16[40,768]{1,0:T(8,128)(2,1)S(1)}, bf16[40,768]{1,0:T(8,128)(2,1)S(1)}, u32[]{:S(2)}, u32[]{:S(2)}) collective-permute-start(bf16[40,768]{1,0:T(8,128)(2,1)S(1)} %get-tuple-element.138), channel_id=1, source_target_pairs={{0,2},{1,3},{2,0},{3,1},{4,6},{5,7},{6,4},{7,5},{8,10},{9,11},{10,... | collective-permute-start | bytes 184328 | tf_op jit(solution)/shard_map/ppermute | solution.py:742
  128.7 8.9 %collective-permute-start.40 = (bf16[40,768]{1,0:T(8,128)(2,1)S(1)}, bf16[40,768]{1,0:T(8,128)(2,1)S(1)}, u32[]{:S(2)}, u32[]{:S(2)}) collective-permute-start(bf16[40,768]{1,0:T(8,128)(2,1)S(1)} %get-tuple-element.139), channel_id=1, source_target_pairs={{0,3},{1,0},{2,1},{3,2},{4,7},{5,4},{6,5},{7,6},{8,11},{9,8},{10,9... | collective-permute-start | bytes 184328 | tf_op jit(solution)/shard_map/ppermute | solution.py:742
  (4 other events, 34.3 us)

commit v6 on v5

--- a/solution.py
+++ b/solution.py
@@ -699,21 +699,14 @@
     core = lax.axis_index("dp") & 1
     block = keep.shape[1]
     for q in range(chips):
-        for c in range(2):
-            d = 2 * q + c
-            lines = slice(d * block, (d + 1) * block)
-            value = dot(act_t[lines, :], low[...])
-
-            @pl.when(core == c)
-            def _():
-                keep[q, :, 0:inner] = value
-                keep[q, :, inner : inner + LANES] = extra[lines]
-
-            @pl.when(core != c)
-            def _():
-                send = (send_low, send_high)[q // half]
-                send[q % half, :, 0:inner] = value.astype(BF)
-                send[q % half, :, inner : inner + LANES] = extra[lines].astype(BF)
+        even = slice(2 * q * block, (2 * q + 1) * block)
+        odd = slice((2 * q + 1) * block, (2 * q + 2) * block)
+        send = (send_low, send_high)[q // half]
+        first, second = dot(act_t[even, :], low[...]), dot(act_t[odd, :], low[...])
+        keep[q, :, 0:inner] = jnp.where(core == 1, second, first)
+        send[q % half, :, 0:inner] = jnp.where(core == 1, first, second).astype(BF)
+        keep[q, :, inner : inner + LANES] = jnp.where(core == 1, extra[odd], extra[even])
+        send[q % half, :, inner : inner + LANES] = jnp.where(core == 1, extra[even], extra[odd]).astype(BF)
 
 
 def input_kernel(e1, n1, r1, wide_v, bundle, extras, input_grad, token, work):

time: 140 us -> 138 us (0.986)
  starting transfers between devices: 52.9 us -> 54.8 us
  waiting for transfers between devices: 44.5 us -> 42.7 us
  Pallas kernels: 37.3 us -> 35.7 us
    ppermute x12, starting transfers between devices: 21.3 us -> 23.1 us  [shifted(): lax.ppermute(value, 'seq', [(i, (i + k) % size) for i in range(size)])]
    pallas_call x15, Pallas kernels: 37.3 us -> 35.7 us  [call(): pl.pallas_call(body, out_shape=list(outs), in_specs=[pl.BlockSpec(memory_...]
  transfers between devices with their start and end apart: 44 -> 44, of which waited for: 17 -> 17; matrix products, arithmetic and copies ran while one was open for 1% -> 1% of each run, Pallas kernels for 18% -> 17%
where the time goes in v6:
time: 138 us
  starting transfers between devices  54.8 us (40%)
  waiting for transfers between devices  42.7 us (31%)
  Pallas kernels  35.7 us (26%)
  between operations  2.75 us (2%)
  local copies, waits for them, and re-layouts  1.45 us (1%)
    pallas_call x15, Pallas kernels, call(): pl.pallas_call(body, out_shape=list(outs), in_specs=[pl.BlockSpec(memory_...  35.7 us
    ppermute x28, waiting for transfers between devices, swap(): return lax.ppermute(value, 'dp', [(i, i ^ mask) for i in range(count)])  24.9 us
    ppermute x12, starting transfers between devices, shifted(): lax.ppermute(value, 'seq', [(i, (i + k) % size) for i in range(size)])  23.1 us
    ppermute x28, starting transfers between devices, swap(): return lax.ppermute(value, 'dp', [(i, i ^ mask) for i in range(count)])  20 us
    ppermute x2, starting transfers between devices, halo(): lax.ppermute(series, 'seq', [(i, i + h) for i in range(size - h)])  8.72 us
    ppermute x2, waiting for transfers between devices, halo(): lax.ppermute(series, 'seq', [(i + h, i) for i in range(size - h)])  6.06 us
    ppermute x2, waiting for transfers between devices, halo(): lax.ppermute(series, 'seq', [(i, i + h) for i in range(size - h)])  5.98 us
    ppermute x12, waiting for transfers between devices, shifted(): lax.ppermute(value, 'seq', [(i, (i + k) % size) for i in range(size)])  5.73 us
  transfers between devices with their start and end apart: 44, of which 17 were waited for; matrix products, arithmetic and copies ran while one was open for 1% of the time, Pallas kernels for 17%

profile of v6, /device:TPU:0, one launch (start us, length us, event | category | flops | bytes accessed | tf_op | source)
XLA Modules:
  0.0 137.9 jit_solution(8152059114325214322)
XLA Ops:
  0.7 1.6 %pack_a.1.refs_2_.refs_0_ = bf16[40,768]{1,0:T(8,128)(2,1)} custom-call(bf16[40,640]{1,0:T(8,128)(2,1)} %refs_0_.1, bf16[30,40]{1,0:T(8,128)(2,1)} %bitcast.30, bf16[40]{0:T(256)(128)(2,1)} %refs_2_.1, bf16[40]{0:T(256)(128)(2,1)} %refs_3_.1, bf16[40]{0:T(256)(128)(2,1)} %refs_4_.2, bf16[20]{0:T(256)(128)(2,1)} %refs_5_.2, bf16[20]{0:T(256)(128)(2,1)} %refs_6_.2, ...), custom_call_target="tpu_custom_call" | custom-call | flops 1000000000 | bytes 1000 | tf_op jit(solution)/shard_map/pack_a/pallas_call | solution.py:136
  2.3 3.1 %collective-permute-start = (bf16[40,768]{1,0:T(8,128)(2,1)}, bf16[40,768]{1,0:T(8,128)(2,1)S(1)}, u32[]{:S(2)}, u32[]{:S(2)}) collective-permute-start(bf16[40,768]{1,0:T(8,128)(2,1)} %pack_a.1.refs_2_.refs_0_), channel_id=1, source_target_pairs={{0,1},{1,2},{2,3},{3,0},{4,5},{5,6},{6,7},{7,4},{8,9},{9,10},{10,1... | collective-permute-start | bytes 184328 | tf_op jit(solution)/shard_map/ppermute | solution.py:735
  5.4 2.6 %collective-permute-start.1 = (bf16[40,768]{1,0:T(8,128)(2,1)}, bf16[40,768]{1,0:T(8,128)(2,1)S(1)}, u32[]{:S(2)}, u32[]{:S(2)}) collective-permute-start(bf16[40,768]{1,0:T(8,128)(2,1)} %pack_a.1.refs_2_.refs_0_), channel_id=1, source_target_pairs={{0,2},{1,3},{2,0},{3,1},{4,6},{5,7},{6,4},{7,5},{8,10},{9,11},{10,... | collective-permute-start | bytes 184328 | tf_op jit(solution)/shard_map/ppermute | solution.py:735
  8.0 1.3 collective-permute-start.2
  9.3 0.7 collective-permute-done.refs_1_
  10.1 2.4 %collective-permute-done.1.refs_2_ = bf16[40,768]{1,0:T(8,128)(2,1)S(1)} collective-permute-done((bf16[40,768]{1,0:T(8,128)(2,1)}, bf16[40,768]{1,0:T(8,128)(2,1)S(1)}, u32[]{:S(2)}, u32[]{:S(2)}) %collective-permute-start.1) | collective-permute-done | bytes 61472 | tf_op jit(solution)/shard_map/ppermute | solution.py:735
  12.8 0.8 copy-done.3
  13.7 1.6 %collective-permute-start.3 = (bf16[160,768]{1,0:T(8,128)(2,1)S(1)}, bf16[160,768]{1,0:T(8,128)(2,1)S(1)}, u32[]{:S(2)}, u32[]{:S(2)}) collective-permute-start(bf16[160,768]{1,0:T(8,128)(2,1)S(1)} %line_a.1.refs_2_), channel_id=1, source_target_pairs={{0,8},{4,12},{8,0},{12,4},{16,24},{20,28},{24,16},{28,20},{1,9},{5... | collective-permute-start | bytes 737288 | tf_op jit(solution)/shard_map/ppermute | solution.py:730
  15.6 1.4 %collective-permute-start.10 = (bf16[140,640]{1,0:T(8,128)(2,1)S(1)}, bf16[140,640]{1,0:T(8,128)(2,1)S(1)}, u32[]{:S(2)}, u32[]{:S(2)}) collective-permute-start(bf16[140,640]{1,0:T(8,128)(2,1)S(1)} %pack_b.1.refs_1_.refs_0_), channel_id=1, source_target_pairs={{0,1},{1,2},{2,3},{3,0},{4,5},{5,6},{6,7},{7,4},{8,9},{9,10},{10,1... | collective-permute-start | bytes 537608 | tf_op jit(solution)/shard_map/ppermute | solution.py:735
  17.0 2.1 %collective-permute-start.11 = (bf16[140,640]{1,0:T(8,128)(2,1)S(1)}, bf16[140,640]{1,0:T(8,128)(2,1)S(1)}, u32[]{:S(2)}, u32[]{:S(2)}) collective-permute-start(bf16[140,640]{1,0:T(8,128)(2,1)S(1)} %pack_b.1.refs_1_.refs_0_), channel_id=1, source_target_pairs={{0,2},{1,3},{2,0},{3,1},{4,6},{5,7},{6,4},{7,5},{8,10},{9,11},{10,... | collective-permute-start | bytes 537608 | tf_op jit(solution)/shard_map/ppermute | solution.py:735
  19.5 1.5 %collective-permute-start.4 = (bf16[160,768]{1,0:T(8,128)(2,1)S(1)}, bf16[160,768]{1,0:T(8,128)(2,1)S(1)}, u32[]{:S(2)}, u32[]{:S(2)}) collective-permute-start(bf16[160,768]{1,0:T(8,128)(2,1)S(1)} %line_a.1.refs_2_), channel_id=1, source_target_pairs={{0,16},{4,20},{8,24},{12,28},{16,0},{20,4},{24,8},{28,12},{1,17},{... | collective-permute-start | bytes 737288 | tf_op jit(solution)/shard_map/ppermute | solution.py:730
  21.1 1.8 %collective-permute-start.5 = (bf16[160,768]{1,0:T(8,128)(2,1)S(1)}, bf16[160,768]{1,0:T(8,128)(2,1)S(1)}, u32[]{:S(2)}, u32[]{:S(2)}) collective-permute-start(bf16[160,768]{1,0:T(8,128)(2,1)S(1)} %line_a.1.refs_2_), channel_id=1, source_target_pairs={{0,24},{4,28},{8,16},{12,20},{16,8},{20,12},{24,0},{28,4},{1,25},{... | collective-permute-start | bytes 737288 | tf_op jit(solution)/shard_map/ppermute | solution.py:730
  22.8 1.6 %first.1 = (f32[512,1280]{1,0:T(8,128)S(1)}, f32[512,128]{1,0:T(8,128)S(1)}, bf16[1280,640]{1,0:T(8,128)(2,1)S(1)}) custom-call(bf16[512,1280]{1,0:T(8,128)(2,1)S(1)} %bitcast.22, bf16[140,640]{1,0:T(8,128)(2,1)S(1)} %pack_b.1.refs_1_.refs_0_), custom_call_target="tpu_custom_call" | custom-call | flops 6000000000 | bytes 1000 | tf_op jit(solution)/shard_map/first/pallas_call | solution.py:136
  24.4 7.0 %collective-permute-done.4.refs_4_ = bf16[160,768]{1,0:T(8,128)(2,1)S(1)} collective-permute-done((bf16[160,768]{1,0:T(8,128)(2,1)S(1)}, bf16[160,768]{1,0:T(8,128)(2,1)S(1)}, u32[]{:S(2)}, u32[]{:S(2)}) %collective-permute-start.4) | collective-permute-done | bytes 245792 | tf_op jit(solution)/shard_map/ppermute | solution.py:730
  32.7 0.9 collective-permute-start.15
  33.6 1.2 collective-permute-start.16
  34.9 4.7 %second.1 = (bf16[1280,640]{1,0:T(8,128)(2,1)S(1)}, bf16[1280,128]{1,0:T(8,128)(2,1)S(1)}, f32[8,1280]{1,0:T(8,128)S(1)}, f32[8,640]{1,0:T(8,128)S(1)}, bf16[512...) custom-call(f32[512,1280]{1,0:T(8,128)S(1)} %get-tuple-element.89.re, ...), custom_call_target="tpu_custom_call" | custom-call | flops 8999999488 | bytes 1000 | tf_op jit(solution)/shard_map/second/pallas_call | solution.py:136
  39.6 4.4 %collective-permute-start.13 = (bf16[2,256,640]{2,1,0:T(8,128)(2,1)S(1)}, bf16[2,256,640]{2,1,0:T(8,128)(2,1)S(1)}, u32[]{:S(2)}, u32[]{:S(2)}) collective-permute-start(bf16[2,256,640]{2,1,0:T(8,128)(2,1)S(1)} %bitcast.24), channel_id=1, source_target_pairs={{0,1},{1,2},{2,3},{4,5},{5,6},{6,7},{8,9},{9,10},{10,11},{12,13},{... | collective-permute-start | bytes 1966088 | tf_op jit(solution)/shard_map/ppermute | solution.py:752
  44.0 1.5 %collective-permute-start.14 = (bf16[2,256,640]{2,1,0:T(8,128)(2,1)S(1)}, bf16[2,256,640]{2,1,0:T(8,128)(2,1)S(1)}, u32[]{:S(2)}, u32[]{:S(2)}) collective-permute-start(bf16[2,256,640]{2,1,0:T(8,128)(2,1)S(1)} %bitcast.25), channel_id=1, source_target_pairs={{1,0},{2,1},{3,2},{5,4},{6,5},{7,6},{9,8},{10,9},{11,10},{13,12},{... | collective-permute-start | bytes 1966088 | tf_op jit(solution)/shard_map/ppermute | solution.py:756
  45.5 5.3 %collective-permute-done.15.refs_12_ = bf16[7,80,640]{2,1,0:T(8,128)(2,1)S(1)} collective-permute-done((bf16[7,80,640]{2,1,0:T(8,128)(2,1)S(1)}, bf16[7,80,640]{2,1,0:T(8,128)(2,1)S(1)}, u32[]{:S(2)}, u32[]{:S(2)}) %collective-permute-start.15) | collective-permute-done | bytes 716832 | tf_op jit(solution)/shard_map/ppermute | solution.py:730
  50.9 1.6 %collective-permute-start.17 = (bf16[3,80,640]{2,1,0:T(8,128)(2,1)S(1)}, bf16[3,80,640]{2,1,0:T(8,128)(2,1)S(1)}, u32[]{:S(2)}, u32[]{:S(2)}) collective-permute-start(bf16[3,80,640]{2,1,0:T(8,128)(2,1)S(1)} %slice.24), channel_id=1, source_target_pairs={{0,16},{4,20},{8,24},{12,28},{16,0},{20,4},{24,8},{28,12},{1,17},{... | collective-permute-start | bytes 921608 | tf_op jit(solution)/shard_map/ppermute | solution.py:730
  53.1 6.2 %collective-permute-done.17.refs_14_ = bf16[3,80,640]{2,1,0:T(8,128)(2,1)S(1)} collective-permute-done((bf16[3,80,640]{2,1,0:T(8,128)(2,1)S(1)}, bf16[3,80,640]{2,1,0:T(8,128)(2,1)S(1)}, u32[]{:S(2)}, u32[]{:S(2)}) %collective-permute-start.17) | collective-permute-done | bytes 307232 | tf_op jit(solution)/shard_map/ppermute | solution.py:730
  59.8 1.9 %collective-permute-done.14.refs_10_.refs_5_ = bf16[2,256,640]{2,1,0:T(8,128)(2,1)S(1)} collective-permute-done((bf16[2,256,640]{2,1,0:T(8,128)(2,1)S(1)}, bf16[2,256,640]{2,1,0:T(8,128)(2,1)S(1)}, u32[]{:S(2)}, u32[]{:S(2)}) %collective-permute-start.14) | collective-permute-done | bytes 655392 | tf_op jit(solution)/shard_map/ppermute | solution.py:756
  61.7 1.1 collective-permute-done.18.refs_15_
  63.4 1.6 %collective-permute-done.22.refs_19_ = bf16[3,80,640]{2,1,0:T(8,128)(2,1)S(1)} collective-permute-done((bf16[3,80,640]{2,1,0:T(8,128)(2,1)S(1)}, bf16[3,80,640]{2,1,0:T(8,128)(2,1)S(1)}, u32[]{:S(2)}, u32[]{:S(2)}) %collective-permute-start.22) | collective-permute-done | bytes 307232 | tf_op jit(solution)/shard_map/ppermute | solution.py:730
  65.1 9.0 %middle.1 = (bf16[7,640,640]{2,1,0:T(8,128)(2,1)S(1)}, bf16[512,1280]{1,0:T(8,128)(2,1)}, bf16[528,1408]{1,0:T(8,128)(2,1)S(1)}, f32[1280,128]{1,0:T(8,128)S(1)}...) custom-call(f32[8,1280]{1,0:T(8,128)S(1)} %get-tuple-element.96.refs_0_.refs_8_.refs_3_, ...), custom_call_target="tpu_custom_call" | custom-call | flops 16999999488 | bytes 1000 | tf_op jit(solution)/shard_map/middle/pallas_call | solution.py:136
  75.2 4.3 %collective-permute-start.24 = (bf16[2,256,640]{2,1,0:T(8,128)(2,1)S(1)}, bf16[2,256,640]{2,1,0:T(8,128)(2,1)S(1)}, u32[]{:S(2)}, u32[]{:S(2)}) collective-permute-start(bf16[2,256,640]{2,1,0:T(8,128)(2,1)S(1)} %bitcast.19), channel_id=1, source_target_pairs={{0,1},{1,2},{2,3},{4,5},{5,6},{6,7},{8,9},{9,10},{10,11},{12,13},{... | collective-permute-start | bytes 1966088 | tf_op jit(solution)/shard_map/ppermute | solution.py:752
  79.5 1.5 %collective-permute-start.25 = (bf16[2,256,640]{2,1,0:T(8,128)(2,1)S(1)}, bf16[2,256,640]{2,1,0:T(8,128)(2,1)S(1)}, u32[]{:S(2)}, u32[]{:S(2)}) collective-permute-start(bf16[2,256,640]{2,1,0:T(8,128)(2,1)S(1)} %bitcast.20), channel_id=1, source_target_pairs={{1,0},{2,1},{3,2},{5,4},{6,5},{7,6},{9,8},{10,9},{11,10},{13,12},{... | collective-permute-start | bytes 1966088 | tf_op jit(solution)/shard_map/ppermute | solution.py:756
  81.0 3.1 %conv_grad.1 = (f32[5,80,640]{2,1,0:T(8,128)S(1)}, f32[8,128]{1,0:T(8,128)S(1)}, f32[80,128]{1,0:T(8,128)S(1)}, bf16[432,640]{1,0:T(8,128)(2,1)S(1)}, bf16[432,6...) custom-call(bf16[528,1408]{1,0:T(8,128)(2,1)S(1)} %get-tuple-element.114.refs_0_.refs_4_, ...), custom_call_target="tpu_custom_call" | custom-call | flops 7000000000 | bytes 1000 | tf_op jit(solution)/shard_map/conv_grad/pallas_call | solution.py:136
  84.8 1.2 collective-permute-start.31
  86.0 1.8 %collective-permute-start.32 = (bf16[432,640]{1,0:T(8,128)(2,1)S(1)}, bf16[432,640]{1,0:T(8,128)(2,1)S(1)}, u32[]{:S(2)}, u32[]{:S(2)}) collective-permute-start(bf16[432,640]{1,0:T(8,128)(2,1)S(1)} %get-tuple-element.121), channel_id=1, source_target_pairs={{0,24},{4,28},{8,16},{12,20},{16,8},{20,12},{24,0},{28,4},{1,25},{... | collective-permute-start | bytes 1658888 | tf_op jit(solution)/shard_map/ppermute | solution.py:730
  87.7 6.0 %collective-permute-done.24.refs_14_ = bf16[2,256,640]{2,1,0:T(8,128)(2,1)S(1)} collective-permute-done((bf16[2,256,640]{2,1,0:T(8,128)(2,1)S(1)}, bf16[2,256,640]{2,1,0:T(8,128)(2,1)S(1)}, u32[]{:S(2)}, u32[]{:S(2)}) %collective-permute-start.24) | collective-permute-done | bytes 655392 | tf_op jit(solution)/shard_map/ppermute | solution.py:752
  93.7 4.2 %collective-permute-done.25.refs_16_ = bf16[2,256,640]{2,1,0:T(8,128)(2,1)S(1)} collective-permute-done((bf16[2,256,640]{2,1,0:T(8,128)(2,1)S(1)}, bf16[2,256,640]{2,1,0:T(8,128)(2,1)S(1)}, u32[]{:S(2)}, u32[]{:S(2)}) %collective-permute-start.25) | collective-permute-done | bytes 655392 | tf_op jit(solution)/shard_map/ppermute | solution.py:756
  97.9 9.2 %back.1 = (f32[4,160,768]{2,1,0:T(8,128)S(1)}, bf16[2,160,768]{2,1,0:T(8,128)(2,1)S(1)}, bf16[2,160,768]{2,1,0:T(8,128)(2,1)S(1)}, f32[512,1280]{1,0:T(8,128)S(1)}) custom-call(bf16[7,640,640]{2,1,0:T(8,128)(2,1)S(1)} %get-tuple-element.103.refs_0_, f32[512,640]{1,0:T(8,128)S(1)} %get-tuple-element.104.refs_1_, f32[512,640]{1,0:T(8,128)S(1)} %get-tuple-element.105.refs_2_, ...), custom_call_target="tpu_custom_call" | custom-call | flops 100000000 | bytes 1000 | tf_op jit(solution)/shard_map/back/pallas_call | solution.py:136
  107.6 1.4 collective-permute-done.33.refs_1_
  109.0 0.7 collective-permute-done.34.refs_2_
  111.1 1.6 %collective-permute-start.35 = (bf16[160,768]{1,0:T(8,128)(2,1)S(1)}, bf16[160,768]{1,0:T(8,128)(2,1)S(1)}, u32[]{:S(2)}, u32[]{:S(2)}) collective-permute-start(bf16[160,768]{1,0:T(8,128)(2,1)S(1)} %get-tuple-element.132), channel_id=1, source_target_pairs={{0,8},{4,12},{8,0},{12,4},{16,24},{20,28},{24,16},{28,20},{1,9},{5... | collective-permute-start | bytes 737288 | tf_op jit(solution)/shard_map/ppermute | solution.py:730
  113.2 1.5 %collective-permute-start.37 = (bf16[160,768]{1,0:T(8,128)(2,1)S(1)}, bf16[160,768]{1,0:T(8,128)(2,1)S(1)}, u32[]{:S(2)}, u32[]{:S(2)}) collective-permute-start(bf16[160,768]{1,0:T(8,128)(2,1)S(1)} %get-tuple-element.134), channel_id=1, source_target_pairs={{0,24},{4,28},{8,16},{12,20},{16,8},{20,12},{24,0},{28,4},{1,25},{... | collective-permute-start | bytes 737288 | tf_op jit(solution)/shard_map/ppermute | solution.py:730
  114.7 2.4 %collective-permute-start.41 = (bf16[128,640]{1,0:T(8,128)(2,1)S(1)}, bf16[128,640]{1,0:T(8,128)(2,1)S(1)}, u32[]{:S(2)}, u32[]{:S(2)}) collective-permute-start(bf16[128,640]{1,0:T(8,128)(2,1)S(1)} %get-tuple-element.148), channel_id=1, source_target_pairs={{0,1},{1,2},{2,3},{3,0},{4,5},{5,6},{6,7},{7,4},{8,9},{9,10},{10,1... | collective-permute-start | bytes 491528 | tf_op jit(solution)/shard_map/ppermute | solution.py:735
  117.0 2.1 %collective-permute-start.42 = (bf16[128,640]{1,0:T(8,128)(2,1)S(1)}, bf16[128,640]{1,0:T(8,128)(2,1)S(1)}, u32[]{:S(2)}, u32[]{:S(2)}) collective-permute-start(bf16[128,640]{1,0:T(8,128)(2,1)S(1)} %get-tuple-element.149), channel_id=1, source_target_pairs={{0,2},{1,3},{2,0},{3,1},{4,6},{5,7},{6,4},{7,5},{8,10},{9,11},{10,... | collective-permute-start | bytes 491528 | tf_op jit(solution)/shard_map/ppermute | solution.py:735
  119.2 0.9 collective-permute-done.35.refs_1_
  120.1 3.9 %collective-permute-start.43 = (bf16[128,640]{1,0:T(8,128)(2,1)S(1)}, bf16[128,640]{1,0:T(8,128)(2,1)S(1)}, u32[]{:S(2)}, u32[]{:S(2)}) collective-permute-start(bf16[128,640]{1,0:T(8,128)(2,1)S(1)} %get-tuple-element.150), channel_id=1, source_target_pairs={{0,3},{1,0},{2,1},{3,2},{4,7},{5,4},{6,5},{7,6},{8,11},{9,8},{10,9... | collective-permute-start | bytes 491528 | tf_op jit(solution)/shard_map/ppermute | solution.py:735
  124.0 2.8 %input.1 = (bf16[512,1280]{1,0:T(8,128)(2,1)}, f32[8,128]{1,0:T(8,128)S(1)}) custom-call(f32[512,1280]{1,0:T(8,128)S(1)} %get-tuple-element.116.refs_0_, f32[512,1280]{1,0:T(8,128)S(1)} %get-tuple-element.89.refs_0_.refs_4_.refs_1_, f32[512,128]{1,0:T(8,128)S(1)} %get-tuple-element.91.refs_4_.refs_2_, ...), custom_call_target="tpu_custom_call" | custom-call | flops 3000000000 | bytes 1000 | tf_op jit(solution)/shard_map/input/pallas_call | solution.py:136
  127.0 1.7 %collective-permute-start.39 = (bf16[40,768]{1,0:T(8,128)(2,1)S(1)}, bf16[40,768]{1,0:T(8,128)(2,1)S(1)}, u32[]{:S(2)}, u32[]{:S(2)}) collective-permute-start(bf16[40,768]{1,0:T(8,128)(2,1)S(1)} %get-tuple-element.138), channel_id=1, source_target_pairs={{0,2},{1,3},{2,0},{3,1},{4,6},{5,7},{6,4},{7,5},{8,10},{9,11},{10,... | collective-permute-start | bytes 184328 | tf_op jit(solution)/shard_map/ppermute | solution.py:735
  128.7 2.1 %collective-permute-start.40 = (bf16[40,768]{1,0:T(8,128)(2,1)S(1)}, bf16[40,768]{1,0:T(8,128)(2,1)S(1)}, u32[]{:S(2)}, u32[]{:S(2)}) collective-permute-start(bf16[40,768]{1,0:T(8,128)(2,1)S(1)} %get-tuple-element.139), channel_id=1, source_target_pairs={{0,3},{1,0},{2,1},{3,2},{4,7},{5,4},{6,5},{7,6},{8,11},{9,8},{10,9... | collective-permute-start | bytes 184328 | tf_op jit(solution)/shard_map/ppermute | solution.py:735
  130.8 1.2 end_b.1
  133.7 2.3 %collective-permute-done.39.refs_2_ = bf16[40,768]{1,0:T(8,128)(2,1)S(1)} collective-permute-done((bf16[40,768]{1,0:T(8,128)(2,1)S(1)}, bf16[40,768]{1,0:T(8,128)(2,1)S(1)}, u32[]{:S(2)}, u32[]{:S(2)}) %collective-permute-start.39) | collective-permute-done | bytes 61472 | tf_op jit(solution)/shard_map/ppermute | solution.py:735
  136.0 0.7 end_a.1
  (76 shorter events, 9.8 us)
Async XLA Ops:
  2.3 7.8 %collective-permute-start = (bf16[40,768]{1,0:T(8,128)(2,1)}, bf16[40,768]{1,0:T(8,128)(2,1)S(1)}, u32[]{:S(2)}, u32[]{:S(2)}) collective-permute-start(bf16[40,768]{1,0:T(8,128)(2,1)} %pack_a.1.refs_2_.refs_0_), channel_id=1, source_target_pairs={{0,1},{1,2},{2,3},{3,0},{4,5},{5,6},{6,7},{7,4},{8,9},{9,10},{10,1... | collective-permute-start | bytes 184328 | tf_op jit(solution)/shard_map/ppermute | solution.py:735
  5.4 7.1 %collective-permute-start.1 = (bf16[40,768]{1,0:T(8,128)(2,1)}, bf16[40,768]{1,0:T(8,128)(2,1)S(1)}, u32[]{:S(2)}, u32[]{:S(2)}) collective-permute-start(bf16[40,768]{1,0:T(8,128)(2,1)} %pack_a.1.refs_2_.refs_0_), channel_id=1, source_target_pairs={{0,2},{1,3},{2,0},{3,1},{4,6},{5,7},{6,4},{7,5},{8,10},{9,11},{10,... | collective-permute-start | bytes 184328 | tf_op jit(solution)/shard_map/ppermute | solution.py:735
  8.0 4.8 %collective-permute-start.2 = (bf16[40,768]{1,0:T(8,128)(2,1)}, bf16[40,768]{1,0:T(8,128)(2,1)S(1)}, u32[]{:S(2)}, u32[]{:S(2)}) collective-permute-start(bf16[40,768]{1,0:T(8,128)(2,1)} %pack_a.1.refs_2_.refs_0_), channel_id=1, source_target_pairs={{0,3},{1,0},{2,1},{3,2},{4,7},{5,4},{6,5},{7,6},{8,11},{9,8},{10,9... | collective-permute-start | bytes 184328 | tf_op jit(solution)/shard_map/ppermute | solution.py:735
  13.7 7.3 %collective-permute-start.3 = (bf16[160,768]{1,0:T(8,128)(2,1)S(1)}, bf16[160,768]{1,0:T(8,128)(2,1)S(1)}, u32[]{:S(2)}, u32[]{:S(2)}) collective-permute-start(bf16[160,768]{1,0:T(8,128)(2,1)S(1)} %line_a.1.refs_2_), channel_id=1, source_target_pairs={{0,8},{4,12},{8,0},{12,4},{16,24},{20,28},{24,16},{28,20},{1,9},{5... | collective-permute-start | bytes 737288 | tf_op jit(solution)/shard_map/ppermute | solution.py:730
  15.6 16.3 %collective-permute-start.10 = (bf16[140,640]{1,0:T(8,128)(2,1)S(1)}, bf16[140,640]{1,0:T(8,128)(2,1)S(1)}, u32[]{:S(2)}, u32[]{:S(2)}) collective-permute-start(bf16[140,640]{1,0:T(8,128)(2,1)S(1)} %pack_b.1.refs_1_.refs_0_), channel_id=1, source_target_pairs={{0,1},{1,2},{2,3},{3,0},{4,5},{5,6},{6,7},{7,4},{8,9},{9,10},{10,1... | collective-permute-start | bytes 537608 | tf_op jit(solution)/shard_map/ppermute | solution.py:735
  17.0 14.9 %collective-permute-start.11 = (bf16[140,640]{1,0:T(8,128)(2,1)S(1)}, bf16[140,640]{1,0:T(8,128)(2,1)S(1)}, u32[]{:S(2)}, u32[]{:S(2)}) collective-permute-start(bf16[140,640]{1,0:T(8,128)(2,1)S(1)} %pack_b.1.refs_1_.refs_0_), channel_id=1, source_target_pairs={{0,2},{1,3},{2,0},{3,1},{4,6},{5,7},{6,4},{7,5},{8,10},{9,11},{10,... | collective-permute-start | bytes 537608 | tf_op jit(solution)/shard_map/ppermute | solution.py:735
  19.1 13.3 %collective-permute-start.12 = (bf16[140,640]{1,0:T(8,128)(2,1)S(1)}, bf16[140,640]{1,0:T(8,128)(2,1)S(1)}, u32[]{:S(2)}, u32[]{:S(2)}) collective-permute-start(bf16[140,640]{1,0:T(8,128)(2,1)S(1)} %pack_b.1.refs_1_.refs_0_), channel_id=1, source_target_pairs={{0,3},{1,0},{2,1},{3,2},{4,7},{5,4},{6,5},{7,6},{8,11},{9,8},{10,9... | collective-permute-start | bytes 537608 | tf_op jit(solution)/shard_map/ppermute | solution.py:735
  19.5 11.9 %collective-permute-start.4 = (bf16[160,768]{1,0:T(8,128)(2,1)S(1)}, bf16[160,768]{1,0:T(8,128)(2,1)S(1)}, u32[]{:S(2)}, u32[]{:S(2)}) collective-permute-start(bf16[160,768]{1,0:T(8,128)(2,1)S(1)} %line_a.1.refs_2_), channel_id=1, source_target_pairs={{0,16},{4,20},{8,24},{12,28},{16,0},{20,4},{24,8},{28,12},{1,17},{... | collective-permute-start | bytes 737288 | tf_op jit(solution)/shard_map/ppermute | solution.py:730
  21.1 10.3 %collective-permute-start.5 = (bf16[160,768]{1,0:T(8,128)(2,1)S(1)}, bf16[160,768]{1,0:T(8,128)(2,1)S(1)}, u32[]{:S(2)}, u32[]{:S(2)}) collective-permute-start(bf16[160,768]{1,0:T(8,128)(2,1)S(1)} %line_a.1.refs_2_), channel_id=1, source_target_pairs={{0,24},{4,28},{8,16},{12,20},{16,8},{20,12},{24,0},{28,4},{1,25},{... | collective-permute-start | bytes 737288 | tf_op jit(solution)/shard_map/ppermute | solution.py:730
  31.4 2.2 %collective-permute-start.6 = (bf16[160,768]{1,0:T(8,128)(2,1)S(1)}, bf16[160,768]{1,0:T(8,128)(2,1)S(1)}, u32[]{:S(2)}, u32[]{:S(2)}) collective-permute-start(bf16[160,768]{1,0:T(8,128)(2,1)S(1)} %line_a.1.refs_2_), channel_id=1, source_target_pairs={{0,4},{4,0},{8,12},{12,8},{16,20},{20,16},{24,28},{28,24},{1,5},{5... | collective-permute-start | bytes 737288 | tf_op jit(solution)/shard_map/ppermute | solution.py:730
  31.4 3.5 %collective-permute-start.7 = (bf16[160,768]{1,0:T(8,128)(2,1)S(1)}, bf16[160,768]{1,0:T(8,128)(2,1)S(1)}, u32[]{:S(2)}, u32[]{:S(2)}) collective-permute-start(bf16[160,768]{1,0:T(8,128)(2,1)S(1)} %collective-permute-done.3.refs_3_), channel_id=1, source_target_pairs={{0,4},{4,0},{8,12},{12,8},{16,20},{20,16},{24,28},{28,24},{1,5},{5... | collective-permute-start | bytes 737288 | tf_op jit(solution)/shard_map/ppermute | solution.py:730
  31.9 3.0 %collective-permute-start.8 = (bf16[160,768]{1,0:T(8,128)(2,1)S(1)}, bf16[160,768]{1,0:T(8,128)(2,1)S(1)}, u32[]{:S(2)}, u32[]{:S(2)}) collective-permute-start(bf16[160,768]{1,0:T(8,128)(2,1)S(1)} %collective-permute-done.4.refs_4_), channel_id=1, source_target_pairs={{0,4},{4,0},{8,12},{12,8},{16,20},{20,16},{24,28},{28,24},{1,5},{5... | collective-permute-start | bytes 737288 | tf_op jit(solution)/shard_map/ppermute | solution.py:730
  31.9 2.9 %collective-permute-start.9 = (bf16[160,768]{1,0:T(8,128)(2,1)S(1)}, bf16[160,768]{1,0:T(8,128)(2,1)S(1)}, u32[]{:S(2)}, u32[]{:S(2)}) collective-permute-start(bf16[160,768]{1,0:T(8,128)(2,1)S(1)} %collective-permute-done.5.refs_5_), channel_id=1, source_target_pairs={{0,4},{4,0},{8,12},{12,8},{16,20},{20,16},{24,28},{28,24},{1,5},{5... | collective-permute-start | bytes 737288 | tf_op jit(solution)/shard_map/ppermute | solution.py:730
  32.7 18.1 %collective-permute-start.15 = (bf16[7,80,640]{2,1,0:T(8,128)(2,1)S(1)}, bf16[7,80,640]{2,1,0:T(8,128)(2,1)S(1)}, u32[]{:S(2)}, u32[]{:S(2)}) collective-permute-start(bf16[7,80,640]{2,1,0:T(8,128)(2,1)S(1)} %line_b.1.refs_10_.refs_11_), channel_id=1, source_target_pairs={{0,8},{4,12},{8,0},{12,4},{16,24},{20,28},{24,16},{28,20},{1,9},{5... | collective-permute-start | bytes 2150408 | tf_op jit(solution)/shard_map/ppermute | solution.py:730
  33.6 18.8 %collective-permute-start.16 = (bf16[7,80,640]{2,1,0:T(8,128)(2,1)S(1)}, bf16[7,80,640]{2,1,0:T(8,128)(2,1)S(1)}, u32[]{:S(2)}, u32[]{:S(2)}) collective-permute-start(bf16[7,80,640]{2,1,0:T(8,128)(2,1)S(1)} %line_b.1.refs_10_.refs_11_), channel_id=1, source_target_pairs={{0,16},{4,20},{8,24},{12,28},{16,0},{20,4},{24,8},{28,12},{1,17},{... | collective-permute-start | bytes 2150408 | tf_op jit(solution)/shard_map/ppermute | solution.py:730
  34.9 28.5 %copy-start.7 = (bf16[30]{0:T(256)(128)(2,1)S(1)}, bf16[30]{0:T(256)(128)(2,1)}, u32[]{:S(2)}) copy-start(bf16[30]{0:T(256)(128)(2,1)} %param.32) | copy-start | bytes 184
  34.9 30.2 %copy-start.4 = (s32[2,256]{1,0:T(2,128)S(1)}, s32[2,256]{1,0:T(2,128)}, u32[]{:S(2)}) copy-start(s32[2,256]{1,0:T(2,128)} %refs_4_.3) | copy-start | bytes 6148
  34.9 30.2 %copy-start.5 = (s32[2,153]{1,0:T(2,128)S(1)}, s32[2,153]{1,0:T(2,128)}, u32[]{:S(2)}) copy-start(s32[2,153]{1,0:T(2,128)} %refs_5_.3) | copy-start | bytes 3676
  34.9 30.2 %copy-start.6 = (s32[2,153]{1,0:T(2,128)S(1)}, s32[2,153]{1,0:T(2,128)}, u32[]{:S(2)}) copy-start(s32[2,153]{1,0:T(2,128)} %refs_6_.3) | copy-start | bytes 3676
  39.6 19.7 %collective-permute-start.13 = (bf16[2,256,640]{2,1,0:T(8,128)(2,1)S(1)}, bf16[2,256,640]{2,1,0:T(8,128)(2,1)S(1)}, u32[]{:S(2)}, u32[]{:S(2)}) collective-permute-start(bf16[2,256,640]{2,1,0:T(8,128)(2,1)S(1)} %bitcast.24), channel_id=1, source_target_pairs={{0,1},{1,2},{2,3},{4,5},{5,6},{6,7},{8,9},{9,10},{10,11},{12,13},{... | collective-permute-start | bytes 1966088 | tf_op jit(solution)/shard_map/ppermute | solution.py:752
  44.0 17.7 %collective-permute-start.14 = (bf16[2,256,640]{2,1,0:T(8,128)(2,1)S(1)}, bf16[2,256,640]{2,1,0:T(8,128)(2,1)S(1)}, u32[]{:S(2)}, u32[]{:S(2)}) collective-permute-start(bf16[2,256,640]{2,1,0:T(8,128)(2,1)S(1)} %bitcast.25), channel_id=1, source_target_pairs={{1,0},{2,1},{3,2},{5,4},{6,5},{7,6},{9,8},{10,9},{11,10},{13,12},{... | collective-permute-start | bytes 1966088 | tf_op jit(solution)/shard_map/ppermute | solution.py:756
  50.9 8.5 %collective-permute-start.17 = (bf16[3,80,640]{2,1,0:T(8,128)(2,1)S(1)}, bf16[3,80,640]{2,1,0:T(8,128)(2,1)S(1)}, u32[]{:S(2)}, u32[]{:S(2)}) collective-permute-start(bf16[3,80,640]{2,1,0:T(8,128)(2,1)S(1)} %slice.24), channel_id=1, source_target_pairs={{0,16},{4,20},{8,24},{12,28},{16,0},{20,4},{24,8},{28,12},{1,17},{... | collective-permute-start | bytes 921608 | tf_op jit(solution)/shard_map/ppermute | solution.py:730
  52.5 10.4 %collective-permute-start.18 = (bf16[4,80,640]{2,1,0:T(8,128)(2,1)S(1)}, bf16[4,80,640]{2,1,0:T(8,128)(2,1)S(1)}, u32[]{:S(2)}, u32[]{:S(2)}) collective-permute-start(bf16[4,80,640]{2,1,0:T(8,128)(2,1)S(1)} %slice.25), channel_id=1, source_target_pairs={{0,8},{4,12},{8,0},{12,4},{16,24},{20,28},{24,16},{28,20},{1,9},{5... | collective-permute-start | bytes 1228808 | tf_op jit(solution)/shard_map/ppermute | solution.py:730
  53.1 10.3 %collective-permute-start.19 = (bf16[7,80,640]{2,1,0:T(8,128)(2,1)S(1)}, bf16[7,80,640]{2,1,0:T(8,128)(2,1)S(1)}, u32[]{:S(2)}, u32[]{:S(2)}) collective-permute-start(bf16[7,80,640]{2,1,0:T(8,128)(2,1)S(1)} %line_b.1.refs_10_.refs_11_), channel_id=1, source_target_pairs={{0,4},{4,0},{8,12},{12,8},{16,20},{20,16},{24,28},{28,24},{1,5},{5... | collective-permute-start | bytes 2150408 | tf_op jit(solution)/shard_map/ppermute | solution.py:730
  59.3 4.1 %collective-permute-start.20 = (bf16[7,80,640]{2,1,0:T(8,128)(2,1)S(1)}, bf16[7,80,640]{2,1,0:T(8,128)(2,1)S(1)}, u32[]{:S(2)}, u32[]{:S(2)}) collective-permute-start(bf16[7,80,640]{2,1,0:T(8,128)(2,1)S(1)} %collective-permute-done.15.refs_12_), channel_id=1, source_target_pairs={{0,4},{4,0},{8,12},{12,8},{16,20},{20,16},{24,28},{28,24},{1,5},{5... | collective-permute-start | bytes 2150408 | tf_op jit(solution)/shard_map/ppermute | solution.py:730
  59.3 4.1 %collective-permute-start.21 = (bf16[7,80,640]{2,1,0:T(8,128)(2,1)S(1)}, bf16[7,80,640]{2,1,0:T(8,128)(2,1)S(1)}, u32[]{:S(2)}, u32[]{:S(2)}) collective-permute-start(bf16[7,80,640]{2,1,0:T(8,128)(2,1)S(1)} %collective-permute-done.16.refs_13_), channel_id=1, source_target_pairs={{0,4},{4,0},{8,12},{12,8},{16,20},{20,16},{24,28},{28,24},{1,5},{5... | collective-permute-start | bytes 2150408 | tf_op jit(solution)/shard_map/ppermute | solution.py:730
  62.9 2.2 %collective-permute-start.23 = (bf16[4,80,640]{2,1,0:T(8,128)(2,1)S(1)}, bf16[4,80,640]{2,1,0:T(8,128)(2,1)S(1)}, u32[]{:S(2)}, u32[]{:S(2)}) collective-permute-start(bf16[4,80,640]{2,1,0:T(8,128)(2,1)S(1)} %collective-permute-done.18.refs_15_), channel_id=1, source_target_pairs={{0,4},{4,0},{8,12},{12,8},{16,20},{20,16},{24,28},{28,24},{1,5},{5... | collective-permute-start | bytes 1228808 | tf_op jit(solution)/shard_map/ppermute | solution.py:730
  62.9 2.2 %collective-permute-start.22 = (bf16[3,80,640]{2,1,0:T(8,128)(2,1)S(1)}, bf16[3,80,640]{2,1,0:T(8,128)(2,1)S(1)}, u32[]{:S(2)}, u32[]{:S(2)}) collective-permute-start(bf16[3,80,640]{2,1,0:T(8,128)(2,1)S(1)} %collective-permute-done.17.refs_14_), channel_id=1, source_target_pairs={{0,4},{4,0},{8,12},{12,8},{16,20},{20,16},{24,28},{28,24},{1,5},{5... | collective-permute-start | bytes 921608 | tf_op jit(solution)/shard_map/ppermute | solution.py:730
  74.1 7.0 %collective-permute-start.26 = (bf16[528,1408]{1,0:T(8,128)(2,1)S(1)}, bf16[528,1408]{1,0:T(8,128)(2,1)S(1)}, u32[]{:S(2)}, u32[]{:S(2)}) collective-permute-start(bf16[528,1408]{1,0:T(8,128)(2,1)S(1)} %get-tuple-element.114.refs_0_.refs_4_), channel_id=1, source_target_pairs={{0,4},{4,0},{8,12},{12,8},{16,20},{20,16},{24,28},{28,24},{1,5},{5... | collective-permute-start | bytes 4460552 | tf_op jit(solution)/shard_map/ppermute | solution.py:730
  74.3 5.2 %collective-permute-start.28 = (bf16[2,256,640]{2,1,0:T(8,128)(2,1)S(1)}, bf16[2,256,640]{2,1,0:T(8,128)(2,1)S(1)}, u32[]{:S(2)}, u32[]{:S(2)}) collective-permute-start(bf16[2,256,640]{2,1,0:T(8,128)(2,1)S(1)} %bitcast.27), channel_id=1, source_target_pairs={{0,4},{4,0},{8,12},{12,8},{16,20},{20,16},{24,28},{28,24},{1,5},{5... | collective-permute-start | bytes 1966088 | tf_op jit(solution)/shard_map/ppermute | solution.py:730
  74.7 6.4 %collective-permute-start.27 = (bf16[2,256,640]{2,1,0:T(8,128)(2,1)S(1)}, bf16[2,256,640]{2,1,0:T(8,128)(2,1)S(1)}, u32[]{:S(2)}, u32[]{:S(2)}) collective-permute-start(bf16[2,256,640]{2,1,0:T(8,128)(2,1)S(1)} %collective-permute-done.13.refs_8_.refs_3_), channel_id=1, source_target_pairs={{0,4},{4,0},{8,12},{12,8},{16,20},{20,16},{24,28},{28,24},{1,5},{5... | collective-permute-start | bytes 1966088 | tf_op jit(solution)/shard_map/ppermute | solution.py:730
  74.8 6.2 %collective-permute-start.29 = (bf16[2,256,640]{2,1,0:T(8,128)(2,1)S(1)}, bf16[2,256,640]{2,1,0:T(8,128)(2,1)S(1)}, u32[]{:S(2)}, u32[]{:S(2)}) collective-permute-start(bf16[2,256,640]{2,1,0:T(8,128)(2,1)S(1)} %collective-permute-done.14.refs_10_.refs_5_), channel_id=1, source_target_pairs={{0,4},{4,0},{8,12},{12,8},{16,20},{20,16},{24,28},{28,24},{1,5},{5... | collective-permute-start | bytes 1966088 | tf_op jit(solution)/shard_map/ppermute | solution.py:730
  75.2 18.5 %collective-permute-start.24 = (bf16[2,256,640]{2,1,0:T(8,128)(2,1)S(1)}, bf16[2,256,640]{2,1,0:T(8,128)(2,1)S(1)}, u32[]{:S(2)}, u32[]{:S(2)}) collective-permute-start(bf16[2,256,640]{2,1,0:T(8,128)(2,1)S(1)} %bitcast.19), channel_id=1, source_target_pairs={{0,1},{1,2},{2,3},{4,5},{5,6},{6,7},{8,9},{9,10},{10,11},{12,13},{... | collective-permute-start | bytes 1966088 | tf_op jit(solution)/shard_map/ppermute | solution.py:752
  79.5 18.4 %collective-permute-start.25 = (bf16[2,256,640]{2,1,0:T(8,128)(2,1)S(1)}, bf16[2,256,640]{2,1,0:T(8,128)(2,1)S(1)}, u32[]{:S(2)}, u32[]{:S(2)}) collective-permute-start(bf16[2,256,640]{2,1,0:T(8,128)(2,1)S(1)} %bitcast.20), channel_id=1, source_target_pairs={{1,0},{2,1},{3,2},{5,4},{6,5},{7,6},{9,8},{10,9},{11,10},{13,12},{... | collective-permute-start | bytes 1966088 | tf_op jit(solution)/shard_map/ppermute | solution.py:756
  84.2 25.9 %collective-permute-start.30 = (bf16[432,640]{1,0:T(8,128)(2,1)S(1)}, bf16[432,640]{1,0:T(8,128)(2,1)S(1)}, u32[]{:S(2)}, u32[]{:S(2)}) collective-permute-start(bf16[432,640]{1,0:T(8,128)(2,1)S(1)} %get-tuple-element.119), channel_id=1, source_target_pairs={{0,8},{4,12},{8,0},{12,4},{16,24},{20,28},{24,16},{28,20},{1,9},{5... | collective-permute-start | bytes 1658888 | tf_op jit(solution)/shard_map/ppermute | solution.py:730
  84.8 25.9 %collective-permute-start.31 = (bf16[432,640]{1,0:T(8,128)(2,1)S(1)}, bf16[432,640]{1,0:T(8,128)(2,1)S(1)}, u32[]{:S(2)}, u32[]{:S(2)}) collective-permute-start(bf16[432,640]{1,0:T(8,128)(2,1)S(1)} %get-tuple-element.120), channel_id=1, source_target_pairs={{0,16},{4,20},{8,24},{12,28},{16,0},{20,4},{24,8},{28,12},{1,17},{... | collective-permute-start | bytes 1658888 | tf_op jit(solution)/shard_map/ppermute | solution.py:730
  86.0 24.7 %collective-permute-start.32 = (bf16[432,640]{1,0:T(8,128)(2,1)S(1)}, bf16[432,640]{1,0:T(8,128)(2,1)S(1)}, u32[]{:S(2)}, u32[]{:S(2)}) collective-permute-start(bf16[432,640]{1,0:T(8,128)(2,1)S(1)} %get-tuple-element.121), channel_id=1, source_target_pairs={{0,24},{4,28},{8,16},{12,20},{16,8},{20,12},{24,0},{28,4},{1,25},{... | collective-permute-start | bytes 1658888 | tf_op jit(solution)/shard_map/ppermute | solution.py:730
  107.0 1.9 %collective-permute-start.33 = (bf16[2,160,768]{2,1,0:T(8,128)(2,1)S(1)}, bf16[2,160,768]{2,1,0:T(8,128)(2,1)S(1)}, u32[]{:S(2)}, u32[]{:S(2)}) collective-permute-start(bf16[2,160,768]{2,1,0:T(8,128)(2,1)S(1)} %get-tuple-element.123), channel_id=1, source_target_pairs={{0,4},{4,0},{8,12},{12,8},{16,20},{20,16},{24,28},{28,24},{1,5},{5... | collective-permute-start | bytes 1474568 | tf_op jit(solution)/shard_map/ppermute | solution.py:730
  107.1 2.6 %collective-permute-start.34 = (bf16[2,160,768]{2,1,0:T(8,128)(2,1)S(1)}, bf16[2,160,768]{2,1,0:T(8,128)(2,1)S(1)}, u32[]{:S(2)}, u32[]{:S(2)}) collective-permute-start(bf16[2,160,768]{2,1,0:T(8,128)(2,1)S(1)} %get-tuple-element.124), channel_id=1, source_target_pairs={{0,4},{4,0},{8,12},{12,8},{16,20},{20,16},{24,28},{28,24},{1,5},{5... | collective-permute-start | bytes 1474568 | tf_op jit(solution)/shard_map/ppermute | solution.py:730
  111.1 8.9 %collective-permute-start.35 = (bf16[160,768]{1,0:T(8,128)(2,1)S(1)}, bf16[160,768]{1,0:T(8,128)(2,1)S(1)}, u32[]{:S(2)}, u32[]{:S(2)}) collective-permute-start(bf16[160,768]{1,0:T(8,128)(2,1)S(1)} %get-tuple-element.132), channel_id=1, source_target_pairs={{0,8},{4,12},{8,0},{12,4},{16,24},{20,28},{24,16},{28,20},{1,9},{5... | collective-permute-start | bytes 737288 | tf_op jit(solution)/shard_map/ppermute | solution.py:730
  112.7 14.1 %collective-permute-start.36 = (bf16[160,768]{1,0:T(8,128)(2,1)S(1)}, bf16[160,768]{1,0:T(8,128)(2,1)S(1)}, u32[]{:S(2)}, u32[]{:S(2)}) collective-permute-start(bf16[160,768]{1,0:T(8,128)(2,1)S(1)} %get-tuple-element.133), channel_id=1, source_target_pairs={{0,16},{4,20},{8,24},{12,28},{16,0},{20,4},{24,8},{28,12},{1,17},{... | collective-permute-start | bytes 737288 | tf_op jit(solution)/shard_map/ppermute | solution.py:730
  113.2 13.6 %collective-permute-start.37 = (bf16[160,768]{1,0:T(8,128)(2,1)S(1)}, bf16[160,768]{1,0:T(8,128)(2,1)S(1)}, u32[]{:S(2)}, u32[]{:S(2)}) collective-permute-start(bf16[160,768]{1,0:T(8,128)(2,1)S(1)} %get-tuple-element.134), channel_id=1, source_target_pairs={{0,24},{4,28},{8,16},{12,20},{16,8},{20,12},{24,0},{28,4},{1,25},{... | collective-permute-start | bytes 737288 | tf_op jit(solution)/shard_map/ppermute | solution.py:730
  114.7 14.0 %collective-permute-start.41 = (bf16[128,640]{1,0:T(8,128)(2,1)S(1)}, bf16[128,640]{1,0:T(8,128)(2,1)S(1)}, u32[]{:S(2)}, u32[]{:S(2)}) collective-permute-start(bf16[128,640]{1,0:T(8,128)(2,1)S(1)} %get-tuple-element.148), channel_id=1, source_target_pairs={{0,1},{1,2},{2,3},{3,0},{4,5},{5,6},{6,7},{7,4},{8,9},{9,10},{10,1... | collective-permute-start | bytes 491528 | tf_op jit(solution)/shard_map/ppermute | solution.py:735
  117.0 13.8 %collective-permute-start.42 = (bf16[128,640]{1,0:T(8,128)(2,1)S(1)}, bf16[128,640]{1,0:T(8,128)(2,1)S(1)}, u32[]{:S(2)}, u32[]{:S(2)}) collective-permute-start(bf16[128,640]{1,0:T(8,128)(2,1)S(1)} %get-tuple-element.149), channel_id=1, source_target_pairs={{0,2},{1,3},{2,0},{3,1},{4,6},{5,7},{6,4},{7,5},{8,10},{9,11},{10,... | collective-permute-start | bytes 491528 | tf_op jit(solution)/shard_map/ppermute | solution.py:735
  120.1 10.8 %collective-permute-start.43 = (bf16[128,640]{1,0:T(8,128)(2,1)S(1)}, bf16[128,640]{1,0:T(8,128)(2,1)S(1)}, u32[]{:S(2)}, u32[]{:S(2)}) collective-permute-start(bf16[128,640]{1,0:T(8,128)(2,1)S(1)} %get-tuple-element.150), channel_id=1, source_target_pairs={{0,3},{1,0},{2,1},{3,2},{4,7},{5,4},{6,5},{7,6},{8,11},{9,8},{10,9... | collective-permute-start | bytes 491528 | tf_op jit(solution)/shard_map/ppermute | solution.py:735
  126.9 6.8 %collective-permute-start.38 = (bf16[40,768]{1,0:T(8,128)(2,1)S(1)}, bf16[40,768]{1,0:T(8,128)(2,1)S(1)}, u32[]{:S(2)}, u32[]{:S(2)}) collective-permute-start(bf16[40,768]{1,0:T(8,128)(2,1)S(1)} %get-tuple-element.137), channel_id=1, source_target_pairs={{0,1},{1,2},{2,3},{3,0},{4,5},{5,6},{6,7},{7,4},{8,9},{9,10},{10,1... | collective-permute-start | bytes 184328 | tf_op jit(solution)/shard_map/ppermute | solution.py:735
  127.0 9.0 %collective-permute-start.39 = (bf16[40,768]{1,0:T(8,128)(2,1)S(1)}, bf16[40,768]{1,0:T(8,128)(2,1)S(1)}, u32[]{:S(2)}, u32[]{:S(2)}) collective-permute-start(bf16[40,768]{1,0:T(8,128)(2,1)S(1)} %get-tuple-element.138), channel_id=1, source_target_pairs={{0,2},{1,3},{2,0},{3,1},{4,6},{5,7},{6,4},{7,5},{8,10},{9,11},{10,... | collective-permute-start | bytes 184328 | tf_op jit(solution)/shard_map/ppermute | solution.py:735
  128.7 7.3 %collective-permute-start.40 = (bf16[40,768]{1,0:T(8,128)(2,1)S(1)}, bf16[40,768]{1,0:T(8,128)(2,1)S(1)}, u32[]{:S(2)}, u32[]{:S(2)}) collective-permute-start(bf16[40,768]{1,0:T(8,128)(2,1)S(1)} %get-tuple-element.139), channel_id=1, source_target_pairs={{0,3},{1,0},{2,1},{3,2},{4,7},{5,4},{6,5},{7,6},{8,11},{9,8},{10,9... | collective-permute-start | bytes 184328 | tf_op jit(solution)/shard_map/ppermute | solution.py:735
  (4 other events, 34.3 us)
